TPU v7x, 32 devices: a whole 2x2x4 slice. The times are simulated.
32 devices in a mesh: mach: 2 (over x), panel: 16 (over z, y, core).
Axes of the slice: x: 2, y: 2, z: 4, core: 2. Of those that a mesh axis runs over, the one named last changes fastest.
Arguments:
- adjoint: bfloat16 [2, 128, 4, 128], P('mach', 'panel'), may hold values from -6 to 6
- near_blocks: bfloat16 [2, 128, 8, 128, 128], P('mach', 'panel'), may hold values from -0.1875 to 0.1875
- pattern: int32 [128, 8], P('panel'), may hold values from 0 to 127, as said below
- trim_mask: int32 [2, 4], P('mach'), may hold values 0 or 1
- spline_blocks: bfloat16 [128, 6, 128, 128], P('panel'), may hold values from -0.21875 to 0.21875
- spline_owner: int32 [128, 6], P('panel'), may hold values from 0 to 15, all different within a row; in each aligned block of 8 rows (0 to 7, 8 to 15, ...) at most 6 rows name the same one
- spline_local: int32 [128, 6], P('panel'), may hold values from 0 to 7
- struct_inverse: bfloat16 [128, 128, 128], P('panel'), may hold values from -0.375 to 0.375
Outputs:
- panel_loads: float32 [2, 128, 4, 128], P('mach', 'panel')
- struct_adjoint: float32 [128, 4, 128], P('panel')
Inputs may be any that keep to these rules, and one draw needn't show every extreme that they name: `pattern`: entry 0 of row i is i itself; entry 1 is the mirror block (i + 64) mod 128; every other entry lies within 8 blocks of its row, and each row has one entry exactly 8 blocks away unless that falls outside the grid, where it is clipped to the end. `spline_owner`: the targets of one row are different owners; among the rows of one device no owner is named more than 6 times, a bound that some block reaches.
All inputs are finite; a program needn't handle non-finite values. No bound on the sum of `trim_mask` on one device may be relied on, other than what follows from the above.
Results may differ from a plain program's by a relative error of at most 0.004.
Values may be sent and summed in bfloat16 or wider, within the bound.
No kernel may reach another device: no remote copies, remote signals or barrier semaphores. Data moves between devices by JAX's collectives and lax.ppermute only.
A program may use at most 64 MiB of HBM per device.

v0:
```python
import jax
import jax.numpy as jnp
from jax import lax
from jax.sharding import PartitionSpec as P


def with_halo(block, sides, width):
    for axis, dim in sides:
        count = lax.axis_size(axis)
        forward = [(i, i + 1) for i in range(count - 1)]
        backward = [(target, source) for source, target in forward]
        low = lax.ppermute(
            lax.slice_in_dim(block, block.shape[dim] - width, None, axis=dim), axis, forward
        )
        high = lax.ppermute(lax.slice_in_dim(block, 0, width, axis=dim), axis, backward)
        block = jnp.concatenate([low, block, high], axis=dim)
    return block


def shifted(value, axis, steps):
    count = lax.axis_size(axis)
    pairs = [(source, (source + steps) % count) for source in range(count)]
    return lax.ppermute(value, axis, pairs)


def pack_rows(flat_rows, owners_flat, locals_flat, keep, slot_index, owner_count, slots):
    destination = jnp.where(keep, owners_flat * slots + slot_index, -1)
    place_int = (
        destination[:, None] == jnp.arange(owner_count * slots, dtype=jnp.int32)[None, :]
    ).astype(jnp.int32)
    send_loads = jnp.dot(
        place_int.astype(jnp.float32).T,
        flat_rows,
        precision=lax.Precision.HIGHEST,
        preferred_element_type=jnp.float32,
    )
    send_loads = send_loads.reshape(owner_count, slots, flat_rows.shape[1])
    send_index = (jnp.sum(place_int * (locals_flat + 1)[:, None], axis=0) - 1).reshape(
        owner_count, slots
    )
    return (send_loads, send_index)


def on_device(
    adjoint,
    near_blocks,
    pattern,
    trim_mask,
    spline_blocks,
    spline_owner,
    spline_local,
    struct_inverse,
):
    block_count = adjoint.shape[1]
    rhs_count = adjoint.shape[2]
    width = adjoint.shape[3]
    owner_count = lax.axis_size("panel")
    spline_count = spline_blocks.shape[1]
    capacity = max(2, 2 * block_count * spline_count // owner_count)
    window = with_halo(adjoint[0], (("panel", 0),), block_count)
    half_way = owner_count // 2
    mirrored = shifted(adjoint[0], "panel", half_way)
    pool = jnp.concatenate([window, mirrored], axis=0)
    here = lax.axis_index("panel")
    mirror_device = (here + half_way) % owner_count
    relative = pattern - (here * block_count - block_count)
    from_mirror = pattern // block_count == mirror_device
    lookup = jnp.where(from_mirror, 3 * block_count + pattern % block_count, relative)
    picked = jnp.take(pool, lookup, axis=0)
    near = jnp.einsum("bkrp,bkpq->brq", picked, near_blocks[0], preferred_element_type=jnp.float32)
    loads = near * trim_mask[0].astype(jnp.float32)[None, :, None]
    rounded = loads.astype(jnp.bfloat16)
    owners_flat = spline_owner.reshape(-1)
    locals_flat = spline_local.reshape(-1)
    owner_hits = (owners_flat[:, None] == jnp.arange(owner_count, dtype=jnp.int32)[None, :]).astype(
        jnp.int32
    )
    earlier = jnp.cumsum(owner_hits, axis=0) - owner_hits
    slot_index = jnp.sum(earlier * owner_hits, axis=1)
    contrib = jnp.einsum(
        "brp,bspq->bsrq", rounded, spline_blocks, preferred_element_type=jnp.float32
    )
    flat_rows = contrib.reshape(block_count * spline_count, rhs_count * width)
    keep = slot_index >= 0
    send_loads, send_index = pack_rows(
        flat_rows, owners_flat, locals_flat, keep, slot_index, owner_count, capacity
    )
    got_loads, got_index = (
        lax.all_to_all(send_loads, "panel", split_axis=0, concat_axis=0, tiled=True),
        lax.all_to_all(send_index, "panel", split_axis=0, concat_axis=0, tiled=True),
    )
    struct_count = struct_inverse.shape[0]
    pick_rows = (
        got_index.reshape(-1)[None, :] == jnp.arange(struct_count, dtype=jnp.int32)[:, None]
    ).astype(jnp.float32)
    mine = jnp.dot(
        pick_rows,
        got_loads.reshape(owner_count * capacity, rhs_count * width),
        precision=lax.Precision.HIGHEST,
        preferred_element_type=jnp.float32,
    )
    total = lax.psum(mine, "mach")
    struct_rounded = total.reshape(struct_count, rhs_count, width).astype(jnp.bfloat16)
    struct_adjoint = jnp.einsum(
        "trp,tpq->trq", struct_rounded, struct_inverse, preferred_element_type=jnp.float32
    )
    return (loads[None], struct_adjoint)


def solution(mesh):
    in_specs = (
        P("mach", "panel", None, None),
        P("mach", "panel", None, None, None),
        P("panel", None),
        P("mach", None),
        P("panel", None, None, None),
        P("panel", None),
        P("panel", None),
        P("panel", None, None),
    )
    out_specs = (P("mach", "panel", None, None), P("panel", None, None))
    return jax.shard_map(
        on_device, mesh=mesh, in_specs=in_specs, out_specs=out_specs, check_vma=False
    )
```

profile of v0, /device:TPU:0, one launch (start us, length us, event | category | flops | bytes accessed | tf_op | source)
XLA Modules:
  0.0 48.1 jit_solution(11611711685320491415)
XLA Ops:
  0.6 0.0 copy-start
  0.6 4.1 %collective-permute-start.2 = (bf16[8,4,128]{2,1,0:T(4,128)(2,1)}, bf16[8,4,128]{2,1,0:T(4,128)(2,1)S(1)}, u32[]{:S(2)}, u32[]{:S(2)}) collective-permute-start(bf16[8,4,128]{2,1,0:T(4,128)(2,1)} %bitcast.35), channel_id=1, source_target_pairs={{0,8},{1,9},{2,10},{3,11},{4,12},{5,13},{6,14},{7,15},{8,0},{9,1},... | collective-permute-start | bytes 24584 | tf_op jit(solution)/shard_map/ppermute | solution.py:23
  4.7 1.3 %collective-permute-start.1 = (bf16[8,4,128]{2,1,0:T(4,128)(2,1)}, bf16[8,4,128]{2,1,0:T(4,128)(2,1)S(1)}, u32[]{:S(2)}, u32[]{:S(2)}) collective-permute-start(bf16[8,4,128]{2,1,0:T(4,128)(2,1)} %bitcast.36), channel_id=1, source_target_pairs={{1,0},{2,1},{3,2},{4,3},{5,4},{6,5},{7,6},{8,7},{9,8},{10,9},{11,1... | collective-permute-start | bytes 24584 | tf_op jit(solution)/shard_map/ppermute | solution.py:15
  6.0 3.0 %collective-permute-start = (bf16[8,4,128]{2,1,0:T(4,128)(2,1)}, bf16[8,4,128]{2,1,0:T(4,128)(2,1)S(1)}, u32[]{:S(2)}, u32[]{:S(2)}) collective-permute-start(bf16[8,4,128]{2,1,0:T(4,128)(2,1)} %bitcast.37), channel_id=1, source_target_pairs={{0,1},{1,2},{2,3},{3,4},{4,5},{5,6},{6,7},{7,8},{8,9},{9,10},{10,1... | collective-permute-start | bytes 24584 | tf_op jit(solution)/shard_map/ppermute | solution.py:12
  9.1 0.8 %eq.77 = s32[48]{0:T(128)S(1)} reshape(s32[8,6]{1,0:T(8,128)} %param.13) | data formatting | bytes 384 | tf_op jit(solution)/shard_map/eq | solution.py:75
  9.8 0.7 %broadcast_add_fusion = s32[8,6]{1,0:T(8,128)S(1)} fusion(s32[8,6]{1,0:T(8,128)} %param.14), kind=kLoop, calls=%fused_computation.44 | loop fusion | flops 48 | bytes 384 | tf_op jit(solution)/shard_map/add | solution.py:38
  10.5 0.1 add.75
  10.6 0.1 fusion.17
  10.7 0.1 reduce_window_sum.11
  10.8 0.2 select_reduce_fusion.1
  11.0 0.1 select_reduce_fusion
  11.1 0.7 %sub.30 = s32[16,1,6]{2,0,1:T(8,128)} reshape(s32[96]{0:T(128)S(1)} %broadcast_add_fusion.1) | data formatting | bytes 768 | tf_op jit(solution)/shard_map/sub | solution.py:38
  11.8 5.2 %all-to-all-start = ((s32[16,1,6]{2,1,0:T(1,128)}), s32[16,1,6]{2,1,0:T(1,128)S(1)}, u32[]{:S(2)}, u32[]{:S(2)}) async-start(s32[16,1,6]{2,1,0:T(1,128)} %bitcast.7), calls=%async_computation | async-start | bytes 16384 | tf_op jit(solution)/shard_map/all_to_all | solution.py:90
  17.0 0.7 %convert_bitcast_fusion.1 = f32[4]{0:T(128)S(1)} fusion(s32[1,4]{1,0:T(1,128)} %param.11), kind=kLoop, calls=%fused_computation.46 | loop fusion | flops 4 | bytes 32 | tf_op jit(solution)/shard_map/convert_element_type | solution.py:71
  17.7 0.7 %compare_and_fusion = (pred[8,8]{1,0:T(8,128)(4,1)S(1)}, s32[8,8]{1,0:T(8,128)S(1)}) fusion(s32[8,8]{1,0:T(8,128)} %param.10, s32[]{:T(128)S(6)} %sub.25, s32[]{:T(128)S(6)} %select_n.38), kind=kLoop, calls=%fused_computation.41 | loop fusion | flops 1856 | bytes 584 | tf_op jit(solution)/shard_map/jit(_take)/and | solution.py:69
  18.4 0.1 reshape.85
  18.5 0.7 %pad_maximum_fusion = bf16[32,4,128]{2,1,0:T(4,128)(2,1)S(1)} fusion(bf16[8,4,128]{2,1,0:T(4,128)(2,1)S(1)} %collective-permute-done.2, bf16[8,4,128]{2,1,0:T(4,128)(2,1)S(1)} %collective-permute-done.1, bf16[8,4,128]{2,1,0:T(4,128)(2,1)} %bitcast.38, bf16[8,4,128]{2,1,0:T(4,128)(2,1)S(1)} %collective-permute-done), kind=kLoop, calls=%fused_computation.12 | loop fusion | flops 49152 | bytes 65536 | tf_op jit(solution)/shard_map/concatenate | solution.py:63
  19.2 0.7 %gather_fusion = bf16[64,4,128]{2,1,0:T(4,128)(2,1)S(1)} fusion(bf16[32,4,128]{2,1,0:T(4,128)(2,1)S(1)} %pad_maximum_fusion, s32[1024]{0:T(1024)S(1)} %pad_clamp_fusion), kind=kCustom, calls=%fused_computation | custom fusion | bytes 131328 | tf_op jit(solution)/shard_map/jit(_take)/gather | solution.py:69
  19.9 0.4 fusion.5
  20.3 0.9 %copy-done.1 = bf16[8,6,128,128]{3,2,1,0:T(8,128)(2,1)S(1)} copy-done((bf16[8,6,128,128]{3,2,1,0:T(8,128)(2,1)S(1)}, bf16[8,6,128,128]{3,2,1,0:T(8,128)(2,1)}, u32[]{:S(2)}) %copy-start.1) | copy-done | bytes 1572888
  21.3 0.3 convolution_bitcast_fusion
  21.7 0.4 fusion.10
  22.0 0.8 %copy.17 = f32[16,6,512]{2,1,0:T(8,128)} copy(f32[16,6,512]{2,0,1:T(8,128)S(1)} %fusion.10) | data formatting | bytes 393216 | tf_op jit(solution)/shard_map/dot_general | solution.py:31
  22.8 0.5 all-to-all-done
  23.3 5.5 %all-to-all-start.1 = ((f32[16,6,512]{2,1,0:T(8,128)}), f32[16,6,512]{2,1,0:T(8,128)S(1)}, u32[]{:S(2)}, u32[]{:S(2)}) async-start(f32[16,6,512]{2,1,0:T(8,128)} %copy.17), calls=%async_computation.1 | async-start | bytes 524288 | tf_op jit(solution)/shard_map/all_to_all | solution.py:89
  28.8 0.5 %broadcast.93 = s32[]{:T(128)} broadcast(s32[]{:T(128)} %constant.63.clone.1), dimensions={} | broadcast | bytes 8 | tf_op jit(solution)/shard_map/all_to_all | solution.py:90
  29.4 0.7 %reduce.3 = s32[16,6]{1,0:T(8,128)S(1)} reduce(s32[16,1,6]{2,1,0:T(1,128)S(1)} %all-to-all-done, s32[]{:T(128)} %broadcast.93), dimensions={1}, to_apply=%all_to_all.7.reduce_sub_computation.3 | reduce | bytes 772 | tf_op jit(solution)/shard_map/all_to_all | solution.py:90
  30.0 0.1 eq.84
  30.1 8.8 %all-to-all-done.1 = f32[16,6,512]{2,1,0:T(8,128)S(1)} async-done(((f32[16,6,512]{2,1,0:T(8,128)}), f32[16,6,512]{2,1,0:T(8,128)S(1)}, u32[]{:S(2)}, u32[]{:S(2)}) %all-to-all-start.1) | async-done | bytes 196640 | tf_op jit(solution)/shard_map/all_to_all | solution.py:89
  38.9 0.2 fusion.26
  39.1 8.2 %psum.7 = bf16[8,512]{1,0:T(8,128)(2,1)S(1)} all-reduce(f32[8,512]{1,0:T(8,128)S(1)} %fusion.26), channel_id=1, replica_groups=mesh['mach'=2,'panel'=16] {'mach'}, use_global_device_ids=true, to_apply=%region_3.4 | all-reduce | flops 4096 | bytes 24576 | tf_op jit(solution)/shard_map/psum | solution.py:102
  47.3 0.8 %fusion.19 = f32[8,4,128]{2,1,0:T(4,128)} fusion(bf16[8,128,128]{2,1,0:T(8,128)(2,1)S(1)} %copy-done.2, bf16[8,4,128]{2,0,1:T(8,128)(2,1)S(1)} %bitcast.33), kind=kOutput, calls=%fused_computation.23 | convolution fusion | flops 1048576 | bytes 286720 | tf_op jit(solution)/shard_map/trp,tpq->trq/dot_general | solution.py:104
  (15 shorter events, 0.1 us)
Async XLA Ops:
  0.6 19.3 %copy-start = (bf16[1,8,8,128,128]{4,3,2,1,0:T(8,128)(2,1)S(1)}, bf16[1,8,8,128,128]{4,3,2,1,0:T(8,128)(2,1)}, u32[]{:S(2)}) copy-start(bf16[1,8,8,128,128]{4,3,2,1,0:T(8,128)(2,1)} %param.9) | copy-start | bytes 6291460
  0.6 17.8 %collective-permute-start.2 = (bf16[8,4,128]{2,1,0:T(4,128)(2,1)}, bf16[8,4,128]{2,1,0:T(4,128)(2,1)S(1)}, u32[]{:S(2)}, u32[]{:S(2)}) collective-permute-start(bf16[8,4,128]{2,1,0:T(4,128)(2,1)} %bitcast.35), channel_id=1, source_target_pairs={{0,8},{1,9},{2,10},{3,11},{4,12},{5,13},{6,14},{7,15},{8,0},{9,1},... | collective-permute-start | bytes 24584 | tf_op jit(solution)/shard_map/ppermute | solution.py:23
  4.7 13.7 %collective-permute-start.1 = (bf16[8,4,128]{2,1,0:T(4,128)(2,1)}, bf16[8,4,128]{2,1,0:T(4,128)(2,1)S(1)}, u32[]{:S(2)}, u32[]{:S(2)}) collective-permute-start(bf16[8,4,128]{2,1,0:T(4,128)(2,1)} %bitcast.36), channel_id=1, source_target_pairs={{1,0},{2,1},{3,2},{4,3},{5,4},{6,5},{7,6},{8,7},{9,8},{10,9},{11,1... | collective-permute-start | bytes 24584 | tf_op jit(solution)/shard_map/ppermute | solution.py:15
  6.0 12.4 %collective-permute-start = (bf16[8,4,128]{2,1,0:T(4,128)(2,1)}, bf16[8,4,128]{2,1,0:T(4,128)(2,1)S(1)}, u32[]{:S(2)}, u32[]{:S(2)}) collective-permute-start(bf16[8,4,128]{2,1,0:T(4,128)(2,1)} %bitcast.37), channel_id=1, source_target_pairs={{0,1},{1,2},{2,3},{3,4},{4,5},{5,6},{6,7},{7,8},{8,9},{9,10},{10,1... | collective-permute-start | bytes 24584 | tf_op jit(solution)/shard_map/ppermute | solution.py:12
  11.8 11.6 %all-to-all-start = ((s32[16,1,6]{2,1,0:T(1,128)}), s32[16,1,6]{2,1,0:T(1,128)S(1)}, u32[]{:S(2)}, u32[]{:S(2)}) async-start(s32[16,1,6]{2,1,0:T(1,128)} %bitcast.7), calls=%async_computation | async-start | bytes 16384 | tf_op jit(solution)/shard_map/all_to_all | solution.py:90
  19.9 1.4 %copy-start.1 = (bf16[8,6,128,128]{3,2,1,0:T(8,128)(2,1)S(1)}, bf16[8,6,128,128]{3,2,1,0:T(8,128)(2,1)}, u32[]{:S(2)}) copy-start(bf16[8,6,128,128]{3,2,1,0:T(8,128)(2,1)} %param.12) | copy-start | bytes 4718596
  21.3 26.8 %copy-start.3 = (f32[8,4,128]{2,1,0:T(4,128)}, f32[8,4,128]{2,1,0:T(4,128)S(1)}, u32[]{:S(2)}) copy-start(f32[8,4,128]{2,1,0:T(4,128)S(1)} %fusion.5) | copy-start | bytes 49156
  21.3 26.0 %copy-start.2 = (bf16[8,128,128]{2,1,0:T(8,128)(2,1)S(1)}, bf16[8,128,128]{2,1,0:T(8,128)(2,1)}, u32[]{:S(2)}) copy-start(bf16[8,128,128]{2,1,0:T(8,128)(2,1)} %param.15) | copy-start | bytes 786436
  23.3 15.6 %all-to-all-start.1 = ((f32[16,6,512]{2,1,0:T(8,128)}), f32[16,6,512]{2,1,0:T(8,128)S(1)}, u32[]{:S(2)}, u32[]{:S(2)}) async-start(f32[16,6,512]{2,1,0:T(8,128)} %copy.17), calls=%async_computation.1 | async-start | bytes 524288 | tf_op jit(solution)/shard_map/all_to_all | solution.py:89
where the time goes:
time: 48.6 us; the launch traced here: 48.1 us
  starting transfers between devices  19.1 us (39%)
  waiting for transfers between devices  9.26 us (19%)
  blocking collectives  8.15 us (17%)
  local copies, waits for them, and re-layouts  4.73 us (10%)
  other arithmetic  3.91 us (8%)
  matrix products  2.08 us (4%)
  between operations  0.78 us (2%)
    all_to_all x1, waiting for transfers between devices, on_device(): lax.all_to_all(send_loads, 'panel', split_axis=0, concat_axis=0, tiled=True)  8.77 us
    psum x1, blocking collectives, on_device(): total = lax.psum(mine, 'mach')  8.15 us
    all_to_all x1, starting transfers between devices, on_device(): lax.all_to_all(send_loads, 'panel', split_axis=0, concat_axis=0, tiled=True)  5.52 us
    all_to_all x1, starting transfers between devices, on_device(): lax.all_to_all(send_index, 'panel', split_axis=0, concat_axis=0, tiled=True)  5.21 us
    ppermute x1, starting transfers between devices, shifted(): return lax.ppermute(value, axis, pairs)  4.1 us
    ppermute x1, starting transfers between devices, with_halo(): lax.ppermute(lax.slice_in_dim(block, block.shape[dim] - width, None, axis...  3.03 us
    ppermute x1, starting transfers between devices, with_halo(): lax.ppermute(lax.slice_in_dim(block, 0, width, axis=dim), axis, backward)  1.28 us
  transfers between devices with their start and end apart: 5, of which 2 were waited for; matrix products, arithmetic and copies ran while one was open for 18% of the time, Pallas kernels for 0%

commit v1 on v0

v1 whole, which is shorter than its diff:
```python
import functools

import jax
import jax.numpy as jnp
from jax import lax
from jax.experimental import pallas as pl
from jax.experimental.pallas import tpu as pltpu
from jax.sharding import PartitionSpec as P

SMEM = pl.BlockSpec(memory_space=pltpu.SMEM)
VMEM = pl.BlockSpec(memory_space=pltpu.VMEM)
PACK = 16
TILE = 8


def near_kernel(
    panels, rhs, pattern_ref, trim_ref, own_ref, pair_ref, cross_ref, mirror_ref, near_ref,
    loads_ref, rounded_ref,
):
    block_count, entries = pattern_ref.shape
    rows, width = own_ref.shape
    here = lax.axis_index("panel")
    pair = here + 1 - 2 * (here % 2)
    mirror = (here + panels // 2) % panels
    pool = jnp.concatenate(
        [own_ref[...], pair_ref[...], cross_ref[...], mirror_ref[...]], axis=0
    )
    shape = (rows, pool.shape[0])
    row = lax.broadcasted_iota(jnp.int32, shape, 0)
    offset = lax.broadcasted_iota(jnp.int32, shape, 1) - row % rhs
    picked = []
    for k in range(entries):
        first = jnp.zeros(shape, jnp.int32)
        for i in range(block_count):
            block = pattern_ref[i, k]
            owner = block // block_count
            slot = jnp.where(
                owner == here, 0, jnp.where(owner == mirror, 3, jnp.where(owner == pair, 1, 2))
            )
            base = (slot * block_count + block % block_count) * rhs
            first = jnp.where(row // rhs == i, base, first)
        hot = (offset == first).astype(jnp.bfloat16)
        picked.append(
            jnp.dot(hot, pool, preferred_element_type=jnp.float32).astype(jnp.bfloat16)
        )
    picked = jnp.concatenate(picked, axis=1)
    group_row = lax.broadcasted_iota(jnp.int32, (PACK, width), 0)
    gate = jnp.zeros((PACK, width), jnp.float32)
    for r in range(rhs):
        gate = jnp.where(group_row % rhs == r, trim_ref[0, r].astype(jnp.float32), gate)
    per_group = PACK // rhs
    for g in range(rows // PACK):
        left = picked[g * PACK : (g + 1) * PACK]
        loads = jnp.zeros((PACK, width), jnp.float32)
        for j in range(per_group):
            blocks = near_ref[g * per_group + j].reshape(entries * width, width)
            product = jnp.dot(left, blocks, preferred_element_type=jnp.float32)
            loads = jnp.where(group_row // rhs == j, product, loads)
        loads = loads * gate
        loads_ref[g * PACK : (g + 1) * PACK] = loads
        rounded_ref[g * PACK : (g + 1) * PACK] = loads.astype(jnp.bfloat16)


def spline_kernel(
    rhs, struct_count, owner_ref, local_ref, *refs
):
    machs = len(refs) - 3
    rounded_refs, spline_ref, out_ref, acc = refs[:machs], refs[machs], refs[-2], refs[-1]
    block_count, splines = owner_ref.shape
    rows, width = rounded_refs[0].shape
    acc[...] = jnp.zeros(acc.shape, jnp.float32)
    every = jnp.concatenate([ref[...] for ref in rounded_refs], axis=0)
    shape = (block_count * machs * TILE, machs * rows)
    row = lax.broadcasted_iota(jnp.int32, shape, 0)
    source = (
        (row // TILE) % machs * rows + row // (TILE * machs) * rhs + row % rhs
    )
    hot = (lax.broadcasted_iota(jnp.int32, shape, 1) == source).astype(jnp.bfloat16)
    left = jnp.dot(hot, every, preferred_element_type=jnp.float32).astype(jnp.bfloat16)
    part = lax.broadcasted_iota(jnp.int32, (TILE, width), 0) // rhs
    per_tile = TILE // rhs
    for i in range(block_count):
        mine = left[i * machs * TILE : (i + 1) * machs * TILE]
        for s in range(splines):
            product = jnp.dot(mine, spline_ref[i, s], preferred_element_type=jnp.float32)
            total = product[:TILE]
            for m in range(1, machs):
                total = total + product[m * TILE : (m + 1) * TILE]
            target = owner_ref[i, s] * struct_count + local_ref[i, s]
            place = target // per_tile
            acc[place] = acc[place] + jnp.where(part == target % per_tile, total, 0.0)
    out_ref[...] = acc[...].reshape(out_ref.shape).astype(jnp.bfloat16)


def inverse_kernel(rhs, got_ref, inverse_ref, out_ref):
    sources, rows, width = got_ref.shape
    total = got_ref[0].astype(jnp.float32)
    for source in range(1, sources):
        total = total + got_ref[source].astype(jnp.float32)
    rounded = total.astype(jnp.bfloat16)
    group_row = lax.broadcasted_iota(jnp.int32, (PACK, width), 0)
    per_group = PACK // rhs
    for g in range(rows // PACK):
        left = rounded[g * PACK : (g + 1) * PACK]
        out = jnp.zeros((PACK, width), jnp.float32)
        for j in range(per_group):
            product = jnp.dot(
                left, inverse_ref[g * per_group + j], preferred_element_type=jnp.float32
            )
            out = jnp.where(group_row // rhs == j, product, out)
        out_ref[g * PACK : (g + 1) * PACK] = out


def on_device(
    adjoint, near_blocks, pattern, trim_mask, spline_blocks, spline_owner, spline_local,
    struct_inverse,
):
    _, block_count, rhs, width = adjoint.shape
    panels, machs = lax.axis_size("panel"), lax.axis_size("mach")
    struct_count = struct_inverse.shape[0]
    rows = block_count * rhs
    own = adjoint.reshape(rows, width)
    half = panels // 2
    mirror = lax.ppermute(own, "panel", [(i, (i + half) % panels) for i in range(panels)])
    cross = lax.ppermute(
        own, "panel", [(i, i - 1 + 2 * (i % 2)) for i in range(1, panels - 1)]
    )
    pair = lax.ppermute(own, "panel", [(i, i + 1 - 2 * (i % 2)) for i in range(panels)])
    params = pltpu.CompilerParams(vmem_limit_bytes=16 * 1024 * 1024)
    loads, rounded = pl.pallas_call(
        functools.partial(near_kernel, panels, rhs),
        out_shape=(
            jax.ShapeDtypeStruct((rows, width), jnp.float32),
            jax.ShapeDtypeStruct((rows, width), jnp.bfloat16),
        ),
        in_specs=[SMEM, SMEM, VMEM, VMEM, VMEM, VMEM, VMEM],
        out_specs=(VMEM, VMEM),
        compiler_params=params,
        name="near_field",
    )(pattern, trim_mask, own, pair, cross, mirror, near_blocks[0])
    every = [rounded]
    for step in range(1, machs):
        every.append(
            lax.ppermute(rounded, "mach", [(i, (i + step) % machs) for i in range(machs)])
        )
    total_rows = panels * struct_count * rhs
    send = pl.pallas_call(
        functools.partial(spline_kernel, rhs, struct_count),
        out_shape=jax.ShapeDtypeStruct((panels, struct_count * rhs, width), jnp.bfloat16),
        in_specs=[SMEM, SMEM] + [VMEM] * (machs + 1),
        out_specs=VMEM,
        scratch_shapes=[pltpu.VMEM((total_rows // TILE, TILE, width), jnp.float32)],
        compiler_params=params,
        name="spline_loads",
    )(spline_owner, spline_local, *every, spline_blocks)
    got = lax.all_to_all(send, "panel", split_axis=0, concat_axis=0, tiled=True)
    struct_adjoint = pl.pallas_call(
        functools.partial(inverse_kernel, rhs),
        out_shape=jax.ShapeDtypeStruct((struct_count * rhs, width), jnp.float32),
        in_specs=[VMEM, VMEM],
        out_specs=VMEM,
        compiler_params=params,
        name="struct_solve",
    )(got, struct_inverse)
    return (
        loads.reshape(1, block_count, rhs, width),
        struct_adjoint.reshape(struct_count, rhs, width),
    )


def solution(mesh):
    in_specs = (
        P("mach", "panel", None, None),
        P("mach", "panel", None, None, None),
        P("panel", None),
        P("mach", None),
        P("panel", None, None, None),
        P("panel", None),
        P("panel", None),
        P("panel", None, None),
    )
    out_specs = (P("mach", "panel", None, None), P("panel", None, None))
    return jax.shard_map(
        on_device, mesh=mesh, in_specs=in_specs, out_specs=out_specs, check_vma=False
    )
```

time: 48.6 us -> 33.5 us (0.69)
  starting transfers between devices: 19.1 us -> 9.19 us
  waiting for transfers between devices: 9.26 us -> 3.2 us
  Pallas kernels: 0 us -> 4.31 us
  blocking collectives: 8.15 us -> 12.2 us
  other arithmetic: 3.91 us -> 0 us
  matrix products: 2.08 us -> 0 us
  local copies, waits for them, and re-layouts: 4.73 us -> 3.64 us
    all_to_all x0 -> x1, blocking collectives: none -> 12.2 us  [on_device(): got = lax.all_to_all(send, 'panel', split_axis=0, concat_axis=0, tiled=True)]
    all_to_all x2 -> x0, starting transfers between devices: 10.7 us -> none  [the longest x1 5.52 us: on_device(): lax.all_to_all(send_loads, 'panel', split_axis=0, concat_axis=0, tiled=True)]
    all_to_all x2 -> x0, waiting for transfers between devices: 9.25 us -> none  [the longest x1 8.77 us: on_device(): lax.all_to_all(send_loads, 'panel', split_axis=0, concat_axis=0, tiled=True)]
    psum x1 -> x0, blocking collectives: 8.15 us -> none  [on_device(): total = lax.psum(mine, 'mach')]
    pallas_call x0 -> x3, Pallas kernels: none -> 4.31 us  [the longest x1 2.2 us: on_device(): pl.pallas_call(functools.partial(near_kernel, panels, rhs), out_shape=(ja...]
    ppermute x3 -> x4, waiting for transfers between devices: 0.01 us -> 3.2 us  [the longest x1 2.16 us: on_device(): lax.ppermute(rounded, 'mach', [(i, (i + step) % machs) for i in range(mac...]
    unnamed x8 -> x16, local copies, waits for them, and re-layouts: 0.97 us -> 3.64 us
    dot_general x5 -> x0, matrix products: 2.08 us -> none  [the longest x1 0.79 us: on_device(): jnp.einsum('trp,tpq->trq', struct_rounded, struct_inverse, preferred_elem...]
  transfers between devices with their start and end apart: 5 -> 4, of which waited for: 2 -> 2; matrix products, arithmetic and copies ran while one was open for 18% -> 0% of each run, Pallas kernels for 0% -> 0%
where the time goes in v1:
time: 33.5 us; the launch traced here: 33.2 us
  blocking collectives  12.2 us (36%)
  starting transfers between devices  9.19 us (27%)
  Pallas kernels  4.31 us (13%)
  local copies, waits for them, and re-layouts  3.64 us (11%)
  waiting for transfers between devices  3.2 us (10%)
  between operations  0.67 us (2%)
    all_to_all x1, blocking collectives, on_device(): got = lax.all_to_all(send, 'panel', split_axis=0, concat_axis=0, tiled=True)  12.2 us
    ppermute x1, starting transfers between devices, on_device(): lax.ppermute(own, 'panel', [(i, (i + half) % panels) for i in range(panel...  4.1 us
    unnamed x16, local copies, waits for them, and re-layouts  3.64 us
    ppermute x1, starting transfers between devices, on_device(): lax.ppermute(own, 'panel', [(i, i + 1 - 2 * (i % 2)) for i in range(panel...  2.95 us
    pallas_call x1, Pallas kernels, on_device(): pl.pallas_call(functools.partial(near_kernel, panels, rhs), out_shape=(ja...  2.2 us
    ppermute x1, waiting for transfers between devices, on_device(): lax.ppermute(rounded, 'mach', [(i, (i + step) % machs) for i in range(mac...  2.16 us
    ppermute x1, starting transfers between devices, on_device(): lax.ppermute(rounded, 'mach', [(i, (i + step) % machs) for i in range(mac...  1.49 us
    pallas_call x1, Pallas kernels, on_device(): pl.pallas_call(functools.partial(spline_kernel, rhs, struct_count), out_s...  1.32 us
  transfers between devices with their start and end apart: 4, of which 2 were waited for; matrix products, arithmetic and copies ran while one was open for 0% of the time, Pallas kernels for 0%

profile of v1, /device:TPU:0, one launch (start us, length us, event | category | flops | bytes accessed | tf_op | source)
XLA Modules:
  0.0 33.2 jit_solution(11318190228896883672)
XLA Ops:
  0.6 4.1 %collective-permute-start.2 = (bf16[32,128]{1,0:T(8,128)(2,1)}, bf16[32,128]{1,0:T(8,128)(2,1)S(1)}, u32[]{:S(2)}, u32[]{:S(2)}) collective-permute-start(bf16[32,128]{1,0:T(8,128)(2,1)} %bitcast.5), channel_id=1, source_target_pairs={{0,8},{1,9},{2,10},{3,11},{4,12},{5,13},{6,14},{7,15},{8,0},{9,1},... | collective-permute-start | bytes 24584 | tf_op jit(solution)/shard_map/ppermute | solution.py:124
  4.7 0.6 %collective-permute-start.1 = (bf16[32,128]{1,0:T(8,128)(2,1)}, bf16[32,128]{1,0:T(8,128)(2,1)S(1)}, u32[]{:S(2)}, u32[]{:S(2)}) collective-permute-start(bf16[32,128]{1,0:T(8,128)(2,1)} %bitcast.6), channel_id=1, source_target_pairs={{1,2},{2,1},{3,4},{4,3},{5,6},{6,5},{7,8},{8,7},{9,10},{10,9},{11,... | collective-permute-start | bytes 24584 | tf_op jit(solution)/shard_map/ppermute | solution.py:125
  5.4 2.9 %collective-permute-start = (bf16[32,128]{1,0:T(8,128)(2,1)}, bf16[32,128]{1,0:T(8,128)(2,1)S(1)}, u32[]{:S(2)}, u32[]{:S(2)}) collective-permute-start(bf16[32,128]{1,0:T(8,128)(2,1)} %bitcast.7), channel_id=1, source_target_pairs={{0,1},{1,0},{2,3},{3,2},{4,5},{5,4},{6,7},{7,6},{8,9},{9,8},{10,11... | collective-permute-start | bytes 24584 | tf_op jit(solution)/shard_map/ppermute | solution.py:128
  8.3 0.0 collective-permute-done.2.mirror_ref
  8.3 0.0 collective-permute-done.1.cross_ref
  8.3 1.0 %collective-permute-done.pair_ref = bf16[32,128]{1,0:T(8,128)(2,1)S(1)} collective-permute-done((bf16[32,128]{1,0:T(8,128)(2,1)}, bf16[32,128]{1,0:T(8,128)(2,1)S(1)}, u32[]{:S(2)}, u32[]{:S(2)}) %collective-permute-start) | collective-permute-done | bytes 8224 | tf_op jit(solution)/shard_map/ppermute | solution.py:128
  9.4 0.0 copy-start
  9.4 1.6 %copy-done = bf16[1,8,8,128,128]{4,3,2,1,0:T(8,128)(2,1)S(1)} copy-done((bf16[1,8,8,128,128]{4,3,2,1,0:T(8,128)(2,1)S(1)}, bf16[1,8,8,128,128]{4,3,2,1,0:T(8,128)(2,1)}, u32[]{:S(2)}) %copy-start) | copy-done | bytes 2097176
  11.0 0.0 copy-start.3
  11.0 0.7 %copy-done.3 = bf16[1,8,4,128]{3,2,1,0:T(4,128)(2,1)S(1)} copy-done((bf16[1,8,4,128]{3,2,1,0:T(4,128)(2,1)S(1)}, bf16[1,8,4,128]{3,2,1,0:T(4,128)(2,1)}, u32[]{:S(2)}) %copy-start.3) | copy-done | bytes 8216
  11.7 0.0 copy-start.4
  11.7 0.7 %copy-done.4 = s32[8,8]{1,0:T(8,128)S(1)} copy-done((s32[8,8]{1,0:T(8,128)S(1)}, s32[8,8]{1,0:T(8,128)}, u32[]{:S(2)}) %copy-start.4) | copy-done | bytes 280
  12.4 0.0 copy-start.7
  12.4 0.7 %copy-done.7 = s32[1,4]{1,0:T(1,128)S(1)} copy-done((s32[1,4]{1,0:T(1,128)S(1)}, s32[1,4]{1,0:T(1,128)}, u32[]{:S(2)}) %copy-start.7) | copy-done | bytes 40
  13.0 0.0 copy-start.1
  13.0 0.0 copy-start.5
  13.0 0.0 copy-start.6
  13.0 0.0 copy-start.2
  13.0 2.2 %near_field.1 = (f32[32,128]{1,0:T(8,128)}, bf16[32,128]{1,0:T(8,128)(2,1)S(1)}) custom-call(s32[8,8]{1,0:T(8,128)S(1)} %copy-done.4, s32[1,4]{1,0:T(1,128)S(1)} %copy-done.7, bf16[32,128]{1,0:T(8,128)(2,1)S(1)} %bitcast.8, bf16[32,128]{1,0:T(8,128)(2,1)S(1)} %collective-permute-done.pair_ref, bf16[32,128]{1,0:T(8,128)(2,1)S(1)} %collective-permute-done.1.cross_ref, ...), custom_call_target="tpu_custom_call" | custom-call | tf_op jit(solution)/shard_map/near_field/pallas_call | solution.py:130
  15.2 1.5 %collective-permute-start.3 = (bf16[32,128]{1,0:T(8,128)(2,1)S(1)}, bf16[32,128]{1,0:T(8,128)(2,1)S(1)}, u32[]{:S(2)}, u32[]{:S(2)}) collective-permute-start(bf16[32,128]{1,0:T(8,128)(2,1)S(1)} %get-tuple-element.5.refs_0_), channel_id=1, source_target_pairs={{0,16},{16,0},{1,17},{17,1},{2,18},{18,2},{3,19},{19,3},{4,20},{20... | collective-permute-start | bytes 24584 | tf_op jit(solution)/shard_map/ppermute | solution.py:144
  16.7 2.2 %collective-permute-done.3.refs_1_ = bf16[32,128]{1,0:T(8,128)(2,1)S(1)} collective-permute-done((bf16[32,128]{1,0:T(8,128)(2,1)S(1)}, bf16[32,128]{1,0:T(8,128)(2,1)S(1)}, u32[]{:S(2)}, u32[]{:S(2)}) %collective-permute-start.3) | collective-permute-done | bytes 8224 | tf_op jit(solution)/shard_map/ppermute | solution.py:144
  18.9 0.0 copy-done.1
  18.9 0.0 copy-done.5
  18.9 0.0 copy-done.6
  18.9 1.3 %spline_loads.1 = bf16[16,32,128]{2,1,0:T(8,128)(2,1)S(1)} custom-call(s32[8,6]{1,0:T(8,128)S(1)} %copy-done.5, s32[8,6]{1,0:T(8,128)S(1)} %copy-done.6, bf16[32,128]{1,0:T(8,128)(2,1)S(1)} %get-tuple-element.5.refs_0_, bf16[32,128]{1,0:T(8,128)(2,1)S(1)} %collective-permute-done.3.refs_1_, bf16[8,6,128,128]{3,2,1,0:T(8,128)(2,1)S(1)} %copy-done.1), custom_call_target="tpu_custom_call" | custom-call | tf_op jit(solution)/shard_map/spline_loads/pallas_call | solution.py:147
  20.2 12.2 %all_to_all.5.got_ref = bf16[16,32,128]{2,1,0:T(8,128)(2,1)S(1)} all-to-all(bf16[16,32,128]{2,1,0:T(8,128)(2,1)S(1)} %spline_loads.1), channel_id=1, replica_groups=mesh['mach'=2,'panel'=16] {'panel'}, dimensions={0} | all-to-all | bytes 262144 | tf_op jit(solution)/shard_map/all_to_all | solution.py:156
  32.4 0.0 copy-done.2
  32.4 0.8 %struct_solve.1 = f32[32,128]{1,0:T(8,128)} custom-call(bf16[16,32,128]{2,1,0:T(8,128)(2,1)S(1)} %all_to_all.5.got_ref, bf16[8,128,128]{2,1,0:T(8,128)(2,1)S(1)} %copy-done.2), custom_call_target="tpu_custom_call" | custom-call | tf_op jit(solution)/shard_map/struct_solve/pallas_call | solution.py:157
Async XLA Ops:
  0.6 7.7 %collective-permute-start.2 = (bf16[32,128]{1,0:T(8,128)(2,1)}, bf16[32,128]{1,0:T(8,128)(2,1)S(1)}, u32[]{:S(2)}, u32[]{:S(2)}) collective-permute-start(bf16[32,128]{1,0:T(8,128)(2,1)} %bitcast.5), channel_id=1, source_target_pairs={{0,8},{1,9},{2,10},{3,11},{4,12},{5,13},{6,14},{7,15},{8,0},{9,1},... | collective-permute-start | bytes 24584 | tf_op jit(solution)/shard_map/ppermute | solution.py:124
  4.7 3.6 %collective-permute-start.1 = (bf16[32,128]{1,0:T(8,128)(2,1)}, bf16[32,128]{1,0:T(8,128)(2,1)S(1)}, u32[]{:S(2)}, u32[]{:S(2)}) collective-permute-start(bf16[32,128]{1,0:T(8,128)(2,1)} %bitcast.6), channel_id=1, source_target_pairs={{1,2},{2,1},{3,4},{4,3},{5,6},{6,5},{7,8},{8,7},{9,10},{10,9},{11,... | collective-permute-start | bytes 24584 | tf_op jit(solution)/shard_map/ppermute | solution.py:125
  5.4 4.0 %collective-permute-start = (bf16[32,128]{1,0:T(8,128)(2,1)}, bf16[32,128]{1,0:T(8,128)(2,1)S(1)}, u32[]{:S(2)}, u32[]{:S(2)}) collective-permute-start(bf16[32,128]{1,0:T(8,128)(2,1)} %bitcast.7), channel_id=1, source_target_pairs={{0,1},{1,0},{2,3},{3,2},{4,5},{5,4},{6,7},{7,6},{8,9},{9,8},{10,11... | collective-permute-start | bytes 24584 | tf_op jit(solution)/shard_map/ppermute | solution.py:128
  9.4 1.6 %copy-start = (bf16[1,8,8,128,128]{4,3,2,1,0:T(8,128)(2,1)S(1)}, bf16[1,8,8,128,128]{4,3,2,1,0:T(8,128)(2,1)}, u32[]{:S(2)}) copy-start(bf16[1,8,8,128,128]{4,3,2,1,0:T(8,128)(2,1)} %param.9) | copy-start | bytes 6291460
  11.0 0.7 %copy-start.3 = (bf16[1,8,4,128]{3,2,1,0:T(4,128)(2,1)S(1)}, bf16[1,8,4,128]{3,2,1,0:T(4,128)(2,1)}, u32[]{:S(2)}) copy-start(bf16[1,8,4,128]{3,2,1,0:T(4,128)(2,1)} %param.8) | copy-start | bytes 24580
  11.7 0.7 %copy-start.4 = (s32[8,8]{1,0:T(8,128)S(1)}, s32[8,8]{1,0:T(8,128)}, u32[]{:S(2)}) copy-start(s32[8,8]{1,0:T(8,128)} %pattern_ref.1) | copy-start | bytes 772
  12.4 0.7 %copy-start.7 = (s32[1,4]{1,0:T(1,128)S(1)}, s32[1,4]{1,0:T(1,128)}, u32[]{:S(2)}) copy-start(s32[1,4]{1,0:T(1,128)} %trim_ref.1) | copy-start | bytes 52
  13.0 5.9 %copy-start.1 = (bf16[8,6,128,128]{3,2,1,0:T(8,128)(2,1)S(1)}, bf16[8,6,128,128]{3,2,1,0:T(8,128)(2,1)}, u32[]{:S(2)}) copy-start(bf16[8,6,128,128]{3,2,1,0:T(8,128)(2,1)} %refs_2_.1) | copy-start | bytes 4718596
  13.0 5.9 %copy-start.5 = (s32[8,6]{1,0:T(8,128)S(1)}, s32[8,6]{1,0:T(8,128)}, u32[]{:S(2)}) copy-start(s32[8,6]{1,0:T(8,128)} %owner_ref.1) | copy-start | bytes 580
  13.0 5.9 %copy-start.6 = (s32[8,6]{1,0:T(8,128)S(1)}, s32[8,6]{1,0:T(8,128)}, u32[]{:S(2)}) copy-start(s32[8,6]{1,0:T(8,128)} %local_ref.1) | copy-start | bytes 580
  13.0 19.4 %copy-start.2 = (bf16[8,128,128]{2,1,0:T(8,128)(2,1)S(1)}, bf16[8,128,128]{2,1,0:T(8,128)(2,1)}, u32[]{:S(2)}) copy-start(bf16[8,128,128]{2,1,0:T(8,128)(2,1)} %inverse_ref.1) | copy-start | bytes 786436
  15.2 3.7 %collective-permute-start.3 = (bf16[32,128]{1,0:T(8,128)(2,1)S(1)}, bf16[32,128]{1,0:T(8,128)(2,1)S(1)}, u32[]{:S(2)}, u32[]{:S(2)}) collective-permute-start(bf16[32,128]{1,0:T(8,128)(2,1)S(1)} %get-tuple-element.5.refs_0_), channel_id=1, source_target_pairs={{0,16},{16,0},{1,17},{17,1},{2,18},{18,2},{3,19},{19,3},{4,20},{20... | collective-permute-start | bytes 24584 | tf_op jit(solution)/shard_map/ppermute | solution.py:144

commit v2 on v1

--- a/solution.py
+++ b/solution.py
@@ -13,41 +13,35 @@
 TILE = 8
 
 
-def near_kernel(
-    panels, rhs, pattern_ref, trim_ref, own_ref, pair_ref, cross_ref, mirror_ref, near_ref,
-    loads_ref, rounded_ref,
-):
+def pick_kernel(rhs, pattern_ref, trim_ref, hot_ref, gate_ref):
     block_count, entries = pattern_ref.shape
-    rows, width = own_ref.shape
-    here = lax.axis_index("panel")
-    pair = here + 1 - 2 * (here % 2)
-    mirror = (here + panels // 2) % panels
-    pool = jnp.concatenate(
-        [own_ref[...], pair_ref[...], cross_ref[...], mirror_ref[...]], axis=0
-    )
-    shape = (rows, pool.shape[0])
+    shape = hot_ref.shape[1:]
     row = lax.broadcasted_iota(jnp.int32, shape, 0)
     offset = lax.broadcasted_iota(jnp.int32, shape, 1) - row % rhs
-    picked = []
     for k in range(entries):
         first = jnp.zeros(shape, jnp.int32)
         for i in range(block_count):
-            block = pattern_ref[i, k]
-            owner = block // block_count
-            slot = jnp.where(
-                owner == here, 0, jnp.where(owner == mirror, 3, jnp.where(owner == pair, 1, 2))
-            )
-            base = (slot * block_count + block % block_count) * rhs
-            first = jnp.where(row // rhs == i, base, first)
-        hot = (offset == first).astype(jnp.bfloat16)
-        picked.append(
-            jnp.dot(hot, pool, preferred_element_type=jnp.float32).astype(jnp.bfloat16)
-        )
-    picked = jnp.concatenate(picked, axis=1)
+            first = jnp.where(row // rhs == i, pattern_ref[i, k] * rhs, first)
+        hot_ref[k] = (offset == first).astype(jnp.bfloat16)
+    row = lax.broadcasted_iota(jnp.int32, gate_ref.shape, 0)
+    gate = jnp.zeros(gate_ref.shape, jnp.float32)
+    for r in range(rhs):
+        gate = jnp.where(row % rhs == r, trim_ref[0, r].astype(jnp.float32), gate)
+    gate_ref[...] = gate
+
+
+def near_kernel(rhs, hot_ref, gate_ref, pool_ref, near_ref, loads_ref, rounded_ref):
+    entries, rows, _ = hot_ref.shape
+    width = pool_ref.shape[1]
+    pool = pool_ref[...]
+    picked = jnp.concatenate(
+        [
+            jnp.dot(hot_ref[k], pool, preferred_element_type=jnp.float32).astype(jnp.bfloat16)
+            for k in range(entries)
+        ],
+        axis=1,
+    )
     group_row = lax.broadcasted_iota(jnp.int32, (PACK, width), 0)
-    gate = jnp.zeros((PACK, width), jnp.float32)
-    for r in range(rhs):
-        gate = jnp.where(group_row % rhs == r, trim_ref[0, r].astype(jnp.float32), gate)
     per_group = PACK // rhs
     for g in range(rows // PACK):
         left = picked[g * PACK : (g + 1) * PACK]
@@ -56,7 +50,7 @@
             blocks = near_ref[g * per_group + j].reshape(entries * width, width)
             product = jnp.dot(left, blocks, preferred_element_type=jnp.float32)
             loads = jnp.where(group_row // rhs == j, product, loads)
-        loads = loads * gate
+        loads = loads * gate_ref[...]
         loads_ref[g * PACK : (g + 1) * PACK] = loads
         rounded_ref[g * PACK : (g + 1) * PACK] = loads.astype(jnp.bfloat16)
 
@@ -89,7 +83,7 @@
             target = owner_ref[i, s] * struct_count + local_ref[i, s]
             place = target // per_tile
             acc[place] = acc[place] + jnp.where(part == target % per_tile, total, 0.0)
-    out_ref[...] = acc[...].reshape(out_ref.shape).astype(jnp.bfloat16)
+    out_ref[...] = acc[...].reshape(out_ref.shape).astype(out_ref.dtype)
 
 
 def inverse_kernel(rhs, got_ref, inverse_ref, out_ref):
@@ -120,24 +114,33 @@
     struct_count = struct_inverse.shape[0]
     rows = block_count * rhs
     own = adjoint.reshape(rows, width)
-    half = panels // 2
-    mirror = lax.ppermute(own, "panel", [(i, (i + half) % panels) for i in range(panels)])
-    cross = lax.ppermute(
-        own, "panel", [(i, i - 1 + 2 * (i % 2)) for i in range(1, panels - 1)]
-    )
-    pair = lax.ppermute(own, "panel", [(i, i + 1 - 2 * (i % 2)) for i in range(panels)])
+    pool = lax.all_gather(own, "panel", axis=0, tiled=True)
+    entries = pattern.shape[1]
     params = pltpu.CompilerParams(vmem_limit_bytes=16 * 1024 * 1024)
+    hot, gate = pl.pallas_call(
+        functools.partial(pick_kernel, rhs),
+        out_shape=(
+            jax.ShapeDtypeStruct((entries, rows, panels * rows), jnp.bfloat16),
+            jax.ShapeDtypeStruct((PACK, width), jnp.float32),
+        ),
+        in_specs=[SMEM, SMEM],
+        out_specs=(VMEM, VMEM),
+        compiler_params=params,
+        cost_estimate=pl.CostEstimate(flops=4 * 10**9, bytes_accessed=16 * 2**20, transcendentals=0),
+        name="pick_rows",
+    )(pattern, trim_mask)
     loads, rounded = pl.pallas_call(
-        functools.partial(near_kernel, panels, rhs),
+        functools.partial(near_kernel, rhs),
         out_shape=(
             jax.ShapeDtypeStruct((rows, width), jnp.float32),
             jax.ShapeDtypeStruct((rows, width), jnp.bfloat16),
         ),
-        in_specs=[SMEM, SMEM, VMEM, VMEM, VMEM, VMEM, VMEM],
+        in_specs=[VMEM] * 4,
         out_specs=(VMEM, VMEM),
         compiler_params=params,
+        cost_estimate=pl.CostEstimate(flops=2 * 10**9, bytes_accessed=4 * 2**20, transcendentals=0),
         name="near_field",
-    )(pattern, trim_mask, own, pair, cross, mirror, near_blocks[0])
+    )(hot, gate, pool, near_blocks[0])
     every = [rounded]
     for step in range(1, machs):
         every.append(
@@ -146,14 +149,14 @@
     total_rows = panels * struct_count * rhs
     send = pl.pallas_call(
         functools.partial(spline_kernel, rhs, struct_count),
-        out_shape=jax.ShapeDtypeStruct((panels, struct_count * rhs, width), jnp.bfloat16),
+        out_shape=jax.ShapeDtypeStruct((panels, struct_count * rhs, width), jnp.float32),
         in_specs=[SMEM, SMEM] + [VMEM] * (machs + 1),
         out_specs=VMEM,
         scratch_shapes=[pltpu.VMEM((total_rows // TILE, TILE, width), jnp.float32)],
         compiler_params=params,
         name="spline_loads",
     )(spline_owner, spline_local, *every, spline_blocks)
-    got = lax.all_to_all(send, "panel", split_axis=0, concat_axis=0, tiled=True)
+    got = lax.psum_scatter(send, "panel", scatter_dimension=0, tiled=True)
     struct_adjoint = pl.pallas_call(
         functools.partial(inverse_kernel, rhs),
         out_shape=jax.ShapeDtypeStruct((struct_count * rhs, width), jnp.float32),

time: 33.5 us -> 102 us (3.04)
  waiting for transfers between devices: 3.2 us -> 54.9 us
  between operations: 0.67 us -> 14 us
  blocking collectives: 12.2 us -> 23.7 us
  starting transfers between devices: 9.19 us -> 1.53 us
    reduce_scatter x0 -> x1, waiting for transfers between devices: none -> 52.7 us  [on_device(): got = lax.psum_scatter(send, 'panel', scatter_dimension=0, tiled=True)]
    all_gather x0 -> x1, blocking collectives: none -> 23.7 us  [on_device(): pool = lax.all_gather(own, 'panel', axis=0, tiled=True)]
    all_to_all x1 -> x0, blocking collectives: 12.2 us -> none  [on_device(): got = lax.all_to_all(send, 'panel', split_axis=0, concat_axis=0, tiled=True)]
    ppermute x3 -> x0, starting transfers between devices: 7.7 us -> none  [the longest x1 4.1 us: on_device(): lax.ppermute(own, 'panel', [(i, (i + half) % panels) for i in range(panel...]
    ppermute x3 -> x0, waiting for transfers between devices: 1.04 us -> none  [the longest x1 1.03 us: on_device(): lax.ppermute(own, 'panel', [(i, i + 1 - 2 * (i % 2)) for i in range(panel...]
    pallas_call x1 -> x2, Pallas kernels: 2.2 us -> 1.92 us  [the longest x1 1.23 us: on_device(): pl.pallas_call(functools.partial(near_kernel, rhs), out_shape=(jax.ShapeD...]
  transfers between devices with their start and end apart: 4 -> 2, of which waited for: 2 -> 2; matrix products, arithmetic and copies ran while one was open for 0% -> 0% of each run, Pallas kernels for 0% -> 0%
where the time goes in v2:
time: 102 us
  waiting for transfers between devices  54.9 us (54%)
  blocking collectives  23.7 us (23%)
  between operations  14 us (14%)
  Pallas kernels  4.74 us (5%)
  local copies, waits for them, and re-layouts  2.97 us (3%)
  starting transfers between devices  1.53 us (2%)
    reduce_scatter x1, waiting for transfers between devices, on_device(): got = lax.psum_scatter(send, 'panel', scatter_dimension=0, tiled=True)  52.7 us
    all_gather x1, blocking collectives, on_device(): pool = lax.all_gather(own, 'panel', axis=0, tiled=True)  23.7 us
    unnamed x16, local copies, waits for them, and re-layouts  2.97 us
    ppermute x1, waiting for transfers between devices, on_device(): lax.ppermute(rounded, 'mach', [(i, (i + step) % machs) for i in range(mac...  2.16 us
  transfers between devices with their start and end apart: 2, of which 2 were waited for; matrix products, arithmetic and copies ran while one was open for 0% of the time, Pallas kernels for 0%

profile of v2, /device:TPU:0, one launch (start us, length us, event | category | flops | bytes accessed | tf_op | source)
XLA Modules:
  0.0 101.9 jit_solution(9676844604578369647)
XLA Ops:
  7.2 0.0 reduce-scatter.2.cloned.1.call-start
  7.2 23.7 %all_gather.3.pool_ref = bf16[512,128]{1,0:T(8,128)(2,1)S(1)} all-gather(bf16[32,128]{1,0:T(8,128)(2,1)} %bitcast.6), channel_id=1, replica_groups=mesh['mach'=2,'panel'=16] {'panel'}, dimensions={0}, use_global_device_ids=true | all-gather | bytes 139264 | tf_op jit(solution)/shard_map/all_gather | solution.py:117
  30.9 0.0 copy-start.6
  30.9 0.7 copy-done.6
  31.6 0.0 copy-start.7
  31.6 0.7 copy-done.7
  32.2 0.0 copy-start.5
  32.2 0.7 pick_rows.1
  32.9 0.9 copy-done.5
  33.8 0.0 copy-start
  33.8 0.0 copy-start.3
  33.8 0.0 copy-start.4
  33.8 1.2 %near_field.1 = (f32[32,128]{1,0:T(8,128)}, bf16[32,128]{1,0:T(8,128)(2,1)S(1)}) custom-call(bf16[8,32,512]{2,1,0:T(8,128)(2,1)S(1)} %get-tuple-element.6.hot_ref, f32[16,128]{1,0:T(8,128)S(1)} %get-tuple-element.7.gate_ref, bf16[512,128]{1,0:T(8,128)(2,1)S(1)} %all_gather.3.pool_ref, bf16[8,8,128,128]{3,2,1,0:T(8,128)(2,1)S(1)} %bitcast.4), custom_call_target="tpu_custom_call" | custom-call | flops 2000000000 | bytes 4194304 | tf_op jit(solution)/shard_map/near_field/pallas_call | solution.py:132
  35.1 0.0 copy-start.1
  35.1 1.5 %collective-permute-start = (bf16[32,128]{1,0:T(8,128)(2,1)S(1)}, bf16[32,128]{1,0:T(8,128)(2,1)S(1)}, u32[]{:S(2)}, u32[]{:S(2)}) collective-permute-start(bf16[32,128]{1,0:T(8,128)(2,1)S(1)} %get-tuple-element.9.refs_0_), channel_id=1, source_target_pairs={{0,16},{16,0},{1,17},{17,1},{2,18},{18,2},{3,19},{19,3},{4,20},{20... | collective-permute-start | bytes 24584 | tf_op jit(solution)/shard_map/ppermute | solution.py:147
  36.6 2.2 %collective-permute-done.refs_1_ = bf16[32,128]{1,0:T(8,128)(2,1)S(1)} collective-permute-done((bf16[32,128]{1,0:T(8,128)(2,1)S(1)}, bf16[32,128]{1,0:T(8,128)(2,1)S(1)}, u32[]{:S(2)}, u32[]{:S(2)}) %collective-permute-start) | collective-permute-done | bytes 8224 | tf_op jit(solution)/shard_map/ppermute | solution.py:147
  38.7 0.0 copy-done
  38.7 0.0 copy-done.3
  38.7 0.0 copy-done.4
  38.7 2.0 %spline_loads.1 = f32[16,32,128]{2,1,0:T(8,128)} custom-call(s32[8,6]{1,0:T(8,128)S(1)} %copy-done.3, s32[8,6]{1,0:T(8,128)S(1)} %copy-done.4, bf16[32,128]{1,0:T(8,128)(2,1)S(1)} %get-tuple-element.9.refs_0_, bf16[32,128]{1,0:T(8,128)(2,1)S(1)} %collective-permute-done.refs_1_, bf16[8,6,128,128]{3,2,1,0:T(8,128)(2,1)S(1)} %copy-done), custom_call_target="tpu_custom_call" | custom-call | tf_op jit(solution)/shard_map/spline_loads/pallas_call | solution.py:150
  40.8 0.0 reduce-scatter.2.cloned.1.call-update
  40.8 52.7 %reduce-scatter.2.cloned.1.call-done.got_ref = f32[1,32,128]{2,1,0:T(8,128)} async-done(((f32[16,32,128]{2,1,0:T(8,128)}), f32[1,32,128]{2,1,0:T(8,128)}) %reduce-scatter.2.cloned.1.call-update) | async-done | bytes 16400 | tf_op jit(solution)/shard_map/reduce_scatter | solution.py:159
  93.5 0.0 copy-done.1
  93.5 0.0 copy-start.2
  93.5 0.7 copy-done.2
  94.2 0.8 struct_solve.1
Async XLA Ops:
  7.2 86.3 %reduce-scatter.2.cloned.1.call-start = ((), (), s32[]{:S(2)}) async-start(), calls=%async_computation.1 | async-start | bytes 278528 | tf_op jit(solution)/shard_map/reduce_scatter | solution.py:159
  30.9 0.7 copy-start.6
  31.6 0.7 copy-start.7
  32.2 1.6 %copy-start.5 = (bf16[1,8,8,128,128]{4,3,2,1,0:T(8,128)(2,1)S(1)}, bf16[1,8,8,128,128]{4,3,2,1,0:T(8,128)(2,1)}, u32[]{:S(2)}) copy-start(bf16[1,8,8,128,128]{4,3,2,1,0:T(8,128)(2,1)} %param.9) | copy-start | bytes 6291460
  33.8 4.9 %copy-start = (bf16[8,6,128,128]{3,2,1,0:T(8,128)(2,1)S(1)}, bf16[8,6,128,128]{3,2,1,0:T(8,128)(2,1)}, u32[]{:S(2)}) copy-start(bf16[8,6,128,128]{3,2,1,0:T(8,128)(2,1)} %refs_2_.1) | copy-start | bytes 4718596
  33.8 4.9 %copy-start.3 = (s32[8,6]{1,0:T(8,128)S(1)}, s32[8,6]{1,0:T(8,128)}, u32[]{:S(2)}) copy-start(s32[8,6]{1,0:T(8,128)} %owner_ref.1) | copy-start | bytes 580
  33.8 4.9 %copy-start.4 = (s32[8,6]{1,0:T(8,128)S(1)}, s32[8,6]{1,0:T(8,128)}, u32[]{:S(2)}) copy-start(s32[8,6]{1,0:T(8,128)} %local_ref.1) | copy-start | bytes 580
  35.1 58.4 %copy-start.1 = (bf16[8,128,128]{2,1,0:T(8,128)(2,1)S(1)}, bf16[8,128,128]{2,1,0:T(8,128)(2,1)}, u32[]{:S(2)}) copy-start(bf16[8,128,128]{2,1,0:T(8,128)(2,1)} %inverse_ref.1) | copy-start | bytes 786436
  35.1 3.7 %collective-permute-start = (bf16[32,128]{1,0:T(8,128)(2,1)S(1)}, bf16[32,128]{1,0:T(8,128)(2,1)S(1)}, u32[]{:S(2)}, u32[]{:S(2)}) collective-permute-start(bf16[32,128]{1,0:T(8,128)(2,1)S(1)} %get-tuple-element.9.refs_0_), channel_id=1, source_target_pairs={{0,16},{16,0},{1,17},{17,1},{2,18},{18,2},{3,19},{19,3},{4,20},{20... | collective-permute-start | bytes 24584 | tf_op jit(solution)/shard_map/ppermute | solution.py:147
  93.5 0.7 copy-start.2
Sparse Core Ops, SparseCore 0:
  40.9 52.5 reduce-scatter.1

commit v3 on v2

v3 whole, which is shorter than its diff:
```python
import functools

import jax
import jax.numpy as jnp
from jax import lax
from jax.experimental import pallas as pl
from jax.experimental.pallas import tpu as pltpu
from jax.sharding import PartitionSpec as P

SMEM = pl.BlockSpec(memory_space=pltpu.SMEM)
VMEM = pl.BlockSpec(memory_space=pltpu.VMEM)
PACK = 16
TILE = 8


def pick_kernel(panels, rhs, pattern_ref, trim_ref, own_ref, hot_ref, gate_ref, held_ref):
    block_count, entries = pattern_ref.shape
    here = lax.axis_index("panel")
    shape = hot_ref.shape[1:]
    row = lax.broadcasted_iota(jnp.int32, shape, 0)
    offset = lax.broadcasted_iota(jnp.int32, shape, 1) - row % rhs
    for k in range(entries):
        first = jnp.zeros(shape, jnp.int32)
        for i in range(block_count):
            block = pattern_ref[i, k]
            apart = (block // block_count) ^ here
            slot = jnp.where(
                apart == 0, 0, jnp.where(apart == panels // 2, 3, jnp.where(apart == 1, 1, 2))
            )
            base = (slot * block_count + block % block_count) * rhs
            first = jnp.where(row // rhs == i, base, first)
        hot_ref[k] = (offset == first).astype(jnp.bfloat16)
    row = lax.broadcasted_iota(jnp.int32, gate_ref.shape, 0)
    gate = jnp.zeros(gate_ref.shape, jnp.float32)
    for r in range(rhs):
        gate = jnp.where(row % rhs == r, trim_ref[0, r].astype(jnp.float32), gate)
    gate_ref[...] = gate
    held_ref[...] = own_ref[...]


def near_kernel(
    rhs, hot_ref, gate_ref, own_ref, pair_ref, cross_ref, mirror_ref, near_ref,
    loads_ref, rounded_ref,
):
    entries, rows, _ = hot_ref.shape
    width = own_ref.shape[1]
    pool = jnp.concatenate(
        [own_ref[...], pair_ref[...], cross_ref[...], mirror_ref[...]], axis=0
    )
    picked = jnp.concatenate(
        [
            jnp.dot(hot_ref[k], pool, preferred_element_type=jnp.float32).astype(jnp.bfloat16)
            for k in range(entries)
        ],
        axis=1,
    )
    group_row = lax.broadcasted_iota(jnp.int32, (PACK, width), 0)
    per_group = PACK // rhs
    for g in range(rows // PACK):
        left = picked[g * PACK : (g + 1) * PACK]
        loads = jnp.zeros((PACK, width), jnp.float32)
        for j in range(per_group):
            blocks = near_ref[g * per_group + j].reshape(entries * width, width)
            product = jnp.dot(left, blocks, preferred_element_type=jnp.float32)
            loads = jnp.where(group_row // rhs == j, product, loads)
        loads = loads * gate_ref[...]
        loads_ref[g * PACK : (g + 1) * PACK] = loads
        rounded_ref[g * PACK : (g + 1) * PACK] = loads.astype(jnp.bfloat16)


def spline_kernel(machs, rhs, struct_count, owner_ref, local_ref, *refs):
    rounded_refs, spline_ref, out_refs, acc = refs[:machs], refs[machs], refs[machs + 1 : -1], refs[-1]
    block_count, splines = owner_ref.shape
    rows, width = rounded_refs[0].shape
    near_by = len(out_refs)
    here = lax.axis_index("panel")
    acc[...] = jnp.zeros(acc.shape, jnp.float32)
    every = jnp.concatenate([ref[...] for ref in rounded_refs], axis=0)
    shape = (block_count * machs * TILE, machs * rows)
    row = lax.broadcasted_iota(jnp.int32, shape, 0)
    source = (
        (row // TILE) % machs * rows + row // (TILE * machs) * rhs + row % rhs
    )
    hot = (lax.broadcasted_iota(jnp.int32, shape, 1) == source).astype(jnp.bfloat16)
    left = jnp.dot(hot, every, preferred_element_type=jnp.float32).astype(jnp.bfloat16)
    part = lax.broadcasted_iota(jnp.int32, (TILE, width), 0) // rhs
    per_tile = TILE // rhs
    tiles = acc.shape[1]
    owner_tiles = struct_count // per_tile
    for i in range(block_count):
        mine = left[i * machs * TILE : (i + 1) * machs * TILE]
        for s in range(splines):
            product = jnp.dot(mine, spline_ref[i, s], preferred_element_type=jnp.float32)
            total = product[:TILE]
            for m in range(1, machs):
                total = total + product[m * TILE : (m + 1) * TILE]
            apart = owner_ref[i, s] ^ here
            local = local_ref[i, s]
            group = apart % near_by
            place = apart // near_by * owner_tiles + local // per_tile
            acc[group, place] = acc[group, place] + jnp.where(
                part == local % per_tile, total, 0.0
            )
    for group, out_ref in enumerate(out_refs):
        out_ref[...] = acc[group].reshape(out_ref.shape).astype(out_ref.dtype)


def sum_kernel(near_by, *refs):
    in_refs, out_refs = refs[:near_by], refs[near_by:]
    for step, out_ref in enumerate(out_refs):
        total = in_refs[0][step]
        for ref in in_refs[1:]:
            total = total + ref[step].astype(jnp.float32)
        out_ref[...] = total.astype(out_ref.dtype)


def inverse_kernel(rhs, *refs):
    in_refs, inverse_ref, out_ref = refs[:-2], refs[-2], refs[-1]
    total = in_refs[0][...]
    for ref in in_refs[1:]:
        total = total + ref[...].astype(jnp.float32)
    rows, width = total.shape
    rounded = total.astype(jnp.bfloat16)
    group_row = lax.broadcasted_iota(jnp.int32, (PACK, width), 0)
    per_group = PACK // rhs
    for g in range(rows // PACK):
        left = rounded[g * PACK : (g + 1) * PACK]
        out = jnp.zeros((PACK, width), jnp.float32)
        for j in range(per_group):
            product = jnp.dot(
                left, inverse_ref[g * per_group + j], preferred_element_type=jnp.float32
            )
            out = jnp.where(group_row // rhs == j, product, out)
        out_ref[g * PACK : (g + 1) * PACK] = out


def swap(value, panels, apart):
    return lax.ppermute(value, "panel", [(i, i ^ apart) for i in range(panels)])


def cost(flops, size):
    return pl.CostEstimate(flops=flops, bytes_accessed=size, transcendentals=0)


def on_device(
    adjoint, near_blocks, pattern, trim_mask, spline_blocks, spline_owner, spline_local,
    struct_inverse,
):
    _, block_count, rhs, width = adjoint.shape
    entries = pattern.shape[1]
    panels, machs = lax.axis_size("panel"), lax.axis_size("mach")
    struct_count = struct_inverse.shape[0]
    rows, struct_rows = block_count * rhs, struct_count * rhs
    params = pltpu.CompilerParams(vmem_limit_bytes=16 * 1024 * 1024)
    f32, bf16 = jnp.float32, jnp.bfloat16
    own = adjoint.reshape(rows, width)
    mirror = swap(own, panels, panels // 2)
    cross = lax.ppermute(
        own, "panel", [(i, i - 1 + 2 * (i % 2)) for i in range(1, panels - 1)]
    )
    pair = swap(own, panels, 1)
    hot, gate, held = pl.pallas_call(
        functools.partial(pick_kernel, panels, rhs),
        out_shape=(
            jax.ShapeDtypeStruct((entries, rows, 4 * rows), bf16),
            jax.ShapeDtypeStruct((PACK, width), f32),
            jax.ShapeDtypeStruct((rows, width), bf16),
        ),
        in_specs=[SMEM, SMEM, VMEM],
        out_specs=(VMEM, VMEM, VMEM),
        compiler_params=params,
        cost_estimate=cost(4 * 10**9, 16 * 2**20),
        name="pick_rows",
    )(pattern, trim_mask, own)
    loads, rounded = pl.pallas_call(
        functools.partial(near_kernel, rhs),
        out_shape=(
            jax.ShapeDtypeStruct((rows, width), f32),
            jax.ShapeDtypeStruct((rows, width), bf16),
        ),
        in_specs=[VMEM] * 7,
        out_specs=(VMEM, VMEM),
        compiler_params=params,
        cost_estimate=cost(2 * 10**9, 4 * 2**20),
        name="near_field",
    )(hot, gate, held, pair, cross, mirror, near_blocks[0])
    every = [rounded]
    for step in range(1, machs):
        every.append(
            lax.ppermute(rounded, "mach", [(i, (i + step) % machs) for i in range(machs)])
        )
    near_by = 1 << ((panels.bit_length() - 1) // 2)
    far = panels // near_by
    parts = pl.pallas_call(
        functools.partial(spline_kernel, machs, rhs, struct_count),
        out_shape=tuple(
            jax.ShapeDtypeStruct((far, struct_rows, width), f32 if group == 0 else bf16)
            for group in range(near_by)
        ),
        in_specs=[SMEM, SMEM] + [VMEM] * (machs + 1),
        out_specs=(VMEM,) * near_by,
        scratch_shapes=[pltpu.VMEM((near_by, far * struct_rows // TILE, TILE, width), f32)],
        compiler_params=params,
        cost_estimate=cost(2 * 10**9, 4 * 2**20),
        name="spline_loads",
    )(spline_owner, spline_local, *every, spline_blocks)
    got = [parts[0]] + [swap(parts[step], panels, step) for step in range(1, near_by)]
    sums = pl.pallas_call(
        functools.partial(sum_kernel, near_by),
        out_shape=tuple(
            jax.ShapeDtypeStruct((struct_rows, width), f32 if step == 0 else bf16)
            for step in range(far)
        ),
        in_specs=[VMEM] * near_by,
        out_specs=(VMEM,) * far,
        compiler_params=params,
        cost_estimate=cost(10**6, 2**20),
        name="group_sum",
    )(*got)
    got = [sums[0]] + [swap(sums[step], panels, step * near_by) for step in range(1, far)]
    struct_adjoint = pl.pallas_call(
        functools.partial(inverse_kernel, rhs),
        out_shape=jax.ShapeDtypeStruct((struct_rows, width), f32),
        in_specs=[VMEM] * (far + 1),
        out_specs=VMEM,
        compiler_params=params,
        name="struct_solve",
    )(*got, struct_inverse)
    return (
        loads.reshape(1, block_count, rhs, width),
        struct_adjoint.reshape(struct_count, rhs, width),
    )


def solution(mesh):
    in_specs = (
        P("mach", "panel", None, None),
        P("mach", "panel", None, None, None),
        P("panel", None),
        P("mach", None),
        P("panel", None, None, None),
        P("panel", None),
        P("panel", None),
        P("panel", None, None),
    )
    out_specs = (P("mach", "panel", None, None), P("panel", None, None))
    return jax.shard_map(
        on_device, mesh=mesh, in_specs=in_specs, out_specs=out_specs, check_vma=False
    )
```

time: 102 us -> 30.8 us (0.30)
  waiting for transfers between devices: 54.9 us -> 7.57 us
  blocking collectives: 23.7 us -> 0 us
  starting transfers between devices: 1.53 us -> 15.6 us
  between operations: 14 us -> 0.74 us
    reduce_scatter x1 -> x0, waiting for transfers between devices: 52.7 us -> none  [on_device(): got = lax.psum_scatter(send, 'panel', scatter_dimension=0, tiled=True)]
    all_gather x1 -> x0, blocking collectives: 23.7 us -> none  [on_device(): pool = lax.all_gather(own, 'panel', axis=0, tiled=True)]
    ppermute x0 -> x9, starting transfers between devices: none -> 14.1 us  [the longest x8 13.4 us: swap(): return lax.ppermute(value, 'panel', [(i, i ^ apart) for i in range(panels)])]
    ppermute x0 -> x9, waiting for transfers between devices: none -> 5.41 us  [the longest x8 5.41 us: swap(): return lax.ppermute(value, 'panel', [(i, i ^ apart) for i in range(panels)])]
    pallas_call x2 -> x3, Pallas kernels: 2.72 us -> 2.62 us  [the longest x1 1.46 us: on_device(): pl.pallas_call(functools.partial(spline_kernel, machs, rhs, struct_count)...]
  transfers between devices with their start and end apart: 2 -> 10, of which waited for: 2 -> 5; matrix products, arithmetic and copies ran while one was open for 0% -> 0% of each run, Pallas kernels for 0% -> 4%
where the time goes in v3:
time: 30.8 us; the launch traced here: 30.5 us
  starting transfers between devices  15.6 us (51%)
  waiting for transfers between devices  7.57 us (25%)
  Pallas kernels  4.56 us (15%)
  local copies, waits for them, and re-layouts  2.06 us (7%)
  between operations  0.74 us (2%)
    ppermute x8, starting transfers between devices, swap(): return lax.ppermute(value, 'panel', [(i, i ^ apart) for i in range(panels)])  13.4 us
    ppermute x8, waiting for transfers between devices, swap(): return lax.ppermute(value, 'panel', [(i, i ^ apart) for i in range(panels)])  5.41 us
    ppermute x1, waiting for transfers between devices, on_device(): lax.ppermute(rounded, 'mach', [(i, (i + step) % machs) for i in range(mac...  2.16 us
    unnamed x16, local copies, waits for them, and re-layouts  2.06 us
    ppermute x1, starting transfers between devices, on_device(): lax.ppermute(rounded, 'mach', [(i, (i + step) % machs) for i in range(mac...  1.49 us
    pallas_call x1, Pallas kernels, on_device(): pl.pallas_call(functools.partial(spline_kernel, machs, rhs, struct_count)...  1.46 us
    pallas_call x1, Pallas kernels, on_device(): pl.pallas_call(functools.partial(near_kernel, rhs), out_shape=(jax.ShapeD...  1.15 us
    pallas_call x1, Pallas kernels, on_device(): pl.pallas_call(functools.partial(pick_kernel, panels, rhs), out_shape=(ja...  1.13 us
  transfers between devices with their start and end apart: 10, of which 5 were waited for; matrix products, arithmetic and copies ran while one was open for 0% of the time, Pallas kernels for 4%

profile of v3, /device:TPU:0, one launch (start us, length us, event | category | flops | bytes accessed | tf_op | source)
XLA Modules:
  0.0 30.5 jit_solution(12530025294269444596)
XLA Ops:
  0.6 0.0 copy-start.1
  0.6 4.1 %collective-permute-start.2 = (bf16[32,128]{1,0:T(8,128)(2,1)}, bf16[32,128]{1,0:T(8,128)(2,1)S(1)}, u32[]{:S(2)}, u32[]{:S(2)}) collective-permute-start(bf16[32,128]{1,0:T(8,128)(2,1)} %bitcast.5), channel_id=1, source_target_pairs={{0,8},{1,9},{2,10},{3,11},{4,12},{5,13},{6,14},{7,15},{8,0},{9,1},... | collective-permute-start | bytes 24584 | tf_op jit(solution)/shard_map/ppermute | solution.py:138
  4.7 0.6 %collective-permute-start.1 = (bf16[32,128]{1,0:T(8,128)(2,1)}, bf16[32,128]{1,0:T(8,128)(2,1)S(1)}, u32[]{:S(2)}, u32[]{:S(2)}) collective-permute-start(bf16[32,128]{1,0:T(8,128)(2,1)} %bitcast.6), channel_id=1, source_target_pairs={{1,2},{2,1},{3,4},{4,3},{5,6},{6,5},{7,8},{8,7},{9,10},{10,9},{11,... | collective-permute-start | bytes 24584 | tf_op jit(solution)/shard_map/ppermute | solution.py:158
  5.4 2.9 %collective-permute-start = (bf16[32,128]{1,0:T(8,128)(2,1)}, bf16[32,128]{1,0:T(8,128)(2,1)S(1)}, u32[]{:S(2)}, u32[]{:S(2)}) collective-permute-start(bf16[32,128]{1,0:T(8,128)(2,1)} %bitcast.7), channel_id=1, source_target_pairs={{0,1},{1,0},{2,3},{3,2},{4,5},{5,4},{6,7},{7,6},{8,9},{9,8},{10,11... | collective-permute-start | bytes 24584 | tf_op jit(solution)/shard_map/ppermute | solution.py:138
  8.3 0.7 %copy-done.3 = bf16[1,8,4,128]{3,2,1,0:T(4,128)(2,1)S(1)} copy-done((bf16[1,8,4,128]{3,2,1,0:T(4,128)(2,1)S(1)}, bf16[1,8,4,128]{3,2,1,0:T(4,128)(2,1)}, u32[]{:S(2)}) %copy-start.3) | copy-done | bytes 8216
  9.0 0.7 %copy-done.4 = s32[8,8]{1,0:T(8,128)S(1)} copy-done((s32[8,8]{1,0:T(8,128)S(1)}, s32[8,8]{1,0:T(8,128)}, u32[]{:S(2)}) %copy-start.4) | copy-done | bytes 280
  9.7 0.7 %copy-done.7 = s32[1,4]{1,0:T(1,128)S(1)} copy-done((s32[1,4]{1,0:T(1,128)S(1)}, s32[1,4]{1,0:T(1,128)}, u32[]{:S(2)}) %copy-start.7) | copy-done | bytes 40
  10.4 1.1 %pick_rows.1 = (bf16[8,32,128]{2,1,0:T(8,128)(2,1)S(1)}, f32[16,128]{1,0:T(8,128)S(1)}, bf16[32,128]{1,0:T(8,128)(2,1)S(1)}) custom-call(s32[8,8]{1,0:T(8,128)S(1)} %copy-done.4, s32[1,4]{1,0:T(1,128)S(1)} %copy-done.7, bf16[32,128]{1,0:T(8,128)(2,1)S(1)} %bitcast.8), custom_call_target="tpu_custom_call" | custom-call | flops 4000000000 | bytes 16777216 | tf_op jit(solution)/shard_map/pick_rows/pallas_call | solution.py:162
  11.5 0.0 collective-permute-done.2.mirror_ref
  11.5 0.0 collective-permute-done.1.cross_ref
  11.5 0.0 collective-permute-done.pair_ref
  11.6 0.0 copy-start.2
  11.6 0.0 copy-start.5
  11.6 0.0 copy-start.6
  11.6 1.2 %near_field.1 = (f32[32,128]{1,0:T(8,128)}, bf16[32,128]{1,0:T(8,128)(2,1)S(1)}) custom-call(bf16[8,32,128]{2,1,0:T(8,128)(2,1)S(1)} %get-tuple-element.15.hot_ref, f32[16,128]{1,0:T(8,128)S(1)} %get-tuple-element.16.gate_ref, bf16[32,128]{1,0:T(8,128)(2,1)S(1)} %get-tuple-element.17.own_ref, bf16[32,128]{1,0:T(8,128)(2,1)S(1)} %collective-permute-done.pair_ref, ...), custom_call_target="tpu_custom_call" | custom-call | flops 2000000000 | bytes 4194304 | tf_op jit(solution)/shard_map/near_field/pallas_call | solution.py:175
  12.8 1.5 %collective-permute-start.3 = (bf16[32,128]{1,0:T(8,128)(2,1)S(1)}, bf16[32,128]{1,0:T(8,128)(2,1)S(1)}, u32[]{:S(2)}, u32[]{:S(2)}) collective-permute-start(bf16[32,128]{1,0:T(8,128)(2,1)S(1)} %get-tuple-element.19.refs_0_), channel_id=1, source_target_pairs={{0,16},{16,0},{1,17},{17,1},{2,18},{18,2},{3,19},{19,3},{4,20},{20... | collective-permute-start | bytes 24584 | tf_op jit(solution)/shard_map/ppermute | solution.py:190
  14.3 2.2 %collective-permute-done.3.refs_1_ = bf16[32,128]{1,0:T(8,128)(2,1)S(1)} collective-permute-done((bf16[32,128]{1,0:T(8,128)(2,1)S(1)}, bf16[32,128]{1,0:T(8,128)(2,1)S(1)}, u32[]{:S(2)}, u32[]{:S(2)}) %collective-permute-start.3) | collective-permute-done | bytes 8224 | tf_op jit(solution)/shard_map/ppermute | solution.py:190
  16.4 1.5 %spline_loads.1 = (f32[4,32,128]{2,1,0:T(8,128)S(1)}, bf16[4,32,128]{2,1,0:T(8,128)(2,1)S(1)}, bf16[4,32,128]{2,1,0:T(8,128)(2,1)S(1)}, bf16[4,32,128]{2,1,0:T(8,128)(2,1)S(1)}) custom-call(s32[8,6]{1,0:T(8,128)S(1)} %copy-done.5, s32[8,6]{1,0:T(8,128)S(1)} %copy-done.6, bf16[32,128]{1,0:T(8,128)(2,1)S(1)} %get-tuple-element.19.refs_0_, ...), custom_call_target="tpu_custom_call" | custom-call | flops 2000000000 | bytes 4194304 | tf_op jit(solution)/shard_map/spline_loads/pallas_call | solution.py:194
  17.9 0.1 collective-permute-start.4
  18.0 1.6 %collective-permute-start.5 = (bf16[4,32,128]{2,1,0:T(8,128)(2,1)S(1)}, bf16[4,32,128]{2,1,0:T(8,128)(2,1)S(1)}, u32[]{:S(2)}, u32[]{:S(2)}) collective-permute-start(bf16[4,32,128]{2,1,0:T(8,128)(2,1)S(1)} %get-tuple-element.22), channel_id=1, source_target_pairs={{0,2},{1,3},{2,0},{3,1},{4,6},{5,7},{6,4},{7,5},{8,10},{9,11},{10,... | collective-permute-start | bytes 98312 | tf_op jit(solution)/shard_map/ppermute | solution.py:138
  19.6 0.3 collective-permute-start.6
  19.8 0.0 collective-permute-done.4.refs_1_
  19.8 2.1 %collective-permute-done.5.refs_2_ = bf16[4,32,128]{2,1,0:T(8,128)(2,1)S(1)} collective-permute-done((bf16[4,32,128]{2,1,0:T(8,128)(2,1)S(1)}, bf16[4,32,128]{2,1,0:T(8,128)(2,1)S(1)}, u32[]{:S(2)}, u32[]{:S(2)}) %collective-permute-start.5) | collective-permute-done | bytes 32800 | tf_op jit(solution)/shard_map/ppermute | solution.py:138
  22.0 0.9 %collective-permute-done.6.refs_3_ = bf16[4,32,128]{2,1,0:T(8,128)(2,1)S(1)} collective-permute-done((bf16[4,32,128]{2,1,0:T(8,128)(2,1)S(1)}, bf16[4,32,128]{2,1,0:T(8,128)(2,1)S(1)}, u32[]{:S(2)}, u32[]{:S(2)}) %collective-permute-start.6) | collective-permute-done | bytes 32800 | tf_op jit(solution)/shard_map/ppermute | solution.py:138
  22.9 0.9 %collective-permute-start.7 = (bf16[32,128]{1,0:T(8,128)(2,1)S(1)}, bf16[32,128]{1,0:T(8,128)(2,1)S(1)}, u32[]{:S(2)}, u32[]{:S(2)}) collective-permute-start(bf16[32,128]{1,0:T(8,128)(2,1)S(1)} %get-tuple-element.25), channel_id=1, source_target_pairs={{0,4},{1,5},{2,6},{3,7},{4,0},{5,1},{6,2},{7,3},{8,12},{9,13},{10,... | collective-permute-start | bytes 24584 | tf_op jit(solution)/shard_map/ppermute | solution.py:138
  23.8 0.5 %collective-permute-start.8 = (bf16[32,128]{1,0:T(8,128)(2,1)S(1)}, bf16[32,128]{1,0:T(8,128)(2,1)S(1)}, u32[]{:S(2)}, u32[]{:S(2)}) collective-permute-start(bf16[32,128]{1,0:T(8,128)(2,1)S(1)} %get-tuple-element.26), channel_id=1, source_target_pairs={{0,8},{1,9},{2,10},{3,11},{4,12},{5,13},{6,14},{7,15},{8,0},{9,1},... | collective-permute-start | bytes 24584 | tf_op jit(solution)/shard_map/ppermute | solution.py:138
  24.3 3.1 %collective-permute-start.9 = (bf16[32,128]{1,0:T(8,128)(2,1)S(1)}, bf16[32,128]{1,0:T(8,128)(2,1)S(1)}, u32[]{:S(2)}, u32[]{:S(2)}) collective-permute-start(bf16[32,128]{1,0:T(8,128)(2,1)S(1)} %get-tuple-element.27), channel_id=1, source_target_pairs={{0,12},{1,13},{2,14},{3,15},{4,8},{5,9},{6,10},{7,11},{8,4},{9,5},... | collective-permute-start | bytes 24584 | tf_op jit(solution)/shard_map/ppermute | solution.py:138
  27.4 0.0 collective-permute-done.7.refs_1_
  27.4 1.0 %collective-permute-done.8.refs_2_ = bf16[32,128]{1,0:T(8,128)(2,1)S(1)} collective-permute-done((bf16[32,128]{1,0:T(8,128)(2,1)S(1)}, bf16[32,128]{1,0:T(8,128)(2,1)S(1)}, u32[]{:S(2)}, u32[]{:S(2)}) %collective-permute-start.8) | collective-permute-done | bytes 8224 | tf_op jit(solution)/shard_map/ppermute | solution.py:138
  28.4 1.4 %collective-permute-done.9.refs_3_ = bf16[32,128]{1,0:T(8,128)(2,1)S(1)} collective-permute-done((bf16[32,128]{1,0:T(8,128)(2,1)S(1)}, bf16[32,128]{1,0:T(8,128)(2,1)S(1)}, u32[]{:S(2)}, u32[]{:S(2)}) %collective-permute-start.9) | collective-permute-done | bytes 8224 | tf_op jit(solution)/shard_map/ppermute | solution.py:138
  29.7 0.0 copy-done
  29.7 0.8 %struct_solve.1 = f32[32,128]{1,0:T(8,128)} custom-call(f32[32,128]{1,0:T(8,128)S(1)} %get-tuple-element.24.refs_0_, bf16[32,128]{1,0:T(8,128)(2,1)S(1)} %collective-permute-done.7.refs_1_, bf16[32,128]{1,0:T(8,128)(2,1)S(1)} %collective-permute-done.8.refs_2_, bf16[32,128]{1,0:T(8,128)(2,1)S(1)} %collective-permute-done.9.refs_3_, ...), custom_call_target="tpu_custom_call" | custom-call | tf_op jit(solution)/shard_map/struct_solve/pallas_call | solution.py:221
  (9 shorter events, 0.0 us)
Async XLA Ops:
  0.6 10.9 %copy-start.1 = (bf16[1,8,8,128,128]{4,3,2,1,0:T(8,128)(2,1)S(1)}, bf16[1,8,8,128,128]{4,3,2,1,0:T(8,128)(2,1)}, u32[]{:S(2)}) copy-start(bf16[1,8,8,128,128]{4,3,2,1,0:T(8,128)(2,1)} %param.9) | copy-start | bytes 6291460
  0.6 10.9 %collective-permute-start.2 = (bf16[32,128]{1,0:T(8,128)(2,1)}, bf16[32,128]{1,0:T(8,128)(2,1)S(1)}, u32[]{:S(2)}, u32[]{:S(2)}) collective-permute-start(bf16[32,128]{1,0:T(8,128)(2,1)} %bitcast.5), channel_id=1, source_target_pairs={{0,8},{1,9},{2,10},{3,11},{4,12},{5,13},{6,14},{7,15},{8,0},{9,1},... | collective-permute-start | bytes 24584 | tf_op jit(solution)/shard_map/ppermute | solution.py:138
  4.7 6.8 %collective-permute-start.1 = (bf16[32,128]{1,0:T(8,128)(2,1)}, bf16[32,128]{1,0:T(8,128)(2,1)S(1)}, u32[]{:S(2)}, u32[]{:S(2)}) collective-permute-start(bf16[32,128]{1,0:T(8,128)(2,1)} %bitcast.6), channel_id=1, source_target_pairs={{1,2},{2,1},{3,4},{4,3},{5,6},{6,5},{7,8},{8,7},{9,10},{10,9},{11,... | collective-permute-start | bytes 24584 | tf_op jit(solution)/shard_map/ppermute | solution.py:158
  5.4 6.2 %collective-permute-start = (bf16[32,128]{1,0:T(8,128)(2,1)}, bf16[32,128]{1,0:T(8,128)(2,1)S(1)}, u32[]{:S(2)}, u32[]{:S(2)}) collective-permute-start(bf16[32,128]{1,0:T(8,128)(2,1)} %bitcast.7), channel_id=1, source_target_pairs={{0,1},{1,0},{2,3},{3,2},{4,5},{5,4},{6,7},{7,6},{8,9},{9,8},{10,11... | collective-permute-start | bytes 24584 | tf_op jit(solution)/shard_map/ppermute | solution.py:138
  8.3 0.7 %copy-start.3 = (bf16[1,8,4,128]{3,2,1,0:T(4,128)(2,1)S(1)}, bf16[1,8,4,128]{3,2,1,0:T(4,128)(2,1)}, u32[]{:S(2)}) copy-start(bf16[1,8,4,128]{3,2,1,0:T(4,128)(2,1)} %param.8) | copy-start | bytes 24580
  9.0 0.7 %copy-start.4 = (s32[8,8]{1,0:T(8,128)S(1)}, s32[8,8]{1,0:T(8,128)}, u32[]{:S(2)}) copy-start(s32[8,8]{1,0:T(8,128)} %pattern_ref.1) | copy-start | bytes 772
  9.7 0.7 %copy-start.7 = (s32[1,4]{1,0:T(1,128)S(1)}, s32[1,4]{1,0:T(1,128)}, u32[]{:S(2)}) copy-start(s32[1,4]{1,0:T(1,128)} %trim_ref.1) | copy-start | bytes 52
  11.6 4.8 %copy-start.2 = (bf16[8,6,128,128]{3,2,1,0:T(8,128)(2,1)S(1)}, bf16[8,6,128,128]{3,2,1,0:T(8,128)(2,1)}, u32[]{:S(2)}) copy-start(bf16[8,6,128,128]{3,2,1,0:T(8,128)(2,1)} %refs_2_.1) | copy-start | bytes 4718596
  11.6 4.8 %copy-start.5 = (s32[8,6]{1,0:T(8,128)S(1)}, s32[8,6]{1,0:T(8,128)}, u32[]{:S(2)}) copy-start(s32[8,6]{1,0:T(8,128)} %owner_ref.1) | copy-start | bytes 580
  11.6 4.8 %copy-start.6 = (s32[8,6]{1,0:T(8,128)S(1)}, s32[8,6]{1,0:T(8,128)}, u32[]{:S(2)}) copy-start(s32[8,6]{1,0:T(8,128)} %local_ref.1) | copy-start | bytes 580
  12.8 17.0 %copy-start = (bf16[8,128,128]{2,1,0:T(8,128)(2,1)S(1)}, bf16[8,128,128]{2,1,0:T(8,128)(2,1)}, u32[]{:S(2)}) copy-start(bf16[8,128,128]{2,1,0:T(8,128)(2,1)} %refs_4_.1) | copy-start | bytes 786436
  12.8 3.7 %collective-permute-start.3 = (bf16[32,128]{1,0:T(8,128)(2,1)S(1)}, bf16[32,128]{1,0:T(8,128)(2,1)S(1)}, u32[]{:S(2)}, u32[]{:S(2)}) collective-permute-start(bf16[32,128]{1,0:T(8,128)(2,1)S(1)} %get-tuple-element.19.refs_0_), channel_id=1, source_target_pairs={{0,16},{16,0},{1,17},{17,1},{2,18},{18,2},{3,19},{19,3},{4,20},{20... | collective-permute-start | bytes 24584 | tf_op jit(solution)/shard_map/ppermute | solution.py:190
  17.9 1.9 %collective-permute-start.4 = (bf16[4,32,128]{2,1,0:T(8,128)(2,1)S(1)}, bf16[4,32,128]{2,1,0:T(8,128)(2,1)S(1)}, u32[]{:S(2)}, u32[]{:S(2)}) collective-permute-start(bf16[4,32,128]{2,1,0:T(8,128)(2,1)S(1)} %get-tuple-element.21), channel_id=1, source_target_pairs={{0,1},{1,0},{2,3},{3,2},{4,5},{5,4},{6,7},{7,6},{8,9},{9,8},{10,11... | collective-permute-start | bytes 98312 | tf_op jit(solution)/shard_map/ppermute | solution.py:138
  18.0 4.0 %collective-permute-start.5 = (bf16[4,32,128]{2,1,0:T(8,128)(2,1)S(1)}, bf16[4,32,128]{2,1,0:T(8,128)(2,1)S(1)}, u32[]{:S(2)}, u32[]{:S(2)}) collective-permute-start(bf16[4,32,128]{2,1,0:T(8,128)(2,1)S(1)} %get-tuple-element.22), channel_id=1, source_target_pairs={{0,2},{1,3},{2,0},{3,1},{4,6},{5,7},{6,4},{7,5},{8,10},{9,11},{10,... | collective-permute-start | bytes 98312 | tf_op jit(solution)/shard_map/ppermute | solution.py:138
  19.6 3.3 %collective-permute-start.6 = (bf16[4,32,128]{2,1,0:T(8,128)(2,1)S(1)}, bf16[4,32,128]{2,1,0:T(8,128)(2,1)S(1)}, u32[]{:S(2)}, u32[]{:S(2)}) collective-permute-start(bf16[4,32,128]{2,1,0:T(8,128)(2,1)S(1)} %get-tuple-element.23), channel_id=1, source_target_pairs={{0,3},{1,2},{2,1},{3,0},{4,7},{5,6},{6,5},{7,4},{8,11},{9,10},{10,... | collective-permute-start | bytes 98312 | tf_op jit(solution)/shard_map/ppermute | solution.py:138
  22.9 4.5 %collective-permute-start.7 = (bf16[32,128]{1,0:T(8,128)(2,1)S(1)}, bf16[32,128]{1,0:T(8,128)(2,1)S(1)}, u32[]{:S(2)}, u32[]{:S(2)}) collective-permute-start(bf16[32,128]{1,0:T(8,128)(2,1)S(1)} %get-tuple-element.25), channel_id=1, source_target_pairs={{0,4},{1,5},{2,6},{3,7},{4,0},{5,1},{6,2},{7,3},{8,12},{9,13},{10,... | collective-permute-start | bytes 24584 | tf_op jit(solution)/shard_map/ppermute | solution.py:138
  23.8 4.6 %collective-permute-start.8 = (bf16[32,128]{1,0:T(8,128)(2,1)S(1)}, bf16[32,128]{1,0:T(8,128)(2,1)S(1)}, u32[]{:S(2)}, u32[]{:S(2)}) collective-permute-start(bf16[32,128]{1,0:T(8,128)(2,1)S(1)} %get-tuple-element.26), channel_id=1, source_target_pairs={{0,8},{1,9},{2,10},{3,11},{4,12},{5,13},{6,14},{7,15},{8,0},{9,1},... | collective-permute-start | bytes 24584 | tf_op jit(solution)/shard_map/ppermute | solution.py:138
  24.3 5.4 %collective-permute-start.9 = (bf16[32,128]{1,0:T(8,128)(2,1)S(1)}, bf16[32,128]{1,0:T(8,128)(2,1)S(1)}, u32[]{:S(2)}, u32[]{:S(2)}) collective-permute-start(bf16[32,128]{1,0:T(8,128)(2,1)S(1)} %get-tuple-element.27), channel_id=1, source_target_pairs={{0,12},{1,13},{2,14},{3,15},{4,8},{5,9},{6,10},{7,11},{8,4},{9,5},... | collective-permute-start | bytes 24584 | tf_op jit(solution)/shard_map/ppermute | solution.py:138

commit v4 on v3

v4 whole, which is shorter than its diff:
```python
import functools

import jax
import jax.numpy as jnp
from jax import lax
from jax.experimental import pallas as pl
from jax.experimental.pallas import tpu as pltpu
from jax.sharding import PartitionSpec as P

SMEM = pl.BlockSpec(memory_space=pltpu.SMEM)
VMEM = pl.BlockSpec(memory_space=pltpu.VMEM)
PACK = 16
TILE = 8


def spread_kernel(machs, rhs, block_count, expand_ref, order_ref):
    shape = expand_ref.shape
    expand_ref[...] = (
        lax.broadcasted_iota(jnp.int32, shape, 0) // rhs == lax.broadcasted_iota(jnp.int32, shape, 1)
    ).astype(jnp.bfloat16)
    shape = order_ref.shape
    row = lax.broadcasted_iota(jnp.int32, shape, 0)
    source = (
        (row // TILE) % machs * (block_count * rhs) + row // (TILE * machs) * rhs + row % rhs
    )
    order_ref[...] = (lax.broadcasted_iota(jnp.int32, shape, 1) == source).astype(jnp.bfloat16)


def pick_kernel(
    panels, rhs, expand_ref, pattern_ref, trim_ref, own_ref, hot_ref, gate_ref, held_ref
):
    block_count, entries = pattern_ref.shape
    rows = own_ref.shape[0]
    here = lax.axis_index("panel")
    shape = (rows, hot_ref.shape[1])
    offset = lax.broadcasted_iota(jnp.int32, shape, 1) - (
        lax.broadcasted_iota(jnp.int32, shape, 0) % rhs
    )
    block = pattern_ref[...]
    apart = (block // block_count) ^ here
    slot = jnp.where(
        apart == 0, 0, jnp.where(apart == panels // 2, 3, jnp.where(apart == 1, 1, 2))
    )
    first = (slot * block_count + block % block_count) * rhs
    first = jnp.dot(
        expand_ref[...],
        first.astype(jnp.float32).astype(jnp.bfloat16),
        preferred_element_type=jnp.float32,
    ).astype(jnp.int32)
    for k in range(entries):
        hot_ref[k * rows : (k + 1) * rows] = (offset == first[:, k : k + 1]).astype(jnp.bfloat16)
    shape = (gate_ref.shape[0], rhs)
    mine = lax.broadcasted_iota(jnp.int32, shape, 0) % rhs == lax.broadcasted_iota(
        jnp.int32, shape, 1
    )
    gate = jnp.sum(jnp.where(mine, trim_ref[...], 0).astype(jnp.float32), axis=1, keepdims=True)
    gate_ref[...] = jnp.broadcast_to(gate, gate_ref.shape)
    held_ref[...] = own_ref[...]


def grouped_product(rhs, left, blocks_of, group):
    per_group = PACK // rhs
    every = jnp.concatenate([blocks_of(group * per_group + j) for j in range(per_group)], axis=1)
    product = jnp.dot(left, every, preferred_element_type=jnp.float32)
    width = product.shape[1] // per_group
    row = lax.broadcasted_iota(jnp.int32, (PACK, width), 0)
    out = product[:, :width]
    for j in range(1, per_group):
        out = jnp.where(row // rhs == j, product[:, j * width : (j + 1) * width], out)
    return out


def near_kernel(
    rhs, hot_ref, gate_ref, own_ref, pair_ref, cross_ref, mirror_ref, near_ref,
    loads_ref, rounded_ref,
):
    rows, width = own_ref.shape
    entries = hot_ref.shape[0] // rows
    pool = jnp.concatenate(
        [own_ref[...], pair_ref[...], cross_ref[...], mirror_ref[...]], axis=0
    )
    picked = jnp.dot(hot_ref[...], pool, preferred_element_type=jnp.float32)
    picked = picked.astype(jnp.bfloat16)
    for g in range(rows // PACK):
        left = jnp.concatenate(
            [picked[k * rows + g * PACK : k * rows + (g + 1) * PACK] for k in range(entries)],
            axis=1,
        )
        loads = gate_ref[...] * grouped_product(
            rhs, left, lambda i: near_ref[i].reshape(entries * width, width), g
        )
        loads_ref[g * PACK : (g + 1) * PACK] = loads
        rounded_ref[g * PACK : (g + 1) * PACK] = loads.astype(jnp.bfloat16)


def spline_kernel(machs, rhs, struct_count, owner_ref, local_ref, order_ref, *refs):
    rounded_refs, spline_ref, keep_ref, send_ref, acc = refs[:machs], *refs[machs:]
    block_count, splines = owner_ref.shape
    rows, width = rounded_refs[0].shape
    here = lax.axis_index("panel")
    acc[...] = jnp.zeros(acc.shape, jnp.float32)
    every = jnp.concatenate([ref[...] for ref in rounded_refs], axis=0)
    left = jnp.dot(order_ref[...], every, preferred_element_type=jnp.float32)
    left = left.astype(jnp.bfloat16)
    part = lax.broadcasted_iota(jnp.int32, (TILE, width), 0) // rhs
    per_tile = TILE // rhs
    owner_tiles = struct_count // per_tile
    height = machs * TILE
    blank = jnp.zeros((height, width), jnp.bfloat16)
    for pair in range(0, block_count, 2):
        mine = left[pair * height : (pair + 2) * height]
        mine = jnp.concatenate(
            [
                jnp.concatenate([mine[:height], blank], axis=1),
                jnp.concatenate([blank, mine[height:]], axis=1),
            ],
            axis=0,
        )
        blocks = jnp.concatenate(
            [
                jnp.concatenate([spline_ref[i, s] for s in range(splines)], axis=1)
                for i in (pair, pair + 1)
            ],
            axis=0,
        )
        product = jnp.dot(mine, blocks, preferred_element_type=jnp.float32)
        for i in (pair, pair + 1):
            total = product[(i - pair) * height : (i - pair) * height + TILE]
            for m in range(1, machs):
                start = (i - pair) * height + m * TILE
                total = total + product[start : start + TILE]
            places, sums = [], []
            for s in range(splines):
                apart = owner_ref[i, s] ^ here
                local = local_ref[i, s]
                place = (apart % 2, apart // 2 * owner_tiles + local // per_tile)
                added = jnp.where(
                    part == local % per_tile, total[:, s * width : (s + 1) * width], 0.0
                )
                places.append(place)
                sums.append(acc[place] + added)
            for place, value in zip(places, sums):
                acc[place] = value
    keep_ref[...] = acc[0].reshape(keep_ref.shape)
    send_ref[...] = acc[1].reshape(send_ref.shape).astype(send_ref.dtype)


def sum_kernel(held_ref, got_ref, keep_ref, send_ref):
    for place in range(held_ref.shape[0]):
        total = held_ref[place] + got_ref[place].astype(jnp.float32)
        if place % 2 == 0:
            keep_ref[place // 2] = total
        else:
            send_ref[place // 2] = total.astype(send_ref.dtype)


def inverse_kernel(rhs, held_ref, got_ref, inverse_ref, out_ref):
    total = held_ref[0] + got_ref[0].astype(jnp.float32)
    rounded = total.astype(jnp.bfloat16)
    for g in range(total.shape[0] // PACK):
        out_ref[g * PACK : (g + 1) * PACK] = grouped_product(
            rhs, rounded[g * PACK : (g + 1) * PACK], lambda t: inverse_ref[t], g
        )


def swap(value, panels, apart):
    return lax.ppermute(value, "panel", [(i, i ^ apart) for i in range(panels)])


def cost(flops, size):
    return pl.CostEstimate(flops=flops, bytes_accessed=size, transcendentals=0)


def on_device(
    adjoint, near_blocks, pattern, trim_mask, spline_blocks, spline_owner, spline_local,
    struct_inverse,
):
    _, block_count, rhs, width = adjoint.shape
    entries = pattern.shape[1]
    panels, machs = lax.axis_size("panel"), lax.axis_size("mach")
    struct_count = struct_inverse.shape[0]
    rows, struct_rows = block_count * rhs, struct_count * rhs
    params = pltpu.CompilerParams(vmem_limit_bytes=16 * 1024 * 1024)
    f32, bf16 = jnp.float32, jnp.bfloat16
    own = adjoint.reshape(rows, width)
    mirror = swap(own, panels, panels // 2)
    cross = lax.ppermute(
        own, "panel", [(i, min(max(i - 1 + 2 * (i % 2), 0), panels - 1)) for i in range(panels)]
    )
    pair = swap(own, panels, 1)
    expand, order = pl.pallas_call(
        functools.partial(spread_kernel, machs, rhs, block_count),
        out_shape=(
            jax.ShapeDtypeStruct((rows, block_count), bf16),
            jax.ShapeDtypeStruct((block_count * machs * TILE, machs * rows), bf16),
        ),
        out_specs=(VMEM, VMEM),
        compiler_params=params,
        cost_estimate=cost(4 * 10**9, 16 * 2**20),
        name="row_order",
    )()
    hot, gate, held = pl.pallas_call(
        functools.partial(pick_kernel, panels, rhs),
        out_shape=(
            jax.ShapeDtypeStruct((entries * rows, 4 * rows), bf16),
            jax.ShapeDtypeStruct((PACK, width), f32),
            jax.ShapeDtypeStruct((rows, width), bf16),
        ),
        in_specs=[VMEM] * 4,
        out_specs=(VMEM, VMEM, VMEM),
        compiler_params=params,
        cost_estimate=cost(10**6, 2**17),
        name="pick_rows",
    )(expand, pattern, trim_mask, own)
    loads, rounded = pl.pallas_call(
        functools.partial(near_kernel, rhs),
        out_shape=(
            jax.ShapeDtypeStruct((rows, width), f32),
            jax.ShapeDtypeStruct((rows, width), bf16),
        ),
        in_specs=[VMEM] * 7,
        out_specs=(VMEM, VMEM),
        compiler_params=params,
        cost_estimate=cost(2 * 10**9, 4 * 2**20),
        name="near_field",
    )(hot, gate, held, pair, cross, mirror, near_blocks[0])
    every = [rounded]
    for step in range(1, machs):
        every.append(
            lax.ppermute(rounded, "mach", [(i, (i + step) % machs) for i in range(machs)])
        )
    half = (panels // 2, struct_rows, width)
    keep, send = pl.pallas_call(
        functools.partial(spline_kernel, machs, rhs, struct_count),
        out_shape=(jax.ShapeDtypeStruct(half, f32), jax.ShapeDtypeStruct(half, bf16)),
        in_specs=[SMEM, SMEM] + [VMEM] * (machs + 2),
        out_specs=(VMEM, VMEM),
        scratch_shapes=[pltpu.VMEM((2, panels // 2 * struct_rows // TILE, TILE, width), f32)],
        compiler_params=params,
        cost_estimate=cost(2 * 10**9, 4 * 2**20),
        name="spline_loads",
    )(spline_owner, spline_local, order, *every, spline_blocks)
    apart = 1
    got = swap(send, panels, apart)
    while 2 * apart < panels:
        apart *= 2
        half = (panels // (2 * apart), struct_rows, width)
        keep, send = pl.pallas_call(
            sum_kernel,
            out_shape=(jax.ShapeDtypeStruct(half, f32), jax.ShapeDtypeStruct(half, bf16)),
            in_specs=[VMEM, VMEM],
            out_specs=(VMEM, VMEM),
            compiler_params=params,
            cost_estimate=cost(10**6, 2**20),
            name="pair_sum",
        )(keep, got)
        got = swap(send, panels, apart)
    struct_adjoint = pl.pallas_call(
        functools.partial(inverse_kernel, rhs),
        out_shape=jax.ShapeDtypeStruct((struct_rows, width), f32),
        in_specs=[VMEM] * 3,
        out_specs=VMEM,
        compiler_params=params,
        cost_estimate=cost(10**9, 2**20),
        name="struct_solve",
    )(keep, got, struct_inverse)
    return (
        loads.reshape(1, block_count, rhs, width),
        struct_adjoint.reshape(struct_count, rhs, width),
    )


def solution(mesh):
    in_specs = (
        P("mach", "panel", None, None),
        P("mach", "panel", None, None, None),
        P("panel", None),
        P("mach", None),
        P("panel", None, None, None),
        P("panel", None),
        P("panel", None),
        P("panel", None, None),
    )
    out_specs = (P("mach", "panel", None, None), P("panel", None, None))
    return jax.shard_map(
        on_device, mesh=mesh, in_specs=in_specs, out_specs=out_specs, check_vma=False
    )
```

time: 30.8 us -> 31.4 us (1.019)
  waiting for transfers between devices: 7.57 us -> 11.3 us
  local copies, waits for them, and re-layouts: 2.06 us -> 0.03 us
  Pallas kernels: 4.56 us -> 3.69 us
    ppermute x8 -> x6, waiting for transfers between devices: 5.41 us -> 9.1 us  [swap(): return lax.ppermute(value, 'panel', [(i, i ^ apart) for i in range(panels)])]
    unnamed x16, local copies, waits for them, and re-layouts: 2.06 us -> 0.03 us
    pallas_call x1, Pallas kernels: 1.13 us -> 0.26 us  [on_device(): pl.pallas_call(functools.partial(pick_kernel, panels, rhs), out_shape=(ja...]
    ppermute x8 -> x6, starting transfers between devices: 13.4 us -> 12.6 us  [swap(): return lax.ppermute(value, 'panel', [(i, i ^ apart) for i in range(panels)])]
    ppermute x1, starting transfers between devices: 0.65 us -> 1.34 us  [on_device(): lax.ppermute(own, 'panel', [(i, min(max(i - 1 + 2 * (i % 2), 0), panels -...]
  transfers between devices with their start and end apart: 10 -> 8, of which waited for: 5 -> 6; matrix products, arithmetic and copies ran while one was open for 0% -> 0% of each run, Pallas kernels for 4% -> 1%
where the time goes in v4:
time: 31.4 us; the launch traced here: 31.2 us
  starting transfers between devices  15.4 us (49%)
  waiting for transfers between devices  11.3 us (36%)
  Pallas kernels  3.69 us (12%)
  between operations  0.76 us (2%)
    ppermute x6, starting transfers between devices, swap(): return lax.ppermute(value, 'panel', [(i, i ^ apart) for i in range(panels)])  12.6 us
    ppermute x6, waiting for transfers between devices, swap(): return lax.ppermute(value, 'panel', [(i, i ^ apart) for i in range(panels)])  9.1 us
    ppermute x1, waiting for transfers between devices, on_device(): lax.ppermute(rounded, 'mach', [(i, (i + step) % machs) for i in range(mac...  2.16 us
    ppermute x1, starting transfers between devices, on_device(): lax.ppermute(rounded, 'mach', [(i, (i + step) % machs) for i in range(mac...  1.49 us
    pallas_call x1, Pallas kernels, on_device(): pl.pallas_call(functools.partial(spline_kernel, machs, rhs, struct_count)...  1.49 us
    ppermute x1, starting transfers between devices, on_device(): lax.ppermute(own, 'panel', [(i, min(max(i - 1 + 2 * (i % 2), 0), panels -...  1.34 us
    pallas_call x1, Pallas kernels, on_device(): pl.pallas_call(functools.partial(near_kernel, rhs), out_shape=(jax.ShapeD...  1.11 us
    pallas_call x1, Pallas kernels, on_device(): pl.pallas_call(functools.partial(inverse_kernel, rhs), out_shape=jax.Shap...  0.76 us
  transfers between devices with their start and end apart: 8, of which 6 were waited for; matrix products, arithmetic and copies ran while one was open for 0% of the time, Pallas kernels for 1%

profile of v4, /device:TPU:0, one launch (start us, length us, event | category | flops | bytes accessed | tf_op | source)
XLA Modules:
  0.0 31.2 jit_solution(13886910689232467319)
XLA Ops:
  0.6 0.0 copy-start
  0.6 0.0 copy-start.1
  0.7 0.0 copy-start.2
  0.7 0.0 copy-start.3
  0.7 4.1 %collective-permute-start.2 = (bf16[32,128]{1,0:T(8,128)(2,1)}, bf16[32,128]{1,0:T(8,128)(2,1)S(1)}, u32[]{:S(2)}, u32[]{:S(2)}) collective-permute-start(bf16[32,128]{1,0:T(8,128)(2,1)} %bitcast.4), channel_id=1, source_target_pairs={{0,8},{1,9},{2,10},{3,11},{4,12},{5,13},{6,14},{7,15},{8,0},{9,1},... | collective-permute-start | bytes 24584 | tf_op jit(solution)/shard_map/ppermute | solution.py:167
  4.8 1.3 %collective-permute-start.1 = (bf16[32,128]{1,0:T(8,128)(2,1)}, bf16[32,128]{1,0:T(8,128)(2,1)S(1)}, u32[]{:S(2)}, u32[]{:S(2)}) collective-permute-start(bf16[32,128]{1,0:T(8,128)(2,1)} %bitcast.5), channel_id=1, source_target_pairs={{0,0},{1,2},{2,1},{3,4},{4,3},{5,6},{6,5},{7,8},{8,7},{9,10},{10,9... | collective-permute-start | bytes 24584 | tf_op jit(solution)/shard_map/ppermute | solution.py:187
  6.1 2.3 %collective-permute-start = (bf16[32,128]{1,0:T(8,128)(2,1)}, bf16[32,128]{1,0:T(8,128)(2,1)S(1)}, u32[]{:S(2)}, u32[]{:S(2)}) collective-permute-start(bf16[32,128]{1,0:T(8,128)(2,1)} %bitcast.6), channel_id=1, source_target_pairs={{0,1},{1,0},{2,3},{3,2},{4,5},{5,4},{6,7},{7,6},{8,9},{9,8},{10,11... | collective-permute-start | bytes 24584 | tf_op jit(solution)/shard_map/ppermute | solution.py:167
  8.4 0.0 copy-done
  8.4 0.0 copy-done.1
  8.4 0.0 copy-done.2
  8.4 0.3 pick_rows.1
  8.7 0.0 collective-permute-done.2.mirror_ref
  8.7 0.0 collective-permute-done.1.cross_ref
  8.7 0.7 %collective-permute-done.pair_ref = bf16[32,128]{1,0:T(8,128)(2,1)S(1)} collective-permute-done((bf16[32,128]{1,0:T(8,128)(2,1)}, bf16[32,128]{1,0:T(8,128)(2,1)S(1)}, u32[]{:S(2)}, u32[]{:S(2)}) %collective-permute-start) | collective-permute-done | bytes 8224 | tf_op jit(solution)/shard_map/ppermute | solution.py:167
  9.4 0.0 copy-done.3
  9.4 1.1 %near_field.1 = (f32[32,128]{1,0:T(8,128)}, bf16[32,128]{1,0:T(8,128)(2,1)S(1)}) custom-call(bf16[256,128]{1,0:T(8,128)(2,1)S(1)} %get-tuple-element.18.hot_ref, f32[16,128]{1,0:T(8,128)S(1)} %get-tuple-element.19.gate_ref, bf16[32,128]{1,0:T(8,128)(2,1)S(1)} %get-tuple-element.20.own_ref, bf16[32,128]{1,0:T(8,128)(2,1)S(1)} %collective-permute-done.pair_ref, ...), custom_call_target="tpu_custom_call" | custom-call | flops 2000000000 | bytes 4194304 | tf_op jit(solution)/shard_map/near_field/pallas_call | solution.py:215
  10.5 1.5 %collective-permute-start.3 = (bf16[32,128]{1,0:T(8,128)(2,1)S(1)}, bf16[32,128]{1,0:T(8,128)(2,1)S(1)}, u32[]{:S(2)}, u32[]{:S(2)}) collective-permute-start(bf16[32,128]{1,0:T(8,128)(2,1)S(1)} %get-tuple-element.23.refs_0_), channel_id=1, source_target_pairs={{0,16},{16,0},{1,17},{17,1},{2,18},{18,2},{3,19},{19,3},{4,20},{20... | collective-permute-start | bytes 24584 | tf_op jit(solution)/shard_map/ppermute | solution.py:230
  12.0 2.2 %collective-permute-done.3.refs_1_ = bf16[32,128]{1,0:T(8,128)(2,1)S(1)} collective-permute-done((bf16[32,128]{1,0:T(8,128)(2,1)S(1)}, bf16[32,128]{1,0:T(8,128)(2,1)S(1)}, u32[]{:S(2)}, u32[]{:S(2)}) %collective-permute-start.3) | collective-permute-done | bytes 8224 | tf_op jit(solution)/shard_map/ppermute | solution.py:230
  14.2 0.0 copy-done.4
  14.2 0.0 copy-done.6
  14.2 0.0 copy-done.7
  14.2 0.0 copy-start.5
  14.2 1.5 %spline_loads.1 = (f32[8,32,128]{2,1,0:T(8,128)S(1)}, bf16[8,32,128]{2,1,0:T(8,128)(2,1)S(1)}) custom-call(s32[8,6]{1,0:T(8,128)S(1)} %copy-done.6, s32[8,6]{1,0:T(8,128)S(1)} %copy-done.7, bf16[128,64]{1,0:T(8,128)(2,1)S(1)} %get-tuple-element.22.order_ref, bf16[32,128]{1,0:T(8,128)(2,1)S(1)} %get-tuple-element.23.refs_0_, ...), custom_call_target="tpu_custom_call" | custom-call | flops 2000000000 | bytes 4194304 | tf_op jit(solution)/shard_map/spline_loads/pallas_call | solution.py:233
  15.7 0.1 collective-permute-start.4
  15.8 1.2 %collective-permute-done.4.got_ref = bf16[8,32,128]{2,1,0:T(8,128)(2,1)S(1)} collective-permute-done((bf16[8,32,128]{2,1,0:T(8,128)(2,1)S(1)}, bf16[8,32,128]{2,1,0:T(8,128)(2,1)S(1)}, u32[]{:S(2)}, u32[]{:S(2)}) %collective-permute-start.4) | collective-permute-done | bytes 65568 | tf_op jit(solution)/shard_map/ppermute | solution.py:167
  17.0 2.1 %collective-permute-start.5 = (bf16[4,32,128]{2,1,0:T(8,128)(2,1)S(1)}, bf16[4,32,128]{2,1,0:T(8,128)(2,1)S(1)}, u32[]{:S(2)}, u32[]{:S(2)}) collective-permute-start(bf16[4,32,128]{2,1,0:T(8,128)(2,1)S(1)} %get-tuple-element.27), channel_id=1, source_target_pairs={{0,2},{1,3},{2,0},{3,1},{4,6},{5,7},{6,4},{7,5},{8,10},{9,11},{10,... | collective-permute-start | bytes 98312 | tf_op jit(solution)/shard_map/ppermute | solution.py:167
  19.2 1.9 %collective-permute-done.5.got_ref = bf16[4,32,128]{2,1,0:T(8,128)(2,1)S(1)} collective-permute-done((bf16[4,32,128]{2,1,0:T(8,128)(2,1)S(1)}, bf16[4,32,128]{2,1,0:T(8,128)(2,1)S(1)}, u32[]{:S(2)}, u32[]{:S(2)}) %collective-permute-start.5) | collective-permute-done | bytes 32800 | tf_op jit(solution)/shard_map/ppermute | solution.py:167
  21.1 3.0 %collective-permute-start.6 = (bf16[2,32,128]{2,1,0:T(8,128)(2,1)S(1)}, bf16[2,32,128]{2,1,0:T(8,128)(2,1)S(1)}, u32[]{:S(2)}, u32[]{:S(2)}) collective-permute-start(bf16[2,32,128]{2,1,0:T(8,128)(2,1)S(1)} %get-tuple-element.29), channel_id=1, source_target_pairs={{0,4},{1,5},{2,6},{3,7},{4,0},{5,1},{6,2},{7,3},{8,12},{9,13},{10,... | collective-permute-start | bytes 49160 | tf_op jit(solution)/shard_map/ppermute | solution.py:167
  24.1 1.7 %collective-permute-done.6.got_ref = bf16[2,32,128]{2,1,0:T(8,128)(2,1)S(1)} collective-permute-done((bf16[2,32,128]{2,1,0:T(8,128)(2,1)S(1)}, bf16[2,32,128]{2,1,0:T(8,128)(2,1)S(1)}, u32[]{:S(2)}, u32[]{:S(2)}) %collective-permute-start.6) | collective-permute-done | bytes 16416 | tf_op jit(solution)/shard_map/ppermute | solution.py:167
  25.9 1.0 %collective-permute-start.7 = (bf16[1,32,128]{2,1,0:T(8,128)(2,1)S(1)}, bf16[1,32,128]{2,1,0:T(8,128)(2,1)S(1)}, u32[]{:S(2)}, u32[]{:S(2)}) collective-permute-start(bf16[1,32,128]{2,1,0:T(8,128)(2,1)S(1)} %get-tuple-element.31), channel_id=1, source_target_pairs={{0,8},{1,9},{2,10},{3,11},{4,12},{5,13},{6,14},{7,15},{8,0},{9,1},... | collective-permute-start | bytes 24584 | tf_op jit(solution)/shard_map/ppermute | solution.py:167
  26.8 3.6 %collective-permute-done.7.got_ref = bf16[1,32,128]{2,1,0:T(8,128)(2,1)S(1)} collective-permute-done((bf16[1,32,128]{2,1,0:T(8,128)(2,1)S(1)}, bf16[1,32,128]{2,1,0:T(8,128)(2,1)S(1)}, u32[]{:S(2)}, u32[]{:S(2)}) %collective-permute-start.7) | collective-permute-done | bytes 8224 | tf_op jit(solution)/shard_map/ppermute | solution.py:167
  30.4 0.8 %struct_solve.1 = f32[32,128]{1,0:T(8,128)} custom-call(f32[1,32,128]{2,1,0:T(8,128)S(1)} %get-tuple-element.30.held_ref, bf16[1,32,128]{2,1,0:T(8,128)(2,1)S(1)} %collective-permute-done.7.got_ref, bf16[8,128,128]{2,1,0:T(8,128)(2,1)S(1)} %copy-done.5), custom_call_target="tpu_custom_call" | custom-call | flops 1000000000 | bytes 1048576 | tf_op jit(solution)/shard_map/struct_solve/pallas_call | solution.py:258
  (8 shorter events, 0.1 us)
Async XLA Ops:
  0.6 7.8 %copy-start = (bf16[1,8,4,128]{3,2,1,0:T(4,128)(2,1)S(1)}, bf16[1,8,4,128]{3,2,1,0:T(4,128)(2,1)}, u32[]{:S(2)}) copy-start(bf16[1,8,4,128]{3,2,1,0:T(4,128)(2,1)} %param.8) | copy-start | bytes 24580
  0.6 7.8 %copy-start.1 = (s32[8,8]{1,0:T(8,128)S(1)}, s32[8,8]{1,0:T(8,128)}, u32[]{:S(2)}) copy-start(s32[8,8]{1,0:T(8,128)} %pattern_ref.1) | copy-start | bytes 772
  0.7 7.8 %copy-start.2 = (s32[1,4]{1,0:T(1,128)S(1)}, s32[1,4]{1,0:T(1,128)}, u32[]{:S(2)}) copy-start(s32[1,4]{1,0:T(1,128)} %trim_ref.1) | copy-start | bytes 52
  0.7 8.8 %copy-start.3 = (bf16[1,8,8,128,128]{4,3,2,1,0:T(8,128)(2,1)S(1)}, bf16[1,8,8,128,128]{4,3,2,1,0:T(8,128)(2,1)}, u32[]{:S(2)}) copy-start(bf16[1,8,8,128,128]{4,3,2,1,0:T(8,128)(2,1)} %param.9) | copy-start | bytes 6291460
  0.7 8.0 %collective-permute-start.2 = (bf16[32,128]{1,0:T(8,128)(2,1)}, bf16[32,128]{1,0:T(8,128)(2,1)S(1)}, u32[]{:S(2)}, u32[]{:S(2)}) collective-permute-start(bf16[32,128]{1,0:T(8,128)(2,1)} %bitcast.4), channel_id=1, source_target_pairs={{0,8},{1,9},{2,10},{3,11},{4,12},{5,13},{6,14},{7,15},{8,0},{9,1},... | collective-permute-start | bytes 24584 | tf_op jit(solution)/shard_map/ppermute | solution.py:167
  4.8 4.0 %collective-permute-start.1 = (bf16[32,128]{1,0:T(8,128)(2,1)}, bf16[32,128]{1,0:T(8,128)(2,1)S(1)}, u32[]{:S(2)}, u32[]{:S(2)}) collective-permute-start(bf16[32,128]{1,0:T(8,128)(2,1)} %bitcast.5), channel_id=1, source_target_pairs={{0,0},{1,2},{2,1},{3,4},{4,3},{5,6},{6,5},{7,8},{8,7},{9,10},{10,9... | collective-permute-start | bytes 24584 | tf_op jit(solution)/shard_map/ppermute | solution.py:187
  6.1 3.3 %collective-permute-start = (bf16[32,128]{1,0:T(8,128)(2,1)}, bf16[32,128]{1,0:T(8,128)(2,1)S(1)}, u32[]{:S(2)}, u32[]{:S(2)}) collective-permute-start(bf16[32,128]{1,0:T(8,128)(2,1)} %bitcast.6), channel_id=1, source_target_pairs={{0,1},{1,0},{2,3},{3,2},{4,5},{5,4},{6,7},{7,6},{8,9},{9,8},{10,11... | collective-permute-start | bytes 24584 | tf_op jit(solution)/shard_map/ppermute | solution.py:167
  9.4 4.8 %copy-start.4 = (bf16[8,6,128,128]{3,2,1,0:T(8,128)(2,1)S(1)}, bf16[8,6,128,128]{3,2,1,0:T(8,128)(2,1)}, u32[]{:S(2)}) copy-start(bf16[8,6,128,128]{3,2,1,0:T(8,128)(2,1)} %refs_2_.1) | copy-start | bytes 4718596
  9.4 4.8 %copy-start.6 = (s32[8,6]{1,0:T(8,128)S(1)}, s32[8,6]{1,0:T(8,128)}, u32[]{:S(2)}) copy-start(s32[8,6]{1,0:T(8,128)} %owner_ref.1) | copy-start | bytes 580
  9.4 4.8 %copy-start.7 = (s32[8,6]{1,0:T(8,128)S(1)}, s32[8,6]{1,0:T(8,128)}, u32[]{:S(2)}) copy-start(s32[8,6]{1,0:T(8,128)} %local_ref.1) | copy-start | bytes 580
  10.5 3.7 %collective-permute-start.3 = (bf16[32,128]{1,0:T(8,128)(2,1)S(1)}, bf16[32,128]{1,0:T(8,128)(2,1)S(1)}, u32[]{:S(2)}, u32[]{:S(2)}) collective-permute-start(bf16[32,128]{1,0:T(8,128)(2,1)S(1)} %get-tuple-element.23.refs_0_), channel_id=1, source_target_pairs={{0,16},{16,0},{1,17},{17,1},{2,18},{18,2},{3,19},{19,3},{4,20},{20... | collective-permute-start | bytes 24584 | tf_op jit(solution)/shard_map/ppermute | solution.py:230
  14.2 16.2 %copy-start.5 = (bf16[8,128,128]{2,1,0:T(8,128)(2,1)S(1)}, bf16[8,128,128]{2,1,0:T(8,128)(2,1)}, u32[]{:S(2)}) copy-start(bf16[8,128,128]{2,1,0:T(8,128)(2,1)} %inverse_ref.1) | copy-start | bytes 786436
  15.7 1.3 %collective-permute-start.4 = (bf16[8,32,128]{2,1,0:T(8,128)(2,1)S(1)}, bf16[8,32,128]{2,1,0:T(8,128)(2,1)S(1)}, u32[]{:S(2)}, u32[]{:S(2)}) collective-permute-start(bf16[8,32,128]{2,1,0:T(8,128)(2,1)S(1)} %get-tuple-element.25), channel_id=1, source_target_pairs={{0,1},{1,0},{2,3},{3,2},{4,5},{5,4},{6,7},{7,6},{8,9},{9,8},{10,11... | collective-permute-start | bytes 196616 | tf_op jit(solution)/shard_map/ppermute | solution.py:167
  17.0 4.0 %collective-permute-start.5 = (bf16[4,32,128]{2,1,0:T(8,128)(2,1)S(1)}, bf16[4,32,128]{2,1,0:T(8,128)(2,1)S(1)}, u32[]{:S(2)}, u32[]{:S(2)}) collective-permute-start(bf16[4,32,128]{2,1,0:T(8,128)(2,1)S(1)} %get-tuple-element.27), channel_id=1, source_target_pairs={{0,2},{1,3},{2,0},{3,1},{4,6},{5,7},{6,4},{7,5},{8,10},{9,11},{10,... | collective-permute-start | bytes 98312 | tf_op jit(solution)/shard_map/ppermute | solution.py:167
  21.1 4.8 %collective-permute-start.6 = (bf16[2,32,128]{2,1,0:T(8,128)(2,1)S(1)}, bf16[2,32,128]{2,1,0:T(8,128)(2,1)S(1)}, u32[]{:S(2)}, u32[]{:S(2)}) collective-permute-start(bf16[2,32,128]{2,1,0:T(8,128)(2,1)S(1)} %get-tuple-element.29), channel_id=1, source_target_pairs={{0,4},{1,5},{2,6},{3,7},{4,0},{5,1},{6,2},{7,3},{8,12},{9,13},{10,... | collective-permute-start | bytes 49160 | tf_op jit(solution)/shard_map/ppermute | solution.py:167
  25.9 4.5 %collective-permute-start.7 = (bf16[1,32,128]{2,1,0:T(8,128)(2,1)S(1)}, bf16[1,32,128]{2,1,0:T(8,128)(2,1)S(1)}, u32[]{:S(2)}, u32[]{:S(2)}) collective-permute-start(bf16[1,32,128]{2,1,0:T(8,128)(2,1)S(1)} %get-tuple-element.31), channel_id=1, source_target_pairs={{0,8},{1,9},{2,10},{3,11},{4,12},{5,13},{6,14},{7,15},{8,0},{9,1},... | collective-permute-start | bytes 24584 | tf_op jit(solution)/shard_map/ppermute | solution.py:167

commit v5 on v4

--- a/solution.py
+++ b/solution.py
@@ -13,16 +13,14 @@
 TILE = 8
 
 
-def spread_kernel(machs, rhs, block_count, expand_ref, order_ref):
+def spread_kernel(rhs, expand_ref, order_ref):
     shape = expand_ref.shape
     expand_ref[...] = (
         lax.broadcasted_iota(jnp.int32, shape, 0) // rhs == lax.broadcasted_iota(jnp.int32, shape, 1)
     ).astype(jnp.bfloat16)
     shape = order_ref.shape
     row = lax.broadcasted_iota(jnp.int32, shape, 0)
-    source = (
-        (row // TILE) % machs * (block_count * rhs) + row // (TILE * machs) * rhs + row % rhs
-    )
+    source = row // TILE * rhs + row % rhs
     order_ref[...] = (lax.broadcasted_iota(jnp.int32, shape, 1) == source).astype(jnp.bfloat16)
 
 
@@ -93,19 +91,20 @@
         rounded_ref[g * PACK : (g + 1) * PACK] = loads.astype(jnp.bfloat16)
 
 
-def spline_kernel(machs, rhs, struct_count, owner_ref, local_ref, order_ref, *refs):
-    rounded_refs, spline_ref, keep_ref, send_ref, acc = refs[:machs], *refs[machs:]
+def spline_kernel(
+    rhs, struct_count, owner_ref, local_ref, order_ref, rounded_ref, spline_ref,
+    keep_ref, send_ref, acc,
+):
     block_count, splines = owner_ref.shape
-    rows, width = rounded_refs[0].shape
+    width = rounded_ref.shape[1]
     here = lax.axis_index("panel")
     acc[...] = jnp.zeros(acc.shape, jnp.float32)
-    every = jnp.concatenate([ref[...] for ref in rounded_refs], axis=0)
-    left = jnp.dot(order_ref[...], every, preferred_element_type=jnp.float32)
+    left = jnp.dot(order_ref[...], rounded_ref[...], preferred_element_type=jnp.float32)
     left = left.astype(jnp.bfloat16)
     part = lax.broadcasted_iota(jnp.int32, (TILE, width), 0) // rhs
     per_tile = TILE // rhs
     owner_tiles = struct_count // per_tile
-    height = machs * TILE
+    height = TILE
     blank = jnp.zeros((height, width), jnp.bfloat16)
     for pair in range(0, block_count, 2):
         mine = left[pair * height : (pair + 2) * height]
@@ -125,15 +124,12 @@
         )
         product = jnp.dot(mine, blocks, preferred_element_type=jnp.float32)
         for i in (pair, pair + 1):
-            total = product[(i - pair) * height : (i - pair) * height + TILE]
-            for m in range(1, machs):
-                start = (i - pair) * height + m * TILE
-                total = total + product[start : start + TILE]
+            total = product[(i - pair) * height : (i - pair + 1) * height]
             places, sums = [], []
             for s in range(splines):
-                apart = owner_ref[i, s] ^ here
+                apart = owner_ref[i, s] ^ (here - here % 2)
                 local = local_ref[i, s]
-                place = (apart % 2, apart // 2 * owner_tiles + local // per_tile)
+                place = apart * owner_tiles + local // per_tile
                 added = jnp.where(
                     part == local % per_tile, total[:, s * width : (s + 1) * width], 0.0
                 )
@@ -141,23 +137,45 @@
                 sums.append(acc[place] + added)
             for place, value in zip(places, sums):
                 acc[place] = value
-    keep_ref[...] = acc[0].reshape(keep_ref.shape)
-    send_ref[...] = acc[1].reshape(send_ref.shape).astype(send_ref.dtype)
-
-
-def sum_kernel(held_ref, got_ref, keep_ref, send_ref):
+    total = acc[...].reshape(keep_ref.shape)
+    keep_ref[...] = total
+    send_ref[...] = total.astype(send_ref.dtype)
+
+
+def split_kernel(held_ref, got_ref, *out_refs):
+    size = out_refs[0].shape[0]
+    for step, out_ref in enumerate(out_refs):
+        for place in range(size):
+            total = held_ref[step * size + place] + got_ref[step * size + place].astype(jnp.float32)
+            out_ref[place] = total.astype(out_ref.dtype)
+
+
+def column_kernel(held_ref, *refs):
+    got_refs, out_refs = refs[:-2], refs[-2:]
+    size = out_refs[0].shape[0]
     for place in range(held_ref.shape[0]):
-        total = held_ref[place] + got_ref[place].astype(jnp.float32)
-        if place % 2 == 0:
-            keep_ref[place // 2] = total
-        else:
-            send_ref[place // 2] = total.astype(send_ref.dtype)
-
-
-def inverse_kernel(rhs, held_ref, got_ref, inverse_ref, out_ref):
-    total = held_ref[0] + got_ref[0].astype(jnp.float32)
-    rounded = total.astype(jnp.bfloat16)
-    for g in range(total.shape[0] // PACK):
+        total = held_ref[place]
+        for got_ref in got_refs:
+            total = total + got_ref[place].astype(jnp.float32)
+        out_ref = out_refs[place // size]
+        out_ref[place % size] = total.astype(out_ref.dtype)
+
+
+def round_kernel(machs, *refs):
+    same_refs, other_refs, out_refs = refs[:machs], refs[machs : 2 * machs], refs[2 * machs :]
+    for place, out_ref in enumerate(out_refs):
+        parts = [
+            same[place].astype(jnp.float32) + other[place].astype(jnp.float32)
+            for same, other in zip(same_refs, other_refs)
+        ]
+        out_ref[...] = sum(parts[1:], parts[0]).astype(out_ref.dtype)
+
+
+def inverse_kernel(rhs, mine_ref, got_ref, inverse_ref, out_ref):
+    leads = jnp.broadcast_to(lax.axis_index("panel") % 2, mine_ref.shape) == 1
+    rounded = jnp.where(leads, mine_ref[...].astype(jnp.float32), got_ref[...].astype(jnp.float32))
+    rounded = rounded.astype(jnp.bfloat16)
+    for g in range(rounded.shape[0] // PACK):
         out_ref[g * PACK : (g + 1) * PACK] = grouped_product(
             rhs, rounded[g * PACK : (g + 1) * PACK], lambda t: inverse_ref[t], g
         )
@@ -165,6 +183,15 @@
 
 def swap(value, panels, apart):
     return lax.ppermute(value, "panel", [(i, i ^ apart) for i in range(panels)])
+
+
+def leader_swap(value, machs, panels, turn, apart):
+    pairs = [
+        (m * panels + i, (m + turn) % machs * panels + (i ^ apart))
+        for m in range(machs)
+        for i in range(1, panels, 2)
+    ]
+    return lax.ppermute(value, ("mach", "panel"), pairs)
 
 
 def cost(flops, size):
@@ -183,16 +210,11 @@
     params = pltpu.CompilerParams(vmem_limit_bytes=16 * 1024 * 1024)
     f32, bf16 = jnp.float32, jnp.bfloat16
     own = adjoint.reshape(rows, width)
-    mirror = swap(own, panels, panels // 2)
-    cross = lax.ppermute(
-        own, "panel", [(i, min(max(i - 1 + 2 * (i % 2), 0), panels - 1)) for i in range(panels)]
-    )
-    pair = swap(own, panels, 1)
     expand, order = pl.pallas_call(
-        functools.partial(spread_kernel, machs, rhs, block_count),
+        functools.partial(spread_kernel, rhs),
         out_shape=(
             jax.ShapeDtypeStruct((rows, block_count), bf16),
-            jax.ShapeDtypeStruct((block_count * machs * TILE, machs * rows), bf16),
+            jax.ShapeDtypeStruct((block_count * TILE, rows), bf16),
         ),
         out_specs=(VMEM, VMEM),
         compiler_params=params,
@@ -212,6 +234,11 @@
         cost_estimate=cost(10**6, 2**17),
         name="pick_rows",
     )(expand, pattern, trim_mask, own)
+    mirror = swap(held, panels, panels // 2)
+    cross = lax.ppermute(
+        held, "panel", [(i, i - 1 + 2 * (i % 2)) for i in range(1, panels - 1)]
+    )
+    pair = swap(held, panels, 1)
     loads, rounded = pl.pallas_call(
         functools.partial(near_kernel, rhs),
         out_shape=(
@@ -224,37 +251,55 @@
         cost_estimate=cost(2 * 10**9, 4 * 2**20),
         name="near_field",
     )(hot, gate, held, pair, cross, mirror, near_blocks[0])
-    every = [rounded]
-    for step in range(1, machs):
-        every.append(
-            lax.ppermute(rounded, "mach", [(i, (i + step) % machs) for i in range(machs)])
-        )
-    half = (panels // 2, struct_rows, width)
+    whole = (panels, struct_rows, width)
     keep, send = pl.pallas_call(
-        functools.partial(spline_kernel, machs, rhs, struct_count),
-        out_shape=(jax.ShapeDtypeStruct(half, f32), jax.ShapeDtypeStruct(half, bf16)),
-        in_specs=[SMEM, SMEM] + [VMEM] * (machs + 2),
-        out_specs=(VMEM, VMEM),
-        scratch_shapes=[pltpu.VMEM((2, panels // 2 * struct_rows // TILE, TILE, width), f32)],
+        functools.partial(spline_kernel, rhs, struct_count),
+        out_shape=(jax.ShapeDtypeStruct(whole, f32), jax.ShapeDtypeStruct(whole, bf16)),
+        in_specs=[SMEM, SMEM, VMEM, VMEM, VMEM],
+        out_specs=(VMEM, VMEM),
+        scratch_shapes=[pltpu.VMEM((panels * struct_rows // TILE, TILE, width), f32)],
         compiler_params=params,
         cost_estimate=cost(2 * 10**9, 4 * 2**20),
         name="spline_loads",
-    )(spline_owner, spline_local, order, *every, spline_blocks)
-    apart = 1
-    got = swap(send, panels, apart)
-    while 2 * apart < panels:
-        apart *= 2
-        half = (panels // (2 * apart), struct_rows, width)
-        keep, send = pl.pallas_call(
-            sum_kernel,
-            out_shape=(jax.ShapeDtypeStruct(half, f32), jax.ShapeDtypeStruct(half, bf16)),
-            in_specs=[VMEM, VMEM],
-            out_specs=(VMEM, VMEM),
-            compiler_params=params,
-            cost_estimate=cost(10**6, 2**20),
-            name="pair_sum",
-        )(keep, got)
-        got = swap(send, panels, apart)
+    )(spline_owner, spline_local, order, rounded, spline_blocks)
+    got = lax.ppermute(send, "panel", [(i, i + 1) for i in range(0, panels, 2)])
+    steps = panels // 4
+    quarter = (4, struct_rows, width)
+    keep, *sends = pl.pallas_call(
+        split_kernel,
+        out_shape=tuple(
+            jax.ShapeDtypeStruct(quarter, f32 if step == 0 else bf16) for step in range(steps)
+        ),
+        in_specs=[VMEM, VMEM],
+        out_specs=(VMEM,) * steps,
+        compiler_params=params,
+        cost_estimate=cost(10**6, 2**20),
+        name="pair_sum",
+    )(keep, got)
+    got = [leader_swap(sends[step - 1], machs, panels, 0, 4 * step) for step in range(steps - 1, 0, -1)]
+    two = jax.ShapeDtypeStruct((2, struct_rows, width), bf16)
+    same, other = pl.pallas_call(
+        column_kernel,
+        out_shape=(two, two),
+        in_specs=[VMEM] * steps,
+        out_specs=(VMEM, VMEM),
+        compiler_params=params,
+        cost_estimate=cost(10**6, 2**20),
+        name="column_sum",
+    )(keep, *got)
+    others = [leader_swap(other, machs, panels, turn, 2) for turn in range(machs - 1, -1, -1)]
+    sames = [same] + [leader_swap(same, machs, panels, turn, 0) for turn in range(1, machs)]
+    one = (struct_rows, width)
+    even, odd = pl.pallas_call(
+        functools.partial(round_kernel, machs),
+        out_shape=(jax.ShapeDtypeStruct(one, bf16), jax.ShapeDtypeStruct(one, bf16)),
+        in_specs=[VMEM] * (2 * machs),
+        out_specs=(VMEM, VMEM),
+        compiler_params=params,
+        cost_estimate=cost(10**6, 2**20),
+        name="mach_sum",
+    )(*sames, *others[::-1])
+    even = lax.ppermute(even, "panel", [(i + 1, i) for i in range(0, panels, 2)])
     struct_adjoint = pl.pallas_call(
         functools.partial(inverse_kernel, rhs),
         out_shape=jax.ShapeDtypeStruct((struct_rows, width), f32),
@@ -263,7 +308,7 @@
         compiler_params=params,
         cost_estimate=cost(10**9, 2**20),
         name="struct_solve",
-    )(keep, got, struct_inverse)
+    )(odd, even, struct_inverse)
     return (
         loads.reshape(1, block_count, rhs, width),
         struct_adjoint.reshape(struct_count, rhs, width),

time: 31.4 us -> 41.8 us (1.33)
  waiting for transfers between devices: 11.3 us -> 21 us
  local copies, waits for them, and re-layouts: 0.03 us -> 0.98 us
    ppermute x2 -> x9, waiting for transfers between devices: 2.16 us -> 20.1 us  [the longest x1 19.2 us: on_device(): lax.ppermute(even, 'panel', [(i + 1, i) for i in range(0, panels, 2)])]
    ppermute x6 -> x2, waiting for transfers between devices: 9.1 us -> 0.82 us  [swap(): return lax.ppermute(value, 'panel', [(i, i ^ apart) for i in range(panels)])]
    ppermute x6 -> x2, starting transfers between devices: 12.6 us -> 7.05 us  [swap(): return lax.ppermute(value, 'panel', [(i, i ^ apart) for i in range(panels)])]
    ppermute x2 -> x9, starting transfers between devices: 2.83 us -> 8.26 us  [the longest x6 3.98 us: leader_swap(): return lax.ppermute(value, ('mach', 'panel'), pairs)]
    unnamed x16, local copies, waits for them, and re-layouts: 0.03 us -> 0.98 us
  transfers between devices with their start and end apart: 8 -> 11, of which waited for: 6 -> 3; matrix products, arithmetic and copies ran while one was open for 0% -> 0% of each run, Pallas kernels for 1% -> 0%
where the time goes in v5:
time: 41.8 us; the launch traced here: 41.5 us
  waiting for transfers between devices  21 us (50%)
  starting transfers between devices  15.3 us (37%)
  Pallas kernels  3.39 us (8%)
  local copies, waits for them, and re-layouts  0.98 us (2%)
  between operations  0.83 us (2%)
    ppermute x1, waiting for transfers between devices, on_device(): lax.ppermute(even, 'panel', [(i + 1, i) for i in range(0, panels, 2)])  19.2 us
    ppermute x2, starting transfers between devices, swap(): return lax.ppermute(value, 'panel', [(i, i ^ apart) for i in range(panels)])  7.05 us
    ppermute x6, starting transfers between devices, leader_swap(): return lax.ppermute(value, ('mach', 'panel'), pairs)  3.98 us
    ppermute x1, starting transfers between devices, on_device(): got = lax.ppermute(send, 'panel', [(i, i + 1) for i in range(0, panels, 2)])  2.34 us
    ppermute x1, starting transfers between devices, on_device(): lax.ppermute(even, 'panel', [(i + 1, i) for i in range(0, panels, 2)])  1.29 us
    pallas_call x1, Pallas kernels, on_device(): pl.pallas_call(functools.partial(spline_kernel, rhs, struct_count), out_s...  1.19 us
    pallas_call x1, Pallas kernels, on_device(): pl.pallas_call(functools.partial(near_kernel, rhs), out_shape=(jax.ShapeD...  1.11 us
    unnamed x16, local copies, waits for them, and re-layouts  0.98 us
  transfers between devices with their start and end apart: 11, of which 3 were waited for; matrix products, arithmetic and copies ran while one was open for 0% of the time, Pallas kernels for 0%

profile of v5, /device:TPU:0, one launch (start us, length us, event | category | flops | bytes accessed | tf_op | source)
XLA Modules:
  0.0 41.5 jit_solution(4820466715512913345)
XLA Ops:
  0.6 0.0 copy-start.2
  0.6 0.0 copy-start.1
  0.7 0.6 %copy-done.2 = s32[1,4]{1,0:T(1,128)S(1)} copy-done((s32[1,4]{1,0:T(1,128)S(1)}, s32[1,4]{1,0:T(1,128)}, u32[]{:S(2)}) %copy-start.2) | copy-done | bytes 40
  1.3 0.0 copy-done.1
  1.3 0.0 copy-done
  1.4 0.3 pick_rows.1
  1.6 4.1 %collective-permute-start.2 = (bf16[32,128]{1,0:T(8,128)(2,1)S(1)}, bf16[32,128]{1,0:T(8,128)(2,1)S(1)}, u32[]{:S(2)}, u32[]{:S(2)}) collective-permute-start(bf16[32,128]{1,0:T(8,128)(2,1)S(1)} %get-tuple-element.22.own_ref), channel_id=1, source_target_pairs={{0,8},{1,9},{2,10},{3,11},{4,12},{5,13},{6,14},{7,15},{8,0},{9,1},... | collective-permute-start | bytes 24584 | tf_op jit(solution)/shard_map/ppermute | solution.py:185
  5.7 0.6 %collective-permute-start.1 = (bf16[32,128]{1,0:T(8,128)(2,1)S(1)}, bf16[32,128]{1,0:T(8,128)(2,1)S(1)}, u32[]{:S(2)}, u32[]{:S(2)}) collective-permute-start(bf16[32,128]{1,0:T(8,128)(2,1)S(1)} %get-tuple-element.22.own_ref), channel_id=1, source_target_pairs={{1,2},{2,1},{3,4},{4,3},{5,6},{6,5},{7,8},{8,7},{9,10},{10,9},{11,... | collective-permute-start | bytes 24584 | tf_op jit(solution)/shard_map/ppermute | solution.py:238
  6.4 2.9 %collective-permute-start = (bf16[32,128]{1,0:T(8,128)(2,1)S(1)}, bf16[32,128]{1,0:T(8,128)(2,1)S(1)}, u32[]{:S(2)}, u32[]{:S(2)}) collective-permute-start(bf16[32,128]{1,0:T(8,128)(2,1)S(1)} %get-tuple-element.22.own_ref), channel_id=1, source_target_pairs={{0,1},{1,0},{2,3},{3,2},{4,5},{5,4},{6,7},{7,6},{8,9},{9,8},{10,11... | collective-permute-start | bytes 24584 | tf_op jit(solution)/shard_map/ppermute | solution.py:185
  9.3 0.0 collective-permute-done.2.mirror_ref
  9.3 0.0 collective-permute-done.1.cross_ref
  9.3 0.8 %collective-permute-done.pair_ref = bf16[32,128]{1,0:T(8,128)(2,1)S(1)} collective-permute-done((bf16[32,128]{1,0:T(8,128)(2,1)S(1)}, bf16[32,128]{1,0:T(8,128)(2,1)S(1)}, u32[]{:S(2)}, u32[]{:S(2)}) %collective-permute-start) | collective-permute-done | bytes 8224 | tf_op jit(solution)/shard_map/ppermute | solution.py:185
  10.2 1.1 %near_field.1 = (f32[32,128]{1,0:T(8,128)}, bf16[32,128]{1,0:T(8,128)(2,1)S(1)}) custom-call(bf16[256,128]{1,0:T(8,128)(2,1)S(1)} %get-tuple-element.20.hot_ref, f32[16,128]{1,0:T(8,128)S(1)} %get-tuple-element.21.gate_ref, bf16[32,128]{1,0:T(8,128)(2,1)S(1)} %get-tuple-element.22.own_ref, bf16[32,128]{1,0:T(8,128)(2,1)S(1)} %collective-permute-done.pair_ref, ...), custom_call_target="tpu_custom_call" | custom-call | flops 2000000000 | bytes 4194304 | tf_op jit(solution)/shard_map/near_field/pallas_call | solution.py:242
  11.3 0.3 copy-done.4
  11.6 1.2 %spline_loads.1 = (f32[16,32,128]{2,1,0:T(8,128)S(1)}, bf16[16,32,128]{2,1,0:T(8,128)(2,1)S(1)}) custom-call(s32[8,6]{1,0:T(8,128)S(1)} %copy-done.6, s32[8,6]{1,0:T(8,128)S(1)} %copy-done.7, bf16[64,32]{1,0:T(8,128)(2,1)S(1)} %get-tuple-element.24.order_ref, bf16[32,128]{1,0:T(8,128)(2,1)S(1)} %get-tuple-element.25.rounded_ref, ...), custom_call_target="tpu_custom_call" | custom-call | flops 2000000000 | bytes 4194304 | tf_op jit(solution)/shard_map/spline_loads/pallas_call | solution.py:255
  12.8 2.3 %collective-permute-start.3 = (bf16[16,32,128]{2,1,0:T(8,128)(2,1)S(1)}, bf16[16,32,128]{2,1,0:T(8,128)(2,1)S(1)}, u32[]{:S(2)}, u32[]{:S(2)}) collective-permute-start(bf16[16,32,128]{2,1,0:T(8,128)(2,1)S(1)} %get-tuple-element.27), channel_id=1, source_target_pairs={{0,1},{2,3},{4,5},{6,7},{8,9},{10,11},{12,13},{14,15},{16,17},{18,... | collective-permute-start | bytes 393224 | tf_op jit(solution)/shard_map/ppermute | solution.py:265
  15.1 1.0 %collective-permute-done.3.got_ref = bf16[16,32,128]{2,1,0:T(8,128)(2,1)S(1)} collective-permute-done((bf16[16,32,128]{2,1,0:T(8,128)(2,1)S(1)}, bf16[16,32,128]{2,1,0:T(8,128)(2,1)S(1)}, u32[]{:S(2)}, u32[]{:S(2)}) %collective-permute-start.3) | collective-permute-done | bytes 131104 | tf_op jit(solution)/shard_map/ppermute | solution.py:265
  16.1 0.7 %collective-permute-start.4 = (bf16[4,32,128]{2,1,0:T(8,128)(2,1)S(1)}, bf16[4,32,128]{2,1,0:T(8,128)(2,1)S(1)}, u32[]{:S(2)}, u32[]{:S(2)}) collective-permute-start(bf16[4,32,128]{2,1,0:T(8,128)(2,1)S(1)} %get-tuple-element.29), channel_id=1, source_target_pairs={{1,13},{3,15},{5,9},{7,11},{9,5},{11,7},{13,1},{15,3},{17,29},{19,... | collective-permute-start | bytes 98312 | tf_op jit(solution)/shard_map/ppermute | solution.py:194
  16.8 0.7 %collective-permute-start.5 = (bf16[4,32,128]{2,1,0:T(8,128)(2,1)S(1)}, bf16[4,32,128]{2,1,0:T(8,128)(2,1)S(1)}, u32[]{:S(2)}, u32[]{:S(2)}) collective-permute-start(bf16[4,32,128]{2,1,0:T(8,128)(2,1)S(1)} %get-tuple-element.30), channel_id=1, source_target_pairs={{1,9},{3,11},{5,13},{7,15},{9,1},{11,3},{13,5},{15,7},{17,25},{19,... | collective-permute-start | bytes 98312 | tf_op jit(solution)/shard_map/ppermute | solution.py:194
  17.5 0.7 %collective-permute-start.6 = (bf16[4,32,128]{2,1,0:T(8,128)(2,1)S(1)}, bf16[4,32,128]{2,1,0:T(8,128)(2,1)S(1)}, u32[]{:S(2)}, u32[]{:S(2)}) collective-permute-start(bf16[4,32,128]{2,1,0:T(8,128)(2,1)S(1)} %get-tuple-element.31), channel_id=1, source_target_pairs={{1,5},{3,7},{5,1},{7,3},{9,13},{11,15},{13,9},{15,11},{17,21},{19,... | collective-permute-start | bytes 98312 | tf_op jit(solution)/shard_map/ppermute | solution.py:194
  18.1 0.0 collective-permute-done.4.refs_0_
  18.1 0.0 collective-permute-done.5.refs_1_
  18.1 0.0 collective-permute-done.6.refs_2_
  18.2 0.7 %collective-permute-start.7 = (bf16[2,32,128]{2,1,0:T(8,128)(2,1)S(1)}, bf16[2,32,128]{2,1,0:T(8,128)(2,1)S(1)}, u32[]{:S(2)}, u32[]{:S(2)}) collective-permute-start(bf16[2,32,128]{2,1,0:T(8,128)(2,1)S(1)} %get-tuple-element.32.refs_0_), channel_id=1, source_target_pairs={{1,17},{3,19},{5,21},{7,23},{9,25},{11,27},{13,29},{15,31},{17,1},... | collective-permute-start | bytes 49160 | tf_op jit(solution)/shard_map/ppermute | solution.py:194
  18.9 0.7 %collective-permute-start.9 = (bf16[2,32,128]{2,1,0:T(8,128)(2,1)S(1)}, bf16[2,32,128]{2,1,0:T(8,128)(2,1)S(1)}, u32[]{:S(2)}, u32[]{:S(2)}) collective-permute-start(bf16[2,32,128]{2,1,0:T(8,128)(2,1)S(1)} %get-tuple-element.33), channel_id=1, source_target_pairs={{1,19},{3,17},{5,23},{7,21},{9,27},{11,25},{13,31},{15,29},{17,3},... | collective-permute-start | bytes 49160 | tf_op jit(solution)/shard_map/ppermute | solution.py:194
  19.5 0.7 %collective-permute-start.8 = (bf16[2,32,128]{2,1,0:T(8,128)(2,1)S(1)}, bf16[2,32,128]{2,1,0:T(8,128)(2,1)S(1)}, u32[]{:S(2)}, u32[]{:S(2)}) collective-permute-start(bf16[2,32,128]{2,1,0:T(8,128)(2,1)S(1)} %get-tuple-element.33), channel_id=1, source_target_pairs={{1,3},{3,1},{5,7},{7,5},{9,11},{11,9},{13,15},{15,13},{17,19},{19,... | collective-permute-start | bytes 49160 | tf_op jit(solution)/shard_map/ppermute | solution.py:194
  20.2 0.0 collective-permute-done.7.refs_1_
  20.2 0.0 collective-permute-done.9.refs_3_
  20.2 0.0 collective-permute-done.8.refs_2_
  20.2 1.3 %collective-permute-start.10 = (bf16[32,128]{1,0:T(8,128)(2,1)S(1)}, bf16[32,128]{1,0:T(8,128)(2,1)S(1)}, u32[]{:S(2)}, u32[]{:S(2)}) collective-permute-start(bf16[32,128]{1,0:T(8,128)(2,1)S(1)} %get-tuple-element.35), channel_id=1, source_target_pairs={{1,0},{3,2},{5,4},{7,6},{9,8},{11,10},{13,12},{15,14},{17,16},{19,... | collective-permute-start | bytes 24584 | tf_op jit(solution)/shard_map/ppermute | solution.py:302
  21.5 19.2 %collective-permute-done.10.got_ref = bf16[32,128]{1,0:T(8,128)(2,1)S(1)} collective-permute-done((bf16[32,128]{1,0:T(8,128)(2,1)S(1)}, bf16[32,128]{1,0:T(8,128)(2,1)S(1)}, u32[]{:S(2)}, u32[]{:S(2)}) %collective-permute-start.10) | collective-permute-done | bytes 8224 | tf_op jit(solution)/shard_map/ppermute | solution.py:302
  40.7 0.8 %struct_solve.1 = f32[32,128]{1,0:T(8,128)} custom-call(bf16[32,128]{1,0:T(8,128)(2,1)S(1)} %get-tuple-element.34.mine_ref, bf16[32,128]{1,0:T(8,128)(2,1)S(1)} %collective-permute-done.10.got_ref, bf16[8,128,128]{2,1,0:T(8,128)(2,1)S(1)} %copy-done.5), custom_call_target="tpu_custom_call" | custom-call | flops 1000000000 | bytes 1048576 | tf_op jit(solution)/shard_map/struct_solve/pallas_call | solution.py:303
  (14 shorter events, 0.1 us)
Async XLA Ops:
  0.6 0.7 %copy-start.2 = (s32[1,4]{1,0:T(1,128)S(1)}, s32[1,4]{1,0:T(1,128)}, u32[]{:S(2)}) copy-start(s32[1,4]{1,0:T(1,128)} %trim_ref.1) | copy-start | bytes 52
  0.6 0.7 %copy-start.1 = (s32[8,8]{1,0:T(8,128)S(1)}, s32[8,8]{1,0:T(8,128)}, u32[]{:S(2)}) copy-start(s32[8,8]{1,0:T(8,128)} %pattern_ref.1) | copy-start | bytes 772
  0.7 0.7 %copy-start = (bf16[1,8,4,128]{3,2,1,0:T(4,128)(2,1)S(1)}, bf16[1,8,4,128]{3,2,1,0:T(4,128)(2,1)}, u32[]{:S(2)}) copy-start(bf16[1,8,4,128]{3,2,1,0:T(4,128)(2,1)} %param.8) | copy-start | bytes 24580
  0.7 9.5 %copy-start.3 = (bf16[1,8,8,128,128]{4,3,2,1,0:T(8,128)(2,1)S(1)}, bf16[1,8,8,128,128]{4,3,2,1,0:T(8,128)(2,1)}, u32[]{:S(2)}) copy-start(bf16[1,8,8,128,128]{4,3,2,1,0:T(8,128)(2,1)} %param.9) | copy-start | bytes 6291460
  1.6 7.7 %collective-permute-start.2 = (bf16[32,128]{1,0:T(8,128)(2,1)S(1)}, bf16[32,128]{1,0:T(8,128)(2,1)S(1)}, u32[]{:S(2)}, u32[]{:S(2)}) collective-permute-start(bf16[32,128]{1,0:T(8,128)(2,1)S(1)} %get-tuple-element.22.own_ref), channel_id=1, source_target_pairs={{0,8},{1,9},{2,10},{3,11},{4,12},{5,13},{6,14},{7,15},{8,0},{9,1},... | collective-permute-start | bytes 24584 | tf_op jit(solution)/shard_map/ppermute | solution.py:185
  5.7 3.6 %collective-permute-start.1 = (bf16[32,128]{1,0:T(8,128)(2,1)S(1)}, bf16[32,128]{1,0:T(8,128)(2,1)S(1)}, u32[]{:S(2)}, u32[]{:S(2)}) collective-permute-start(bf16[32,128]{1,0:T(8,128)(2,1)S(1)} %get-tuple-element.22.own_ref), channel_id=1, source_target_pairs={{1,2},{2,1},{3,4},{4,3},{5,6},{6,5},{7,8},{8,7},{9,10},{10,9},{11,... | collective-permute-start | bytes 24584 | tf_op jit(solution)/shard_map/ppermute | solution.py:238
  6.4 3.8 %collective-permute-start = (bf16[32,128]{1,0:T(8,128)(2,1)S(1)}, bf16[32,128]{1,0:T(8,128)(2,1)S(1)}, u32[]{:S(2)}, u32[]{:S(2)}) collective-permute-start(bf16[32,128]{1,0:T(8,128)(2,1)S(1)} %get-tuple-element.22.own_ref), channel_id=1, source_target_pairs={{0,1},{1,0},{2,3},{3,2},{4,5},{5,4},{6,7},{7,6},{8,9},{9,8},{10,11... | collective-permute-start | bytes 24584 | tf_op jit(solution)/shard_map/ppermute | solution.py:185
  10.2 1.4 %copy-start.4 = (bf16[8,6,128,128]{3,2,1,0:T(8,128)(2,1)S(1)}, bf16[8,6,128,128]{3,2,1,0:T(8,128)(2,1)}, u32[]{:S(2)}) copy-start(bf16[8,6,128,128]{3,2,1,0:T(8,128)(2,1)} %spline_ref.1) | copy-start | bytes 4718596
  10.2 1.4 %copy-start.6 = (s32[8,6]{1,0:T(8,128)S(1)}, s32[8,6]{1,0:T(8,128)}, u32[]{:S(2)}) copy-start(s32[8,6]{1,0:T(8,128)} %owner_ref.1) | copy-start | bytes 580
  10.2 1.4 %copy-start.7 = (s32[8,6]{1,0:T(8,128)S(1)}, s32[8,6]{1,0:T(8,128)}, u32[]{:S(2)}) copy-start(s32[8,6]{1,0:T(8,128)} %local_ref.1) | copy-start | bytes 580
  11.6 29.1 %copy-start.5 = (bf16[8,128,128]{2,1,0:T(8,128)(2,1)S(1)}, bf16[8,128,128]{2,1,0:T(8,128)(2,1)}, u32[]{:S(2)}) copy-start(bf16[8,128,128]{2,1,0:T(8,128)(2,1)} %inverse_ref.1) | copy-start | bytes 786436
  12.8 3.3 %collective-permute-start.3 = (bf16[16,32,128]{2,1,0:T(8,128)(2,1)S(1)}, bf16[16,32,128]{2,1,0:T(8,128)(2,1)S(1)}, u32[]{:S(2)}, u32[]{:S(2)}) collective-permute-start(bf16[16,32,128]{2,1,0:T(8,128)(2,1)S(1)} %get-tuple-element.27), channel_id=1, source_target_pairs={{0,1},{2,3},{4,5},{6,7},{8,9},{10,11},{12,13},{14,15},{16,17},{18,... | collective-permute-start | bytes 393224 | tf_op jit(solution)/shard_map/ppermute | solution.py:265
  16.1 2.0 %collective-permute-start.4 = (bf16[4,32,128]{2,1,0:T(8,128)(2,1)S(1)}, bf16[4,32,128]{2,1,0:T(8,128)(2,1)S(1)}, u32[]{:S(2)}, u32[]{:S(2)}) collective-permute-start(bf16[4,32,128]{2,1,0:T(8,128)(2,1)S(1)} %get-tuple-element.29), channel_id=1, source_target_pairs={{1,13},{3,15},{5,9},{7,11},{9,5},{11,7},{13,1},{15,3},{17,29},{19,... | collective-permute-start | bytes 98312 | tf_op jit(solution)/shard_map/ppermute | solution.py:194
  16.8 1.4 %collective-permute-start.5 = (bf16[4,32,128]{2,1,0:T(8,128)(2,1)S(1)}, bf16[4,32,128]{2,1,0:T(8,128)(2,1)S(1)}, u32[]{:S(2)}, u32[]{:S(2)}) collective-permute-start(bf16[4,32,128]{2,1,0:T(8,128)(2,1)S(1)} %get-tuple-element.30), channel_id=1, source_target_pairs={{1,9},{3,11},{5,13},{7,15},{9,1},{11,3},{13,5},{15,7},{17,25},{19,... | collective-permute-start | bytes 98312 | tf_op jit(solution)/shard_map/ppermute | solution.py:194
  17.5 0.7 %collective-permute-start.6 = (bf16[4,32,128]{2,1,0:T(8,128)(2,1)S(1)}, bf16[4,32,128]{2,1,0:T(8,128)(2,1)S(1)}, u32[]{:S(2)}, u32[]{:S(2)}) collective-permute-start(bf16[4,32,128]{2,1,0:T(8,128)(2,1)S(1)} %get-tuple-element.31), channel_id=1, source_target_pairs={{1,5},{3,7},{5,1},{7,3},{9,13},{11,15},{13,9},{15,11},{17,21},{19,... | collective-permute-start | bytes 98312 | tf_op jit(solution)/shard_map/ppermute | solution.py:194
  18.2 2.0 %collective-permute-start.7 = (bf16[2,32,128]{2,1,0:T(8,128)(2,1)S(1)}, bf16[2,32,128]{2,1,0:T(8,128)(2,1)S(1)}, u32[]{:S(2)}, u32[]{:S(2)}) collective-permute-start(bf16[2,32,128]{2,1,0:T(8,128)(2,1)S(1)} %get-tuple-element.32.refs_0_), channel_id=1, source_target_pairs={{1,17},{3,19},{5,21},{7,23},{9,25},{11,27},{13,29},{15,31},{17,1},... | collective-permute-start | bytes 49160 | tf_op jit(solution)/shard_map/ppermute | solution.py:194
  18.9 1.4 %collective-permute-start.9 = (bf16[2,32,128]{2,1,0:T(8,128)(2,1)S(1)}, bf16[2,32,128]{2,1,0:T(8,128)(2,1)S(1)}, u32[]{:S(2)}, u32[]{:S(2)}) collective-permute-start(bf16[2,32,128]{2,1,0:T(8,128)(2,1)S(1)} %get-tuple-element.33), channel_id=1, source_target_pairs={{1,19},{3,17},{5,23},{7,21},{9,27},{11,25},{13,31},{15,29},{17,3},... | collective-permute-start | bytes 49160 | tf_op jit(solution)/shard_map/ppermute | solution.py:194
  19.5 0.7 %collective-permute-start.8 = (bf16[2,32,128]{2,1,0:T(8,128)(2,1)S(1)}, bf16[2,32,128]{2,1,0:T(8,128)(2,1)S(1)}, u32[]{:S(2)}, u32[]{:S(2)}) collective-permute-start(bf16[2,32,128]{2,1,0:T(8,128)(2,1)S(1)} %get-tuple-element.33), channel_id=1, source_target_pairs={{1,3},{3,1},{5,7},{7,5},{9,11},{11,9},{13,15},{15,13},{17,19},{19,... | collective-permute-start | bytes 49160 | tf_op jit(solution)/shard_map/ppermute | solution.py:194
  20.2 20.5 %collective-permute-start.10 = (bf16[32,128]{1,0:T(8,128)(2,1)S(1)}, bf16[32,128]{1,0:T(8,128)(2,1)S(1)}, u32[]{:S(2)}, u32[]{:S(2)}) collective-permute-start(bf16[32,128]{1,0:T(8,128)(2,1)S(1)} %get-tuple-element.35), channel_id=1, source_target_pairs={{1,0},{3,2},{5,4},{7,6},{9,8},{11,10},{13,12},{15,14},{17,16},{19,... | collective-permute-start | bytes 24584 | tf_op jit(solution)/shard_map/ppermute | solution.py:302

commit v6 on v4

--- a/solution.py
+++ b/solution.py
@@ -133,7 +133,7 @@
             for s in range(splines):
                 apart = owner_ref[i, s] ^ here
                 local = local_ref[i, s]
-                place = (apart % 2, apart // 2 * owner_tiles + local // per_tile)
+                place = (apart % 2, owner_ref[i, s] // 2 * owner_tiles + local // per_tile)
                 added = jnp.where(
                     part == local % per_tile, total[:, s * width : (s + 1) * width], 0.0
                 )
@@ -145,17 +145,16 @@
     send_ref[...] = acc[1].reshape(send_ref.shape).astype(send_ref.dtype)
 
 
-def sum_kernel(held_ref, got_ref, keep_ref, send_ref):
+def sum_kernel(held_ref, got_ref, out_ref):
     for place in range(held_ref.shape[0]):
         total = held_ref[place] + got_ref[place].astype(jnp.float32)
-        if place % 2 == 0:
-            keep_ref[place // 2] = total
-        else:
-            send_ref[place // 2] = total.astype(send_ref.dtype)
-
-
-def inverse_kernel(rhs, held_ref, got_ref, inverse_ref, out_ref):
-    total = held_ref[0] + got_ref[0].astype(jnp.float32)
+        out_ref[place] = total.astype(out_ref.dtype)
+
+
+def inverse_kernel(rhs, got_ref, inverse_ref, out_ref):
+    total = got_ref[0].astype(jnp.float32)
+    for source in range(1, got_ref.shape[0]):
+        total = total + got_ref[source].astype(jnp.float32)
     rounded = total.astype(jnp.bfloat16)
     for g in range(total.shape[0] // PACK):
         out_ref[g * PACK : (g + 1) * PACK] = grouped_product(
@@ -185,7 +184,7 @@
     own = adjoint.reshape(rows, width)
     mirror = swap(own, panels, panels // 2)
     cross = lax.ppermute(
-        own, "panel", [(i, min(max(i - 1 + 2 * (i % 2), 0), panels - 1)) for i in range(panels)]
+        own, "panel", [(i, (i - 1 + 2 * (i % 2)) % panels) for i in range(panels)]
     )
     pair = swap(own, panels, 1)
     expand, order = pl.pallas_call(
@@ -240,30 +239,29 @@
         cost_estimate=cost(2 * 10**9, 4 * 2**20),
         name="spline_loads",
     )(spline_owner, spline_local, order, *every, spline_blocks)
-    apart = 1
-    got = swap(send, panels, apart)
-    while 2 * apart < panels:
-        apart *= 2
-        half = (panels // (2 * apart), struct_rows, width)
-        keep, send = pl.pallas_call(
-            sum_kernel,
-            out_shape=(jax.ShapeDtypeStruct(half, f32), jax.ShapeDtypeStruct(half, bf16)),
-            in_specs=[VMEM, VMEM],
-            out_specs=(VMEM, VMEM),
-            compiler_params=params,
-            cost_estimate=cost(10**6, 2**20),
-            name="pair_sum",
-        )(keep, got)
-        got = swap(send, panels, apart)
+    got = swap(send, panels, 1)
+    send = pl.pallas_call(
+        sum_kernel,
+        out_shape=jax.ShapeDtypeStruct(half, bf16),
+        in_specs=[VMEM, VMEM],
+        out_specs=VMEM,
+        compiler_params=params,
+        cost_estimate=cost(10**6, 2**20),
+        name="pair_sum",
+    )(keep, got)
+    got = lax.all_to_all(
+        send, "panel", split_axis=0, concat_axis=0, tiled=True,
+        axis_index_groups=[list(range(core, panels, 2)) for core in range(2)],
+    )
     struct_adjoint = pl.pallas_call(
         functools.partial(inverse_kernel, rhs),
         out_shape=jax.ShapeDtypeStruct((struct_rows, width), f32),
-        in_specs=[VMEM] * 3,
+        in_specs=[VMEM] * 2,
         out_specs=VMEM,
         compiler_params=params,
         cost_estimate=cost(10**9, 2**20),
         name="struct_solve",
-    )(keep, got, struct_inverse)
+    )(got, struct_inverse)
     return (
         loads.reshape(1, block_count, rhs, width),
         struct_adjoint.reshape(struct_count, rhs, width),

time: 31.4 us -> 28.7 us (0.914)
  blocking collectives: 0 us -> 9.29 us
  starting transfers between devices: 15.4 us -> 7.3 us
  waiting for transfers between devices: 11.3 us -> 7.4 us
    all_to_all x0 -> x1, blocking collectives: none -> 9.29 us  [on_device(): lax.all_to_all(send, 'panel', split_axis=0, concat_axis=0, tiled=True, ax...]
    ppermute x6 -> x3, starting transfers between devices: 12.6 us -> 4.32 us  [swap(): return lax.ppermute(value, 'panel', [(i, i ^ apart) for i in range(panels)])]
    ppermute x6 -> x3, waiting for transfers between devices: 9.1 us -> 1.25 us  [swap(): return lax.ppermute(value, 'panel', [(i, i ^ apart) for i in range(panels)])]
    ppermute x1, waiting for transfers between devices: 0.01 us -> 4 us  [on_device(): lax.ppermute(own, 'panel', [(i, (i - 1 + 2 * (i % 2)) % panels) for i in...]
  transfers between devices with their start and end apart: 8 -> 5, of which waited for: 6 -> 3; matrix products, arithmetic and copies ran while one was open for 0% -> 0% of each run, Pallas kernels for 1% -> 1%
where the time goes in v6:
time: 28.7 us; the launch traced here: 28.5 us
  blocking collectives  9.29 us (32%)
  waiting for transfers between devices  7.4 us (26%)
  starting transfers between devices  7.3 us (25%)
  Pallas kernels  3.73 us (13%)
  between operations  0.76 us (3%)
    all_to_all x1, blocking collectives, on_device(): lax.all_to_all(send, 'panel', split_axis=0, concat_axis=0, tiled=True, ax...  9.29 us
    ppermute x3, starting transfers between devices, swap(): return lax.ppermute(value, 'panel', [(i, i ^ apart) for i in range(panels)])  4.32 us
    ppermute x1, waiting for transfers between devices, on_device(): lax.ppermute(own, 'panel', [(i, (i - 1 + 2 * (i % 2)) % panels) for i in...  4 us
    ppermute x1, waiting for transfers between devices, on_device(): lax.ppermute(rounded, 'mach', [(i, (i + step) % machs) for i in range(mac...  2.16 us
    pallas_call x1, Pallas kernels, on_device(): pl.pallas_call(functools.partial(spline_kernel, machs, rhs, struct_count)...  1.54 us
    ppermute x1, starting transfers between devices, on_device(): lax.ppermute(rounded, 'mach', [(i, (i + step) % machs) for i in range(mac...  1.49 us
    ppermute x1, starting transfers between devices, on_device(): lax.ppermute(own, 'panel', [(i, (i - 1 + 2 * (i % 2)) % panels) for i in...  1.49 us
    ppermute x3, waiting for transfers between devices, swap(): return lax.ppermute(value, 'panel', [(i, i ^ apart) for i in range(panels)])  1.25 us
  transfers between devices with their start and end apart: 5, of which 3 were waited for; matrix products, arithmetic and copies ran while one was open for 0% of the time, Pallas kernels for 1%

profile of v6, /device:TPU:0, one launch (start us, length us, event | category | flops | bytes accessed | tf_op | source)
XLA Modules:
  0.0 28.5 jit_solution(7782439535084244473)
XLA Ops:
  0.6 0.0 copy-start
  0.6 0.0 copy-start.1
  0.7 0.0 copy-start.2
  0.7 0.0 copy-start.3
  0.7 4.1 %collective-permute-start.2 = (bf16[32,128]{1,0:T(8,128)(2,1)}, bf16[32,128]{1,0:T(8,128)(2,1)S(1)}, u32[]{:S(2)}, u32[]{:S(2)}) collective-permute-start(bf16[32,128]{1,0:T(8,128)(2,1)} %bitcast.4), channel_id=1, source_target_pairs={{0,8},{1,9},{2,10},{3,11},{4,12},{5,13},{6,14},{7,15},{8,0},{9,1},... | collective-permute-start | bytes 24584 | tf_op jit(solution)/shard_map/ppermute | solution.py:166
  4.8 1.5 %collective-permute-start.1 = (bf16[32,128]{1,0:T(8,128)(2,1)}, bf16[32,128]{1,0:T(8,128)(2,1)S(1)}, u32[]{:S(2)}, u32[]{:S(2)}) collective-permute-start(bf16[32,128]{1,0:T(8,128)(2,1)} %bitcast.5), channel_id=1, source_target_pairs={{0,15},{1,2},{2,1},{3,4},{4,3},{5,6},{6,5},{7,8},{8,7},{9,10},{10,... | collective-permute-start | bytes 24584 | tf_op jit(solution)/shard_map/ppermute | solution.py:186
  6.3 0.1 collective-permute-start
  6.4 0.0 copy-done
  6.5 0.0 copy-done.1
  6.5 0.0 copy-done.2
  6.5 0.3 pick_rows.1
  6.7 0.0 collective-permute-done.2.mirror_ref
  6.8 4.0 %collective-permute-done.1.cross_ref = bf16[32,128]{1,0:T(8,128)(2,1)S(1)} collective-permute-done((bf16[32,128]{1,0:T(8,128)(2,1)}, bf16[32,128]{1,0:T(8,128)(2,1)S(1)}, u32[]{:S(2)}, u32[]{:S(2)}) %collective-permute-start.1) | collective-permute-done | bytes 8224 | tf_op jit(solution)/shard_map/ppermute | solution.py:186
  10.8 0.0 collective-permute-done.pair_ref
  10.8 0.0 copy-done.3
  10.8 0.0 copy-start.4
  10.8 0.0 copy-start.6
  10.8 0.0 copy-start.7
  10.8 1.1 %near_field.1 = (f32[32,128]{1,0:T(8,128)}, bf16[32,128]{1,0:T(8,128)(2,1)S(1)}) custom-call(bf16[256,128]{1,0:T(8,128)(2,1)S(1)} %get-tuple-element.12.hot_ref, f32[16,128]{1,0:T(8,128)S(1)} %get-tuple-element.13.gate_ref, bf16[32,128]{1,0:T(8,128)(2,1)S(1)} %get-tuple-element.14.own_ref, bf16[32,128]{1,0:T(8,128)(2,1)S(1)} %collective-permute-done.pair_ref, ...), custom_call_target="tpu_custom_call" | custom-call | flops 2000000000 | bytes 4194304 | tf_op jit(solution)/shard_map/near_field/pallas_call | solution.py:214
  11.9 1.5 %collective-permute-start.3 = (bf16[32,128]{1,0:T(8,128)(2,1)S(1)}, bf16[32,128]{1,0:T(8,128)(2,1)S(1)}, u32[]{:S(2)}, u32[]{:S(2)}) collective-permute-start(bf16[32,128]{1,0:T(8,128)(2,1)S(1)} %get-tuple-element.17.refs_0_), channel_id=1, source_target_pairs={{0,16},{16,0},{1,17},{17,1},{2,18},{18,2},{3,19},{19,3},{4,20},{20... | collective-permute-start | bytes 24584 | tf_op jit(solution)/shard_map/ppermute | solution.py:229
  13.4 2.2 %collective-permute-done.3.refs_1_ = bf16[32,128]{1,0:T(8,128)(2,1)S(1)} collective-permute-done((bf16[32,128]{1,0:T(8,128)(2,1)S(1)}, bf16[32,128]{1,0:T(8,128)(2,1)S(1)}, u32[]{:S(2)}, u32[]{:S(2)}) %collective-permute-start.3) | collective-permute-done | bytes 8224 | tf_op jit(solution)/shard_map/ppermute | solution.py:229
  15.6 0.0 copy-done.4
  15.6 0.0 copy-done.6
  15.6 0.0 copy-done.7
  15.6 0.0 copy-start.5
  15.6 1.5 %spline_loads.1 = (f32[8,32,128]{2,1,0:T(8,128)S(1)}, bf16[8,32,128]{2,1,0:T(8,128)(2,1)S(1)}) custom-call(s32[8,6]{1,0:T(8,128)S(1)} %copy-done.6, s32[8,6]{1,0:T(8,128)S(1)} %copy-done.7, bf16[128,64]{1,0:T(8,128)(2,1)S(1)} %get-tuple-element.16.order_ref, bf16[32,128]{1,0:T(8,128)(2,1)S(1)} %get-tuple-element.17.refs_0_, ...), custom_call_target="tpu_custom_call" | custom-call | flops 2000000000 | bytes 4194304 | tf_op jit(solution)/shard_map/spline_loads/pallas_call | solution.py:232
  17.1 0.1 collective-permute-start.4
  17.2 1.2 %collective-permute-done.4.got_ref = bf16[8,32,128]{2,1,0:T(8,128)(2,1)S(1)} collective-permute-done((bf16[8,32,128]{2,1,0:T(8,128)(2,1)S(1)}, bf16[8,32,128]{2,1,0:T(8,128)(2,1)S(1)}, u32[]{:S(2)}, u32[]{:S(2)}) %collective-permute-start.4) | collective-permute-done | bytes 65568 | tf_op jit(solution)/shard_map/ppermute | solution.py:166
  18.5 9.3 %all_to_all.5.got_ref = bf16[8,32,128]{2,1,0:T(8,128)(2,1)S(1)} all-to-all(bf16[8,32,128]{2,1,0:T(8,128)(2,1)S(1)} %pair_sum.1), channel_id=1, replica_groups={{0,2,4,6,8,10,12,14},{1,3,5,7,9,11,13,15},{16,18,20,22,24,26,28,30},{17..., dimensions={0} | all-to-all | bytes 131072 | tf_op jit(solution)/shard_map/all_to_all | solution.py:252
  27.8 0.0 copy-done.5
  27.8 0.8 %struct_solve.1 = f32[32,128]{1,0:T(8,128)} custom-call(bf16[8,32,128]{2,1,0:T(8,128)(2,1)S(1)} %all_to_all.5.got_ref, bf16[8,128,128]{2,1,0:T(8,128)(2,1)S(1)} %copy-done.5), custom_call_target="tpu_custom_call" | custom-call | flops 1000000000 | bytes 1048576 | tf_op jit(solution)/shard_map/struct_solve/pallas_call | solution.py:256
  (2 shorter events, 0.1 us)
Async XLA Ops:
  0.6 5.8 %copy-start = (bf16[1,8,4,128]{3,2,1,0:T(4,128)(2,1)S(1)}, bf16[1,8,4,128]{3,2,1,0:T(4,128)(2,1)}, u32[]{:S(2)}) copy-start(bf16[1,8,4,128]{3,2,1,0:T(4,128)(2,1)} %param.8) | copy-start | bytes 24580
  0.6 5.8 %copy-start.1 = (s32[8,8]{1,0:T(8,128)S(1)}, s32[8,8]{1,0:T(8,128)}, u32[]{:S(2)}) copy-start(s32[8,8]{1,0:T(8,128)} %pattern_ref.1) | copy-start | bytes 772
  0.7 5.8 %copy-start.2 = (s32[1,4]{1,0:T(1,128)S(1)}, s32[1,4]{1,0:T(1,128)}, u32[]{:S(2)}) copy-start(s32[1,4]{1,0:T(1,128)} %trim_ref.1) | copy-start | bytes 52
  0.7 10.1 %copy-start.3 = (bf16[1,8,8,128,128]{4,3,2,1,0:T(8,128)(2,1)S(1)}, bf16[1,8,8,128,128]{4,3,2,1,0:T(8,128)(2,1)}, u32[]{:S(2)}) copy-start(bf16[1,8,8,128,128]{4,3,2,1,0:T(8,128)(2,1)} %param.9) | copy-start | bytes 6291460
  0.7 6.1 %collective-permute-start.2 = (bf16[32,128]{1,0:T(8,128)(2,1)}, bf16[32,128]{1,0:T(8,128)(2,1)S(1)}, u32[]{:S(2)}, u32[]{:S(2)}) collective-permute-start(bf16[32,128]{1,0:T(8,128)(2,1)} %bitcast.4), channel_id=1, source_target_pairs={{0,8},{1,9},{2,10},{3,11},{4,12},{5,13},{6,14},{7,15},{8,0},{9,1},... | collective-permute-start | bytes 24584 | tf_op jit(solution)/shard_map/ppermute | solution.py:166
  4.8 6.0 %collective-permute-start.1 = (bf16[32,128]{1,0:T(8,128)(2,1)}, bf16[32,128]{1,0:T(8,128)(2,1)S(1)}, u32[]{:S(2)}, u32[]{:S(2)}) collective-permute-start(bf16[32,128]{1,0:T(8,128)(2,1)} %bitcast.5), channel_id=1, source_target_pairs={{0,15},{1,2},{2,1},{3,4},{4,3},{5,6},{6,5},{7,8},{8,7},{9,10},{10,... | collective-permute-start | bytes 24584 | tf_op jit(solution)/shard_map/ppermute | solution.py:186
  6.3 4.5 %collective-permute-start = (bf16[32,128]{1,0:T(8,128)(2,1)}, bf16[32,128]{1,0:T(8,128)(2,1)S(1)}, u32[]{:S(2)}, u32[]{:S(2)}) collective-permute-start(bf16[32,128]{1,0:T(8,128)(2,1)} %bitcast.6), channel_id=1, source_target_pairs={{0,1},{1,0},{2,3},{3,2},{4,5},{5,4},{6,7},{7,6},{8,9},{9,8},{10,11... | collective-permute-start | bytes 24584 | tf_op jit(solution)/shard_map/ppermute | solution.py:166
  10.8 4.8 %copy-start.4 = (bf16[8,6,128,128]{3,2,1,0:T(8,128)(2,1)S(1)}, bf16[8,6,128,128]{3,2,1,0:T(8,128)(2,1)}, u32[]{:S(2)}) copy-start(bf16[8,6,128,128]{3,2,1,0:T(8,128)(2,1)} %refs_2_.1) | copy-start | bytes 4718596
  10.8 4.8 %copy-start.6 = (s32[8,6]{1,0:T(8,128)S(1)}, s32[8,6]{1,0:T(8,128)}, u32[]{:S(2)}) copy-start(s32[8,6]{1,0:T(8,128)} %owner_ref.1) | copy-start | bytes 580
  10.8 4.8 %copy-start.7 = (s32[8,6]{1,0:T(8,128)S(1)}, s32[8,6]{1,0:T(8,128)}, u32[]{:S(2)}) copy-start(s32[8,6]{1,0:T(8,128)} %local_ref.1) | copy-start | bytes 580
  11.9 3.7 %collective-permute-start.3 = (bf16[32,128]{1,0:T(8,128)(2,1)S(1)}, bf16[32,128]{1,0:T(8,128)(2,1)S(1)}, u32[]{:S(2)}, u32[]{:S(2)}) collective-permute-start(bf16[32,128]{1,0:T(8,128)(2,1)S(1)} %get-tuple-element.17.refs_0_), channel_id=1, source_target_pairs={{0,16},{16,0},{1,17},{17,1},{2,18},{18,2},{3,19},{19,3},{4,20},{20... | collective-permute-start | bytes 24584 | tf_op jit(solution)/shard_map/ppermute | solution.py:229
  15.6 12.2 %copy-start.5 = (bf16[8,128,128]{2,1,0:T(8,128)(2,1)S(1)}, bf16[8,128,128]{2,1,0:T(8,128)(2,1)}, u32[]{:S(2)}) copy-start(bf16[8,128,128]{2,1,0:T(8,128)(2,1)} %inverse_ref.1) | copy-start | bytes 786436
  17.1 1.3 %collective-permute-start.4 = (bf16[8,32,128]{2,1,0:T(8,128)(2,1)S(1)}, bf16[8,32,128]{2,1,0:T(8,128)(2,1)S(1)}, u32[]{:S(2)}, u32[]{:S(2)}) collective-permute-start(bf16[8,32,128]{2,1,0:T(8,128)(2,1)S(1)} %get-tuple-element.19), channel_id=1, source_target_pairs={{0,1},{1,0},{2,3},{3,2},{4,5},{5,4},{6,7},{7,6},{8,9},{9,8},{10,11... | collective-permute-start | bytes 196616 | tf_op jit(solution)/shard_map/ppermute | solution.py:166

commit v7 on v6

--- a/solution.py
+++ b/solution.py
@@ -13,16 +13,14 @@
 TILE = 8
 
 
-def spread_kernel(machs, rhs, block_count, expand_ref, order_ref):
+def spread_kernel(rhs, expand_ref, order_ref):
     shape = expand_ref.shape
     expand_ref[...] = (
         lax.broadcasted_iota(jnp.int32, shape, 0) // rhs == lax.broadcasted_iota(jnp.int32, shape, 1)
     ).astype(jnp.bfloat16)
     shape = order_ref.shape
     row = lax.broadcasted_iota(jnp.int32, shape, 0)
-    source = (
-        (row // TILE) % machs * (block_count * rhs) + row // (TILE * machs) * rhs + row % rhs
-    )
+    source = row // TILE * rhs + row % rhs
     order_ref[...] = (lax.broadcasted_iota(jnp.int32, shape, 1) == source).astype(jnp.bfloat16)
 
 
@@ -93,19 +91,26 @@
         rounded_ref[g * PACK : (g + 1) * PACK] = loads.astype(jnp.bfloat16)
 
 
-def spline_kernel(machs, rhs, struct_count, owner_ref, local_ref, order_ref, *refs):
-    rounded_refs, spline_ref, keep_ref, send_ref, acc = refs[:machs], *refs[machs:]
+def parity(index):
+    for shift in (16, 8, 4, 2, 1):
+        index = index ^ (index >> shift)
+    return index & 1
+
+
+def spline_kernel(
+    rhs, struct_count, owner_ref, local_ref, order_ref, rounded_ref, spline_ref,
+    keep_ref, send_ref, acc,
+):
     block_count, splines = owner_ref.shape
-    rows, width = rounded_refs[0].shape
-    here = lax.axis_index("panel")
+    width = rounded_ref.shape[1]
+    mine_class = parity(lax.axis_index("panel"))
     acc[...] = jnp.zeros(acc.shape, jnp.float32)
-    every = jnp.concatenate([ref[...] for ref in rounded_refs], axis=0)
-    left = jnp.dot(order_ref[...], every, preferred_element_type=jnp.float32)
+    left = jnp.dot(order_ref[...], rounded_ref[...], preferred_element_type=jnp.float32)
     left = left.astype(jnp.bfloat16)
     part = lax.broadcasted_iota(jnp.int32, (TILE, width), 0) // rhs
     per_tile = TILE // rhs
     owner_tiles = struct_count // per_tile
-    height = machs * TILE
+    height = TILE
     blank = jnp.zeros((height, width), jnp.bfloat16)
     for pair in range(0, block_count, 2):
         mine = left[pair * height : (pair + 2) * height]
@@ -125,15 +130,11 @@
         )
         product = jnp.dot(mine, blocks, preferred_element_type=jnp.float32)
         for i in (pair, pair + 1):
-            total = product[(i - pair) * height : (i - pair) * height + TILE]
-            for m in range(1, machs):
-                start = (i - pair) * height + m * TILE
-                total = total + product[start : start + TILE]
+            total = product[(i - pair) * height : (i - pair + 1) * height]
             places, sums = [], []
             for s in range(splines):
-                apart = owner_ref[i, s] ^ here
-                local = local_ref[i, s]
-                place = (apart % 2, owner_ref[i, s] // 2 * owner_tiles + local // per_tile)
+                owner, local = owner_ref[i, s], local_ref[i, s]
+                place = (parity(owner) ^ mine_class, owner // 2 * owner_tiles + local // per_tile)
                 added = jnp.where(
                     part == local % per_tile, total[:, s * width : (s + 1) * width], 0.0
                 )
@@ -148,13 +149,15 @@
 def sum_kernel(held_ref, got_ref, out_ref):
     for place in range(held_ref.shape[0]):
         total = held_ref[place] + got_ref[place].astype(jnp.float32)
-        out_ref[place] = total.astype(out_ref.dtype)
+        for copy in range(out_ref.shape[0]):
+            out_ref[copy, place] = total.astype(out_ref.dtype)
 
 
 def inverse_kernel(rhs, got_ref, inverse_ref, out_ref):
-    total = got_ref[0].astype(jnp.float32)
-    for source in range(1, got_ref.shape[0]):
-        total = total + got_ref[source].astype(jnp.float32)
+    sources = [got_ref[index].astype(jnp.float32) for index in range(got_ref.shape[0])]
+    while len(sources) > 1:
+        sources = [a + b for a, b in zip(sources[::2], sources[1::2])] + sources[len(sources) & ~1 :]
+    total = sources[0]
     rounded = total.astype(jnp.bfloat16)
     for g in range(total.shape[0] // PACK):
         out_ref[g * PACK : (g + 1) * PACK] = grouped_product(
@@ -183,15 +186,24 @@
     f32, bf16 = jnp.float32, jnp.bfloat16
     own = adjoint.reshape(rows, width)
     mirror = swap(own, panels, panels // 2)
+    beside = {0: 0, panels - 1: panels - 1}
     cross = lax.ppermute(
-        own, "panel", [(i, (i - 1 + 2 * (i % 2)) % panels) for i in range(panels)]
+        own, ("mach", "panel"),
+        [
+            (
+                mach * panels + i,
+                (mach ^ (i in beside)) * panels + beside.get(i, i - 1 + 2 * (i % 2)),
+            )
+            for mach in range(machs)
+            for i in range(panels)
+        ],
     )
     pair = swap(own, panels, 1)
     expand, order = pl.pallas_call(
-        functools.partial(spread_kernel, machs, rhs, block_count),
+        functools.partial(spread_kernel, rhs),
         out_shape=(
             jax.ShapeDtypeStruct((rows, block_count), bf16),
-            jax.ShapeDtypeStruct((block_count * machs * TILE, machs * rows), bf16),
+            jax.ShapeDtypeStruct((block_count * TILE, rows), bf16),
         ),
         out_specs=(VMEM, VMEM),
         compiler_params=params,
@@ -223,26 +235,21 @@
         cost_estimate=cost(2 * 10**9, 4 * 2**20),
         name="near_field",
     )(hot, gate, held, pair, cross, mirror, near_blocks[0])
-    every = [rounded]
-    for step in range(1, machs):
-        every.append(
-            lax.ppermute(rounded, "mach", [(i, (i + step) % machs) for i in range(machs)])
-        )
     half = (panels // 2, struct_rows, width)
     keep, send = pl.pallas_call(
-        functools.partial(spline_kernel, machs, rhs, struct_count),
+        functools.partial(spline_kernel, rhs, struct_count),
         out_shape=(jax.ShapeDtypeStruct(half, f32), jax.ShapeDtypeStruct(half, bf16)),
-        in_specs=[SMEM, SMEM] + [VMEM] * (machs + 2),
+        in_specs=[SMEM, SMEM, VMEM, VMEM, VMEM],
         out_specs=(VMEM, VMEM),
         scratch_shapes=[pltpu.VMEM((2, panels // 2 * struct_rows // TILE, TILE, width), f32)],
         compiler_params=params,
         cost_estimate=cost(2 * 10**9, 4 * 2**20),
         name="spline_loads",
-    )(spline_owner, spline_local, order, *every, spline_blocks)
+    )(spline_owner, spline_local, order, rounded, spline_blocks)
     got = swap(send, panels, 1)
     send = pl.pallas_call(
         sum_kernel,
-        out_shape=jax.ShapeDtypeStruct(half, bf16),
+        out_shape=jax.ShapeDtypeStruct((machs, *half), bf16),
         in_specs=[VMEM, VMEM],
         out_specs=VMEM,
         compiler_params=params,
@@ -250,8 +257,16 @@
         name="pair_sum",
     )(keep, got)
     got = lax.all_to_all(
-        send, "panel", split_axis=0, concat_axis=0, tiled=True,
-        axis_index_groups=[list(range(core, panels, 2)) for core in range(2)],
+        send.reshape(machs * panels // 2, struct_rows, width), ("mach", "panel"),
+        split_axis=0, concat_axis=0, tiled=True,
+        axis_index_groups=[
+            [
+                mach * panels + 2 * chip + (parity(2 * chip) ^ which)
+                for mach in range(machs)
+                for chip in range(panels // 2)
+            ]
+            for which in range(2)
+        ],
     )
     struct_adjoint = pl.pallas_call(
         functools.partial(inverse_kernel, rhs),

time: 28.7 us -> 26.4 us (0.920)
  waiting for transfers between devices: 7.4 us -> 3.14 us
  blocking collectives: 9.29 us -> 12.6 us
  starting transfers between devices: 7.3 us -> 5.81 us
    ppermute x2 -> x1, waiting for transfers between devices: 6.16 us -> 1.9 us  [on_device(): lax.ppermute(own, ('mach', 'panel'), [(mach * panels + i, (mach ^ (i in b...]
    all_to_all x1, blocking collectives: 9.29 us -> 12.6 us  [on_device(): lax.all_to_all(send.reshape(machs * panels // 2, struct_rows, width), ('m...]
    ppermute x2 -> x1, starting transfers between devices: 2.98 us -> 1.49 us  [on_device(): lax.ppermute(own, ('mach', 'panel'), [(mach * panels + i, (mach ^ (i in b...]
  transfers between devices with their start and end apart: 5 -> 4, of which waited for: 3 -> 2; matrix products, arithmetic and copies ran while one was open for 0% -> 0% of each run, Pallas kernels for 1% -> 1%
where the time goes in v7:
time: 26.4 us; the launch traced here: 26.3 us
  blocking collectives  12.6 us (48%)
  starting transfers between devices  5.81 us (22%)
  Pallas kernels  3.66 us (14%)
  waiting for transfers between devices  3.14 us (12%)
  between operations  0.75 us (3%)
  local copies, waits for them, and re-layouts  0.31 us (1%)
    all_to_all x1, blocking collectives, on_device(): lax.all_to_all(send.reshape(machs * panels // 2, struct_rows, width), ('m...  12.6 us
    ppermute x3, starting transfers between devices, swap(): return lax.ppermute(value, 'panel', [(i, i ^ apart) for i in range(panels)])  4.32 us
    ppermute x1, waiting for transfers between devices, on_device(): lax.ppermute(own, ('mach', 'panel'), [(mach * panels + i, (mach ^ (i in b...  1.9 us
    ppermute x1, starting transfers between devices, on_device(): lax.ppermute(own, ('mach', 'panel'), [(mach * panels + i, (mach ^ (i in b...  1.49 us
    pallas_call x1, Pallas kernels, on_device(): pl.pallas_call(functools.partial(spline_kernel, rhs, struct_count), out_s...  1.49 us
    ppermute x3, waiting for transfers between devices, swap(): return lax.ppermute(value, 'panel', [(i, i ^ apart) for i in range(panels)])  1.25 us
    pallas_call x1, Pallas kernels, on_device(): pl.pallas_call(functools.partial(near_kernel, rhs), out_shape=(jax.ShapeD...  1.11 us
    pallas_call x1, Pallas kernels, on_device(): pl.pallas_call(functools.partial(inverse_kernel, rhs), out_shape=jax.Shap...  0.76 us
  transfers between devices with their start and end apart: 4, of which 2 were waited for; matrix products, arithmetic and copies ran while one was open for 0% of the time, Pallas kernels for 1%

profile of v7, /device:TPU:0, one launch (start us, length us, event | category | flops | bytes accessed | tf_op | source)
XLA Modules:
  0.0 26.3 jit_solution(12163362661247266600)
XLA Ops:
  0.6 0.0 copy-start
  0.6 0.0 copy-start.1
  0.7 0.0 copy-start.2
  0.7 0.0 copy-start.3
  0.7 4.1 %collective-permute-start.2 = (bf16[32,128]{1,0:T(8,128)(2,1)}, bf16[32,128]{1,0:T(8,128)(2,1)S(1)}, u32[]{:S(2)}, u32[]{:S(2)}) collective-permute-start(bf16[32,128]{1,0:T(8,128)(2,1)} %bitcast.6), channel_id=1, source_target_pairs={{0,8},{1,9},{2,10},{3,11},{4,12},{5,13},{6,14},{7,15},{8,0},{9,1},... | collective-permute-start | bytes 24584 | tf_op jit(solution)/shard_map/ppermute | solution.py:169
  4.8 1.5 %collective-permute-start.1 = (bf16[32,128]{1,0:T(8,128)(2,1)}, bf16[32,128]{1,0:T(8,128)(2,1)S(1)}, u32[]{:S(2)}, u32[]{:S(2)}) collective-permute-start(bf16[32,128]{1,0:T(8,128)(2,1)} %bitcast.7), channel_id=1, source_target_pairs={{0,16},{1,2},{2,1},{3,4},{4,3},{5,6},{6,5},{7,8},{8,7},{9,10},{10,... | collective-permute-start | bytes 24584 | tf_op jit(solution)/shard_map/ppermute | solution.py:190
  6.3 0.1 collective-permute-start
  6.4 0.0 copy-done
  6.4 0.0 copy-done.1
  6.4 0.0 copy-done.2
  6.5 0.3 pick_rows.1
  6.7 0.0 collective-permute-done.2.mirror_ref
  6.7 1.9 %collective-permute-done.1.cross_ref = bf16[32,128]{1,0:T(8,128)(2,1)S(1)} collective-permute-done((bf16[32,128]{1,0:T(8,128)(2,1)}, bf16[32,128]{1,0:T(8,128)(2,1)S(1)}, u32[]{:S(2)}, u32[]{:S(2)}) %collective-permute-start.1) | collective-permute-done | bytes 8224 | tf_op jit(solution)/shard_map/ppermute | solution.py:190
  8.6 0.0 collective-permute-done.pair_ref
  8.6 0.0 copy-done.3
  8.6 0.0 copy-start.4
  8.6 0.0 copy-start.6
  8.7 0.0 copy-start.7
  8.7 1.1 %near_field.1 = (f32[32,128]{1,0:T(8,128)}, bf16[32,128]{1,0:T(8,128)(2,1)S(1)}) custom-call(bf16[256,128]{1,0:T(8,128)(2,1)S(1)} %get-tuple-element.12.hot_ref, f32[16,128]{1,0:T(8,128)S(1)} %get-tuple-element.13.gate_ref, bf16[32,128]{1,0:T(8,128)(2,1)S(1)} %get-tuple-element.14.own_ref, bf16[32,128]{1,0:T(8,128)(2,1)S(1)} %collective-permute-done.pair_ref, ...), custom_call_target="tpu_custom_call" | custom-call | flops 2000000000 | bytes 4194304 | tf_op jit(solution)/shard_map/near_field/pallas_call | solution.py:226
  9.8 0.3 %copy-done.4 = bf16[8,6,128,128]{3,2,1,0:T(8,128)(2,1)S(1)} copy-done((bf16[8,6,128,128]{3,2,1,0:T(8,128)(2,1)S(1)}, bf16[8,6,128,128]{3,2,1,0:T(8,128)(2,1)}, u32[]{:S(2)}) %copy-start.4) | copy-done | bytes 1572888
  10.1 0.0 copy-done.6
  10.1 0.0 copy-done.7
  10.1 0.0 copy-start.5
  10.1 1.5 %spline_loads.1 = (f32[8,32,128]{2,1,0:T(8,128)S(1)}, bf16[8,32,128]{2,1,0:T(8,128)(2,1)S(1)}) custom-call(s32[8,6]{1,0:T(8,128)S(1)} %copy-done.6, s32[8,6]{1,0:T(8,128)S(1)} %copy-done.7, bf16[64,32]{1,0:T(8,128)(2,1)S(1)} %get-tuple-element.16.order_ref, bf16[32,128]{1,0:T(8,128)(2,1)S(1)} %get-tuple-element.17.rounded_ref, ...), custom_call_target="tpu_custom_call" | custom-call | flops 2000000000 | bytes 4194304 | tf_op jit(solution)/shard_map/spline_loads/pallas_call | solution.py:239
  11.6 0.1 collective-permute-start.3
  11.6 1.2 %collective-permute-done.3.got_ref = bf16[8,32,128]{2,1,0:T(8,128)(2,1)S(1)} collective-permute-done((bf16[8,32,128]{2,1,0:T(8,128)(2,1)S(1)}, bf16[8,32,128]{2,1,0:T(8,128)(2,1)S(1)}, u32[]{:S(2)}, u32[]{:S(2)}) %collective-permute-start.3) | collective-permute-done | bytes 65568 | tf_op jit(solution)/shard_map/ppermute | solution.py:169
  12.9 12.6 %all_to_all.5.got_ref = bf16[16,32,128]{2,1,0:T(8,128)(2,1)S(1)} all-to-all(bf16[16,32,128]{2,1,0:T(8,128)(2,1)S(1)} %bitcast.5), channel_id=1, replica_groups={{0,3,5,6,9,10,12,15,16,19,21,22,25,26,28,31},{1,2,4,7,8,11,13,14,17,18,..., dimensions={0} | all-to-all | bytes 262144 | tf_op jit(solution)/shard_map/all_to_all | solution.py:259
  25.5 0.0 copy-done.5
  25.5 0.8 %struct_solve.1 = f32[32,128]{1,0:T(8,128)} custom-call(bf16[16,32,128]{2,1,0:T(8,128)(2,1)S(1)} %all_to_all.5.got_ref, bf16[8,128,128]{2,1,0:T(8,128)(2,1)S(1)} %copy-done.5), custom_call_target="tpu_custom_call" | custom-call | flops 1000000000 | bytes 1048576 | tf_op jit(solution)/shard_map/struct_solve/pallas_call | solution.py:271
  (2 shorter events, 0.0 us)
Async XLA Ops:
  0.6 5.8 %copy-start = (bf16[1,8,4,128]{3,2,1,0:T(4,128)(2,1)S(1)}, bf16[1,8,4,128]{3,2,1,0:T(4,128)(2,1)}, u32[]{:S(2)}) copy-start(bf16[1,8,4,128]{3,2,1,0:T(4,128)(2,1)} %param.8) | copy-start | bytes 24580
  0.6 5.8 %copy-start.1 = (s32[8,8]{1,0:T(8,128)S(1)}, s32[8,8]{1,0:T(8,128)}, u32[]{:S(2)}) copy-start(s32[8,8]{1,0:T(8,128)} %pattern_ref.1) | copy-start | bytes 772
  0.7 5.8 %copy-start.2 = (s32[1,4]{1,0:T(1,128)S(1)}, s32[1,4]{1,0:T(1,128)}, u32[]{:S(2)}) copy-start(s32[1,4]{1,0:T(1,128)} %trim_ref.1) | copy-start | bytes 52
  0.7 8.0 %copy-start.3 = (bf16[1,8,8,128,128]{4,3,2,1,0:T(8,128)(2,1)S(1)}, bf16[1,8,8,128,128]{4,3,2,1,0:T(8,128)(2,1)}, u32[]{:S(2)}) copy-start(bf16[1,8,8,128,128]{4,3,2,1,0:T(8,128)(2,1)} %param.9) | copy-start | bytes 6291460
  0.7 6.1 %collective-permute-start.2 = (bf16[32,128]{1,0:T(8,128)(2,1)}, bf16[32,128]{1,0:T(8,128)(2,1)S(1)}, u32[]{:S(2)}, u32[]{:S(2)}) collective-permute-start(bf16[32,128]{1,0:T(8,128)(2,1)} %bitcast.6), channel_id=1, source_target_pairs={{0,8},{1,9},{2,10},{3,11},{4,12},{5,13},{6,14},{7,15},{8,0},{9,1},... | collective-permute-start | bytes 24584 | tf_op jit(solution)/shard_map/ppermute | solution.py:169
  4.8 3.9 %collective-permute-start.1 = (bf16[32,128]{1,0:T(8,128)(2,1)}, bf16[32,128]{1,0:T(8,128)(2,1)S(1)}, u32[]{:S(2)}, u32[]{:S(2)}) collective-permute-start(bf16[32,128]{1,0:T(8,128)(2,1)} %bitcast.7), channel_id=1, source_target_pairs={{0,16},{1,2},{2,1},{3,4},{4,3},{5,6},{6,5},{7,8},{8,7},{9,10},{10,... | collective-permute-start | bytes 24584 | tf_op jit(solution)/shard_map/ppermute | solution.py:190
  6.3 2.4 %collective-permute-start = (bf16[32,128]{1,0:T(8,128)(2,1)}, bf16[32,128]{1,0:T(8,128)(2,1)S(1)}, u32[]{:S(2)}, u32[]{:S(2)}) collective-permute-start(bf16[32,128]{1,0:T(8,128)(2,1)} %bitcast.8), channel_id=1, source_target_pairs={{0,1},{1,0},{2,3},{3,2},{4,5},{5,4},{6,7},{7,6},{8,9},{9,8},{10,11... | collective-permute-start | bytes 24584 | tf_op jit(solution)/shard_map/ppermute | solution.py:169
  8.6 1.4 %copy-start.4 = (bf16[8,6,128,128]{3,2,1,0:T(8,128)(2,1)S(1)}, bf16[8,6,128,128]{3,2,1,0:T(8,128)(2,1)}, u32[]{:S(2)}) copy-start(bf16[8,6,128,128]{3,2,1,0:T(8,128)(2,1)} %spline_ref.1) | copy-start | bytes 4718596
  8.6 1.4 %copy-start.6 = (s32[8,6]{1,0:T(8,128)S(1)}, s32[8,6]{1,0:T(8,128)}, u32[]{:S(2)}) copy-start(s32[8,6]{1,0:T(8,128)} %owner_ref.1) | copy-start | bytes 580
  8.7 1.4 %copy-start.7 = (s32[8,6]{1,0:T(8,128)S(1)}, s32[8,6]{1,0:T(8,128)}, u32[]{:S(2)}) copy-start(s32[8,6]{1,0:T(8,128)} %local_ref.1) | copy-start | bytes 580
  10.1 15.4 %copy-start.5 = (bf16[8,128,128]{2,1,0:T(8,128)(2,1)S(1)}, bf16[8,128,128]{2,1,0:T(8,128)(2,1)}, u32[]{:S(2)}) copy-start(bf16[8,128,128]{2,1,0:T(8,128)(2,1)} %inverse_ref.1) | copy-start | bytes 786436
  11.6 1.3 %collective-permute-start.3 = (bf16[8,32,128]{2,1,0:T(8,128)(2,1)S(1)}, bf16[8,32,128]{2,1,0:T(8,128)(2,1)S(1)}, u32[]{:S(2)}, u32[]{:S(2)}) collective-permute-start(bf16[8,32,128]{2,1,0:T(8,128)(2,1)S(1)} %get-tuple-element.19), channel_id=1, source_target_pairs={{0,1},{1,0},{2,3},{3,2},{4,5},{5,4},{6,7},{7,6},{8,9},{9,8},{10,11... | collective-permute-start | bytes 196616 | tf_op jit(solution)/shard_map/ppermute | solution.py:169

commit v8 on v7

v8 whole, which is shorter than its diff:
```python
import functools

import jax
import jax.numpy as jnp
from jax import lax
from jax.experimental import pallas as pl
from jax.experimental.pallas import tpu as pltpu
from jax.sharding import PartitionSpec as P

SMEM = pl.BlockSpec(memory_space=pltpu.SMEM)
VMEM = pl.BlockSpec(memory_space=pltpu.VMEM)
PACK = 16
TILE = 8


def parity(index):
    for shift in (16, 8, 4, 2, 1):
        index = index ^ (index >> shift)
    return index & 1


def spread_kernel(rhs, expand_ref):
    shape = expand_ref.shape
    expand_ref[...] = (
        lax.broadcasted_iota(jnp.int32, shape, 0) // rhs == lax.broadcasted_iota(jnp.int32, shape, 1)
    ).astype(jnp.bfloat16)


def pick_kernel(
    panels, rhs, struct_count, expand_ref, pattern_ref, trim_ref, own_ref, owner_ref, local_ref,
    hot_ref, gate_ref, held_ref, code_ref,
):
    block_count, entries = pattern_ref.shape
    rows = own_ref.shape[0]
    here = lax.axis_index("panel")
    shape = (rows, hot_ref.shape[1])
    offset = lax.broadcasted_iota(jnp.int32, shape, 1) - (
        lax.broadcasted_iota(jnp.int32, shape, 0) % rhs
    )
    block = pattern_ref[...]
    apart = (block // block_count) ^ here
    slot = jnp.where(apart == 0, 0, jnp.where(apart == 1, 1, 2))
    first = (slot * block_count + block % block_count) * rhs
    first = jnp.dot(
        expand_ref[...],
        first.astype(jnp.float32).astype(jnp.bfloat16),
        preferred_element_type=jnp.float32,
    ).astype(jnp.int32)
    for k in range(2, entries):
        hot_ref[(k - 2) * rows : (k - 1) * rows] = (offset == first[:, k : k + 1]).astype(
            jnp.bfloat16
        )
    shape = (gate_ref.shape[0], rhs)
    mine = lax.broadcasted_iota(jnp.int32, shape, 0) % rhs == lax.broadcasted_iota(
        jnp.int32, shape, 1
    )
    gate = jnp.sum(jnp.where(mine, trim_ref[...], 0).astype(jnp.float32), axis=1, keepdims=True)
    gate_ref[...] = jnp.broadcast_to(gate, gate_ref.shape)
    held_ref[...] = own_ref[...]
    owner = owner_ref[...]
    code_ref[...] = (
        (parity(owner) ^ parity(here)) * (panels // 2) + owner // 2
    ) * struct_count + local_ref[...]


def grouped_product(rhs, left, blocks_of, group):
    per_group = PACK // rhs
    every = jnp.concatenate([blocks_of(group * per_group + j) for j in range(per_group)], axis=1)
    product = jnp.dot(left, every, preferred_element_type=jnp.float32)
    width = product.shape[1] // per_group
    row = lax.broadcasted_iota(jnp.int32, (PACK, width), 0)
    out = product[:, :width]
    for j in range(1, per_group):
        out = jnp.where(row // rhs == j, product[:, j * width : (j + 1) * width], out)
    return out


def near_kernel(rhs, hot_ref, own_ref, pair_ref, cross_ref, near_ref, part_ref):
    rows, width = own_ref.shape
    others = hot_ref.shape[0] // rows
    own = own_ref[...]
    pool = jnp.concatenate([own, pair_ref[...], cross_ref[...], own], axis=0)
    picked = jnp.dot(hot_ref[...], pool, preferred_element_type=jnp.float32)
    picked = picked.astype(jnp.bfloat16)
    for g in range(rows // PACK):
        left = [own[g * PACK : (g + 1) * PACK]] + [
            picked[k * rows + g * PACK : k * rows + (g + 1) * PACK] for k in range(others)
        ]
        part_ref[g * PACK : (g + 1) * PACK] = grouped_product(
            rhs,
            jnp.concatenate(left, axis=1),
            lambda i: jnp.concatenate(
                [near_ref[i, 0], near_ref[i, 2:].reshape(others * width, width)], axis=0
            ),
            g,
        )


def spline_kernel(
    rhs, code_ref, part_ref, mirror_ref, gate_ref, near_ref, spline_ref,
    loads_hbm, keep_ref, send_ref, loads_ref, acc, sem,
):
    block_count, splines = code_ref.shape
    rows, width = part_ref.shape
    for g in range(rows // PACK):
        group = slice(g * PACK, (g + 1) * PACK)
        far = grouped_product(rhs, mirror_ref[group], lambda i: near_ref[i, 1], g)
        loads_ref[group] = gate_ref[...] * (part_ref[group] + far)
    copy = pltpu.make_async_copy(loads_ref, loads_hbm, sem)
    copy.start()
    acc[...] = jnp.zeros(acc.shape, jnp.float32)
    upper = lax.broadcasted_iota(jnp.int32, (TILE, width), 0) // rhs
    blank = jnp.zeros((TILE, width), jnp.float32)
    for pair in range(0, block_count, 2):
        both = loads_ref[pair * rhs : (pair + 2) * rhs]
        turned = pltpu.roll(both, rhs, 0)
        mine = jnp.concatenate(
            [
                jnp.concatenate([jnp.where(upper == 0, both, turned), blank], axis=1),
                jnp.concatenate([blank, jnp.where(upper == 0, turned, both)], axis=1),
            ],
            axis=0,
        ).astype(jnp.bfloat16)
        blocks = jnp.concatenate(
            [
                jnp.concatenate([spline_ref[i, s] for s in range(splines)], axis=1)
                for i in (pair, pair + 1)
            ],
            axis=0,
        )
        product = jnp.dot(mine, blocks, preferred_element_type=jnp.float32)
        for i in (pair, pair + 1):
            total = product[(i - pair) * TILE : (i - pair + 1) * TILE]
            places, sums = [], []
            for s in range(splines):
                code = code_ref[i, s]
                place = code >> 1
                added = jnp.where(upper == (code & 1), total[:, s * width : (s + 1) * width], 0.0)
                places.append(place)
                sums.append(acc[place] + added)
            for place, value in zip(places, sums):
                acc[place] = value
    tiles = acc.shape[0] // 2
    keep_ref[...] = acc[:tiles].reshape(keep_ref.shape)
    send_ref[...] = acc[tiles:].reshape(send_ref.shape).astype(send_ref.dtype)
    copy.wait()


def sum_kernel(held_ref, got_ref, out_ref):
    for place in range(held_ref.shape[0]):
        total = held_ref[place] + got_ref[place].astype(jnp.float32)
        for copy in range(out_ref.shape[0]):
            out_ref[copy, place] = total.astype(out_ref.dtype)


def inverse_kernel(rhs, got_ref, inverse_ref, out_ref):
    sources = [got_ref[index].astype(jnp.float32) for index in range(got_ref.shape[0])]
    while len(sources) > 1:
        sources = [a + b for a, b in zip(sources[::2], sources[1::2])] + sources[len(sources) & ~1 :]
    total = sources[0]
    rounded = total.astype(jnp.bfloat16)
    for g in range(total.shape[0] // PACK):
        out_ref[g * PACK : (g + 1) * PACK] = grouped_product(
            rhs, rounded[g * PACK : (g + 1) * PACK], lambda t: inverse_ref[t], g
        )


def swap(value, panels, apart):
    return lax.ppermute(value, "panel", [(i, i ^ apart) for i in range(panels)])


def cost(flops, size):
    return pl.CostEstimate(flops=flops, bytes_accessed=size, transcendentals=0)


def on_device(
    adjoint, near_blocks, pattern, trim_mask, spline_blocks, spline_owner, spline_local,
    struct_inverse,
):
    _, block_count, rhs, width = adjoint.shape
    entries = pattern.shape[1]
    panels, machs = lax.axis_size("panel"), lax.axis_size("mach")
    struct_count = struct_inverse.shape[0]
    rows, struct_rows = block_count * rhs, struct_count * rhs
    params = pltpu.CompilerParams(vmem_limit_bytes=16 * 1024 * 1024)
    f32, bf16 = jnp.float32, jnp.bfloat16
    own = adjoint.reshape(rows, width)
    mirror = swap(own, panels, panels // 2)
    beside = {0: 0, panels - 1: panels - 1}
    cross = lax.ppermute(
        own, ("mach", "panel"),
        [
            (
                mach * panels + i,
                (mach ^ (i in beside)) * panels + beside.get(i, i - 1 + 2 * (i % 2)),
            )
            for mach in range(machs)
            for i in range(panels)
        ],
    )
    pair = swap(own, panels, 1)
    expand = pl.pallas_call(
        functools.partial(spread_kernel, rhs),
        out_shape=jax.ShapeDtypeStruct((rows, block_count), bf16),
        out_specs=VMEM,
        compiler_params=params,
        cost_estimate=cost(8 * 10**9, 32 * 2**20),
        name="row_order",
    )()
    hot, gate, held, code = pl.pallas_call(
        functools.partial(pick_kernel, panels, rhs, struct_count),
        out_shape=(
            jax.ShapeDtypeStruct(((entries - 2) * rows, 4 * rows), bf16),
            jax.ShapeDtypeStruct((PACK, width), f32),
            jax.ShapeDtypeStruct((rows, width), bf16),
            jax.ShapeDtypeStruct(spline_owner.shape, jnp.int32),
        ),
        in_specs=[VMEM] * 6,
        out_specs=(VMEM,) * 4,
        compiler_params=params,
        cost_estimate=cost(10**6, 2**17),
        name="pick_rows",
    )(expand, pattern, trim_mask, own, spline_owner, spline_local)
    part = pl.pallas_call(
        functools.partial(near_kernel, rhs),
        out_shape=jax.ShapeDtypeStruct((rows, width), f32),
        in_specs=[VMEM] * 5,
        out_specs=VMEM,
        compiler_params=params,
        cost_estimate=cost(10**6, 2**17),
        name="near_field",
    )(hot, held, pair, cross, near_blocks[0])
    half = (panels // 2, struct_rows, width)
    loads, keep, send = pl.pallas_call(
        functools.partial(spline_kernel, rhs),
        out_shape=(
            jax.ShapeDtypeStruct((rows, width), f32),
            jax.ShapeDtypeStruct(half, f32),
            jax.ShapeDtypeStruct(half, bf16),
        ),
        in_specs=[SMEM] + [VMEM] * 5,
        out_specs=(pl.BlockSpec(memory_space=pl.ANY), VMEM, VMEM),
        scratch_shapes=[
            pltpu.VMEM((rows, width), f32),
            pltpu.VMEM((panels * struct_rows // TILE, TILE, width), f32),
            pltpu.SemaphoreType.DMA,
        ],
        compiler_params=params,
        cost_estimate=cost(10**6, 2**17),
        name="spline_loads",
    )(code, part, mirror, gate, near_blocks[0], spline_blocks)
    got = swap(send, panels, 1)
    send = pl.pallas_call(
        sum_kernel,
        out_shape=jax.ShapeDtypeStruct((machs, *half), bf16),
        in_specs=[VMEM, VMEM],
        out_specs=VMEM,
        compiler_params=params,
        cost_estimate=cost(10**6, 2**20),
        name="pair_sum",
    )(keep, got)
    got = lax.all_to_all(
        send.reshape(machs * panels // 2, struct_rows, width), ("mach", "panel"),
        split_axis=0, concat_axis=0, tiled=True,
        axis_index_groups=[
            [
                mach * panels + 2 * chip + (parity(2 * chip) ^ which)
                for mach in range(machs)
                for chip in range(panels // 2)
            ]
            for which in range(2)
        ],
    )
    struct_adjoint = pl.pallas_call(
        functools.partial(inverse_kernel, rhs),
        out_shape=jax.ShapeDtypeStruct((struct_rows, width), f32),
        in_specs=[VMEM] * 2,
        out_specs=VMEM,
        compiler_params=params,
        cost_estimate=cost(10**9, 2**20),
        name="struct_solve",
    )(got, struct_inverse)
    return (
        loads.reshape(1, block_count, rhs, width),
        struct_adjoint.reshape(struct_count, rhs, width),
    )


def solution(mesh):
    in_specs = (
        P("mach", "panel", None, None),
        P("mach", "panel", None, None, None),
        P("panel", None),
        P("mach", None),
        P("panel", None, None, None),
        P("panel", None),
        P("panel", None),
        P("panel", None, None),
    )
    out_specs = (P("mach", "panel", None, None), P("panel", None, None))
    return jax.shard_map(
        on_device, mesh=mesh, in_specs=in_specs, out_specs=out_specs, check_vma=False
    )
```

time: 26.4 us -> 25.1 us (0.951)
  Pallas kernels: 3.66 us -> 3.03 us
  blocking collectives: 12.6 us -> 12.1 us
  local copies, waits for them, and re-layouts: 0.31 us -> 0.04 us
    pallas_call x4, Pallas kernels: 2.88 us -> 2.25 us  [the longest x1 1.54 us: on_device(): pl.pallas_call(functools.partial(spline_kernel, rhs), out_shape=(jax.Shap...]
    all_to_all x1, blocking collectives: 12.6 us -> 12.1 us  [on_device(): lax.all_to_all(send.reshape(machs * panels // 2, struct_rows, width), ('m...]
    unnamed x16, local copies, waits for them, and re-layouts: 0.31 us -> 0.04 us
  transfers between devices with their start and end apart: 4 -> 4, of which waited for: 2 -> 2; matrix products, arithmetic and copies ran while one was open for 0% -> 0% of each run, Pallas kernels for 1% -> 3%
where the time goes in v8:
time: 25.1 us; the launch traced here: 24.9 us
  blocking collectives  12.1 us (48%)
  starting transfers between devices  5.81 us (23%)
  waiting for transfers between devices  3.15 us (13%)
  Pallas kernels  3.03 us (12%)
  between operations  0.76 us (3%)
    all_to_all x1, blocking collectives, on_device(): lax.all_to_all(send.reshape(machs * panels // 2, struct_rows, width), ('m...  12.1 us
    ppermute x3, starting transfers between devices, swap(): return lax.ppermute(value, 'panel', [(i, i ^ apart) for i in range(panels)])  4.32 us
    ppermute x1, waiting for transfers between devices, on_device(): lax.ppermute(own, ('mach', 'panel'), [(mach * panels + i, (mach ^ (i in b...  1.91 us
    pallas_call x1, Pallas kernels, on_device(): pl.pallas_call(functools.partial(spline_kernel, rhs), out_shape=(jax.Shap...  1.54 us
    ppermute x1, starting transfers between devices, on_device(): lax.ppermute(own, ('mach', 'panel'), [(mach * panels + i, (mach ^ (i in b...  1.49 us
    ppermute x3, waiting for transfers between devices, swap(): return lax.ppermute(value, 'panel', [(i, i ^ apart) for i in range(panels)])  1.25 us
    pallas_call x1, Pallas kernels, on_device(): pl.pallas_call(functools.partial(inverse_kernel, rhs), out_shape=jax.Shap...  0.77 us
  transfers between devices with their start and end apart: 4, of which 2 were waited for; matrix products, arithmetic and copies ran while one was open for 0% of the time, Pallas kernels for 3%

profile of v8, /device:TPU:0, one launch (start us, length us, event | category | flops | bytes accessed | tf_op | source)
XLA Modules:
  0.0 24.9 jit_solution(16656623447037987727)
XLA Ops:
  0.6 0.0 copy-start.2
  0.6 0.0 copy-start.3
  0.7 0.0 copy-start.4
  0.7 0.0 copy-start.5
  0.7 0.0 copy-start.6
  0.7 0.0 copy-start
  0.7 4.1 %collective-permute-start.2 = (bf16[32,128]{1,0:T(8,128)(2,1)}, bf16[32,128]{1,0:T(8,128)(2,1)S(1)}, u32[]{:S(2)}, u32[]{:S(2)}) collective-permute-start(bf16[32,128]{1,0:T(8,128)(2,1)} %bitcast.8), channel_id=1, source_target_pairs={{0,8},{1,9},{2,10},{3,11},{4,12},{5,13},{6,14},{7,15},{8,0},{9,1},... | collective-permute-start | bytes 24584 | tf_op jit(solution)/shard_map/ppermute | solution.py:169
  4.8 1.5 %collective-permute-start.1 = (bf16[32,128]{1,0:T(8,128)(2,1)}, bf16[32,128]{1,0:T(8,128)(2,1)S(1)}, u32[]{:S(2)}, u32[]{:S(2)}) collective-permute-start(bf16[32,128]{1,0:T(8,128)(2,1)} %bitcast.9), channel_id=1, source_target_pairs={{0,16},{1,2},{2,1},{3,4},{4,3},{5,6},{6,5},{7,8},{8,7},{9,10},{10,... | collective-permute-start | bytes 24584 | tf_op jit(solution)/shard_map/ppermute | solution.py:190
  6.3 0.1 collective-permute-start
  6.4 0.0 copy-done.2
  6.4 0.0 copy-done.3
  6.5 0.0 copy-done.4
  6.5 0.0 copy-done.5
  6.5 0.0 copy-done.6
  6.5 0.0 copy-start.1
  6.5 0.2 pick_rows.1
  6.7 1.9 %collective-permute-done.1.cross_ref = bf16[32,128]{1,0:T(8,128)(2,1)S(1)} collective-permute-done((bf16[32,128]{1,0:T(8,128)(2,1)}, bf16[32,128]{1,0:T(8,128)(2,1)S(1)}, u32[]{:S(2)}, u32[]{:S(2)}) %collective-permute-start.1) | collective-permute-done | bytes 8224 | tf_op jit(solution)/shard_map/ppermute | solution.py:190
  8.7 0.0 collective-permute-done.pair_ref
  8.7 0.0 copy-done
  8.7 0.5 %near_field.1.part_ref = f32[32,128]{1,0:T(8,128)S(1)} custom-call(bf16[192,128]{1,0:T(8,128)(2,1)S(1)} %get-tuple-element.10.hot_ref, bf16[32,128]{1,0:T(8,128)(2,1)S(1)} %get-tuple-element.11.own_ref, bf16[32,128]{1,0:T(8,128)(2,1)S(1)} %collective-permute-done.pair_ref, bf16[32,128]{1,0:T(8,128)(2,1)S(1)} %collective-permute-done.1.cross_ref, ...), custom_call_target="tpu_custom_call" | custom-call | flops 1000000 | bytes 131072 | tf_op jit(solution)/shard_map/near_field/pallas_call | solution.py:224
  9.1 0.0 collective-permute-done.2.mirror_ref
  9.1 0.0 copy-done.1
  9.1 0.0 copy-start.7
  9.1 1.5 %spline_loads.1 = (f32[32,128]{1,0:T(8,128)}, f32[8,32,128]{2,1,0:T(8,128)S(1)}, bf16[8,32,128]{2,1,0:T(8,128)(2,1)S(1)}) custom-call(s32[8,6]{1,0:T(8,128)S(1)} %get-tuple-element.9.code_ref, f32[32,128]{1,0:T(8,128)S(1)} %near_field.1.part_ref, bf16[32,128]{1,0:T(8,128)(2,1)S(1)} %collective-permute-done.2.mirror_ref, ...), custom_call_target="tpu_custom_call" | custom-call | flops 1000000 | bytes 131072 | tf_op jit(solution)/shard_map/spline_loads/pallas_call | solution.py:234
  10.7 0.1 collective-permute-start.3
  10.8 1.2 %collective-permute-done.3.got_ref = bf16[8,32,128]{2,1,0:T(8,128)(2,1)S(1)} collective-permute-done((bf16[8,32,128]{2,1,0:T(8,128)(2,1)S(1)}, bf16[8,32,128]{2,1,0:T(8,128)(2,1)S(1)}, u32[]{:S(2)}, u32[]{:S(2)}) %collective-permute-start.3) | collective-permute-done | bytes 65568 | tf_op jit(solution)/shard_map/ppermute | solution.py:169
  12.0 12.1 %all_to_all.5.got_ref = bf16[16,32,128]{2,1,0:T(8,128)(2,1)S(1)} all-to-all(bf16[16,32,128]{2,1,0:T(8,128)(2,1)S(1)} %bitcast.7), channel_id=1, replica_groups={{0,3,5,6,9,10,12,15,16,19,21,22,25,26,28,31},{1,2,4,7,8,11,13,14,17,18,..., dimensions={0} | all-to-all | bytes 262144 | tf_op jit(solution)/shard_map/all_to_all | solution.py:262
  24.1 0.0 copy-done.7
  24.1 0.8 %struct_solve.1 = f32[32,128]{1,0:T(8,128)} custom-call(bf16[16,32,128]{2,1,0:T(8,128)(2,1)S(1)} %all_to_all.5.got_ref, bf16[8,128,128]{2,1,0:T(8,128)(2,1)S(1)} %copy-done.7), custom_call_target="tpu_custom_call" | custom-call | flops 1000000000 | bytes 1048576 | tf_op jit(solution)/shard_map/struct_solve/pallas_call | solution.py:274
  (2 shorter events, 0.0 us)
Async XLA Ops:
  0.6 5.8 %copy-start.2 = (bf16[1,8,4,128]{3,2,1,0:T(4,128)(2,1)S(1)}, bf16[1,8,4,128]{3,2,1,0:T(4,128)(2,1)}, u32[]{:S(2)}) copy-start(bf16[1,8,4,128]{3,2,1,0:T(4,128)(2,1)} %param.8) | copy-start | bytes 24580
  0.6 5.8 %copy-start.3 = (s32[8,8]{1,0:T(8,128)S(1)}, s32[8,8]{1,0:T(8,128)}, u32[]{:S(2)}) copy-start(s32[8,8]{1,0:T(8,128)} %pattern_ref.1) | copy-start | bytes 772
  0.7 5.8 %copy-start.4 = (s32[8,6]{1,0:T(8,128)S(1)}, s32[8,6]{1,0:T(8,128)}, u32[]{:S(2)}) copy-start(s32[8,6]{1,0:T(8,128)} %owner_ref.1) | copy-start | bytes 580
  0.7 5.8 %copy-start.5 = (s32[8,6]{1,0:T(8,128)S(1)}, s32[8,6]{1,0:T(8,128)}, u32[]{:S(2)}) copy-start(s32[8,6]{1,0:T(8,128)} %local_ref.1) | copy-start | bytes 580
  0.7 5.8 %copy-start.6 = (s32[1,4]{1,0:T(1,128)S(1)}, s32[1,4]{1,0:T(1,128)}, u32[]{:S(2)}) copy-start(s32[1,4]{1,0:T(1,128)} %trim_ref.1) | copy-start | bytes 52
  0.7 8.0 %copy-start = (bf16[1,8,8,128,128]{4,3,2,1,0:T(8,128)(2,1)S(1)}, bf16[1,8,8,128,128]{4,3,2,1,0:T(8,128)(2,1)}, u32[]{:S(2)}) copy-start(bf16[1,8,8,128,128]{4,3,2,1,0:T(8,128)(2,1)} %param.9) | copy-start | bytes 6291460
  0.7 8.4 %collective-permute-start.2 = (bf16[32,128]{1,0:T(8,128)(2,1)}, bf16[32,128]{1,0:T(8,128)(2,1)S(1)}, u32[]{:S(2)}, u32[]{:S(2)}) collective-permute-start(bf16[32,128]{1,0:T(8,128)(2,1)} %bitcast.8), channel_id=1, source_target_pairs={{0,8},{1,9},{2,10},{3,11},{4,12},{5,13},{6,14},{7,15},{8,0},{9,1},... | collective-permute-start | bytes 24584 | tf_op jit(solution)/shard_map/ppermute | solution.py:169
  4.8 3.9 %collective-permute-start.1 = (bf16[32,128]{1,0:T(8,128)(2,1)}, bf16[32,128]{1,0:T(8,128)(2,1)S(1)}, u32[]{:S(2)}, u32[]{:S(2)}) collective-permute-start(bf16[32,128]{1,0:T(8,128)(2,1)} %bitcast.9), channel_id=1, source_target_pairs={{0,16},{1,2},{2,1},{3,4},{4,3},{5,6},{6,5},{7,8},{8,7},{9,10},{10,... | collective-permute-start | bytes 24584 | tf_op jit(solution)/shard_map/ppermute | solution.py:190
  6.3 2.4 %collective-permute-start = (bf16[32,128]{1,0:T(8,128)(2,1)}, bf16[32,128]{1,0:T(8,128)(2,1)S(1)}, u32[]{:S(2)}, u32[]{:S(2)}) collective-permute-start(bf16[32,128]{1,0:T(8,128)(2,1)} %bitcast.10), channel_id=1, source_target_pairs={{0,1},{1,0},{2,3},{3,2},{4,5},{5,4},{6,7},{7,6},{8,9},{9,8},{10,11... | collective-permute-start | bytes 24584 | tf_op jit(solution)/shard_map/ppermute | solution.py:169
  6.5 2.6 %copy-start.1 = (bf16[8,6,128,128]{3,2,1,0:T(8,128)(2,1)S(1)}, bf16[8,6,128,128]{3,2,1,0:T(8,128)(2,1)}, u32[]{:S(2)}) copy-start(bf16[8,6,128,128]{3,2,1,0:T(8,128)(2,1)} %spline_ref.1) | copy-start | bytes 4718596
  9.1 15.0 %copy-start.7 = (bf16[8,128,128]{2,1,0:T(8,128)(2,1)S(1)}, bf16[8,128,128]{2,1,0:T(8,128)(2,1)}, u32[]{:S(2)}) copy-start(bf16[8,128,128]{2,1,0:T(8,128)(2,1)} %inverse_ref.1) | copy-start | bytes 786436
  10.7 1.3 %collective-permute-start.3 = (bf16[8,32,128]{2,1,0:T(8,128)(2,1)S(1)}, bf16[8,32,128]{2,1,0:T(8,128)(2,1)S(1)}, u32[]{:S(2)}, u32[]{:S(2)}) collective-permute-start(bf16[8,32,128]{2,1,0:T(8,128)(2,1)S(1)} %get-tuple-element.15), channel_id=1, source_target_pairs={{0,1},{1,0},{2,3},{3,2},{4,5},{5,4},{6,7},{7,6},{8,9},{9,8},{10,11... | collective-permute-start | bytes 196616 | tf_op jit(solution)/shard_map/ppermute | solution.py:169

commit v9 on v8

--- a/solution.py
+++ b/solution.py
@@ -13,10 +13,8 @@
 TILE = 8
 
 
-def parity(index):
-    for shift in (16, 8, 4, 2, 1):
-        index = index ^ (index >> shift)
-    return index & 1
+def device_class(index):
+    return (index ^ (index >> 1) ^ (index >> 2)) & 1
 
 
 def spread_kernel(rhs, expand_ref):
@@ -59,7 +57,7 @@
     held_ref[...] = own_ref[...]
     owner = owner_ref[...]
     code_ref[...] = (
-        (parity(owner) ^ parity(here)) * (panels // 2) + owner // 2
+        (device_class(owner) ^ device_class(here)) * (panels // 2) + ((owner ^ here) >> 1)
     ) * struct_count + local_ref[...]
 
 
@@ -97,20 +95,21 @@
 
 
 def spline_kernel(
-    rhs, code_ref, part_ref, mirror_ref, gate_ref, near_ref, spline_ref,
-    loads_hbm, keep_ref, send_ref, loads_ref, acc, sem,
+    rhs, code_vmem, part_ref, mirror_ref, gate_ref, near_ref, spline_ref,
+    loads_ref, keep_ref, send_ref, code_ref, acc, sem,
 ):
+    copy = pltpu.make_async_copy(code_vmem, code_ref, sem)
+    copy.start()
     block_count, splines = code_ref.shape
     rows, width = part_ref.shape
     for g in range(rows // PACK):
         group = slice(g * PACK, (g + 1) * PACK)
         far = grouped_product(rhs, mirror_ref[group], lambda i: near_ref[i, 1], g)
         loads_ref[group] = gate_ref[...] * (part_ref[group] + far)
-    copy = pltpu.make_async_copy(loads_ref, loads_hbm, sem)
-    copy.start()
     acc[...] = jnp.zeros(acc.shape, jnp.float32)
     upper = lax.broadcasted_iota(jnp.int32, (TILE, width), 0) // rhs
     blank = jnp.zeros((TILE, width), jnp.float32)
+    copy.wait()
     for pair in range(0, block_count, 2):
         both = loads_ref[pair * rhs : (pair + 2) * rhs]
         turned = pltpu.roll(both, rhs, 0)
@@ -143,30 +142,51 @@
     tiles = acc.shape[0] // 2
     keep_ref[...] = acc[:tiles].reshape(keep_ref.shape)
     send_ref[...] = acc[tiles:].reshape(send_ref.shape).astype(send_ref.dtype)
-    copy.wait()
-
-
-def sum_kernel(held_ref, got_ref, out_ref):
-    for place in range(held_ref.shape[0]):
-        total = held_ref[place] + got_ref[place].astype(jnp.float32)
-        for copy in range(out_ref.shape[0]):
-            out_ref[copy, place] = total.astype(out_ref.dtype)
-
-
-def inverse_kernel(rhs, got_ref, inverse_ref, out_ref):
-    sources = [got_ref[index].astype(jnp.float32) for index in range(got_ref.shape[0])]
-    while len(sources) > 1:
-        sources = [a + b for a, b in zip(sources[::2], sources[1::2])] + sources[len(sources) & ~1 :]
-    total = sources[0]
-    rounded = total.astype(jnp.bfloat16)
-    for g in range(total.shape[0] // PACK):
+
+
+def split_kernel(held_ref, got_ref, *out_refs):
+    size = out_refs[0].shape[0]
+    for step, out_ref in enumerate(out_refs):
+        for place in range(size):
+            total = held_ref[step * size + place] + got_ref[step * size + place].astype(jnp.float32)
+            out_ref[place] = total.astype(out_ref.dtype)
+
+
+def column_kernel(machs, held_ref, *refs):
+    got_refs, out_refs = refs[: -2 * machs], refs[-2 * machs :]
+    for place in range(2):
+        total = held_ref[place]
+        for got_ref in got_refs:
+            total = total + got_ref[place].astype(jnp.float32)
+        for out_ref in out_refs[place * machs : (place + 1) * machs]:
+            out_ref[...] = total
+
+
+def inverse_kernel(rhs, machs, loads_ref, *refs):
+    other_refs, same_refs = refs[: 2 * machs : 2], refs[1 : 2 * machs : 2]
+    inverse_ref, loads_hbm, out_ref, sem = refs[2 * machs :]
+    copy = pltpu.make_async_copy(loads_ref, loads_hbm, sem)
+    copy.start()
+    parts = [same[...] + other[...] for same, other in zip(same_refs, other_refs)]
+    rounded = sum(parts[1:], parts[0]).astype(jnp.bfloat16)
+    for g in range(rounded.shape[0] // PACK):
         out_ref[g * PACK : (g + 1) * PACK] = grouped_product(
             rhs, rounded[g * PACK : (g + 1) * PACK], lambda t: inverse_ref[t], g
         )
+    copy.wait()
 
 
 def swap(value, panels, apart):
     return lax.ppermute(value, "panel", [(i, i ^ apart) for i in range(panels)])
+
+
+def mach_swap(value, machs, panels, turn, apart):
+    pairs = [
+        (mach * panels + i, (mach + turn) % machs * panels + (i ^ apart))
+        for mach in range(machs)
+        for i in range(panels)
+    ]
+    return lax.ppermute(value, ("mach", "panel"), pairs)
 
 
 def cost(flops, size):
@@ -185,7 +205,6 @@
     params = pltpu.CompilerParams(vmem_limit_bytes=16 * 1024 * 1024)
     f32, bf16 = jnp.float32, jnp.bfloat16
     own = adjoint.reshape(rows, width)
-    mirror = swap(own, panels, panels // 2)
     beside = {0: 0, panels - 1: panels - 1}
     cross = lax.ppermute(
         own, ("mach", "panel"),
@@ -198,6 +217,7 @@
             for i in range(panels)
         ],
     )
+    mirror = swap(own, panels, panels // 2)
     pair = swap(own, panels, 1)
     expand = pl.pallas_call(
         functools.partial(spread_kernel, rhs),
@@ -238,10 +258,10 @@
             jax.ShapeDtypeStruct(half, f32),
             jax.ShapeDtypeStruct(half, bf16),
         ),
-        in_specs=[SMEM] + [VMEM] * 5,
-        out_specs=(pl.BlockSpec(memory_space=pl.ANY), VMEM, VMEM),
+        in_specs=[VMEM] * 6,
+        out_specs=(VMEM,) * 3,
         scratch_shapes=[
-            pltpu.VMEM((rows, width), f32),
+            pltpu.SMEM(spline_owner.shape, jnp.int32),
             pltpu.VMEM((panels * struct_rows // TILE, TILE, width), f32),
             pltpu.SemaphoreType.DMA,
         ],
@@ -250,36 +270,51 @@
         name="spline_loads",
     )(code, part, mirror, gate, near_blocks[0], spline_blocks)
     got = swap(send, panels, 1)
-    send = pl.pallas_call(
-        sum_kernel,
-        out_shape=jax.ShapeDtypeStruct((machs, *half), bf16),
+    steps = panels // 4
+    two = (2, struct_rows, width)
+    keep, *sends = pl.pallas_call(
+        split_kernel,
+        out_shape=tuple(
+            jax.ShapeDtypeStruct(two, f32 if step == 0 else bf16) for step in range(steps)
+        ),
         in_specs=[VMEM, VMEM],
-        out_specs=VMEM,
-        compiler_params=params,
-        cost_estimate=cost(10**6, 2**20),
+        out_specs=(VMEM,) * steps,
+        compiler_params=params,
+        cost_estimate=cost(10**6, 2**17),
         name="pair_sum",
     )(keep, got)
-    got = lax.all_to_all(
-        send.reshape(machs * panels // 2, struct_rows, width), ("mach", "panel"),
-        split_axis=0, concat_axis=0, tiled=True,
-        axis_index_groups=[
-            [
-                mach * panels + 2 * chip + (parity(2 * chip) ^ which)
-                for mach in range(machs)
-                for chip in range(panels // 2)
-            ]
-            for which in range(2)
-        ],
-    )
-    struct_adjoint = pl.pallas_call(
-        functools.partial(inverse_kernel, rhs),
-        out_shape=jax.ShapeDtypeStruct((struct_rows, width), f32),
-        in_specs=[VMEM] * 2,
-        out_specs=VMEM,
-        compiler_params=params,
-        cost_estimate=cost(10**9, 2**20),
+    got = [
+        swap(sends[step - 1], panels, 4 * step + step % 2) for step in range(steps - 1, 0, -1)
+    ]
+    one = jax.ShapeDtypeStruct((struct_rows, width), f32)
+    columns = pl.pallas_call(
+        functools.partial(column_kernel, machs),
+        out_shape=(one,) * (2 * machs),
+        in_specs=[VMEM] * steps,
+        out_specs=(VMEM,) * (2 * machs),
+        compiler_params=params,
+        cost_estimate=cost(10**6, 2**17),
+        name="column_sum",
+    )(keep, *got)
+    sames = [
+        mach_swap(columns[turn], machs, panels, turn, 0) if turn else columns[0]
+        for turn in range(machs)
+    ]
+    others = [mach_swap(columns[machs + turn], machs, panels, turn, 3) for turn in range(machs)]
+    loads, struct_adjoint = pl.pallas_call(
+        functools.partial(inverse_kernel, rhs, machs),
+        out_shape=(jax.ShapeDtypeStruct((rows, width), f32), one),
+        in_specs=[VMEM] * (2 * machs + 2),
+        out_specs=(pl.BlockSpec(memory_space=pl.ANY), VMEM),
+        scratch_shapes=[pltpu.SemaphoreType.DMA],
+        compiler_params=params,
+        cost_estimate=cost(10**6, 2**17),
         name="struct_solve",
-    )(got, struct_inverse)
+    )(
+        loads,
+        *(value for turn in range(machs - 1, -1, -1) for value in (others[turn], sames[turn])),
+        struct_inverse,
+    )
     return (
         loads.reshape(1, block_count, rhs, width),
         struct_adjoint.reshape(struct_count, rhs, width),

time: 25.1 us -> 24.9 us (level)
  blocking collectives: 12.1 us -> 0 us
  starting transfers between devices: 5.81 us -> 12.7 us
  waiting for transfers between devices: 3.15 us -> 8.25 us
    all_to_all x1 -> x0, blocking collectives: 12.1 us -> none  [on_device(): lax.all_to_all(send.reshape(machs * panels // 2, struct_rows, width), ('m...]
    ppermute x3 -> x6, starting transfers between devices: 4.32 us -> 8.21 us  [swap(): return lax.ppermute(value, 'panel', [(i, i ^ apart) for i in range(panels)])]
    ppermute x0 -> x3, starting transfers between devices: none -> 3.03 us  [mach_swap(): return lax.ppermute(value, ('mach', 'panel'), pairs)]
    ppermute x3 -> x6, waiting for transfers between devices: 1.25 us -> 3.85 us  [swap(): return lax.ppermute(value, 'panel', [(i, i ^ apart) for i in range(panels)])]
    ppermute x0 -> x3, waiting for transfers between devices: none -> 2.49 us  [mach_swap(): return lax.ppermute(value, ('mach', 'panel'), pairs)]
    pallas_call x1, Pallas kernels: 1.54 us -> 0.96 us  [on_device(): pl.pallas_call(functools.partial(spline_kernel, rhs), out_shape=(jax.Shap...]
    pallas_call x2 -> x3, Pallas kernels: 0.79 us -> 1.28 us  [the longest x1 1.25 us: on_device(): pl.pallas_call(functools.partial(inverse_kernel, rhs, machs), out_shape=(...]
  transfers between devices with their start and end apart: 4 -> 10, of which waited for: 2 -> 7; matrix products, arithmetic and copies ran while one was open for 0% -> 0% of each run, Pallas kernels for 3% -> 3%
where the time goes in v9:
time: 24.9 us; the launch traced here: 24.7 us
  starting transfers between devices  12.7 us (51%)
  waiting for transfers between devices  8.25 us (33%)
  Pallas kernels  2.95 us (12%)
  between operations  0.77 us (3%)
    ppermute x6, starting transfers between devices, swap(): return lax.ppermute(value, 'panel', [(i, i ^ apart) for i in range(panels)])  8.21 us
    ppermute x6, waiting for transfers between devices, swap(): return lax.ppermute(value, 'panel', [(i, i ^ apart) for i in range(panels)])  3.85 us
    ppermute x3, starting transfers between devices, mach_swap(): return lax.ppermute(value, ('mach', 'panel'), pairs)  3.03 us
    ppermute x3, waiting for transfers between devices, mach_swap(): return lax.ppermute(value, ('mach', 'panel'), pairs)  2.49 us
    ppermute x1, waiting for transfers between devices, on_device(): lax.ppermute(own, ('mach', 'panel'), [(mach * panels + i, (mach ^ (i in b...  1.9 us
    ppermute x1, starting transfers between devices, on_device(): lax.ppermute(own, ('mach', 'panel'), [(mach * panels + i, (mach ^ (i in b...  1.49 us
    pallas_call x1, Pallas kernels, on_device(): pl.pallas_call(functools.partial(inverse_kernel, rhs, machs), out_shape=(...  1.25 us
    pallas_call x1, Pallas kernels, on_device(): pl.pallas_call(functools.partial(spline_kernel, rhs), out_shape=(jax.Shap...  0.96 us
  transfers between devices with their start and end apart: 10, of which 7 were waited for; matrix products, arithmetic and copies ran while one was open for 0% of the time, Pallas kernels for 3%

profile of v9, /device:TPU:0, one launch (start us, length us, event | category | flops | bytes accessed | tf_op | source)
XLA Modules:
  0.0 24.7 jit_solution(6700305551036940263)
XLA Ops:
  0.6 0.0 copy-start.3
  0.6 0.0 copy-start.4
  0.7 4.1 %collective-permute-start.2 = (bf16[32,128]{1,0:T(8,128)(2,1)}, bf16[32,128]{1,0:T(8,128)(2,1)S(1)}, u32[]{:S(2)}, u32[]{:S(2)}) collective-permute-start(bf16[32,128]{1,0:T(8,128)(2,1)} %bitcast.6), channel_id=1, source_target_pairs={{0,8},{1,9},{2,10},{3,11},{4,12},{5,13},{6,14},{7,15},{8,0},{9,1},... | collective-permute-start | bytes 24584 | tf_op jit(solution)/shard_map/ppermute | solution.py:180
  4.8 1.5 %collective-permute-start.1 = (bf16[32,128]{1,0:T(8,128)(2,1)}, bf16[32,128]{1,0:T(8,128)(2,1)S(1)}, u32[]{:S(2)}, u32[]{:S(2)}) collective-permute-start(bf16[32,128]{1,0:T(8,128)(2,1)} %bitcast.7), channel_id=1, source_target_pairs={{0,16},{1,2},{2,1},{3,4},{4,3},{5,6},{6,5},{7,8},{8,7},{9,10},{10,... | collective-permute-start | bytes 24584 | tf_op jit(solution)/shard_map/ppermute | solution.py:209
  6.3 0.1 collective-permute-start
  6.4 0.0 copy-done.4
  6.5 0.0 copy-done.5
  6.5 0.0 copy-done.6
  6.5 0.0 copy-done.7
  6.5 0.0 copy-start.1
  6.5 0.2 %pick_rows.1 = (bf16[192,128]{1,0:T(8,128)(2,1)S(1)}, f32[16,128]{1,0:T(8,128)S(1)}, bf16[32,128]{1,0:T(8,128)(2,1)S(1)}, s32[8,6]{1,0:T(8,128)S(1)}) custom-call(bf16[32,8]{1,0:T(8,128)(2,1)S(1)} %row_order.1.expand_ref, s32[8,8]{1,0:T(8,128)S(1)} %copy-done.4, s32[1,4]{1,0:T(1,128)S(1)} %copy-done.7, bf16[32,128]{1,0:T(8,128)(2,1)S(1)} %bitcast.9, ...), custom_call_target="tpu_custom_call" | custom-call | flops 1000000 | bytes 131072 | tf_op jit(solution)/shard_map/pick_rows/pallas_call | solution.py:230
  6.8 1.9 %collective-permute-done.1.cross_ref = bf16[32,128]{1,0:T(8,128)(2,1)S(1)} collective-permute-done((bf16[32,128]{1,0:T(8,128)(2,1)}, bf16[32,128]{1,0:T(8,128)(2,1)S(1)}, u32[]{:S(2)}, u32[]{:S(2)}) %collective-permute-start.1) | collective-permute-done | bytes 8224 | tf_op jit(solution)/shard_map/ppermute | solution.py:209
  8.7 0.0 collective-permute-done.pair_ref
  8.7 0.5 %near_field.1.part_ref = f32[32,128]{1,0:T(8,128)S(1)} custom-call(bf16[192,128]{1,0:T(8,128)(2,1)S(1)} %get-tuple-element.20.hot_ref, bf16[32,128]{1,0:T(8,128)(2,1)S(1)} %get-tuple-element.21.own_ref, bf16[32,128]{1,0:T(8,128)(2,1)S(1)} %collective-permute-done.pair_ref, bf16[32,128]{1,0:T(8,128)(2,1)S(1)} %collective-permute-done.1.cross_ref, ...), custom_call_target="tpu_custom_call" | custom-call | flops 1000000 | bytes 131072 | tf_op jit(solution)/shard_map/near_field/pallas_call | solution.py:244
  9.1 0.0 collective-permute-done.2.mirror_ref
  9.1 0.0 copy-done.1
  9.1 1.0 %spline_loads.1 = (f32[32,128]{1,0:T(8,128)S(1)}, f32[8,32,128]{2,1,0:T(8,128)S(1)}, bf16[8,32,128]{2,1,0:T(8,128)(2,1)S(1)}) custom-call(s32[8,6]{1,0:T(8,128)S(1)} %get-tuple-element.19.code_vmem, f32[32,128]{1,0:T(8,128)S(1)} %near_field.1.part_ref, bf16[32,128]{1,0:T(8,128)(2,1)S(1)} %collective-permute-done.2.mirror_ref, ...), custom_call_target="tpu_custom_call" | custom-call | flops 1000000 | bytes 131072 | tf_op jit(solution)/shard_map/spline_loads/pallas_call | solution.py:254
  10.1 0.1 collective-permute-start.3
  10.2 1.2 %collective-permute-done.3.got_ref = bf16[8,32,128]{2,1,0:T(8,128)(2,1)S(1)} collective-permute-done((bf16[8,32,128]{2,1,0:T(8,128)(2,1)S(1)}, bf16[8,32,128]{2,1,0:T(8,128)(2,1)S(1)}, u32[]{:S(2)}, u32[]{:S(2)}) %collective-permute-start.3) | collective-permute-done | bytes 65568 | tf_op jit(solution)/shard_map/ppermute | solution.py:180
  11.4 1.5 %collective-permute-start.4 = (bf16[2,32,128]{2,1,0:T(8,128)(2,1)S(1)}, bf16[2,32,128]{2,1,0:T(8,128)(2,1)S(1)}, u32[]{:S(2)}, u32[]{:S(2)}) collective-permute-start(bf16[2,32,128]{2,1,0:T(8,128)(2,1)S(1)} %get-tuple-element.27), channel_id=1, source_target_pairs={{0,13},{1,12},{2,15},{3,14},{4,9},{5,8},{6,11},{7,10},{8,5},{9,4},... | collective-permute-start | bytes 49160 | tf_op jit(solution)/shard_map/ppermute | solution.py:180
  13.0 1.7 %collective-permute-start.5 = (bf16[2,32,128]{2,1,0:T(8,128)(2,1)S(1)}, bf16[2,32,128]{2,1,0:T(8,128)(2,1)S(1)}, u32[]{:S(2)}, u32[]{:S(2)}) collective-permute-start(bf16[2,32,128]{2,1,0:T(8,128)(2,1)S(1)} %get-tuple-element.28), channel_id=1, source_target_pairs={{0,8},{1,9},{2,10},{3,11},{4,12},{5,13},{6,14},{7,15},{8,0},{9,1},... | collective-permute-start | bytes 49160 | tf_op jit(solution)/shard_map/ppermute | solution.py:180
  14.6 0.7 %collective-permute-start.6 = (bf16[2,32,128]{2,1,0:T(8,128)(2,1)S(1)}, bf16[2,32,128]{2,1,0:T(8,128)(2,1)S(1)}, u32[]{:S(2)}, u32[]{:S(2)}) collective-permute-start(bf16[2,32,128]{2,1,0:T(8,128)(2,1)S(1)} %get-tuple-element.29), channel_id=1, source_target_pairs={{0,5},{1,4},{2,7},{3,6},{4,1},{5,0},{6,3},{7,2},{8,13},{9,12},{10,... | collective-permute-start | bytes 49160 | tf_op jit(solution)/shard_map/ppermute | solution.py:180
  15.3 1.2 %collective-permute-done.4.refs_0_ = bf16[2,32,128]{2,1,0:T(8,128)(2,1)S(1)} collective-permute-done((bf16[2,32,128]{2,1,0:T(8,128)(2,1)S(1)}, bf16[2,32,128]{2,1,0:T(8,128)(2,1)S(1)}, u32[]{:S(2)}, u32[]{:S(2)}) %collective-permute-start.4) | collective-permute-done | bytes 16416 | tf_op jit(solution)/shard_map/ppermute | solution.py:180
  16.5 1.2 %collective-permute-done.5.refs_1_ = bf16[2,32,128]{2,1,0:T(8,128)(2,1)S(1)} collective-permute-done((bf16[2,32,128]{2,1,0:T(8,128)(2,1)S(1)}, bf16[2,32,128]{2,1,0:T(8,128)(2,1)S(1)}, u32[]{:S(2)}, u32[]{:S(2)}) %collective-permute-start.5) | collective-permute-done | bytes 16416 | tf_op jit(solution)/shard_map/ppermute | solution.py:180
  17.7 0.2 collective-permute-done.6.refs_2_
  18.0 1.8 %collective-permute-start.7 = (f32[32,128]{1,0:T(8,128)S(1)}, f32[32,128]{1,0:T(8,128)S(1)}, u32[]{:S(2)}, u32[]{:S(2)}) collective-permute-start(f32[32,128]{1,0:T(8,128)S(1)} %get-tuple-element.30), channel_id=1, source_target_pairs={{0,19},{1,18},{2,17},{3,16},{4,23},{5,22},{6,21},{7,20},{8,27},{9,... | collective-permute-start | bytes 49160 | tf_op jit(solution)/shard_map/ppermute | solution.py:189
  19.7 0.5 %collective-permute-start.8 = (f32[32,128]{1,0:T(8,128)S(1)}, f32[32,128]{1,0:T(8,128)S(1)}, u32[]{:S(2)}, u32[]{:S(2)}) collective-permute-start(f32[32,128]{1,0:T(8,128)S(1)} %get-tuple-element.31), channel_id=1, source_target_pairs={{0,16},{1,17},{2,18},{3,19},{4,20},{5,21},{6,22},{7,23},{8,24},{9,... | collective-permute-start | bytes 49160 | tf_op jit(solution)/shard_map/ppermute | solution.py:189
  20.3 0.7 %collective-permute-start.9 = (f32[32,128]{1,0:T(8,128)S(1)}, f32[32,128]{1,0:T(8,128)S(1)}, u32[]{:S(2)}, u32[]{:S(2)}) collective-permute-start(f32[32,128]{1,0:T(8,128)S(1)} %get-tuple-element.32), channel_id=1, source_target_pairs={{0,3},{1,2},{2,1},{3,0},{4,7},{5,6},{6,5},{7,4},{8,11},{9,10},{10,... | collective-permute-start | bytes 49160 | tf_op jit(solution)/shard_map/ppermute | solution.py:189
  21.0 1.1 %collective-permute-done.7.refs_0_ = f32[32,128]{1,0:T(8,128)S(1)} collective-permute-done((f32[32,128]{1,0:T(8,128)S(1)}, f32[32,128]{1,0:T(8,128)S(1)}, u32[]{:S(2)}, u32[]{:S(2)}) %collective-permute-start.7) | collective-permute-done | bytes 16416 | tf_op jit(solution)/shard_map/ppermute | solution.py:189
  22.1 1.4 %collective-permute-done.8.refs_1_ = f32[32,128]{1,0:T(8,128)S(1)} collective-permute-done((f32[32,128]{1,0:T(8,128)S(1)}, f32[32,128]{1,0:T(8,128)S(1)}, u32[]{:S(2)}, u32[]{:S(2)}) %collective-permute-start.8) | collective-permute-done | bytes 16416 | tf_op jit(solution)/shard_map/ppermute | solution.py:189
  23.5 0.0 collective-permute-done.9.refs_2_
  23.5 1.3 %struct_solve.1 = (f32[32,128]{1,0:T(8,128)}, f32[32,128]{1,0:T(8,128)}) custom-call(f32[32,128]{1,0:T(8,128)S(1)} %get-tuple-element.23.loads_ref, f32[32,128]{1,0:T(8,128)S(1)} %collective-permute-done.7.refs_0_, f32[32,128]{1,0:T(8,128)S(1)} %collective-permute-done.8.refs_1_, f32[32,128]{1,0:T(8,128)S(1)} %collective-permute-done.9.refs_2_, ...), custom_call_target="tpu_custom_call" | custom-call | flops 1000000 | bytes 131072 | tf_op jit(solution)/shard_map/struct_solve/pallas_call | solution.py:304
  (11 shorter events, 0.1 us)
Async XLA Ops:
  0.6 5.8 %copy-start.3 = (bf16[1,8,4,128]{3,2,1,0:T(4,128)(2,1)S(1)}, bf16[1,8,4,128]{3,2,1,0:T(4,128)(2,1)}, u32[]{:S(2)}) copy-start(bf16[1,8,4,128]{3,2,1,0:T(4,128)(2,1)} %param.8) | copy-start | bytes 24580
  0.6 5.8 %copy-start.4 = (s32[8,8]{1,0:T(8,128)S(1)}, s32[8,8]{1,0:T(8,128)}, u32[]{:S(2)}) copy-start(s32[8,8]{1,0:T(8,128)} %pattern_ref.1) | copy-start | bytes 772
  0.7 5.8 %copy-start.5 = (s32[8,6]{1,0:T(8,128)S(1)}, s32[8,6]{1,0:T(8,128)}, u32[]{:S(2)}) copy-start(s32[8,6]{1,0:T(8,128)} %owner_ref.1) | copy-start | bytes 580
  0.7 5.8 %copy-start.6 = (s32[8,6]{1,0:T(8,128)S(1)}, s32[8,6]{1,0:T(8,128)}, u32[]{:S(2)}) copy-start(s32[8,6]{1,0:T(8,128)} %local_ref.1) | copy-start | bytes 580
  0.7 5.8 %copy-start.7 = (s32[1,4]{1,0:T(1,128)S(1)}, s32[1,4]{1,0:T(1,128)}, u32[]{:S(2)}) copy-start(s32[1,4]{1,0:T(1,128)} %trim_ref.1) | copy-start | bytes 52
  0.7 8.0 %copy-start = (bf16[1,8,8,128,128]{4,3,2,1,0:T(8,128)(2,1)S(1)}, bf16[1,8,8,128,128]{4,3,2,1,0:T(8,128)(2,1)}, u32[]{:S(2)}) copy-start(bf16[1,8,8,128,128]{4,3,2,1,0:T(8,128)(2,1)} %param.9) | copy-start | bytes 6291460
  0.7 8.4 %collective-permute-start.2 = (bf16[32,128]{1,0:T(8,128)(2,1)}, bf16[32,128]{1,0:T(8,128)(2,1)S(1)}, u32[]{:S(2)}, u32[]{:S(2)}) collective-permute-start(bf16[32,128]{1,0:T(8,128)(2,1)} %bitcast.6), channel_id=1, source_target_pairs={{0,8},{1,9},{2,10},{3,11},{4,12},{5,13},{6,14},{7,15},{8,0},{9,1},... | collective-permute-start | bytes 24584 | tf_op jit(solution)/shard_map/ppermute | solution.py:180
  4.8 3.9 %collective-permute-start.1 = (bf16[32,128]{1,0:T(8,128)(2,1)}, bf16[32,128]{1,0:T(8,128)(2,1)S(1)}, u32[]{:S(2)}, u32[]{:S(2)}) collective-permute-start(bf16[32,128]{1,0:T(8,128)(2,1)} %bitcast.7), channel_id=1, source_target_pairs={{0,16},{1,2},{2,1},{3,4},{4,3},{5,6},{6,5},{7,8},{8,7},{9,10},{10,... | collective-permute-start | bytes 24584 | tf_op jit(solution)/shard_map/ppermute | solution.py:209
  6.3 2.4 %collective-permute-start = (bf16[32,128]{1,0:T(8,128)(2,1)}, bf16[32,128]{1,0:T(8,128)(2,1)S(1)}, u32[]{:S(2)}, u32[]{:S(2)}) collective-permute-start(bf16[32,128]{1,0:T(8,128)(2,1)} %bitcast.8), channel_id=1, source_target_pairs={{0,1},{1,0},{2,3},{3,2},{4,5},{5,4},{6,7},{7,6},{8,9},{9,8},{10,11... | collective-permute-start | bytes 24584 | tf_op jit(solution)/shard_map/ppermute | solution.py:180
  6.5 2.6 %copy-start.1 = (bf16[8,6,128,128]{3,2,1,0:T(8,128)(2,1)S(1)}, bf16[8,6,128,128]{3,2,1,0:T(8,128)(2,1)}, u32[]{:S(2)}) copy-start(bf16[8,6,128,128]{3,2,1,0:T(8,128)(2,1)} %spline_ref.1) | copy-start | bytes 4718596
  9.1 14.4 %copy-start.2 = (bf16[8,128,128]{2,1,0:T(8,128)(2,1)S(1)}, bf16[8,128,128]{2,1,0:T(8,128)(2,1)}, u32[]{:S(2)}) copy-start(bf16[8,128,128]{2,1,0:T(8,128)(2,1)} %refs_4_.1) | copy-start | bytes 786436
  10.1 1.3 %collective-permute-start.3 = (bf16[8,32,128]{2,1,0:T(8,128)(2,1)S(1)}, bf16[8,32,128]{2,1,0:T(8,128)(2,1)S(1)}, u32[]{:S(2)}, u32[]{:S(2)}) collective-permute-start(bf16[8,32,128]{2,1,0:T(8,128)(2,1)S(1)} %get-tuple-element.25), channel_id=1, source_target_pairs={{0,1},{1,0},{2,3},{3,2},{4,5},{5,4},{6,7},{7,6},{8,9},{9,8},{10,11... | collective-permute-start | bytes 196616 | tf_op jit(solution)/shard_map/ppermute | solution.py:180
  11.4 5.1 %collective-permute-start.4 = (bf16[2,32,128]{2,1,0:T(8,128)(2,1)S(1)}, bf16[2,32,128]{2,1,0:T(8,128)(2,1)S(1)}, u32[]{:S(2)}, u32[]{:S(2)}) collective-permute-start(bf16[2,32,128]{2,1,0:T(8,128)(2,1)S(1)} %get-tuple-element.27), channel_id=1, source_target_pairs={{0,13},{1,12},{2,15},{3,14},{4,9},{5,8},{6,11},{7,10},{8,5},{9,4},... | collective-permute-start | bytes 49160 | tf_op jit(solution)/shard_map/ppermute | solution.py:180
  13.0 4.8 %collective-permute-start.5 = (bf16[2,32,128]{2,1,0:T(8,128)(2,1)S(1)}, bf16[2,32,128]{2,1,0:T(8,128)(2,1)S(1)}, u32[]{:S(2)}, u32[]{:S(2)}) collective-permute-start(bf16[2,32,128]{2,1,0:T(8,128)(2,1)S(1)} %get-tuple-element.28), channel_id=1, source_target_pairs={{0,8},{1,9},{2,10},{3,11},{4,12},{5,13},{6,14},{7,15},{8,0},{9,1},... | collective-permute-start | bytes 49160 | tf_op jit(solution)/shard_map/ppermute | solution.py:180
  14.6 3.3 %collective-permute-start.6 = (bf16[2,32,128]{2,1,0:T(8,128)(2,1)S(1)}, bf16[2,32,128]{2,1,0:T(8,128)(2,1)S(1)}, u32[]{:S(2)}, u32[]{:S(2)}) collective-permute-start(bf16[2,32,128]{2,1,0:T(8,128)(2,1)S(1)} %get-tuple-element.29), channel_id=1, source_target_pairs={{0,5},{1,4},{2,7},{3,6},{4,1},{5,0},{6,3},{7,2},{8,13},{9,12},{10,... | collective-permute-start | bytes 49160 | tf_op jit(solution)/shard_map/ppermute | solution.py:180
  18.0 4.1 %collective-permute-start.7 = (f32[32,128]{1,0:T(8,128)S(1)}, f32[32,128]{1,0:T(8,128)S(1)}, u32[]{:S(2)}, u32[]{:S(2)}) collective-permute-start(f32[32,128]{1,0:T(8,128)S(1)} %get-tuple-element.30), channel_id=1, source_target_pairs={{0,19},{1,18},{2,17},{3,16},{4,23},{5,22},{6,21},{7,20},{8,27},{9,... | collective-permute-start | bytes 49160 | tf_op jit(solution)/shard_map/ppermute | solution.py:189
  19.7 3.7 %collective-permute-start.8 = (f32[32,128]{1,0:T(8,128)S(1)}, f32[32,128]{1,0:T(8,128)S(1)}, u32[]{:S(2)}, u32[]{:S(2)}) collective-permute-start(f32[32,128]{1,0:T(8,128)S(1)} %get-tuple-element.31), channel_id=1, source_target_pairs={{0,16},{1,17},{2,18},{3,19},{4,20},{5,21},{6,22},{7,23},{8,24},{9,... | collective-permute-start | bytes 49160 | tf_op jit(solution)/shard_map/ppermute | solution.py:189
  20.3 3.2 %collective-permute-start.9 = (f32[32,128]{1,0:T(8,128)S(1)}, f32[32,128]{1,0:T(8,128)S(1)}, u32[]{:S(2)}, u32[]{:S(2)}) collective-permute-start(f32[32,128]{1,0:T(8,128)S(1)} %get-tuple-element.32), channel_id=1, source_target_pairs={{0,3},{1,2},{2,1},{3,0},{4,7},{5,6},{6,5},{7,4},{8,11},{9,10},{10,... | collective-permute-start | bytes 49160 | tf_op jit(solution)/shard_map/ppermute | solution.py:189

commit v10 on v9

--- a/solution.py
+++ b/solution.py
@@ -96,7 +96,7 @@
 
 def spline_kernel(
     rhs, code_vmem, part_ref, mirror_ref, gate_ref, near_ref, spline_ref,
-    loads_ref, keep_ref, send_ref, code_ref, acc, sem,
+    sums_ref, keep_ref, send_ref, code_ref, loads_ref, acc, sem,
 ):
     copy = pltpu.make_async_copy(code_vmem, code_ref, sem)
     copy.start()
@@ -105,7 +105,8 @@
     for g in range(rows // PACK):
         group = slice(g * PACK, (g + 1) * PACK)
         far = grouped_product(rhs, mirror_ref[group], lambda i: near_ref[i, 1], g)
-        loads_ref[group] = gate_ref[...] * (part_ref[group] + far)
+        sums_ref[group] = part_ref[group] + far
+        loads_ref[group] = gate_ref[...] * sums_ref[group]
     acc[...] = jnp.zeros(acc.shape, jnp.float32)
     upper = lax.broadcasted_iota(jnp.int32, (TILE, width), 0) // rhs
     blank = jnp.zeros((TILE, width), jnp.float32)
@@ -159,21 +160,21 @@
         for got_ref in got_refs:
             total = total + got_ref[place].astype(jnp.float32)
         for out_ref in out_refs[place * machs : (place + 1) * machs]:
-            out_ref[...] = total
-
-
-def inverse_kernel(rhs, machs, loads_ref, *refs):
+            out_ref[...] = total.astype(out_ref.dtype)
+
+
+def inverse_kernel(rhs, machs, *refs):
     other_refs, same_refs = refs[: 2 * machs : 2], refs[1 : 2 * machs : 2]
-    inverse_ref, loads_hbm, out_ref, sem = refs[2 * machs :]
-    copy = pltpu.make_async_copy(loads_ref, loads_hbm, sem)
-    copy.start()
-    parts = [same[...] + other[...] for same, other in zip(same_refs, other_refs)]
+    inverse_ref, out_ref = refs[2 * machs :]
+    parts = [
+        same[...].astype(jnp.float32) + other[...].astype(jnp.float32)
+        for same, other in zip(same_refs, other_refs)
+    ]
     rounded = sum(parts[1:], parts[0]).astype(jnp.bfloat16)
     for g in range(rounded.shape[0] // PACK):
         out_ref[g * PACK : (g + 1) * PACK] = grouped_product(
             rhs, rounded[g * PACK : (g + 1) * PACK], lambda t: inverse_ref[t], g
         )
-    copy.wait()
 
 
 def swap(value, panels, apart):
@@ -251,7 +252,7 @@
         name="near_field",
     )(hot, held, pair, cross, near_blocks[0])
     half = (panels // 2, struct_rows, width)
-    loads, keep, send = pl.pallas_call(
+    sums, keep, send = pl.pallas_call(
         functools.partial(spline_kernel, rhs),
         out_shape=(
             jax.ShapeDtypeStruct((rows, width), f32),
@@ -262,6 +263,7 @@
         out_specs=(VMEM,) * 3,
         scratch_shapes=[
             pltpu.SMEM(spline_owner.shape, jnp.int32),
+            pltpu.VMEM((rows, width), f32),
             pltpu.VMEM((panels * struct_rows // TILE, TILE, width), f32),
             pltpu.SemaphoreType.DMA,
         ],
@@ -269,6 +271,7 @@
         cost_estimate=cost(10**6, 2**17),
         name="spline_loads",
     )(code, part, mirror, gate, near_blocks[0], spline_blocks)
+    loads = sums.reshape(adjoint.shape) * trim_mask[0].astype(f32)[None, None, :, None]
     got = swap(send, panels, 1)
     steps = panels // 4
     two = (2, struct_rows, width)
@@ -286,7 +289,7 @@
     got = [
         swap(sends[step - 1], panels, 4 * step + step % 2) for step in range(steps - 1, 0, -1)
     ]
-    one = jax.ShapeDtypeStruct((struct_rows, width), f32)
+    one = jax.ShapeDtypeStruct((struct_rows, width), bf16)
     columns = pl.pallas_call(
         functools.partial(column_kernel, machs),
         out_shape=(one,) * (2 * machs),
@@ -301,22 +304,20 @@
         for turn in range(machs)
     ]
     others = [mach_swap(columns[machs + turn], machs, panels, turn, 3) for turn in range(machs)]
-    loads, struct_adjoint = pl.pallas_call(
+    struct_adjoint = pl.pallas_call(
         functools.partial(inverse_kernel, rhs, machs),
-        out_shape=(jax.ShapeDtypeStruct((rows, width), f32), one),
-        in_specs=[VMEM] * (2 * machs + 2),
-        out_specs=(pl.BlockSpec(memory_space=pl.ANY), VMEM),
-        scratch_shapes=[pltpu.SemaphoreType.DMA],
+        out_shape=jax.ShapeDtypeStruct((struct_rows, width), f32),
+        in_specs=[VMEM] * (2 * machs + 1),
+        out_specs=VMEM,
         compiler_params=params,
         cost_estimate=cost(10**6, 2**17),
         name="struct_solve",
     )(
-        loads,
         *(value for turn in range(machs - 1, -1, -1) for value in (others[turn], sames[turn])),
         struct_inverse,
     )
     return (
-        loads.reshape(1, block_count, rhs, width),
+        loads,
         struct_adjoint.reshape(struct_count, rhs, width),
     )
 

time: 24.9 us -> 24.3 us (0.976)
  waiting for transfers between devices: 8.25 us -> 7.47 us
  other arithmetic: 0 us -> 0.68 us
  Pallas kernels: 2.95 us -> 2.46 us
    ppermute x3, waiting for transfers between devices: 2.49 us -> 1.72 us  [mach_swap(): return lax.ppermute(value, ('mach', 'panel'), pairs)]
    mul x0 -> x1, other arithmetic: none -> 0.68 us  [on_device(): sums.reshape(adjoint.shape) * trim_mask[0].astype(f32)[None, None, :, None]]
    pallas_call x1, Pallas kernels: 1.25 us -> 0.76 us  [on_device(): pl.pallas_call(functools.partial(inverse_kernel, rhs, machs), out_shape=j...]
  transfers between devices with their start and end apart: 10 -> 10, of which waited for: 7 -> 7; matrix products, arithmetic and copies ran while one was open for 0% -> 3% of each run, Pallas kernels for 3% -> 3%
where the time goes in v10:
time: 24.3 us; the launch traced here: 24.1 us
  starting transfers between devices  12.7 us (52%)
  waiting for transfers between devices  7.47 us (31%)
  Pallas kernels  2.46 us (10%)
  between operations  0.77 us (3%)
  other arithmetic  0.68 us (3%)
    ppermute x6, starting transfers between devices, swap(): return lax.ppermute(value, 'panel', [(i, i ^ apart) for i in range(panels)])  8.21 us
    ppermute x6, waiting for transfers between devices, swap(): return lax.ppermute(value, 'panel', [(i, i ^ apart) for i in range(panels)])  3.85 us
    ppermute x3, starting transfers between devices, mach_swap(): return lax.ppermute(value, ('mach', 'panel'), pairs)  3.03 us
    ppermute x1, waiting for transfers between devices, on_device(): lax.ppermute(own, ('mach', 'panel'), [(mach * panels + i, (mach ^ (i in b...  1.9 us
    ppermute x3, waiting for transfers between devices, mach_swap(): return lax.ppermute(value, ('mach', 'panel'), pairs)  1.72 us
    ppermute x1, starting transfers between devices, on_device(): lax.ppermute(own, ('mach', 'panel'), [(mach * panels + i, (mach ^ (i in b...  1.49 us
    pallas_call x1, Pallas kernels, on_device(): pl.pallas_call(functools.partial(spline_kernel, rhs), out_shape=(jax.Shap...  0.96 us
    pallas_call x1, Pallas kernels, on_device(): pl.pallas_call(functools.partial(inverse_kernel, rhs, machs), out_shape=j...  0.76 us
  transfers between devices with their start and end apart: 10, of which 7 were waited for; matrix products, arithmetic and copies ran while one was open for 3% of the time, Pallas kernels for 3%

profile of v10, /device:TPU:0, one launch (start us, length us, event | category | flops | bytes accessed | tf_op | source)
XLA Modules:
  0.0 24.1 jit_solution(6432609941669508841)
XLA Ops:
  0.6 0.0 copy-start.3
  0.6 0.0 copy-start.4
  0.7 0.0 copy-start.5
  0.7 0.0 copy-start.6
  0.7 0.0 copy-start.7
  0.7 4.1 %collective-permute-start.2 = (bf16[32,128]{1,0:T(8,128)(2,1)}, bf16[32,128]{1,0:T(8,128)(2,1)S(1)}, u32[]{:S(2)}, u32[]{:S(2)}) collective-permute-start(bf16[32,128]{1,0:T(8,128)(2,1)} %bitcast.9), channel_id=1, source_target_pairs={{0,8},{1,9},{2,10},{3,11},{4,12},{5,13},{6,14},{7,15},{8,0},{9,1},... | collective-permute-start | bytes 24584 | tf_op jit(solution)/shard_map/ppermute | solution.py:181
  4.8 1.5 %collective-permute-start.1 = (bf16[32,128]{1,0:T(8,128)(2,1)}, bf16[32,128]{1,0:T(8,128)(2,1)S(1)}, u32[]{:S(2)}, u32[]{:S(2)}) collective-permute-start(bf16[32,128]{1,0:T(8,128)(2,1)} %bitcast.10), channel_id=1, source_target_pairs={{0,16},{1,2},{2,1},{3,4},{4,3},{5,6},{6,5},{7,8},{8,7},{9,10},{10,... | collective-permute-start | bytes 24584 | tf_op jit(solution)/shard_map/ppermute | solution.py:210
  6.3 0.1 collective-permute-start
  6.5 0.0 copy-start.1
  6.5 0.2 %pick_rows.1 = (bf16[192,128]{1,0:T(8,128)(2,1)S(1)}, f32[16,128]{1,0:T(8,128)S(1)}, bf16[32,128]{1,0:T(8,128)(2,1)S(1)}, s32[8,6]{1,0:T(8,128)S(1)}) custom-call(bf16[32,8]{1,0:T(8,128)(2,1)S(1)} %row_order.1.expand_ref, s32[8,8]{1,0:T(8,128)S(1)} %copy-done.4, s32[1,4]{1,0:T(1,128)S(1)} %copy-done.7, bf16[32,128]{1,0:T(8,128)(2,1)S(1)} %bitcast.12, ...), custom_call_target="tpu_custom_call" | custom-call | flops 1000000 | bytes 131072 | tf_op jit(solution)/shard_map/pick_rows/pallas_call | solution.py:231
  6.8 1.9 %collective-permute-done.1.cross_ref = bf16[32,128]{1,0:T(8,128)(2,1)S(1)} collective-permute-done((bf16[32,128]{1,0:T(8,128)(2,1)}, bf16[32,128]{1,0:T(8,128)(2,1)S(1)}, u32[]{:S(2)}, u32[]{:S(2)}) %collective-permute-start.1) | collective-permute-done | bytes 8224 | tf_op jit(solution)/shard_map/ppermute | solution.py:210
  8.7 0.0 collective-permute-done.pair_ref
  8.7 0.5 %near_field.1.part_ref = f32[32,128]{1,0:T(8,128)S(1)} custom-call(bf16[192,128]{1,0:T(8,128)(2,1)S(1)} %get-tuple-element.18.hot_ref, bf16[32,128]{1,0:T(8,128)(2,1)S(1)} %get-tuple-element.19.own_ref, bf16[32,128]{1,0:T(8,128)(2,1)S(1)} %collective-permute-done.pair_ref, bf16[32,128]{1,0:T(8,128)(2,1)S(1)} %collective-permute-done.1.cross_ref, ...), custom_call_target="tpu_custom_call" | custom-call | flops 1000000 | bytes 131072 | tf_op jit(solution)/shard_map/near_field/pallas_call | solution.py:245
  9.1 0.0 collective-permute-done.2.mirror_ref
  9.1 0.0 copy-done.1
  9.1 1.0 %spline_loads.1 = (f32[32,128]{1,0:T(8,128)S(1)}, f32[8,32,128]{2,1,0:T(8,128)S(1)}, bf16[8,32,128]{2,1,0:T(8,128)(2,1)S(1)}) custom-call(s32[8,6]{1,0:T(8,128)S(1)} %get-tuple-element.17.code_vmem, f32[32,128]{1,0:T(8,128)S(1)} %near_field.1.part_ref, bf16[32,128]{1,0:T(8,128)(2,1)S(1)} %collective-permute-done.2.mirror_ref, ...), custom_call_target="tpu_custom_call" | custom-call | flops 1000000 | bytes 131072 | tf_op jit(solution)/shard_map/spline_loads/pallas_call | solution.py:255
  10.1 0.1 collective-permute-start.3
  10.2 1.2 %collective-permute-done.3.got_ref = bf16[8,32,128]{2,1,0:T(8,128)(2,1)S(1)} collective-permute-done((bf16[8,32,128]{2,1,0:T(8,128)(2,1)S(1)}, bf16[8,32,128]{2,1,0:T(8,128)(2,1)S(1)}, u32[]{:S(2)}, u32[]{:S(2)}) %collective-permute-start.3) | collective-permute-done | bytes 65568 | tf_op jit(solution)/shard_map/ppermute | solution.py:181
  11.4 1.5 %collective-permute-start.4 = (bf16[2,32,128]{2,1,0:T(8,128)(2,1)S(1)}, bf16[2,32,128]{2,1,0:T(8,128)(2,1)S(1)}, u32[]{:S(2)}, u32[]{:S(2)}) collective-permute-start(bf16[2,32,128]{2,1,0:T(8,128)(2,1)S(1)} %get-tuple-element.25), channel_id=1, source_target_pairs={{0,13},{1,12},{2,15},{3,14},{4,9},{5,8},{6,11},{7,10},{8,5},{9,4},... | collective-permute-start | bytes 49160 | tf_op jit(solution)/shard_map/ppermute | solution.py:181
  12.9 1.7 %collective-permute-start.5 = (bf16[2,32,128]{2,1,0:T(8,128)(2,1)S(1)}, bf16[2,32,128]{2,1,0:T(8,128)(2,1)S(1)}, u32[]{:S(2)}, u32[]{:S(2)}) collective-permute-start(bf16[2,32,128]{2,1,0:T(8,128)(2,1)S(1)} %get-tuple-element.26), channel_id=1, source_target_pairs={{0,8},{1,9},{2,10},{3,11},{4,12},{5,13},{6,14},{7,15},{8,0},{9,1},... | collective-permute-start | bytes 49160 | tf_op jit(solution)/shard_map/ppermute | solution.py:181
  14.6 0.7 %collective-permute-start.6 = (bf16[2,32,128]{2,1,0:T(8,128)(2,1)S(1)}, bf16[2,32,128]{2,1,0:T(8,128)(2,1)S(1)}, u32[]{:S(2)}, u32[]{:S(2)}) collective-permute-start(bf16[2,32,128]{2,1,0:T(8,128)(2,1)S(1)} %get-tuple-element.27), channel_id=1, source_target_pairs={{0,5},{1,4},{2,7},{3,6},{4,1},{5,0},{6,3},{7,2},{8,13},{9,12},{10,... | collective-permute-start | bytes 49160 | tf_op jit(solution)/shard_map/ppermute | solution.py:181
  15.3 1.2 %collective-permute-done.4.refs_0_ = bf16[2,32,128]{2,1,0:T(8,128)(2,1)S(1)} collective-permute-done((bf16[2,32,128]{2,1,0:T(8,128)(2,1)S(1)}, bf16[2,32,128]{2,1,0:T(8,128)(2,1)S(1)}, u32[]{:S(2)}, u32[]{:S(2)}) %collective-permute-start.4) | collective-permute-done | bytes 16416 | tf_op jit(solution)/shard_map/ppermute | solution.py:181
  16.5 1.2 %collective-permute-done.5.refs_1_ = bf16[2,32,128]{2,1,0:T(8,128)(2,1)S(1)} collective-permute-done((bf16[2,32,128]{2,1,0:T(8,128)(2,1)S(1)}, bf16[2,32,128]{2,1,0:T(8,128)(2,1)S(1)}, u32[]{:S(2)}, u32[]{:S(2)}) %collective-permute-start.5) | collective-permute-done | bytes 16416 | tf_op jit(solution)/shard_map/ppermute | solution.py:181
  17.7 0.2 collective-permute-done.6.refs_2_
  18.0 1.8 %collective-permute-start.7 = (bf16[32,128]{1,0:T(8,128)(2,1)S(1)}, bf16[32,128]{1,0:T(8,128)(2,1)S(1)}, u32[]{:S(2)}, u32[]{:S(2)}) collective-permute-start(bf16[32,128]{1,0:T(8,128)(2,1)S(1)} %get-tuple-element.28), channel_id=1, source_target_pairs={{0,19},{1,18},{2,17},{3,16},{4,23},{5,22},{6,21},{7,20},{8,27},{9,... | collective-permute-start | bytes 24584 | tf_op jit(solution)/shard_map/ppermute | solution.py:190
  19.7 0.5 %collective-permute-start.8 = (bf16[32,128]{1,0:T(8,128)(2,1)S(1)}, bf16[32,128]{1,0:T(8,128)(2,1)S(1)}, u32[]{:S(2)}, u32[]{:S(2)}) collective-permute-start(bf16[32,128]{1,0:T(8,128)(2,1)S(1)} %get-tuple-element.29), channel_id=1, source_target_pairs={{0,16},{1,17},{2,18},{3,19},{4,20},{5,21},{6,22},{7,23},{8,24},{9,... | collective-permute-start | bytes 24584 | tf_op jit(solution)/shard_map/ppermute | solution.py:190
  20.3 0.7 %collective-permute-start.9 = (bf16[32,128]{1,0:T(8,128)(2,1)S(1)}, bf16[32,128]{1,0:T(8,128)(2,1)S(1)}, u32[]{:S(2)}, u32[]{:S(2)}) collective-permute-start(bf16[32,128]{1,0:T(8,128)(2,1)S(1)} %get-tuple-element.30), channel_id=1, source_target_pairs={{0,3},{1,2},{2,1},{3,0},{4,7},{5,6},{6,5},{7,4},{8,11},{9,10},{10,... | collective-permute-start | bytes 24584 | tf_op jit(solution)/shard_map/ppermute | solution.py:190
  21.0 0.7 %broadcast_multiply_fusion = f32[1,8,4,128]{3,2,1,0:T(4,128)} fusion(f32[1,8,4,128]{3,2,1,0:T(4,128)S(1)} %bitcast.8, f32[4]{0:T(128)S(1)} %convert_bitcast_fusion), kind=kLoop, calls=%fused_computation | loop fusion | flops 4096 | bytes 32784 | tf_op jit(solution)/shard_map/mul | solution.py:274
  21.7 0.3 %collective-permute-done.7.refs_0_ = bf16[32,128]{1,0:T(8,128)(2,1)S(1)} collective-permute-done((bf16[32,128]{1,0:T(8,128)(2,1)S(1)}, bf16[32,128]{1,0:T(8,128)(2,1)S(1)}, u32[]{:S(2)}, u32[]{:S(2)}) %collective-permute-start.7) | collective-permute-done | bytes 8224 | tf_op jit(solution)/shard_map/ppermute | solution.py:190
  22.0 1.4 %collective-permute-done.8.refs_1_ = bf16[32,128]{1,0:T(8,128)(2,1)S(1)} collective-permute-done((bf16[32,128]{1,0:T(8,128)(2,1)S(1)}, bf16[32,128]{1,0:T(8,128)(2,1)S(1)}, u32[]{:S(2)}, u32[]{:S(2)}) %collective-permute-start.8) | collective-permute-done | bytes 8224 | tf_op jit(solution)/shard_map/ppermute | solution.py:190
  23.4 0.0 collective-permute-done.9.refs_2_
  23.4 0.8 %struct_solve.1 = f32[32,128]{1,0:T(8,128)} custom-call(bf16[32,128]{1,0:T(8,128)(2,1)S(1)} %collective-permute-done.7.refs_0_, bf16[32,128]{1,0:T(8,128)(2,1)S(1)} %collective-permute-done.8.refs_1_, bf16[32,128]{1,0:T(8,128)(2,1)S(1)} %collective-permute-done.9.refs_2_, bf16[32,128]{1,0:T(8,128)(2,1)S(1)} %get-tuple-element.31.refs_3_, ...), custom_call_target="tpu_custom_call" | custom-call | flops 1000000 | bytes 131072 | tf_op jit(solution)/shard_map/struct_solve/pallas_call | solution.py:307
  (13 shorter events, 0.1 us)
Async XLA Ops:
  0.6 5.8 %copy-start.3 = (bf16[1,8,4,128]{3,2,1,0:T(4,128)(2,1)S(1)}, bf16[1,8,4,128]{3,2,1,0:T(4,128)(2,1)}, u32[]{:S(2)}) copy-start(bf16[1,8,4,128]{3,2,1,0:T(4,128)(2,1)} %param.8) | copy-start | bytes 24580
  0.6 5.8 %copy-start.4 = (s32[8,8]{1,0:T(8,128)S(1)}, s32[8,8]{1,0:T(8,128)}, u32[]{:S(2)}) copy-start(s32[8,8]{1,0:T(8,128)} %pattern_ref.1) | copy-start | bytes 772
  0.7 5.8 %copy-start.5 = (s32[8,6]{1,0:T(8,128)S(1)}, s32[8,6]{1,0:T(8,128)}, u32[]{:S(2)}) copy-start(s32[8,6]{1,0:T(8,128)} %owner_ref.1) | copy-start | bytes 580
  0.7 5.8 %copy-start.6 = (s32[8,6]{1,0:T(8,128)S(1)}, s32[8,6]{1,0:T(8,128)}, u32[]{:S(2)}) copy-start(s32[8,6]{1,0:T(8,128)} %local_ref.1) | copy-start | bytes 580
  0.7 5.8 %copy-start.7 = (s32[1,4]{1,0:T(1,128)S(1)}, s32[1,4]{1,0:T(1,128)}, u32[]{:S(2)}) copy-start(s32[1,4]{1,0:T(1,128)} %trim_ref.1) | copy-start | bytes 52
  0.7 8.0 %copy-start = (bf16[1,8,8,128,128]{4,3,2,1,0:T(8,128)(2,1)S(1)}, bf16[1,8,8,128,128]{4,3,2,1,0:T(8,128)(2,1)}, u32[]{:S(2)}) copy-start(bf16[1,8,8,128,128]{4,3,2,1,0:T(8,128)(2,1)} %param.9) | copy-start | bytes 6291460
  0.7 8.4 %collective-permute-start.2 = (bf16[32,128]{1,0:T(8,128)(2,1)}, bf16[32,128]{1,0:T(8,128)(2,1)S(1)}, u32[]{:S(2)}, u32[]{:S(2)}) collective-permute-start(bf16[32,128]{1,0:T(8,128)(2,1)} %bitcast.9), channel_id=1, source_target_pairs={{0,8},{1,9},{2,10},{3,11},{4,12},{5,13},{6,14},{7,15},{8,0},{9,1},... | collective-permute-start | bytes 24584 | tf_op jit(solution)/shard_map/ppermute | solution.py:181
  4.8 3.9 %collective-permute-start.1 = (bf16[32,128]{1,0:T(8,128)(2,1)}, bf16[32,128]{1,0:T(8,128)(2,1)S(1)}, u32[]{:S(2)}, u32[]{:S(2)}) collective-permute-start(bf16[32,128]{1,0:T(8,128)(2,1)} %bitcast.10), channel_id=1, source_target_pairs={{0,16},{1,2},{2,1},{3,4},{4,3},{5,6},{6,5},{7,8},{8,7},{9,10},{10,... | collective-permute-start | bytes 24584 | tf_op jit(solution)/shard_map/ppermute | solution.py:210
  6.3 2.4 %collective-permute-start = (bf16[32,128]{1,0:T(8,128)(2,1)}, bf16[32,128]{1,0:T(8,128)(2,1)S(1)}, u32[]{:S(2)}, u32[]{:S(2)}) collective-permute-start(bf16[32,128]{1,0:T(8,128)(2,1)} %bitcast.11), channel_id=1, source_target_pairs={{0,1},{1,0},{2,3},{3,2},{4,5},{5,4},{6,7},{7,6},{8,9},{9,8},{10,11... | collective-permute-start | bytes 24584 | tf_op jit(solution)/shard_map/ppermute | solution.py:181
  6.5 2.6 %copy-start.1 = (bf16[8,6,128,128]{3,2,1,0:T(8,128)(2,1)S(1)}, bf16[8,6,128,128]{3,2,1,0:T(8,128)(2,1)}, u32[]{:S(2)}) copy-start(bf16[8,6,128,128]{3,2,1,0:T(8,128)(2,1)} %spline_ref.1) | copy-start | bytes 4718596
  9.1 14.3 %copy-start.2 = (bf16[8,128,128]{2,1,0:T(8,128)(2,1)S(1)}, bf16[8,128,128]{2,1,0:T(8,128)(2,1)}, u32[]{:S(2)}) copy-start(bf16[8,128,128]{2,1,0:T(8,128)(2,1)} %refs_4_.1) | copy-start | bytes 786436
  10.1 1.3 %collective-permute-start.3 = (bf16[8,32,128]{2,1,0:T(8,128)(2,1)S(1)}, bf16[8,32,128]{2,1,0:T(8,128)(2,1)S(1)}, u32[]{:S(2)}, u32[]{:S(2)}) collective-permute-start(bf16[8,32,128]{2,1,0:T(8,128)(2,1)S(1)} %get-tuple-element.23), channel_id=1, source_target_pairs={{0,1},{1,0},{2,3},{3,2},{4,5},{5,4},{6,7},{7,6},{8,9},{9,8},{10,11... | collective-permute-start | bytes 196616 | tf_op jit(solution)/shard_map/ppermute | solution.py:181
  11.4 5.1 %collective-permute-start.4 = (bf16[2,32,128]{2,1,0:T(8,128)(2,1)S(1)}, bf16[2,32,128]{2,1,0:T(8,128)(2,1)S(1)}, u32[]{:S(2)}, u32[]{:S(2)}) collective-permute-start(bf16[2,32,128]{2,1,0:T(8,128)(2,1)S(1)} %get-tuple-element.25), channel_id=1, source_target_pairs={{0,13},{1,12},{2,15},{3,14},{4,9},{5,8},{6,11},{7,10},{8,5},{9,4},... | collective-permute-start | bytes 49160 | tf_op jit(solution)/shard_map/ppermute | solution.py:181
  12.9 4.8 %collective-permute-start.5 = (bf16[2,32,128]{2,1,0:T(8,128)(2,1)S(1)}, bf16[2,32,128]{2,1,0:T(8,128)(2,1)S(1)}, u32[]{:S(2)}, u32[]{:S(2)}) collective-permute-start(bf16[2,32,128]{2,1,0:T(8,128)(2,1)S(1)} %get-tuple-element.26), channel_id=1, source_target_pairs={{0,8},{1,9},{2,10},{3,11},{4,12},{5,13},{6,14},{7,15},{8,0},{9,1},... | collective-permute-start | bytes 49160 | tf_op jit(solution)/shard_map/ppermute | solution.py:181
  14.6 3.3 %collective-permute-start.6 = (bf16[2,32,128]{2,1,0:T(8,128)(2,1)S(1)}, bf16[2,32,128]{2,1,0:T(8,128)(2,1)S(1)}, u32[]{:S(2)}, u32[]{:S(2)}) collective-permute-start(bf16[2,32,128]{2,1,0:T(8,128)(2,1)S(1)} %get-tuple-element.27), channel_id=1, source_target_pairs={{0,5},{1,4},{2,7},{3,6},{4,1},{5,0},{6,3},{7,2},{8,13},{9,12},{10,... | collective-permute-start | bytes 49160 | tf_op jit(solution)/shard_map/ppermute | solution.py:181
  18.0 4.0 %collective-permute-start.7 = (bf16[32,128]{1,0:T(8,128)(2,1)S(1)}, bf16[32,128]{1,0:T(8,128)(2,1)S(1)}, u32[]{:S(2)}, u32[]{:S(2)}) collective-permute-start(bf16[32,128]{1,0:T(8,128)(2,1)S(1)} %get-tuple-element.28), channel_id=1, source_target_pairs={{0,19},{1,18},{2,17},{3,16},{4,23},{5,22},{6,21},{7,20},{8,27},{9,... | collective-permute-start | bytes 24584 | tf_op jit(solution)/shard_map/ppermute | solution.py:190
  19.7 3.7 %collective-permute-start.8 = (bf16[32,128]{1,0:T(8,128)(2,1)S(1)}, bf16[32,128]{1,0:T(8,128)(2,1)S(1)}, u32[]{:S(2)}, u32[]{:S(2)}) collective-permute-start(bf16[32,128]{1,0:T(8,128)(2,1)S(1)} %get-tuple-element.29), channel_id=1, source_target_pairs={{0,16},{1,17},{2,18},{3,19},{4,20},{5,21},{6,22},{7,23},{8,24},{9,... | collective-permute-start | bytes 24584 | tf_op jit(solution)/shard_map/ppermute | solution.py:190
  20.3 3.1 %collective-permute-start.9 = (bf16[32,128]{1,0:T(8,128)(2,1)S(1)}, bf16[32,128]{1,0:T(8,128)(2,1)S(1)}, u32[]{:S(2)}, u32[]{:S(2)}) collective-permute-start(bf16[32,128]{1,0:T(8,128)(2,1)S(1)} %get-tuple-element.30), channel_id=1, source_target_pairs={{0,3},{1,2},{2,1},{3,0},{4,7},{5,6},{6,5},{7,4},{8,11},{9,10},{10,... | collective-permute-start | bytes 24584 | tf_op jit(solution)/shard_map/ppermute | solution.py:190

commit v11 on v10

--- a/solution.py
+++ b/solution.py
@@ -95,7 +95,7 @@
 
 
 def spline_kernel(
-    rhs, code_vmem, part_ref, mirror_ref, gate_ref, near_ref, spline_ref,
+    rhs, _, mirror_ref, code_vmem, part_ref, gate_ref, near_ref, spline_ref,
     sums_ref, keep_ref, send_ref, code_ref, loads_ref, acc, sem,
 ):
     copy = pltpu.make_async_copy(code_vmem, code_ref, sem)
@@ -259,7 +259,7 @@
             jax.ShapeDtypeStruct(half, f32),
             jax.ShapeDtypeStruct(half, bf16),
         ),
-        in_specs=[VMEM] * 6,
+        in_specs=[VMEM] * 7,
         out_specs=(VMEM,) * 3,
         scratch_shapes=[
             pltpu.SMEM(spline_owner.shape, jnp.int32),
@@ -270,7 +270,7 @@
         compiler_params=params,
         cost_estimate=cost(10**6, 2**17),
         name="spline_loads",
-    )(code, part, mirror, gate, near_blocks[0], spline_blocks)
+    )(pair, mirror, code, part, gate, near_blocks[0], spline_blocks)
     loads = sums.reshape(adjoint.shape) * trim_mask[0].astype(f32)[None, None, :, None]
     got = swap(send, panels, 1)
     steps = panels // 4
@@ -289,7 +289,7 @@
     got = [
         swap(sends[step - 1], panels, 4 * step + step % 2) for step in range(steps - 1, 0, -1)
     ]
-    one = jax.ShapeDtypeStruct((struct_rows, width), bf16)
+    one = jax.ShapeDtypeStruct((struct_rows, width), f32)
     columns = pl.pallas_call(
         functools.partial(column_kernel, machs),
         out_shape=(one,) * (2 * machs),

time: 24.3 us -> 24 us (0.988)
  starting transfers between devices: 12.7 us -> 12.4 us
    ppermute x6, waiting for transfers between devices: 3.85 us -> 6.28 us  [swap(): return lax.ppermute(value, 'panel', [(i, i ^ apart) for i in range(panels)])]
    ppermute x1, waiting for transfers between devices: 1.9 us -> 0.01 us  [on_device(): lax.ppermute(own, ('mach', 'panel'), [(mach * panels + i, (mach ^ (i in b...]
    ppermute x6, starting transfers between devices: 8.21 us -> 6.42 us  [swap(): return lax.ppermute(value, 'panel', [(i, i ^ apart) for i in range(panels)])]
    ppermute x1, starting transfers between devices: 1.49 us -> 3 us  [on_device(): lax.ppermute(own, ('mach', 'panel'), [(mach * panels + i, (mach ^ (i in b...]
    ppermute x3, waiting for transfers between devices: 1.72 us -> 1.13 us  [mach_swap(): return lax.ppermute(value, ('mach', 'panel'), pairs)]
  transfers between devices with their start and end apart: 10 -> 10, of which waited for: 7 -> 8; matrix products, arithmetic and copies ran while one was open for 3% -> 3% of each run, Pallas kernels for 3% -> 3%
where the time goes in v11:
time: 24 us; the launch traced here: 23.8 us
  starting transfers between devices  12.4 us (52%)
  waiting for transfers between devices  7.41 us (31%)
  Pallas kernels  2.46 us (10%)
  between operations  0.77 us (3%)
  other arithmetic  0.68 us (3%)
    ppermute x6, starting transfers between devices, swap(): return lax.ppermute(value, 'panel', [(i, i ^ apart) for i in range(panels)])  6.42 us
    ppermute x6, waiting for transfers between devices, swap(): return lax.ppermute(value, 'panel', [(i, i ^ apart) for i in range(panels)])  6.28 us
    ppermute x1, starting transfers between devices, on_device(): lax.ppermute(own, ('mach', 'panel'), [(mach * panels + i, (mach ^ (i in b...  3 us
    ppermute x3, starting transfers between devices, mach_swap(): return lax.ppermute(value, ('mach', 'panel'), pairs)  2.99 us
    ppermute x3, waiting for transfers between devices, mach_swap(): return lax.ppermute(value, ('mach', 'panel'), pairs)  1.13 us
    pallas_call x1, Pallas kernels, on_device(): pl.pallas_call(functools.partial(spline_kernel, rhs), out_shape=(jax.Shap...  0.96 us
    pallas_call x1, Pallas kernels, on_device(): pl.pallas_call(functools.partial(inverse_kernel, rhs, machs), out_shape=j...  0.76 us
    mul x1, other arithmetic, on_device(): sums.reshape(adjoint.shape) * trim_mask[0].astype(f32)[None, None, :, None]  0.68 us
  transfers between devices with their start and end apart: 10, of which 8 were waited for; matrix products, arithmetic and copies ran while one was open for 3% of the time, Pallas kernels for 3%

profile of v11, /device:TPU:0, one launch (start us, length us, event | category | flops | bytes accessed | tf_op | source)
XLA Modules:
  0.0 23.8 jit_solution(16697025304852561585)
XLA Ops:
  0.6 0.0 copy-start.3
  0.6 0.0 copy-start.4
  0.7 0.0 copy-start.5
  0.7 0.0 copy-start.6
  0.7 3.0 %collective-permute-start.2 = (bf16[32,128]{1,0:T(8,128)(2,1)}, bf16[32,128]{1,0:T(8,128)(2,1)S(1)}, u32[]{:S(2)}, u32[]{:S(2)}) collective-permute-start(bf16[32,128]{1,0:T(8,128)(2,1)} %bitcast.9), channel_id=1, source_target_pairs={{0,16},{1,2},{2,1},{3,4},{4,3},{5,6},{6,5},{7,8},{8,7},{9,10},{10,... | collective-permute-start | bytes 24584 | tf_op jit(solution)/shard_map/ppermute | solution.py:210
  3.7 1.9 %collective-permute-start.1 = (bf16[32,128]{1,0:T(8,128)(2,1)}, bf16[32,128]{1,0:T(8,128)(2,1)S(1)}, u32[]{:S(2)}, u32[]{:S(2)}) collective-permute-start(bf16[32,128]{1,0:T(8,128)(2,1)} %bitcast.10), channel_id=1, source_target_pairs={{0,8},{1,9},{2,10},{3,11},{4,12},{5,13},{6,14},{7,15},{8,0},{9,1},... | collective-permute-start | bytes 24584 | tf_op jit(solution)/shard_map/ppermute | solution.py:181
  5.6 0.5 %collective-permute-start = (bf16[32,128]{1,0:T(8,128)(2,1)}, bf16[32,128]{1,0:T(8,128)(2,1)S(1)}, u32[]{:S(2)}, u32[]{:S(2)}) collective-permute-start(bf16[32,128]{1,0:T(8,128)(2,1)} %bitcast.11), channel_id=1, source_target_pairs={{0,1},{1,0},{2,3},{3,2},{4,5},{5,4},{6,7},{7,6},{8,9},{9,8},{10,11... | collective-permute-start | bytes 24584 | tf_op jit(solution)/shard_map/ppermute | solution.py:181
  6.2 0.0 copy-done.3
  6.2 0.0 copy-start.1
  6.2 0.2 %pick_rows.1 = (bf16[192,128]{1,0:T(8,128)(2,1)S(1)}, f32[16,128]{1,0:T(8,128)S(1)}, bf16[32,128]{1,0:T(8,128)(2,1)S(1)}, s32[8,6]{1,0:T(8,128)S(1)}) custom-call(bf16[32,8]{1,0:T(8,128)(2,1)S(1)} %row_order.1.expand_ref, s32[8,8]{1,0:T(8,128)S(1)} %copy-done.4, s32[1,4]{1,0:T(1,128)S(1)} %copy-done.7, bf16[32,128]{1,0:T(8,128)(2,1)S(1)} %bitcast.12, ...), custom_call_target="tpu_custom_call" | custom-call | flops 1000000 | bytes 131072 | tf_op jit(solution)/shard_map/pick_rows/pallas_call | solution.py:231
  6.5 0.0 collective-permute-done.2.cross_ref
  6.5 0.7 %collective-permute-done.pair_ref._ = bf16[32,128]{1,0:T(8,128)(2,1)S(1)} collective-permute-done((bf16[32,128]{1,0:T(8,128)(2,1)}, bf16[32,128]{1,0:T(8,128)(2,1)S(1)}, u32[]{:S(2)}, u32[]{:S(2)}) %collective-permute-start) | collective-permute-done | bytes 8224 | tf_op jit(solution)/shard_map/ppermute | solution.py:181
  7.2 0.5 %near_field.1.part_ref = f32[32,128]{1,0:T(8,128)S(1)} custom-call(bf16[192,128]{1,0:T(8,128)(2,1)S(1)} %get-tuple-element.18.hot_ref, bf16[32,128]{1,0:T(8,128)(2,1)S(1)} %get-tuple-element.19.own_ref, bf16[32,128]{1,0:T(8,128)(2,1)S(1)} %collective-permute-done.pair_ref._, bf16[32,128]{1,0:T(8,128)(2,1)S(1)} %collective-permute-done.2.cross_ref, ...), custom_call_target="tpu_custom_call" | custom-call | flops 1000000 | bytes 131072 | tf_op jit(solution)/shard_map/near_field/pallas_call | solution.py:245
  7.6 0.8 %collective-permute-done.1.mirror_ref = bf16[32,128]{1,0:T(8,128)(2,1)S(1)} collective-permute-done((bf16[32,128]{1,0:T(8,128)(2,1)}, bf16[32,128]{1,0:T(8,128)(2,1)S(1)}, u32[]{:S(2)}, u32[]{:S(2)}) %collective-permute-start.1) | collective-permute-done | bytes 8224 | tf_op jit(solution)/shard_map/ppermute | solution.py:181
  8.5 0.0 copy-done.1
  8.5 1.0 %spline_loads.1 = (f32[32,128]{1,0:T(8,128)S(1)}, f32[8,32,128]{2,1,0:T(8,128)S(1)}, bf16[8,32,128]{2,1,0:T(8,128)(2,1)S(1)}) custom-call(bf16[32,128]{1,0:T(8,128)(2,1)S(1)} %collective-permute-done.pair_ref._, bf16[32,128]{1,0:T(8,128)(2,1)S(1)} %collective-permute-done.1.mirror_ref, s32[8,6]{1,0:T(8,128)S(1)} %get-tuple-element.17.code_vmem, ...), custom_call_target="tpu_custom_call" | custom-call | flops 1000000 | bytes 131072 | tf_op jit(solution)/shard_map/spline_loads/pallas_call | solution.py:255
  9.4 0.1 collective-permute-start.3
  9.5 1.2 %collective-permute-done.3.got_ref = bf16[8,32,128]{2,1,0:T(8,128)(2,1)S(1)} collective-permute-done((bf16[8,32,128]{2,1,0:T(8,128)(2,1)S(1)}, bf16[8,32,128]{2,1,0:T(8,128)(2,1)S(1)}, u32[]{:S(2)}, u32[]{:S(2)}) %collective-permute-start.3) | collective-permute-done | bytes 65568 | tf_op jit(solution)/shard_map/ppermute | solution.py:181
  10.8 2.8 %collective-permute-start.4 = (bf16[2,32,128]{2,1,0:T(8,128)(2,1)S(1)}, bf16[2,32,128]{2,1,0:T(8,128)(2,1)S(1)}, u32[]{:S(2)}, u32[]{:S(2)}) collective-permute-start(bf16[2,32,128]{2,1,0:T(8,128)(2,1)S(1)} %get-tuple-element.25), channel_id=1, source_target_pairs={{0,13},{1,12},{2,15},{3,14},{4,9},{5,8},{6,11},{7,10},{8,5},{9,4},... | collective-permute-start | bytes 49160 | tf_op jit(solution)/shard_map/ppermute | solution.py:181
  13.5 0.0 collective-permute-start.5
  13.5 1.1 %collective-permute-start.6 = (bf16[2,32,128]{2,1,0:T(8,128)(2,1)S(1)}, bf16[2,32,128]{2,1,0:T(8,128)(2,1)S(1)}, u32[]{:S(2)}, u32[]{:S(2)}) collective-permute-start(bf16[2,32,128]{2,1,0:T(8,128)(2,1)S(1)} %get-tuple-element.27), channel_id=1, source_target_pairs={{0,5},{1,4},{2,7},{3,6},{4,1},{5,0},{6,3},{7,2},{8,13},{9,12},{10,... | collective-permute-start | bytes 49160 | tf_op jit(solution)/shard_map/ppermute | solution.py:181
  14.7 1.1 %collective-permute-done.4.refs_0_ = bf16[2,32,128]{2,1,0:T(8,128)(2,1)S(1)} collective-permute-done((bf16[2,32,128]{2,1,0:T(8,128)(2,1)S(1)}, bf16[2,32,128]{2,1,0:T(8,128)(2,1)S(1)}, u32[]{:S(2)}, u32[]{:S(2)}) %collective-permute-start.4) | collective-permute-done | bytes 16416 | tf_op jit(solution)/shard_map/ppermute | solution.py:181
  15.8 2.4 %collective-permute-done.5.refs_1_ = bf16[2,32,128]{2,1,0:T(8,128)(2,1)S(1)} collective-permute-done((bf16[2,32,128]{2,1,0:T(8,128)(2,1)S(1)}, bf16[2,32,128]{2,1,0:T(8,128)(2,1)S(1)}, u32[]{:S(2)}, u32[]{:S(2)}) %collective-permute-start.5) | collective-permute-done | bytes 16416 | tf_op jit(solution)/shard_map/ppermute | solution.py:181
  18.2 0.0 collective-permute-done.6.refs_2_
  18.2 0.6 %collective-permute-start.7 = (f32[32,128]{1,0:T(8,128)S(1)}, f32[32,128]{1,0:T(8,128)S(1)}, u32[]{:S(2)}, u32[]{:S(2)}) collective-permute-start(f32[32,128]{1,0:T(8,128)S(1)} %get-tuple-element.28), channel_id=1, source_target_pairs={{0,19},{1,18},{2,17},{3,16},{4,23},{5,22},{6,21},{7,20},{8,27},{9,... | collective-permute-start | bytes 49160 | tf_op jit(solution)/shard_map/ppermute | solution.py:190
  18.8 1.0 %collective-permute-start.8 = (f32[32,128]{1,0:T(8,128)S(1)}, f32[32,128]{1,0:T(8,128)S(1)}, u32[]{:S(2)}, u32[]{:S(2)}) collective-permute-start(f32[32,128]{1,0:T(8,128)S(1)} %get-tuple-element.29), channel_id=1, source_target_pairs={{0,16},{1,17},{2,18},{3,19},{4,20},{5,21},{6,22},{7,23},{8,24},{9,... | collective-permute-start | bytes 49160 | tf_op jit(solution)/shard_map/ppermute | solution.py:190
  19.8 1.4 %collective-permute-start.9 = (f32[32,128]{1,0:T(8,128)S(1)}, f32[32,128]{1,0:T(8,128)S(1)}, u32[]{:S(2)}, u32[]{:S(2)}) collective-permute-start(f32[32,128]{1,0:T(8,128)S(1)} %get-tuple-element.30), channel_id=1, source_target_pairs={{0,3},{1,2},{2,1},{3,0},{4,7},{5,6},{6,5},{7,4},{8,11},{9,10},{10,... | collective-permute-start | bytes 49160 | tf_op jit(solution)/shard_map/ppermute | solution.py:190
  21.2 0.7 %broadcast_multiply_fusion = f32[1,8,4,128]{3,2,1,0:T(4,128)} fusion(f32[1,8,4,128]{3,2,1,0:T(4,128)S(1)} %bitcast.8, f32[4]{0:T(128)S(1)} %convert_bitcast_fusion), kind=kLoop, calls=%fused_computation | loop fusion | flops 4096 | bytes 32784 | tf_op jit(solution)/shard_map/mul | solution.py:274
  21.9 0.5 %collective-permute-done.7.refs_0_ = f32[32,128]{1,0:T(8,128)S(1)} collective-permute-done((f32[32,128]{1,0:T(8,128)S(1)}, f32[32,128]{1,0:T(8,128)S(1)}, u32[]{:S(2)}, u32[]{:S(2)}) %collective-permute-start.7) | collective-permute-done | bytes 16416 | tf_op jit(solution)/shard_map/ppermute | solution.py:190
  22.3 0.2 collective-permute-done.8.refs_1_
  22.5 0.5 %collective-permute-done.9.refs_2_ = f32[32,128]{1,0:T(8,128)S(1)} collective-permute-done((f32[32,128]{1,0:T(8,128)S(1)}, f32[32,128]{1,0:T(8,128)S(1)}, u32[]{:S(2)}, u32[]{:S(2)}) %collective-permute-start.9) | collective-permute-done | bytes 16416 | tf_op jit(solution)/shard_map/ppermute | solution.py:190
  23.0 0.8 %struct_solve.1 = f32[32,128]{1,0:T(8,128)} custom-call(f32[32,128]{1,0:T(8,128)S(1)} %collective-permute-done.7.refs_0_, f32[32,128]{1,0:T(8,128)S(1)} %collective-permute-done.8.refs_1_, f32[32,128]{1,0:T(8,128)S(1)} %collective-permute-done.9.refs_2_, f32[32,128]{1,0:T(8,128)S(1)} %get-tuple-element.31.refs_3_, bf16[8,128,128]{2,1,0:T(8,128)(2,1)S(1)} %copy-done.2), custom_call_target="tpu_custom_call" | custom-call | flops 1000000 | bytes 131072 | tf_op jit(solution)/shard_map/struct_solve/pallas_call | solution.py:307
  (13 shorter events, 0.1 us)
Async XLA Ops:
  0.6 5.5 %copy-start.3 = (bf16[1,8,4,128]{3,2,1,0:T(4,128)(2,1)S(1)}, bf16[1,8,4,128]{3,2,1,0:T(4,128)(2,1)}, u32[]{:S(2)}) copy-start(bf16[1,8,4,128]{3,2,1,0:T(4,128)(2,1)} %param.8) | copy-start | bytes 24580
  0.6 5.5 %copy-start.4 = (s32[8,8]{1,0:T(8,128)S(1)}, s32[8,8]{1,0:T(8,128)}, u32[]{:S(2)}) copy-start(s32[8,8]{1,0:T(8,128)} %pattern_ref.1) | copy-start | bytes 772
  0.7 5.5 %copy-start.5 = (s32[8,6]{1,0:T(8,128)S(1)}, s32[8,6]{1,0:T(8,128)}, u32[]{:S(2)}) copy-start(s32[8,6]{1,0:T(8,128)} %owner_ref.1) | copy-start | bytes 580
  0.7 5.5 %copy-start.6 = (s32[8,6]{1,0:T(8,128)S(1)}, s32[8,6]{1,0:T(8,128)}, u32[]{:S(2)}) copy-start(s32[8,6]{1,0:T(8,128)} %local_ref.1) | copy-start | bytes 580
  0.7 5.5 %copy-start.7 = (s32[1,4]{1,0:T(1,128)S(1)}, s32[1,4]{1,0:T(1,128)}, u32[]{:S(2)}) copy-start(s32[1,4]{1,0:T(1,128)} %trim_ref.1) | copy-start | bytes 52
  0.7 6.5 %copy-start = (bf16[1,8,8,128,128]{4,3,2,1,0:T(8,128)(2,1)S(1)}, bf16[1,8,8,128,128]{4,3,2,1,0:T(8,128)(2,1)}, u32[]{:S(2)}) copy-start(bf16[1,8,8,128,128]{4,3,2,1,0:T(8,128)(2,1)} %param.9) | copy-start | bytes 6291460
  0.7 5.8 %collective-permute-start.2 = (bf16[32,128]{1,0:T(8,128)(2,1)}, bf16[32,128]{1,0:T(8,128)(2,1)S(1)}, u32[]{:S(2)}, u32[]{:S(2)}) collective-permute-start(bf16[32,128]{1,0:T(8,128)(2,1)} %bitcast.9), channel_id=1, source_target_pairs={{0,16},{1,2},{2,1},{3,4},{4,3},{5,6},{6,5},{7,8},{8,7},{9,10},{10,... | collective-permute-start | bytes 24584 | tf_op jit(solution)/shard_map/ppermute | solution.py:210
  3.7 4.8 %collective-permute-start.1 = (bf16[32,128]{1,0:T(8,128)(2,1)}, bf16[32,128]{1,0:T(8,128)(2,1)S(1)}, u32[]{:S(2)}, u32[]{:S(2)}) collective-permute-start(bf16[32,128]{1,0:T(8,128)(2,1)} %bitcast.10), channel_id=1, source_target_pairs={{0,8},{1,9},{2,10},{3,11},{4,12},{5,13},{6,14},{7,15},{8,0},{9,1},... | collective-permute-start | bytes 24584 | tf_op jit(solution)/shard_map/ppermute | solution.py:181
  5.6 1.5 %collective-permute-start = (bf16[32,128]{1,0:T(8,128)(2,1)}, bf16[32,128]{1,0:T(8,128)(2,1)S(1)}, u32[]{:S(2)}, u32[]{:S(2)}) collective-permute-start(bf16[32,128]{1,0:T(8,128)(2,1)} %bitcast.11), channel_id=1, source_target_pairs={{0,1},{1,0},{2,3},{3,2},{4,5},{5,4},{6,7},{7,6},{8,9},{9,8},{10,11... | collective-permute-start | bytes 24584 | tf_op jit(solution)/shard_map/ppermute | solution.py:181
  6.2 2.3 %copy-start.1 = (bf16[8,6,128,128]{3,2,1,0:T(8,128)(2,1)S(1)}, bf16[8,6,128,128]{3,2,1,0:T(8,128)(2,1)}, u32[]{:S(2)}) copy-start(bf16[8,6,128,128]{3,2,1,0:T(8,128)(2,1)} %spline_ref.1) | copy-start | bytes 4718596
  7.6 15.4 %copy-start.2 = (bf16[8,128,128]{2,1,0:T(8,128)(2,1)S(1)}, bf16[8,128,128]{2,1,0:T(8,128)(2,1)}, u32[]{:S(2)}) copy-start(bf16[8,128,128]{2,1,0:T(8,128)(2,1)} %refs_4_.1) | copy-start | bytes 786436
  9.4 1.3 %collective-permute-start.3 = (bf16[8,32,128]{2,1,0:T(8,128)(2,1)S(1)}, bf16[8,32,128]{2,1,0:T(8,128)(2,1)S(1)}, u32[]{:S(2)}, u32[]{:S(2)}) collective-permute-start(bf16[8,32,128]{2,1,0:T(8,128)(2,1)S(1)} %get-tuple-element.23), channel_id=1, source_target_pairs={{0,1},{1,0},{2,3},{3,2},{4,5},{5,4},{6,7},{7,6},{8,9},{9,8},{10,11... | collective-permute-start | bytes 196616 | tf_op jit(solution)/shard_map/ppermute | solution.py:181
  10.8 5.0 %collective-permute-start.4 = (bf16[2,32,128]{2,1,0:T(8,128)(2,1)S(1)}, bf16[2,32,128]{2,1,0:T(8,128)(2,1)S(1)}, u32[]{:S(2)}, u32[]{:S(2)}) collective-permute-start(bf16[2,32,128]{2,1,0:T(8,128)(2,1)S(1)} %get-tuple-element.25), channel_id=1, source_target_pairs={{0,13},{1,12},{2,15},{3,14},{4,9},{5,8},{6,11},{7,10},{8,5},{9,4},... | collective-permute-start | bytes 49160 | tf_op jit(solution)/shard_map/ppermute | solution.py:181
  13.5 4.6 %collective-permute-start.5 = (bf16[2,32,128]{2,1,0:T(8,128)(2,1)S(1)}, bf16[2,32,128]{2,1,0:T(8,128)(2,1)S(1)}, u32[]{:S(2)}, u32[]{:S(2)}) collective-permute-start(bf16[2,32,128]{2,1,0:T(8,128)(2,1)S(1)} %get-tuple-element.26), channel_id=1, source_target_pairs={{0,8},{1,9},{2,10},{3,11},{4,12},{5,13},{6,14},{7,15},{8,0},{9,1},... | collective-permute-start | bytes 49160 | tf_op jit(solution)/shard_map/ppermute | solution.py:181
  13.5 4.6 %collective-permute-start.6 = (bf16[2,32,128]{2,1,0:T(8,128)(2,1)S(1)}, bf16[2,32,128]{2,1,0:T(8,128)(2,1)S(1)}, u32[]{:S(2)}, u32[]{:S(2)}) collective-permute-start(bf16[2,32,128]{2,1,0:T(8,128)(2,1)S(1)} %get-tuple-element.27), channel_id=1, source_target_pairs={{0,5},{1,4},{2,7},{3,6},{4,1},{5,0},{6,3},{7,2},{8,13},{9,12},{10,... | collective-permute-start | bytes 49160 | tf_op jit(solution)/shard_map/ppermute | solution.py:181
  18.2 4.1 %collective-permute-start.7 = (f32[32,128]{1,0:T(8,128)S(1)}, f32[32,128]{1,0:T(8,128)S(1)}, u32[]{:S(2)}, u32[]{:S(2)}) collective-permute-start(f32[32,128]{1,0:T(8,128)S(1)} %get-tuple-element.28), channel_id=1, source_target_pairs={{0,19},{1,18},{2,17},{3,16},{4,23},{5,22},{6,21},{7,20},{8,27},{9,... | collective-permute-start | bytes 49160 | tf_op jit(solution)/shard_map/ppermute | solution.py:190
  18.8 3.7 %collective-permute-start.8 = (f32[32,128]{1,0:T(8,128)S(1)}, f32[32,128]{1,0:T(8,128)S(1)}, u32[]{:S(2)}, u32[]{:S(2)}) collective-permute-start(f32[32,128]{1,0:T(8,128)S(1)} %get-tuple-element.29), channel_id=1, source_target_pairs={{0,16},{1,17},{2,18},{3,19},{4,20},{5,21},{6,22},{7,23},{8,24},{9,... | collective-permute-start | bytes 49160 | tf_op jit(solution)/shard_map/ppermute | solution.py:190
  19.8 3.2 %collective-permute-start.9 = (f32[32,128]{1,0:T(8,128)S(1)}, f32[32,128]{1,0:T(8,128)S(1)}, u32[]{:S(2)}, u32[]{:S(2)}) collective-permute-start(f32[32,128]{1,0:T(8,128)S(1)} %get-tuple-element.30), channel_id=1, source_target_pairs={{0,3},{1,2},{2,1},{3,0},{4,7},{5,6},{6,5},{7,4},{8,11},{9,10},{10,... | collective-permute-start | bytes 49160 | tf_op jit(solution)/shard_map/ppermute | solution.py:190

commit v12 on v8

--- a/solution.py
+++ b/solution.py
@@ -13,10 +13,8 @@
 TILE = 8
 
 
-def parity(index):
-    for shift in (16, 8, 4, 2, 1):
-        index = index ^ (index >> shift)
-    return index & 1
+def device_class(index):
+    return (index ^ (index >> 1) ^ (index >> 2)) & 1
 
 
 def spread_kernel(rhs, expand_ref):
@@ -59,7 +57,7 @@
     held_ref[...] = own_ref[...]
     owner = owner_ref[...]
     code_ref[...] = (
-        (parity(owner) ^ parity(here)) * (panels // 2) + owner // 2
+        (device_class(owner) ^ device_class(here)) * (panels // 2) + (owner >> 1)
     ) * struct_count + local_ref[...]
 
 
@@ -97,20 +95,22 @@
 
 
 def spline_kernel(
-    rhs, code_ref, part_ref, mirror_ref, gate_ref, near_ref, spline_ref,
-    loads_hbm, keep_ref, send_ref, loads_ref, acc, sem,
+    rhs, _, mirror_ref, code_vmem, part_ref, gate_ref, near_ref, spline_ref,
+    sums_ref, keep_ref, send_ref, code_ref, loads_ref, acc, sem,
 ):
+    copy = pltpu.make_async_copy(code_vmem, code_ref, sem)
+    copy.start()
     block_count, splines = code_ref.shape
     rows, width = part_ref.shape
     for g in range(rows // PACK):
         group = slice(g * PACK, (g + 1) * PACK)
         far = grouped_product(rhs, mirror_ref[group], lambda i: near_ref[i, 1], g)
-        loads_ref[group] = gate_ref[...] * (part_ref[group] + far)
-    copy = pltpu.make_async_copy(loads_ref, loads_hbm, sem)
-    copy.start()
+        sums_ref[group] = part_ref[group] + far
+        loads_ref[group] = gate_ref[...] * sums_ref[group]
     acc[...] = jnp.zeros(acc.shape, jnp.float32)
     upper = lax.broadcasted_iota(jnp.int32, (TILE, width), 0) // rhs
     blank = jnp.zeros((TILE, width), jnp.float32)
+    copy.wait()
     for pair in range(0, block_count, 2):
         both = loads_ref[pair * rhs : (pair + 2) * rhs]
         turned = pltpu.roll(both, rhs, 0)
@@ -143,7 +143,6 @@
     tiles = acc.shape[0] // 2
     keep_ref[...] = acc[:tiles].reshape(keep_ref.shape)
     send_ref[...] = acc[tiles:].reshape(send_ref.shape).astype(send_ref.dtype)
-    copy.wait()
 
 
 def sum_kernel(held_ref, got_ref, out_ref):
@@ -185,7 +184,6 @@
     params = pltpu.CompilerParams(vmem_limit_bytes=16 * 1024 * 1024)
     f32, bf16 = jnp.float32, jnp.bfloat16
     own = adjoint.reshape(rows, width)
-    mirror = swap(own, panels, panels // 2)
     beside = {0: 0, panels - 1: panels - 1}
     cross = lax.ppermute(
         own, ("mach", "panel"),
@@ -198,6 +196,7 @@
             for i in range(panels)
         ],
     )
+    mirror = swap(own, panels, panels // 2)
     pair = swap(own, panels, 1)
     expand = pl.pallas_call(
         functools.partial(spread_kernel, rhs),
@@ -231,16 +230,17 @@
         name="near_field",
     )(hot, held, pair, cross, near_blocks[0])
     half = (panels // 2, struct_rows, width)
-    loads, keep, send = pl.pallas_call(
+    sums, keep, send = pl.pallas_call(
         functools.partial(spline_kernel, rhs),
         out_shape=(
             jax.ShapeDtypeStruct((rows, width), f32),
             jax.ShapeDtypeStruct(half, f32),
             jax.ShapeDtypeStruct(half, bf16),
         ),
-        in_specs=[SMEM] + [VMEM] * 5,
-        out_specs=(pl.BlockSpec(memory_space=pl.ANY), VMEM, VMEM),
+        in_specs=[VMEM] * 7,
+        out_specs=(VMEM,) * 3,
         scratch_shapes=[
+            pltpu.SMEM(spline_owner.shape, jnp.int32),
             pltpu.VMEM((rows, width), f32),
             pltpu.VMEM((panels * struct_rows // TILE, TILE, width), f32),
             pltpu.SemaphoreType.DMA,
@@ -248,7 +248,8 @@
         compiler_params=params,
         cost_estimate=cost(10**6, 2**17),
         name="spline_loads",
-    )(code, part, mirror, gate, near_blocks[0], spline_blocks)
+    )(pair, mirror, code, part, gate, near_blocks[0], spline_blocks)
+    loads = sums.reshape(adjoint.shape) * trim_mask[0].astype(f32)[None, None, :, None]
     got = swap(send, panels, 1)
     send = pl.pallas_call(
         sum_kernel,
@@ -264,7 +265,7 @@
         split_axis=0, concat_axis=0, tiled=True,
         axis_index_groups=[
             [
-                mach * panels + 2 * chip + (parity(2 * chip) ^ which)
+                mach * panels + 2 * chip + (device_class(2 * chip) ^ which)
                 for mach in range(machs)
                 for chip in range(panels // 2)
             ]
@@ -281,7 +282,7 @@
         name="struct_solve",
     )(got, struct_inverse)
     return (
-        loads.reshape(1, block_count, rhs, width),
+        loads,
         struct_adjoint.reshape(struct_count, rhs, width),
     )
 

time: 25.1 us -> 25.7 us (1.024)
  blocking collectives: 12.1 us -> 0 us
  waiting for transfers between devices: 3.15 us -> 9.87 us
  starting transfers between devices: 5.81 us -> 11 us
  other arithmetic: 0 us -> 0.68 us
    all_to_all x1 -> x0, blocking collectives: 12.1 us -> none  [on_device(): lax.all_to_all(send.reshape(machs * panels // 2, struct_rows, width), ('m...]
    all_to_all x0 -> x1, waiting for transfers between devices: none -> 7.11 us  [on_device(): lax.all_to_all(send.reshape(machs * panels // 2, struct_rows, width), ('m...]
    all_to_all x0 -> x1, starting transfers between devices: none -> 5.45 us  [on_device(): lax.all_to_all(send.reshape(machs * panels // 2, struct_rows, width), ('m...]
    ppermute x1, waiting for transfers between devices: 1.91 us -> 0.01 us  [on_device(): lax.ppermute(own, ('mach', 'panel'), [(mach * panels + i, (mach ^ (i in b...]
    ppermute x3, starting transfers between devices: 4.32 us -> 2.52 us  [swap(): return lax.ppermute(value, 'panel', [(i, i ^ apart) for i in range(panels)])]
    ppermute x1, starting transfers between devices: 1.49 us -> 3 us  [on_device(): lax.ppermute(own, ('mach', 'panel'), [(mach * panels + i, (mach ^ (i in b...]
    ppermute x3, waiting for transfers between devices: 1.25 us -> 2.76 us  [swap(): return lax.ppermute(value, 'panel', [(i, i ^ apart) for i in range(panels)])]
    mul x0 -> x1, other arithmetic: none -> 0.68 us  [on_device(): sums.reshape(adjoint.shape) * trim_mask[0].astype(f32)[None, None, :, None]]
  transfers between devices with their start and end apart: 4 -> 5, of which waited for: 2 -> 4; matrix products, arithmetic and copies ran while one was open for 0% -> 3% of each run, Pallas kernels for 3% -> 3%
where the time goes in v12:
time: 25.7 us; the launch traced here: 25.5 us
  starting transfers between devices  11 us (43%)
  waiting for transfers between devices  9.87 us (38%)
  Pallas kernels  3.11 us (12%)
  between operations  0.77 us (3%)
  other arithmetic  0.68 us (3%)
    all_to_all x1, waiting for transfers between devices, on_device(): lax.all_to_all(send.reshape(machs * panels // 2, struct_rows, width), ('m...  7.11 us
    all_to_all x1, starting transfers between devices, on_device(): lax.all_to_all(send.reshape(machs * panels // 2, struct_rows, width), ('m...  5.45 us
    ppermute x1, starting transfers between devices, on_device(): lax.ppermute(own, ('mach', 'panel'), [(mach * panels + i, (mach ^ (i in b...  3 us
    ppermute x3, waiting for transfers between devices, swap(): return lax.ppermute(value, 'panel', [(i, i ^ apart) for i in range(panels)])  2.76 us
    ppermute x3, starting transfers between devices, swap(): return lax.ppermute(value, 'panel', [(i, i ^ apart) for i in range(panels)])  2.52 us
    pallas_call x1, Pallas kernels, on_device(): pl.pallas_call(functools.partial(spline_kernel, rhs), out_shape=(jax.Shap...  0.96 us
    pallas_call x1, Pallas kernels, on_device(): pl.pallas_call(functools.partial(inverse_kernel, rhs), out_shape=jax.Shap...  0.77 us
    mul x1, other arithmetic, on_device(): sums.reshape(adjoint.shape) * trim_mask[0].astype(f32)[None, None, :, None]  0.68 us
  transfers between devices with their start and end apart: 5, of which 4 were waited for; matrix products, arithmetic and copies ran while one was open for 3% of the time, Pallas kernels for 3%

profile of v12, /device:TPU:0, one launch (start us, length us, event | category | flops | bytes accessed | tf_op | source)
XLA Modules:
  0.0 25.5 jit_solution(7464106853637449481)
XLA Ops:
  0.6 0.0 copy-start.2
  0.6 0.0 copy-start.3
  0.7 0.0 copy-start.4
  0.7 0.0 copy-start.5
  0.7 0.0 copy-start.6
  0.7 0.0 copy-start
  0.7 3.0 %collective-permute-start.2 = (bf16[32,128]{1,0:T(8,128)(2,1)}, bf16[32,128]{1,0:T(8,128)(2,1)S(1)}, u32[]{:S(2)}, u32[]{:S(2)}) collective-permute-start(bf16[32,128]{1,0:T(8,128)(2,1)} %bitcast.10), channel_id=1, source_target_pairs={{0,16},{1,2},{2,1},{3,4},{4,3},{5,6},{6,5},{7,8},{8,7},{9,10},{10,... | collective-permute-start | bytes 24584 | tf_op jit(solution)/shard_map/ppermute | solution.py:188
  3.7 1.9 %collective-permute-start.1 = (bf16[32,128]{1,0:T(8,128)(2,1)}, bf16[32,128]{1,0:T(8,128)(2,1)S(1)}, u32[]{:S(2)}, u32[]{:S(2)}) collective-permute-start(bf16[32,128]{1,0:T(8,128)(2,1)} %bitcast.11), channel_id=1, source_target_pairs={{0,8},{1,9},{2,10},{3,11},{4,12},{5,13},{6,14},{7,15},{8,0},{9,1},... | collective-permute-start | bytes 24584 | tf_op jit(solution)/shard_map/ppermute | solution.py:168
  5.6 0.5 %collective-permute-start = (bf16[32,128]{1,0:T(8,128)(2,1)}, bf16[32,128]{1,0:T(8,128)(2,1)S(1)}, u32[]{:S(2)}, u32[]{:S(2)}) collective-permute-start(bf16[32,128]{1,0:T(8,128)(2,1)} %bitcast.12), channel_id=1, source_target_pairs={{0,1},{1,0},{2,3},{3,2},{4,5},{5,4},{6,7},{7,6},{8,9},{9,8},{10,11... | collective-permute-start | bytes 24584 | tf_op jit(solution)/shard_map/ppermute | solution.py:168
  6.2 0.0 copy-done.2
  6.2 0.0 copy-done.3
  6.2 0.0 copy-done.4
  6.2 0.0 copy-done.5
  6.2 0.0 copy-done.6
  6.2 0.0 copy-start.1
  6.2 0.2 pick_rows.1
  6.5 0.0 collective-permute-done.2.cross_ref
  6.5 0.7 %collective-permute-done.pair_ref._ = bf16[32,128]{1,0:T(8,128)(2,1)S(1)} collective-permute-done((bf16[32,128]{1,0:T(8,128)(2,1)}, bf16[32,128]{1,0:T(8,128)(2,1)S(1)}, u32[]{:S(2)}, u32[]{:S(2)}) %collective-permute-start) | collective-permute-done | bytes 8224 | tf_op jit(solution)/shard_map/ppermute | solution.py:168
  7.2 0.0 copy-done
  7.2 0.5 %near_field.1.part_ref = f32[32,128]{1,0:T(8,128)S(1)} custom-call(bf16[192,128]{1,0:T(8,128)(2,1)S(1)} %get-tuple-element.10.hot_ref, bf16[32,128]{1,0:T(8,128)(2,1)S(1)} %get-tuple-element.11.own_ref, bf16[32,128]{1,0:T(8,128)(2,1)S(1)} %collective-permute-done.pair_ref._, bf16[32,128]{1,0:T(8,128)(2,1)S(1)} %collective-permute-done.2.cross_ref, ...), custom_call_target="tpu_custom_call" | custom-call | flops 1000000 | bytes 131072 | tf_op jit(solution)/shard_map/near_field/pallas_call | solution.py:223
  7.6 0.8 %collective-permute-done.1.mirror_ref = bf16[32,128]{1,0:T(8,128)(2,1)S(1)} collective-permute-done((bf16[32,128]{1,0:T(8,128)(2,1)}, bf16[32,128]{1,0:T(8,128)(2,1)S(1)}, u32[]{:S(2)}, u32[]{:S(2)}) %collective-permute-start.1) | collective-permute-done | bytes 8224 | tf_op jit(solution)/shard_map/ppermute | solution.py:168
  8.5 0.0 copy-done.1
  8.5 0.0 copy-start.7
  8.5 1.0 %spline_loads.1 = (f32[32,128]{1,0:T(8,128)S(1)}, f32[8,32,128]{2,1,0:T(8,128)S(1)}, bf16[8,32,128]{2,1,0:T(8,128)(2,1)S(1)}) custom-call(bf16[32,128]{1,0:T(8,128)(2,1)S(1)} %collective-permute-done.pair_ref._, bf16[32,128]{1,0:T(8,128)(2,1)S(1)} %collective-permute-done.1.mirror_ref, s32[8,6]{1,0:T(8,128)S(1)} %get-tuple-element.9.code_vmem, ...), custom_call_target="tpu_custom_call" | custom-call | flops 1000000 | bytes 131072 | tf_op jit(solution)/shard_map/spline_loads/pallas_call | solution.py:233
  9.4 0.1 collective-permute-start.3
  9.5 1.2 %collective-permute-done.3.got_ref = bf16[8,32,128]{2,1,0:T(8,128)(2,1)S(1)} collective-permute-done((bf16[8,32,128]{2,1,0:T(8,128)(2,1)S(1)}, bf16[8,32,128]{2,1,0:T(8,128)(2,1)S(1)}, u32[]{:S(2)}, u32[]{:S(2)}) %collective-permute-start.3) | collective-permute-done | bytes 65568 | tf_op jit(solution)/shard_map/ppermute | solution.py:168
  10.7 0.7 %pair_sum.1 = bf16[2,8,32,128]{3,2,1,0:T(8,128)(2,1)} custom-call(f32[8,32,128]{2,1,0:T(8,128)S(1)} %get-tuple-element.14.held_ref, bf16[8,32,128]{2,1,0:T(8,128)(2,1)S(1)} %collective-permute-done.3.got_ref), custom_call_target="tpu_custom_call" | custom-call | flops 1000000 | bytes 1048576 | tf_op jit(solution)/shard_map/pair_sum/pallas_call | solution.py:254
  11.4 5.5 %all-to-all-start = ((bf16[16,32,128]{2,1,0:T(8,128)(2,1)}), bf16[16,32,128]{2,1,0:T(8,128)(2,1)S(1)}, u32[]{:S(2)}, u32[]{:S(2)}) async-start(bf16[16,32,128]{2,1,0:T(8,128)(2,1)} %bitcast.4), calls=%async_computation | async-start | bytes 262144 | tf_op jit(solution)/shard_map/all_to_all | solution.py:263
  16.9 0.7 %broadcast_multiply_fusion = f32[1,8,4,128]{3,2,1,0:T(4,128)} fusion(f32[1,8,4,128]{3,2,1,0:T(4,128)S(1)} %bitcast.9, f32[4]{0:T(128)S(1)} %convert_bitcast_fusion), kind=kLoop, calls=%fused_computation | loop fusion | flops 4096 | bytes 32784 | tf_op jit(solution)/shard_map/mul | solution.py:252
  17.6 7.1 %all-to-all-done.got_ref = bf16[16,32,128]{2,1,0:T(8,128)(2,1)S(1)} async-done(((bf16[16,32,128]{2,1,0:T(8,128)(2,1)}), bf16[16,32,128]{2,1,0:T(8,128)(2,1)S(1)}, u32[]{:S(2)}, u32[]{:S(2)}) %all-to-all-start) | async-done | bytes 131104 | tf_op jit(solution)/shard_map/all_to_all | solution.py:263
  24.7 0.0 copy-done.7
  24.7 0.8 %struct_solve.1 = f32[32,128]{1,0:T(8,128)} custom-call(bf16[16,32,128]{2,1,0:T(8,128)(2,1)S(1)} %all-to-all-done.got_ref, bf16[8,128,128]{2,1,0:T(8,128)(2,1)S(1)} %copy-done.7), custom_call_target="tpu_custom_call" | custom-call | flops 1000000000 | bytes 1048576 | tf_op jit(solution)/shard_map/struct_solve/pallas_call | solution.py:275
  (2 shorter events, 0.0 us)
Async XLA Ops:
  0.6 5.5 %copy-start.2 = (bf16[1,8,4,128]{3,2,1,0:T(4,128)(2,1)S(1)}, bf16[1,8,4,128]{3,2,1,0:T(4,128)(2,1)}, u32[]{:S(2)}) copy-start(bf16[1,8,4,128]{3,2,1,0:T(4,128)(2,1)} %param.8) | copy-start | bytes 24580
  0.6 5.5 %copy-start.3 = (s32[8,8]{1,0:T(8,128)S(1)}, s32[8,8]{1,0:T(8,128)}, u32[]{:S(2)}) copy-start(s32[8,8]{1,0:T(8,128)} %pattern_ref.1) | copy-start | bytes 772
  0.7 5.5 %copy-start.4 = (s32[8,6]{1,0:T(8,128)S(1)}, s32[8,6]{1,0:T(8,128)}, u32[]{:S(2)}) copy-start(s32[8,6]{1,0:T(8,128)} %owner_ref.1) | copy-start | bytes 580
  0.7 5.5 %copy-start.5 = (s32[8,6]{1,0:T(8,128)S(1)}, s32[8,6]{1,0:T(8,128)}, u32[]{:S(2)}) copy-start(s32[8,6]{1,0:T(8,128)} %local_ref.1) | copy-start | bytes 580
  0.7 5.5 %copy-start.6 = (s32[1,4]{1,0:T(1,128)S(1)}, s32[1,4]{1,0:T(1,128)}, u32[]{:S(2)}) copy-start(s32[1,4]{1,0:T(1,128)} %trim_ref.1) | copy-start | bytes 52
  0.7 6.5 %copy-start = (bf16[1,8,8,128,128]{4,3,2,1,0:T(8,128)(2,1)S(1)}, bf16[1,8,8,128,128]{4,3,2,1,0:T(8,128)(2,1)}, u32[]{:S(2)}) copy-start(bf16[1,8,8,128,128]{4,3,2,1,0:T(8,128)(2,1)} %param.9) | copy-start | bytes 6291460
  0.7 5.8 %collective-permute-start.2 = (bf16[32,128]{1,0:T(8,128)(2,1)}, bf16[32,128]{1,0:T(8,128)(2,1)S(1)}, u32[]{:S(2)}, u32[]{:S(2)}) collective-permute-start(bf16[32,128]{1,0:T(8,128)(2,1)} %bitcast.10), channel_id=1, source_target_pairs={{0,16},{1,2},{2,1},{3,4},{4,3},{5,6},{6,5},{7,8},{8,7},{9,10},{10,... | collective-permute-start | bytes 24584 | tf_op jit(solution)/shard_map/ppermute | solution.py:188
  3.7 4.8 %collective-permute-start.1 = (bf16[32,128]{1,0:T(8,128)(2,1)}, bf16[32,128]{1,0:T(8,128)(2,1)S(1)}, u32[]{:S(2)}, u32[]{:S(2)}) collective-permute-start(bf16[32,128]{1,0:T(8,128)(2,1)} %bitcast.11), channel_id=1, source_target_pairs={{0,8},{1,9},{2,10},{3,11},{4,12},{5,13},{6,14},{7,15},{8,0},{9,1},... | collective-permute-start | bytes 24584 | tf_op jit(solution)/shard_map/ppermute | solution.py:168
  5.6 1.5 %collective-permute-start = (bf16[32,128]{1,0:T(8,128)(2,1)}, bf16[32,128]{1,0:T(8,128)(2,1)S(1)}, u32[]{:S(2)}, u32[]{:S(2)}) collective-permute-start(bf16[32,128]{1,0:T(8,128)(2,1)} %bitcast.12), channel_id=1, source_target_pairs={{0,1},{1,0},{2,3},{3,2},{4,5},{5,4},{6,7},{7,6},{8,9},{9,8},{10,11... | collective-permute-start | bytes 24584 | tf_op jit(solution)/shard_map/ppermute | solution.py:168
  6.2 2.3 %copy-start.1 = (bf16[8,6,128,128]{3,2,1,0:T(8,128)(2,1)S(1)}, bf16[8,6,128,128]{3,2,1,0:T(8,128)(2,1)}, u32[]{:S(2)}) copy-start(bf16[8,6,128,128]{3,2,1,0:T(8,128)(2,1)} %spline_ref.1) | copy-start | bytes 4718596
  8.5 16.2 %copy-start.7 = (bf16[8,128,128]{2,1,0:T(8,128)(2,1)S(1)}, bf16[8,128,128]{2,1,0:T(8,128)(2,1)}, u32[]{:S(2)}) copy-start(bf16[8,128,128]{2,1,0:T(8,128)(2,1)} %inverse_ref.1) | copy-start | bytes 786436
  9.4 1.3 %collective-permute-start.3 = (bf16[8,32,128]{2,1,0:T(8,128)(2,1)S(1)}, bf16[8,32,128]{2,1,0:T(8,128)(2,1)S(1)}, u32[]{:S(2)}, u32[]{:S(2)}) collective-permute-start(bf16[8,32,128]{2,1,0:T(8,128)(2,1)S(1)} %get-tuple-element.15), channel_id=1, source_target_pairs={{0,1},{1,0},{2,3},{3,2},{4,5},{5,4},{6,7},{7,6},{8,9},{9,8},{10,11... | collective-permute-start | bytes 196616 | tf_op jit(solution)/shard_map/ppermute | solution.py:168
  11.4 13.3 %all-to-all-start = ((bf16[16,32,128]{2,1,0:T(8,128)(2,1)}), bf16[16,32,128]{2,1,0:T(8,128)(2,1)S(1)}, u32[]{:S(2)}, u32[]{:S(2)}) async-start(bf16[16,32,128]{2,1,0:T(8,128)(2,1)} %bitcast.4), calls=%async_computation | async-start | bytes 262144 | tf_op jit(solution)/shard_map/all_to_all | solution.py:263

commit v13 on v11

--- a/solution.py
+++ b/solution.py
@@ -57,7 +57,9 @@
     held_ref[...] = own_ref[...]
     owner = owner_ref[...]
     code_ref[...] = (
-        (device_class(owner) ^ device_class(here)) * (panels // 2) + ((owner ^ here) >> 1)
+        (device_class(owner) ^ device_class(here)) * (panels // 2)
+        + (owner >> 2) * 2
+        + (((owner ^ here) >> 1) & 1)
     ) * struct_count + local_ref[...]
 
 
@@ -145,20 +147,17 @@
     send_ref[...] = acc[tiles:].reshape(send_ref.shape).astype(send_ref.dtype)
 
 
-def split_kernel(held_ref, got_ref, *out_refs):
-    size = out_refs[0].shape[0]
-    for step, out_ref in enumerate(out_refs):
-        for place in range(size):
-            total = held_ref[step * size + place] + got_ref[step * size + place].astype(jnp.float32)
-            out_ref[place] = total.astype(out_ref.dtype)
-
-
-def column_kernel(machs, held_ref, *refs):
-    got_refs, out_refs = refs[: -2 * machs], refs[-2 * machs :]
+def sum_kernel(held_ref, got_ref, out_ref):
+    for place in range(held_ref.shape[0]):
+        total = held_ref[place] + got_ref[place].astype(jnp.float32)
+        out_ref[place] = total.astype(out_ref.dtype)
+
+
+def column_kernel(machs, got_ref, *out_refs):
     for place in range(2):
-        total = held_ref[place]
-        for got_ref in got_refs:
-            total = total + got_ref[place].astype(jnp.float32)
+        total = got_ref[place].astype(jnp.float32)
+        for source in range(place + 2, got_ref.shape[0], 2):
+            total = total + got_ref[source].astype(jnp.float32)
         for out_ref in out_refs[place * machs : (place + 1) * machs]:
             out_ref[...] = total.astype(out_ref.dtype)
 
@@ -273,32 +272,31 @@
     )(pair, mirror, code, part, gate, near_blocks[0], spline_blocks)
     loads = sums.reshape(adjoint.shape) * trim_mask[0].astype(f32)[None, None, :, None]
     got = swap(send, panels, 1)
-    steps = panels // 4
-    two = (2, struct_rows, width)
-    keep, *sends = pl.pallas_call(
-        split_kernel,
-        out_shape=tuple(
-            jax.ShapeDtypeStruct(two, f32 if step == 0 else bf16) for step in range(steps)
-        ),
+    send = pl.pallas_call(
+        sum_kernel,
+        out_shape=jax.ShapeDtypeStruct(half, bf16),
         in_specs=[VMEM, VMEM],
-        out_specs=(VMEM,) * steps,
+        out_specs=VMEM,
         compiler_params=params,
         cost_estimate=cost(10**6, 2**17),
         name="pair_sum",
     )(keep, got)
-    got = [
-        swap(sends[step - 1], panels, 4 * step + step % 2) for step in range(steps - 1, 0, -1)
-    ]
+    got = lax.all_to_all(
+        send, "panel", split_axis=0, concat_axis=0, tiled=True,
+        axis_index_groups=[
+            [4 * far + (start ^ (far & 1)) for far in range(panels // 4)] for start in range(4)
+        ],
+    )
     one = jax.ShapeDtypeStruct((struct_rows, width), f32)
     columns = pl.pallas_call(
         functools.partial(column_kernel, machs),
         out_shape=(one,) * (2 * machs),
-        in_specs=[VMEM] * steps,
+        in_specs=[VMEM],
         out_specs=(VMEM,) * (2 * machs),
         compiler_params=params,
         cost_estimate=cost(10**6, 2**17),
         name="column_sum",
-    )(keep, *got)
+    )(got)
     sames = [
         mach_swap(columns[turn], machs, panels, turn, 0) if turn else columns[0]
         for turn in range(machs)

time: 24 us -> 27.2 us (1.13)
  waiting for transfers between devices: 7.41 us -> 9.83 us
  Pallas kernels: 2.46 us -> 3.08 us
    all_to_all x0 -> x1, waiting for transfers between devices: none -> 5.19 us  [on_device(): lax.all_to_all(send, 'panel', split_axis=0, concat_axis=0, tiled=True, ax...]
    all_to_all x0 -> x1, starting transfers between devices: none -> 3.99 us  [on_device(): lax.all_to_all(send, 'panel', split_axis=0, concat_axis=0, tiled=True, ax...]
    ppermute x6 -> x3, starting transfers between devices: 6.42 us -> 2.52 us  [swap(): return lax.ppermute(value, 'panel', [(i, i ^ apart) for i in range(panels)])]
    ppermute x6 -> x3, waiting for transfers between devices: 6.28 us -> 2.76 us  [swap(): return lax.ppermute(value, 'panel', [(i, i ^ apart) for i in range(panels)])]
    ppermute x3, waiting for transfers between devices: 1.13 us -> 1.88 us  [mach_swap(): return lax.ppermute(value, ('mach', 'panel'), pairs)]
    pallas_call x1, Pallas kernels: 0.02 us -> 0.64 us  [on_device(): pl.pallas_call(sum_kernel, out_shape=jax.ShapeDtypeStruct(half, bf16), in...]
  transfers between devices with their start and end apart: 10 -> 8, of which waited for: 8 -> 7; matrix products, arithmetic and copies ran while one was open for 3% -> 3% of each run, Pallas kernels for 3% -> 3%
where the time goes in v13:
time: 27.2 us; the launch traced here: 26.9 us
  starting transfers between devices  12.5 us (46%)
  waiting for transfers between devices  9.83 us (36%)
  Pallas kernels  3.08 us (11%)
  between operations  0.77 us (3%)
  other arithmetic  0.68 us (2%)
    all_to_all x1, waiting for transfers between devices, on_device(): lax.all_to_all(send, 'panel', split_axis=0, concat_axis=0, tiled=True, ax...  5.19 us
    all_to_all x1, starting transfers between devices, on_device(): lax.all_to_all(send, 'panel', split_axis=0, concat_axis=0, tiled=True, ax...  3.99 us
    ppermute x1, starting transfers between devices, on_device(): lax.ppermute(own, ('mach', 'panel'), [(mach * panels + i, (mach ^ (i in b...  3 us
    ppermute x3, starting transfers between devices, mach_swap(): return lax.ppermute(value, ('mach', 'panel'), pairs)  2.99 us
    ppermute x3, waiting for transfers between devices, swap(): return lax.ppermute(value, 'panel', [(i, i ^ apart) for i in range(panels)])  2.76 us
    ppermute x3, starting transfers between devices, swap(): return lax.ppermute(value, 'panel', [(i, i ^ apart) for i in range(panels)])  2.52 us
    ppermute x3, waiting for transfers between devices, mach_swap(): return lax.ppermute(value, ('mach', 'panel'), pairs)  1.88 us
    pallas_call x1, Pallas kernels, on_device(): pl.pallas_call(functools.partial(spline_kernel, rhs), out_shape=(jax.Shap...  0.95 us
  transfers between devices with their start and end apart: 8, of which 7 were waited for; matrix products, arithmetic and copies ran while one was open for 3% of the time, Pallas kernels for 3%

profile of v13, /device:TPU:0, one launch (start us, length us, event | category | flops | bytes accessed | tf_op | source)
XLA Modules:
  0.0 26.9 jit_solution(9269297848496688077)
XLA Ops:
  0.6 0.0 copy-start.3
  0.6 0.0 copy-start.4
  0.7 0.0 copy-start.5
  0.7 0.0 copy-start.6
  0.7 3.0 %collective-permute-start.2 = (bf16[32,128]{1,0:T(8,128)(2,1)}, bf16[32,128]{1,0:T(8,128)(2,1)S(1)}, u32[]{:S(2)}, u32[]{:S(2)}) collective-permute-start(bf16[32,128]{1,0:T(8,128)(2,1)} %bitcast.9), channel_id=1, source_target_pairs={{0,16},{1,2},{2,1},{3,4},{4,3},{5,6},{6,5},{7,8},{8,7},{9,10},{10,... | collective-permute-start | bytes 24584 | tf_op jit(solution)/shard_map/ppermute | solution.py:209
  3.7 1.9 %collective-permute-start.1 = (bf16[32,128]{1,0:T(8,128)(2,1)}, bf16[32,128]{1,0:T(8,128)(2,1)S(1)}, u32[]{:S(2)}, u32[]{:S(2)}) collective-permute-start(bf16[32,128]{1,0:T(8,128)(2,1)} %bitcast.10), channel_id=1, source_target_pairs={{0,8},{1,9},{2,10},{3,11},{4,12},{5,13},{6,14},{7,15},{8,0},{9,1},... | collective-permute-start | bytes 24584 | tf_op jit(solution)/shard_map/ppermute | solution.py:180
  5.6 0.5 %collective-permute-start = (bf16[32,128]{1,0:T(8,128)(2,1)}, bf16[32,128]{1,0:T(8,128)(2,1)S(1)}, u32[]{:S(2)}, u32[]{:S(2)}) collective-permute-start(bf16[32,128]{1,0:T(8,128)(2,1)} %bitcast.11), channel_id=1, source_target_pairs={{0,1},{1,0},{2,3},{3,2},{4,5},{5,4},{6,7},{7,6},{8,9},{9,8},{10,11... | collective-permute-start | bytes 24584 | tf_op jit(solution)/shard_map/ppermute | solution.py:180
  6.2 0.0 copy-done.4
  6.2 0.0 copy-done.5
  6.2 0.0 copy-done.6
  6.2 0.0 copy-done.7
  6.2 0.0 copy-start.1
  6.2 0.2 pick_rows.1
  6.5 0.0 collective-permute-done.2.cross_ref
  6.5 0.7 %collective-permute-done.pair_ref._ = bf16[32,128]{1,0:T(8,128)(2,1)S(1)} collective-permute-done((bf16[32,128]{1,0:T(8,128)(2,1)}, bf16[32,128]{1,0:T(8,128)(2,1)S(1)}, u32[]{:S(2)}, u32[]{:S(2)}) %collective-permute-start) | collective-permute-done | bytes 8224 | tf_op jit(solution)/shard_map/ppermute | solution.py:180
  7.2 0.0 copy-done
  7.2 0.5 %near_field.1.part_ref = f32[32,128]{1,0:T(8,128)S(1)} custom-call(bf16[192,128]{1,0:T(8,128)(2,1)S(1)} %get-tuple-element.14.hot_ref, bf16[32,128]{1,0:T(8,128)(2,1)S(1)} %get-tuple-element.15.own_ref, bf16[32,128]{1,0:T(8,128)(2,1)S(1)} %collective-permute-done.pair_ref._, bf16[32,128]{1,0:T(8,128)(2,1)S(1)} %collective-permute-done.2.cross_ref, ...), custom_call_target="tpu_custom_call" | custom-call | flops 1000000 | bytes 131072 | tf_op jit(solution)/shard_map/near_field/pallas_call | solution.py:244
  7.6 0.8 %collective-permute-done.1.mirror_ref = bf16[32,128]{1,0:T(8,128)(2,1)S(1)} collective-permute-done((bf16[32,128]{1,0:T(8,128)(2,1)}, bf16[32,128]{1,0:T(8,128)(2,1)S(1)}, u32[]{:S(2)}, u32[]{:S(2)}) %collective-permute-start.1) | collective-permute-done | bytes 8224 | tf_op jit(solution)/shard_map/ppermute | solution.py:180
  8.5 1.0 %spline_loads.1 = (f32[32,128]{1,0:T(8,128)S(1)}, f32[8,32,128]{2,1,0:T(8,128)S(1)}, bf16[8,32,128]{2,1,0:T(8,128)(2,1)S(1)}) custom-call(bf16[32,128]{1,0:T(8,128)(2,1)S(1)} %collective-permute-done.pair_ref._, bf16[32,128]{1,0:T(8,128)(2,1)S(1)} %collective-permute-done.1.mirror_ref, s32[8,6]{1,0:T(8,128)S(1)} %get-tuple-element.13.code_vmem, ...), custom_call_target="tpu_custom_call" | custom-call | flops 1000000 | bytes 131072 | tf_op jit(solution)/shard_map/spline_loads/pallas_call | solution.py:254
  9.4 0.1 collective-permute-start.3
  9.5 1.2 %collective-permute-done.3.got_ref = bf16[8,32,128]{2,1,0:T(8,128)(2,1)S(1)} collective-permute-done((bf16[8,32,128]{2,1,0:T(8,128)(2,1)S(1)}, bf16[8,32,128]{2,1,0:T(8,128)(2,1)S(1)}, u32[]{:S(2)}, u32[]{:S(2)}) %collective-permute-start.3) | collective-permute-done | bytes 65568 | tf_op jit(solution)/shard_map/ppermute | solution.py:180
  10.7 0.6 %pair_sum.1 = bf16[8,32,128]{2,1,0:T(8,128)(2,1)} custom-call(f32[8,32,128]{2,1,0:T(8,128)S(1)} %get-tuple-element.18.held_ref, bf16[8,32,128]{2,1,0:T(8,128)(2,1)S(1)} %collective-permute-done.3.got_ref), custom_call_target="tpu_custom_call" | custom-call | flops 1000000 | bytes 131072 | tf_op jit(solution)/shard_map/pair_sum/pallas_call | solution.py:275
  11.4 4.0 %all-to-all-start = ((bf16[8,32,128]{2,1,0:T(8,128)(2,1)}), bf16[8,32,128]{2,1,0:T(8,128)(2,1)S(1)}, u32[]{:S(2)}, u32[]{:S(2)}) async-start(bf16[8,32,128]{2,1,0:T(8,128)(2,1)} %pair_sum.1), calls=%async_computation | async-start | bytes 131072 | tf_op jit(solution)/shard_map/all_to_all | solution.py:284
  15.4 5.2 %all-to-all-done.got_ref = bf16[8,32,128]{2,1,0:T(8,128)(2,1)S(1)} async-done(((bf16[8,32,128]{2,1,0:T(8,128)(2,1)}), bf16[8,32,128]{2,1,0:T(8,128)(2,1)S(1)}, u32[]{:S(2)}, u32[]{:S(2)}) %all-to-all-start) | async-done | bytes 65568 | tf_op jit(solution)/shard_map/all_to_all | solution.py:284
  20.6 1.7 %collective-permute-start.4 = (f32[32,128]{1,0:T(8,128)S(1)}, f32[32,128]{1,0:T(8,128)S(1)}, u32[]{:S(2)}, u32[]{:S(2)}) collective-permute-start(f32[32,128]{1,0:T(8,128)S(1)} %get-tuple-element.20), channel_id=1, source_target_pairs={{0,19},{1,18},{2,17},{3,16},{4,23},{5,22},{6,21},{7,20},{8,27},{9,... | collective-permute-start | bytes 49160 | tf_op jit(solution)/shard_map/ppermute | solution.py:189
  22.3 0.6 %collective-permute-start.5 = (f32[32,128]{1,0:T(8,128)S(1)}, f32[32,128]{1,0:T(8,128)S(1)}, u32[]{:S(2)}, u32[]{:S(2)}) collective-permute-start(f32[32,128]{1,0:T(8,128)S(1)} %get-tuple-element.21), channel_id=1, source_target_pairs={{0,16},{1,17},{2,18},{3,19},{4,20},{5,21},{6,22},{7,23},{8,24},{9,... | collective-permute-start | bytes 49160 | tf_op jit(solution)/shard_map/ppermute | solution.py:189
  22.9 0.7 %collective-permute-start.6 = (f32[32,128]{1,0:T(8,128)S(1)}, f32[32,128]{1,0:T(8,128)S(1)}, u32[]{:S(2)}, u32[]{:S(2)}) collective-permute-start(f32[32,128]{1,0:T(8,128)S(1)} %get-tuple-element.22), channel_id=1, source_target_pairs={{0,3},{1,2},{2,1},{3,0},{4,7},{5,6},{6,5},{7,4},{8,11},{9,10},{10,... | collective-permute-start | bytes 49160 | tf_op jit(solution)/shard_map/ppermute | solution.py:189
  23.6 0.7 %broadcast_multiply_fusion = f32[1,8,4,128]{3,2,1,0:T(4,128)} fusion(f32[1,8,4,128]{3,2,1,0:T(4,128)S(1)} %bitcast.8, f32[4]{0:T(128)S(1)} %convert_bitcast_fusion), kind=kLoop, calls=%fused_computation | loop fusion | flops 4096 | bytes 32784 | tf_op jit(solution)/shard_map/mul | solution.py:273
  24.3 0.5 %collective-permute-done.4.refs_0_ = f32[32,128]{1,0:T(8,128)S(1)} collective-permute-done((f32[32,128]{1,0:T(8,128)S(1)}, f32[32,128]{1,0:T(8,128)S(1)}, u32[]{:S(2)}, u32[]{:S(2)}) %collective-permute-start.4) | collective-permute-done | bytes 16416 | tf_op jit(solution)/shard_map/ppermute | solution.py:189
  24.7 1.3 %collective-permute-done.5.refs_1_ = f32[32,128]{1,0:T(8,128)S(1)} collective-permute-done((f32[32,128]{1,0:T(8,128)S(1)}, f32[32,128]{1,0:T(8,128)S(1)}, u32[]{:S(2)}, u32[]{:S(2)}) %collective-permute-start.5) | collective-permute-done | bytes 16416 | tf_op jit(solution)/shard_map/ppermute | solution.py:189
  26.0 0.1 collective-permute-done.6.refs_2_
  26.1 0.8 %struct_solve.1 = f32[32,128]{1,0:T(8,128)} custom-call(f32[32,128]{1,0:T(8,128)S(1)} %collective-permute-done.4.refs_0_, f32[32,128]{1,0:T(8,128)S(1)} %collective-permute-done.5.refs_1_, f32[32,128]{1,0:T(8,128)S(1)} %collective-permute-done.6.refs_2_, f32[32,128]{1,0:T(8,128)S(1)} %get-tuple-element.23.refs_3_, bf16[8,128,128]{2,1,0:T(8,128)(2,1)S(1)} %copy-done.2), custom_call_target="tpu_custom_call" | custom-call | flops 1000000 | bytes 131072 | tf_op jit(solution)/shard_map/struct_solve/pallas_call | solution.py:305
  (9 shorter events, 0.0 us)
Async XLA Ops:
  0.6 5.5 %copy-start.3 = (bf16[1,8,4,128]{3,2,1,0:T(4,128)(2,1)S(1)}, bf16[1,8,4,128]{3,2,1,0:T(4,128)(2,1)}, u32[]{:S(2)}) copy-start(bf16[1,8,4,128]{3,2,1,0:T(4,128)(2,1)} %param.8) | copy-start | bytes 24580
  0.6 5.5 %copy-start.4 = (s32[8,8]{1,0:T(8,128)S(1)}, s32[8,8]{1,0:T(8,128)}, u32[]{:S(2)}) copy-start(s32[8,8]{1,0:T(8,128)} %pattern_ref.1) | copy-start | bytes 772
  0.7 5.5 %copy-start.5 = (s32[8,6]{1,0:T(8,128)S(1)}, s32[8,6]{1,0:T(8,128)}, u32[]{:S(2)}) copy-start(s32[8,6]{1,0:T(8,128)} %owner_ref.1) | copy-start | bytes 580
  0.7 5.5 %copy-start.6 = (s32[8,6]{1,0:T(8,128)S(1)}, s32[8,6]{1,0:T(8,128)}, u32[]{:S(2)}) copy-start(s32[8,6]{1,0:T(8,128)} %local_ref.1) | copy-start | bytes 580
  0.7 5.5 %copy-start.7 = (s32[1,4]{1,0:T(1,128)S(1)}, s32[1,4]{1,0:T(1,128)}, u32[]{:S(2)}) copy-start(s32[1,4]{1,0:T(1,128)} %trim_ref.1) | copy-start | bytes 52
  0.7 6.5 %copy-start = (bf16[1,8,8,128,128]{4,3,2,1,0:T(8,128)(2,1)S(1)}, bf16[1,8,8,128,128]{4,3,2,1,0:T(8,128)(2,1)}, u32[]{:S(2)}) copy-start(bf16[1,8,8,128,128]{4,3,2,1,0:T(8,128)(2,1)} %param.9) | copy-start | bytes 6291460
  0.7 5.8 %collective-permute-start.2 = (bf16[32,128]{1,0:T(8,128)(2,1)}, bf16[32,128]{1,0:T(8,128)(2,1)S(1)}, u32[]{:S(2)}, u32[]{:S(2)}) collective-permute-start(bf16[32,128]{1,0:T(8,128)(2,1)} %bitcast.9), channel_id=1, source_target_pairs={{0,16},{1,2},{2,1},{3,4},{4,3},{5,6},{6,5},{7,8},{8,7},{9,10},{10,... | collective-permute-start | bytes 24584 | tf_op jit(solution)/shard_map/ppermute | solution.py:209
  3.7 4.8 %collective-permute-start.1 = (bf16[32,128]{1,0:T(8,128)(2,1)}, bf16[32,128]{1,0:T(8,128)(2,1)S(1)}, u32[]{:S(2)}, u32[]{:S(2)}) collective-permute-start(bf16[32,128]{1,0:T(8,128)(2,1)} %bitcast.10), channel_id=1, source_target_pairs={{0,8},{1,9},{2,10},{3,11},{4,12},{5,13},{6,14},{7,15},{8,0},{9,1},... | collective-permute-start | bytes 24584 | tf_op jit(solution)/shard_map/ppermute | solution.py:180
  5.6 1.5 %collective-permute-start = (bf16[32,128]{1,0:T(8,128)(2,1)}, bf16[32,128]{1,0:T(8,128)(2,1)S(1)}, u32[]{:S(2)}, u32[]{:S(2)}) collective-permute-start(bf16[32,128]{1,0:T(8,128)(2,1)} %bitcast.11), channel_id=1, source_target_pairs={{0,1},{1,0},{2,3},{3,2},{4,5},{5,4},{6,7},{7,6},{8,9},{9,8},{10,11... | collective-permute-start | bytes 24584 | tf_op jit(solution)/shard_map/ppermute | solution.py:180
  6.2 2.3 %copy-start.1 = (bf16[8,6,128,128]{3,2,1,0:T(8,128)(2,1)S(1)}, bf16[8,6,128,128]{3,2,1,0:T(8,128)(2,1)}, u32[]{:S(2)}) copy-start(bf16[8,6,128,128]{3,2,1,0:T(8,128)(2,1)} %spline_ref.1) | copy-start | bytes 4718596
  8.5 17.7 %copy-start.2 = (bf16[8,128,128]{2,1,0:T(8,128)(2,1)S(1)}, bf16[8,128,128]{2,1,0:T(8,128)(2,1)}, u32[]{:S(2)}) copy-start(bf16[8,128,128]{2,1,0:T(8,128)(2,1)} %refs_4_.1) | copy-start | bytes 786436
  9.4 1.3 %collective-permute-start.3 = (bf16[8,32,128]{2,1,0:T(8,128)(2,1)S(1)}, bf16[8,32,128]{2,1,0:T(8,128)(2,1)S(1)}, u32[]{:S(2)}, u32[]{:S(2)}) collective-permute-start(bf16[8,32,128]{2,1,0:T(8,128)(2,1)S(1)} %get-tuple-element.19), channel_id=1, source_target_pairs={{0,1},{1,0},{2,3},{3,2},{4,5},{5,4},{6,7},{7,6},{8,9},{9,8},{10,11... | collective-permute-start | bytes 196616 | tf_op jit(solution)/shard_map/ppermute | solution.py:180
  11.4 9.2 %all-to-all-start = ((bf16[8,32,128]{2,1,0:T(8,128)(2,1)}), bf16[8,32,128]{2,1,0:T(8,128)(2,1)S(1)}, u32[]{:S(2)}, u32[]{:S(2)}) async-start(bf16[8,32,128]{2,1,0:T(8,128)(2,1)} %pair_sum.1), calls=%async_computation | async-start | bytes 131072 | tf_op jit(solution)/shard_map/all_to_all | solution.py:284
  20.6 4.1 %collective-permute-start.4 = (f32[32,128]{1,0:T(8,128)S(1)}, f32[32,128]{1,0:T(8,128)S(1)}, u32[]{:S(2)}, u32[]{:S(2)}) collective-permute-start(f32[32,128]{1,0:T(8,128)S(1)} %get-tuple-element.20), channel_id=1, source_target_pairs={{0,19},{1,18},{2,17},{3,16},{4,23},{5,22},{6,21},{7,20},{8,27},{9,... | collective-permute-start | bytes 49160 | tf_op jit(solution)/shard_map/ppermute | solution.py:189
  22.3 3.7 %collective-permute-start.5 = (f32[32,128]{1,0:T(8,128)S(1)}, f32[32,128]{1,0:T(8,128)S(1)}, u32[]{:S(2)}, u32[]{:S(2)}) collective-permute-start(f32[32,128]{1,0:T(8,128)S(1)} %get-tuple-element.21), channel_id=1, source_target_pairs={{0,16},{1,17},{2,18},{3,19},{4,20},{5,21},{6,22},{7,23},{8,24},{9,... | collective-permute-start | bytes 49160 | tf_op jit(solution)/shard_map/ppermute | solution.py:189
  22.9 3.3 %collective-permute-start.6 = (f32[32,128]{1,0:T(8,128)S(1)}, f32[32,128]{1,0:T(8,128)S(1)}, u32[]{:S(2)}, u32[]{:S(2)}) collective-permute-start(f32[32,128]{1,0:T(8,128)S(1)} %get-tuple-element.22), channel_id=1, source_target_pairs={{0,3},{1,2},{2,1},{3,0},{4,7},{5,6},{6,5},{7,4},{8,11},{9,10},{10,... | collective-permute-start | bytes 49160 | tf_op jit(solution)/shard_map/ppermute | solution.py:189

commit v14 on v11

--- a/solution.py
+++ b/solution.py
@@ -110,8 +110,8 @@
     acc[...] = jnp.zeros(acc.shape, jnp.float32)
     upper = lax.broadcasted_iota(jnp.int32, (TILE, width), 0) // rhs
     blank = jnp.zeros((TILE, width), jnp.float32)
-    copy.wait()
-    for pair in range(0, block_count, 2):
+
+    def pair_product(pair):
         both = loads_ref[pair * rhs : (pair + 2) * rhs]
         turned = pltpu.roll(both, rhs, 0)
         mine = jnp.concatenate(
@@ -128,7 +128,13 @@
             ],
             axis=0,
         )
-        product = jnp.dot(mine, blocks, preferred_element_type=jnp.float32)
+        return jnp.dot(mine, blocks, preferred_element_type=jnp.float32)
+
+    pairs = range(0, block_count, 2)
+    products = {pair: pair_product(pair) for pair in pairs[:-1]}
+    copy.wait()
+    products[pairs[-1]] = pair_product(pairs[-1])
+    for pair, product in products.items():
         for i in (pair, pair + 1):
             total = product[(i - pair) * TILE : (i - pair + 1) * TILE]
             places, sums = [], []

time: 24 us -> 23.9 us (level)
  no operation moved by 1% of the time
where the time goes in v14:
time: 23.9 us; the launch traced here: 23.6 us
  starting transfers between devices  12.4 us (52%)
  waiting for transfers between devices  7.41 us (31%)
  Pallas kernels  2.34 us (10%)
  between operations  0.77 us (3%)
  other arithmetic  0.68 us (3%)
    ppermute x6, starting transfers between devices, swap(): return lax.ppermute(value, 'panel', [(i, i ^ apart) for i in range(panels)])  6.42 us
    ppermute x6, waiting for transfers between devices, swap(): return lax.ppermute(value, 'panel', [(i, i ^ apart) for i in range(panels)])  6.28 us
    ppermute x1, starting transfers between devices, on_device(): lax.ppermute(own, ('mach', 'panel'), [(mach * panels + i, (mach ^ (i in b...  3 us
    ppermute x3, starting transfers between devices, mach_swap(): return lax.ppermute(value, ('mach', 'panel'), pairs)  2.99 us
    ppermute x3, waiting for transfers between devices, mach_swap(): return lax.ppermute(value, ('mach', 'panel'), pairs)  1.13 us
    pallas_call x1, Pallas kernels, on_device(): pl.pallas_call(functools.partial(spline_kernel, rhs), out_shape=(jax.Shap...  0.84 us
    pallas_call x1, Pallas kernels, on_device(): pl.pallas_call(functools.partial(inverse_kernel, rhs, machs), out_shape=j...  0.76 us
    mul x1, other arithmetic, on_device(): sums.reshape(adjoint.shape) * trim_mask[0].astype(f32)[None, None, :, None]  0.68 us
  transfers between devices with their start and end apart: 10, of which 8 were waited for; matrix products, arithmetic and copies ran while one was open for 3% of the time, Pallas kernels for 3%

profile of v14, /device:TPU:0, one launch (start us, length us, event | category | flops | bytes accessed | tf_op | source)
XLA Modules:
  0.0 23.6 jit_solution(9358736410013825343)
XLA Ops:
  0.6 0.0 copy-start.3
  0.6 0.0 copy-start.4
  0.7 0.0 copy-start.5
  0.7 0.0 copy-start.6
  0.7 3.0 %collective-permute-start.2 = (bf16[32,128]{1,0:T(8,128)(2,1)}, bf16[32,128]{1,0:T(8,128)(2,1)S(1)}, u32[]{:S(2)}, u32[]{:S(2)}) collective-permute-start(bf16[32,128]{1,0:T(8,128)(2,1)} %bitcast.9), channel_id=1, source_target_pairs={{0,16},{1,2},{2,1},{3,4},{4,3},{5,6},{6,5},{7,8},{8,7},{9,10},{10,... | collective-permute-start | bytes 24584 | tf_op jit(solution)/shard_map/ppermute | solution.py:216
  3.7 1.9 %collective-permute-start.1 = (bf16[32,128]{1,0:T(8,128)(2,1)}, bf16[32,128]{1,0:T(8,128)(2,1)S(1)}, u32[]{:S(2)}, u32[]{:S(2)}) collective-permute-start(bf16[32,128]{1,0:T(8,128)(2,1)} %bitcast.10), channel_id=1, source_target_pairs={{0,8},{1,9},{2,10},{3,11},{4,12},{5,13},{6,14},{7,15},{8,0},{9,1},... | collective-permute-start | bytes 24584 | tf_op jit(solution)/shard_map/ppermute | solution.py:187
  5.6 0.5 %collective-permute-start = (bf16[32,128]{1,0:T(8,128)(2,1)}, bf16[32,128]{1,0:T(8,128)(2,1)S(1)}, u32[]{:S(2)}, u32[]{:S(2)}) collective-permute-start(bf16[32,128]{1,0:T(8,128)(2,1)} %bitcast.11), channel_id=1, source_target_pairs={{0,1},{1,0},{2,3},{3,2},{4,5},{5,4},{6,7},{7,6},{8,9},{9,8},{10,11... | collective-permute-start | bytes 24584 | tf_op jit(solution)/shard_map/ppermute | solution.py:187
  6.2 0.0 copy-done.3
  6.2 0.0 copy-start.1
  6.2 0.2 %pick_rows.1 = (bf16[192,128]{1,0:T(8,128)(2,1)S(1)}, f32[16,128]{1,0:T(8,128)S(1)}, bf16[32,128]{1,0:T(8,128)(2,1)S(1)}, s32[8,6]{1,0:T(8,128)S(1)}) custom-call(bf16[32,8]{1,0:T(8,128)(2,1)S(1)} %row_order.1.expand_ref, s32[8,8]{1,0:T(8,128)S(1)} %copy-done.4, s32[1,4]{1,0:T(1,128)S(1)} %copy-done.7, bf16[32,128]{1,0:T(8,128)(2,1)S(1)} %bitcast.12, ...), custom_call_target="tpu_custom_call" | custom-call | flops 1000000 | bytes 131072 | tf_op jit(solution)/shard_map/pick_rows/pallas_call | solution.py:237
  6.5 0.0 collective-permute-done.2.cross_ref
  6.5 0.7 %collective-permute-done.pair_ref._ = bf16[32,128]{1,0:T(8,128)(2,1)S(1)} collective-permute-done((bf16[32,128]{1,0:T(8,128)(2,1)}, bf16[32,128]{1,0:T(8,128)(2,1)S(1)}, u32[]{:S(2)}, u32[]{:S(2)}) %collective-permute-start) | collective-permute-done | bytes 8224 | tf_op jit(solution)/shard_map/ppermute | solution.py:187
  7.2 0.5 %near_field.1.part_ref = f32[32,128]{1,0:T(8,128)S(1)} custom-call(bf16[192,128]{1,0:T(8,128)(2,1)S(1)} %get-tuple-element.18.hot_ref, bf16[32,128]{1,0:T(8,128)(2,1)S(1)} %get-tuple-element.19.own_ref, bf16[32,128]{1,0:T(8,128)(2,1)S(1)} %collective-permute-done.pair_ref._, bf16[32,128]{1,0:T(8,128)(2,1)S(1)} %collective-permute-done.2.cross_ref, ...), custom_call_target="tpu_custom_call" | custom-call | flops 1000000 | bytes 131072 | tf_op jit(solution)/shard_map/near_field/pallas_call | solution.py:251
  7.6 0.8 %collective-permute-done.1.mirror_ref = bf16[32,128]{1,0:T(8,128)(2,1)S(1)} collective-permute-done((bf16[32,128]{1,0:T(8,128)(2,1)}, bf16[32,128]{1,0:T(8,128)(2,1)S(1)}, u32[]{:S(2)}, u32[]{:S(2)}) %collective-permute-start.1) | collective-permute-done | bytes 8224 | tf_op jit(solution)/shard_map/ppermute | solution.py:187
  8.5 0.0 copy-done.1
  8.5 0.8 %spline_loads.1 = (f32[32,128]{1,0:T(8,128)S(1)}, f32[8,32,128]{2,1,0:T(8,128)S(1)}, bf16[8,32,128]{2,1,0:T(8,128)(2,1)S(1)}) custom-call(bf16[32,128]{1,0:T(8,128)(2,1)S(1)} %collective-permute-done.pair_ref._, bf16[32,128]{1,0:T(8,128)(2,1)S(1)} %collective-permute-done.1.mirror_ref, s32[8,6]{1,0:T(8,128)S(1)} %get-tuple-element.17.code_vmem, ...), custom_call_target="tpu_custom_call" | custom-call | flops 1000000 | bytes 131072 | tf_op jit(solution)/shard_map/spline_loads/pallas_call | solution.py:261
  9.3 0.1 collective-permute-start.3
  9.4 1.2 %collective-permute-done.3.got_ref = bf16[8,32,128]{2,1,0:T(8,128)(2,1)S(1)} collective-permute-done((bf16[8,32,128]{2,1,0:T(8,128)(2,1)S(1)}, bf16[8,32,128]{2,1,0:T(8,128)(2,1)S(1)}, u32[]{:S(2)}, u32[]{:S(2)}) %collective-permute-start.3) | collective-permute-done | bytes 65568 | tf_op jit(solution)/shard_map/ppermute | solution.py:187
  10.6 2.8 %collective-permute-start.4 = (bf16[2,32,128]{2,1,0:T(8,128)(2,1)S(1)}, bf16[2,32,128]{2,1,0:T(8,128)(2,1)S(1)}, u32[]{:S(2)}, u32[]{:S(2)}) collective-permute-start(bf16[2,32,128]{2,1,0:T(8,128)(2,1)S(1)} %get-tuple-element.25), channel_id=1, source_target_pairs={{0,13},{1,12},{2,15},{3,14},{4,9},{5,8},{6,11},{7,10},{8,5},{9,4},... | collective-permute-start | bytes 49160 | tf_op jit(solution)/shard_map/ppermute | solution.py:187
  13.4 0.0 collective-permute-start.5
  13.4 1.1 %collective-permute-start.6 = (bf16[2,32,128]{2,1,0:T(8,128)(2,1)S(1)}, bf16[2,32,128]{2,1,0:T(8,128)(2,1)S(1)}, u32[]{:S(2)}, u32[]{:S(2)}) collective-permute-start(bf16[2,32,128]{2,1,0:T(8,128)(2,1)S(1)} %get-tuple-element.27), channel_id=1, source_target_pairs={{0,5},{1,4},{2,7},{3,6},{4,1},{5,0},{6,3},{7,2},{8,13},{9,12},{10,... | collective-permute-start | bytes 49160 | tf_op jit(solution)/shard_map/ppermute | solution.py:187
  14.5 1.1 %collective-permute-done.4.refs_0_ = bf16[2,32,128]{2,1,0:T(8,128)(2,1)S(1)} collective-permute-done((bf16[2,32,128]{2,1,0:T(8,128)(2,1)S(1)}, bf16[2,32,128]{2,1,0:T(8,128)(2,1)S(1)}, u32[]{:S(2)}, u32[]{:S(2)}) %collective-permute-start.4) | collective-permute-done | bytes 16416 | tf_op jit(solution)/shard_map/ppermute | solution.py:187
  15.7 2.4 %collective-permute-done.5.refs_1_ = bf16[2,32,128]{2,1,0:T(8,128)(2,1)S(1)} collective-permute-done((bf16[2,32,128]{2,1,0:T(8,128)(2,1)S(1)}, bf16[2,32,128]{2,1,0:T(8,128)(2,1)S(1)}, u32[]{:S(2)}, u32[]{:S(2)}) %collective-permute-start.5) | collective-permute-done | bytes 16416 | tf_op jit(solution)/shard_map/ppermute | solution.py:187
  18.1 0.0 collective-permute-done.6.refs_2_
  18.1 0.6 %collective-permute-start.7 = (f32[32,128]{1,0:T(8,128)S(1)}, f32[32,128]{1,0:T(8,128)S(1)}, u32[]{:S(2)}, u32[]{:S(2)}) collective-permute-start(f32[32,128]{1,0:T(8,128)S(1)} %get-tuple-element.28), channel_id=1, source_target_pairs={{0,19},{1,18},{2,17},{3,16},{4,23},{5,22},{6,21},{7,20},{8,27},{9,... | collective-permute-start | bytes 49160 | tf_op jit(solution)/shard_map/ppermute | solution.py:196
  18.7 1.0 %collective-permute-start.8 = (f32[32,128]{1,0:T(8,128)S(1)}, f32[32,128]{1,0:T(8,128)S(1)}, u32[]{:S(2)}, u32[]{:S(2)}) collective-permute-start(f32[32,128]{1,0:T(8,128)S(1)} %get-tuple-element.29), channel_id=1, source_target_pairs={{0,16},{1,17},{2,18},{3,19},{4,20},{5,21},{6,22},{7,23},{8,24},{9,... | collective-permute-start | bytes 49160 | tf_op jit(solution)/shard_map/ppermute | solution.py:196
  19.7 1.4 %collective-permute-start.9 = (f32[32,128]{1,0:T(8,128)S(1)}, f32[32,128]{1,0:T(8,128)S(1)}, u32[]{:S(2)}, u32[]{:S(2)}) collective-permute-start(f32[32,128]{1,0:T(8,128)S(1)} %get-tuple-element.30), channel_id=1, source_target_pairs={{0,3},{1,2},{2,1},{3,0},{4,7},{5,6},{6,5},{7,4},{8,11},{9,10},{10,... | collective-permute-start | bytes 49160 | tf_op jit(solution)/shard_map/ppermute | solution.py:196
  21.1 0.7 %broadcast_multiply_fusion = f32[1,8,4,128]{3,2,1,0:T(4,128)} fusion(f32[1,8,4,128]{3,2,1,0:T(4,128)S(1)} %bitcast.8, f32[4]{0:T(128)S(1)} %convert_bitcast_fusion), kind=kLoop, calls=%fused_computation | loop fusion | flops 4096 | bytes 32784 | tf_op jit(solution)/shard_map/mul | solution.py:280
  21.8 0.5 %collective-permute-done.7.refs_0_ = f32[32,128]{1,0:T(8,128)S(1)} collective-permute-done((f32[32,128]{1,0:T(8,128)S(1)}, f32[32,128]{1,0:T(8,128)S(1)}, u32[]{:S(2)}, u32[]{:S(2)}) %collective-permute-start.7) | collective-permute-done | bytes 16416 | tf_op jit(solution)/shard_map/ppermute | solution.py:196
  22.2 0.2 collective-permute-done.8.refs_1_
  22.4 0.5 %collective-permute-done.9.refs_2_ = f32[32,128]{1,0:T(8,128)S(1)} collective-permute-done((f32[32,128]{1,0:T(8,128)S(1)}, f32[32,128]{1,0:T(8,128)S(1)}, u32[]{:S(2)}, u32[]{:S(2)}) %collective-permute-start.9) | collective-permute-done | bytes 16416 | tf_op jit(solution)/shard_map/ppermute | solution.py:196
  22.9 0.8 %struct_solve.1 = f32[32,128]{1,0:T(8,128)} custom-call(f32[32,128]{1,0:T(8,128)S(1)} %collective-permute-done.7.refs_0_, f32[32,128]{1,0:T(8,128)S(1)} %collective-permute-done.8.refs_1_, f32[32,128]{1,0:T(8,128)S(1)} %collective-permute-done.9.refs_2_, f32[32,128]{1,0:T(8,128)S(1)} %get-tuple-element.31.refs_3_, bf16[8,128,128]{2,1,0:T(8,128)(2,1)S(1)} %copy-done.2), custom_call_target="tpu_custom_call" | custom-call | flops 1000000 | bytes 131072 | tf_op jit(solution)/shard_map/struct_solve/pallas_call | solution.py:313
  (13 shorter events, 0.1 us)
Async XLA Ops:
  0.6 5.5 %copy-start.3 = (bf16[1,8,4,128]{3,2,1,0:T(4,128)(2,1)S(1)}, bf16[1,8,4,128]{3,2,1,0:T(4,128)(2,1)}, u32[]{:S(2)}) copy-start(bf16[1,8,4,128]{3,2,1,0:T(4,128)(2,1)} %param.8) | copy-start | bytes 24580
  0.6 5.5 %copy-start.4 = (s32[8,8]{1,0:T(8,128)S(1)}, s32[8,8]{1,0:T(8,128)}, u32[]{:S(2)}) copy-start(s32[8,8]{1,0:T(8,128)} %pattern_ref.1) | copy-start | bytes 772
  0.7 5.5 %copy-start.5 = (s32[8,6]{1,0:T(8,128)S(1)}, s32[8,6]{1,0:T(8,128)}, u32[]{:S(2)}) copy-start(s32[8,6]{1,0:T(8,128)} %owner_ref.1) | copy-start | bytes 580
  0.7 5.5 %copy-start.6 = (s32[8,6]{1,0:T(8,128)S(1)}, s32[8,6]{1,0:T(8,128)}, u32[]{:S(2)}) copy-start(s32[8,6]{1,0:T(8,128)} %local_ref.1) | copy-start | bytes 580
  0.7 5.5 %copy-start.7 = (s32[1,4]{1,0:T(1,128)S(1)}, s32[1,4]{1,0:T(1,128)}, u32[]{:S(2)}) copy-start(s32[1,4]{1,0:T(1,128)} %trim_ref.1) | copy-start | bytes 52
  0.7 6.5 %copy-start = (bf16[1,8,8,128,128]{4,3,2,1,0:T(8,128)(2,1)S(1)}, bf16[1,8,8,128,128]{4,3,2,1,0:T(8,128)(2,1)}, u32[]{:S(2)}) copy-start(bf16[1,8,8,128,128]{4,3,2,1,0:T(8,128)(2,1)} %param.9) | copy-start | bytes 6291460
  0.7 5.8 %collective-permute-start.2 = (bf16[32,128]{1,0:T(8,128)(2,1)}, bf16[32,128]{1,0:T(8,128)(2,1)S(1)}, u32[]{:S(2)}, u32[]{:S(2)}) collective-permute-start(bf16[32,128]{1,0:T(8,128)(2,1)} %bitcast.9), channel_id=1, source_target_pairs={{0,16},{1,2},{2,1},{3,4},{4,3},{5,6},{6,5},{7,8},{8,7},{9,10},{10,... | collective-permute-start | bytes 24584 | tf_op jit(solution)/shard_map/ppermute | solution.py:216
  3.7 4.8 %collective-permute-start.1 = (bf16[32,128]{1,0:T(8,128)(2,1)}, bf16[32,128]{1,0:T(8,128)(2,1)S(1)}, u32[]{:S(2)}, u32[]{:S(2)}) collective-permute-start(bf16[32,128]{1,0:T(8,128)(2,1)} %bitcast.10), channel_id=1, source_target_pairs={{0,8},{1,9},{2,10},{3,11},{4,12},{5,13},{6,14},{7,15},{8,0},{9,1},... | collective-permute-start | bytes 24584 | tf_op jit(solution)/shard_map/ppermute | solution.py:187
  5.6 1.5 %collective-permute-start = (bf16[32,128]{1,0:T(8,128)(2,1)}, bf16[32,128]{1,0:T(8,128)(2,1)S(1)}, u32[]{:S(2)}, u32[]{:S(2)}) collective-permute-start(bf16[32,128]{1,0:T(8,128)(2,1)} %bitcast.11), channel_id=1, source_target_pairs={{0,1},{1,0},{2,3},{3,2},{4,5},{5,4},{6,7},{7,6},{8,9},{9,8},{10,11... | collective-permute-start | bytes 24584 | tf_op jit(solution)/shard_map/ppermute | solution.py:187
  6.2 2.3 %copy-start.1 = (bf16[8,6,128,128]{3,2,1,0:T(8,128)(2,1)S(1)}, bf16[8,6,128,128]{3,2,1,0:T(8,128)(2,1)}, u32[]{:S(2)}) copy-start(bf16[8,6,128,128]{3,2,1,0:T(8,128)(2,1)} %spline_ref.1) | copy-start | bytes 4718596
  7.6 15.2 %copy-start.2 = (bf16[8,128,128]{2,1,0:T(8,128)(2,1)S(1)}, bf16[8,128,128]{2,1,0:T(8,128)(2,1)}, u32[]{:S(2)}) copy-start(bf16[8,128,128]{2,1,0:T(8,128)(2,1)} %refs_4_.1) | copy-start | bytes 786436
  9.3 1.3 %collective-permute-start.3 = (bf16[8,32,128]{2,1,0:T(8,128)(2,1)S(1)}, bf16[8,32,128]{2,1,0:T(8,128)(2,1)S(1)}, u32[]{:S(2)}, u32[]{:S(2)}) collective-permute-start(bf16[8,32,128]{2,1,0:T(8,128)(2,1)S(1)} %get-tuple-element.23), channel_id=1, source_target_pairs={{0,1},{1,0},{2,3},{3,2},{4,5},{5,4},{6,7},{7,6},{8,9},{9,8},{10,11... | collective-permute-start | bytes 196616 | tf_op jit(solution)/shard_map/ppermute | solution.py:187
  10.6 5.0 %collective-permute-start.4 = (bf16[2,32,128]{2,1,0:T(8,128)(2,1)S(1)}, bf16[2,32,128]{2,1,0:T(8,128)(2,1)S(1)}, u32[]{:S(2)}, u32[]{:S(2)}) collective-permute-start(bf16[2,32,128]{2,1,0:T(8,128)(2,1)S(1)} %get-tuple-element.25), channel_id=1, source_target_pairs={{0,13},{1,12},{2,15},{3,14},{4,9},{5,8},{6,11},{7,10},{8,5},{9,4},... | collective-permute-start | bytes 49160 | tf_op jit(solution)/shard_map/ppermute | solution.py:187
  13.4 4.6 %collective-permute-start.5 = (bf16[2,32,128]{2,1,0:T(8,128)(2,1)S(1)}, bf16[2,32,128]{2,1,0:T(8,128)(2,1)S(1)}, u32[]{:S(2)}, u32[]{:S(2)}) collective-permute-start(bf16[2,32,128]{2,1,0:T(8,128)(2,1)S(1)} %get-tuple-element.26), channel_id=1, source_target_pairs={{0,8},{1,9},{2,10},{3,11},{4,12},{5,13},{6,14},{7,15},{8,0},{9,1},... | collective-permute-start | bytes 49160 | tf_op jit(solution)/shard_map/ppermute | solution.py:187
  13.4 4.6 %collective-permute-start.6 = (bf16[2,32,128]{2,1,0:T(8,128)(2,1)S(1)}, bf16[2,32,128]{2,1,0:T(8,128)(2,1)S(1)}, u32[]{:S(2)}, u32[]{:S(2)}) collective-permute-start(bf16[2,32,128]{2,1,0:T(8,128)(2,1)S(1)} %get-tuple-element.27), channel_id=1, source_target_pairs={{0,5},{1,4},{2,7},{3,6},{4,1},{5,0},{6,3},{7,2},{8,13},{9,12},{10,... | collective-permute-start | bytes 49160 | tf_op jit(solution)/shard_map/ppermute | solution.py:187
  18.1 4.1 %collective-permute-start.7 = (f32[32,128]{1,0:T(8,128)S(1)}, f32[32,128]{1,0:T(8,128)S(1)}, u32[]{:S(2)}, u32[]{:S(2)}) collective-permute-start(f32[32,128]{1,0:T(8,128)S(1)} %get-tuple-element.28), channel_id=1, source_target_pairs={{0,19},{1,18},{2,17},{3,16},{4,23},{5,22},{6,21},{7,20},{8,27},{9,... | collective-permute-start | bytes 49160 | tf_op jit(solution)/shard_map/ppermute | solution.py:196
  18.7 3.7 %collective-permute-start.8 = (f32[32,128]{1,0:T(8,128)S(1)}, f32[32,128]{1,0:T(8,128)S(1)}, u32[]{:S(2)}, u32[]{:S(2)}) collective-permute-start(f32[32,128]{1,0:T(8,128)S(1)} %get-tuple-element.29), channel_id=1, source_target_pairs={{0,16},{1,17},{2,18},{3,19},{4,20},{5,21},{6,22},{7,23},{8,24},{9,... | collective-permute-start | bytes 49160 | tf_op jit(solution)/shard_map/ppermute | solution.py:196
  19.7 3.2 %collective-permute-start.9 = (f32[32,128]{1,0:T(8,128)S(1)}, f32[32,128]{1,0:T(8,128)S(1)}, u32[]{:S(2)}, u32[]{:S(2)}) collective-permute-start(f32[32,128]{1,0:T(8,128)S(1)} %get-tuple-element.30), channel_id=1, source_target_pairs={{0,3},{1,2},{2,1},{3,0},{4,7},{5,6},{6,5},{7,4},{8,11},{9,10},{10,... | collective-permute-start | bytes 49160 | tf_op jit(solution)/shard_map/ppermute | solution.py:196

commit v15 on v14

--- a/solution.py
+++ b/solution.py
@@ -15,6 +15,11 @@
 
 def device_class(index):
     return (index ^ (index >> 1) ^ (index >> 2)) & 1
+
+
+def exchange_of(far, here):
+    half = 1 - ((here ^ (here >> 2)) & 1)
+    return far ^ (half & ((far >> 1) | (far >> 2) | (far >> 3)) & 1)
 
 
 def spread_kernel(rhs, expand_ref):
@@ -56,8 +61,12 @@
     gate_ref[...] = jnp.broadcast_to(gate, gate_ref.shape)
     held_ref[...] = own_ref[...]
     owner = owner_ref[...]
+    apart = owner ^ here
+    given = device_class(owner) ^ device_class(here)
     code_ref[...] = (
-        (device_class(owner) ^ device_class(here)) * (panels // 2) + ((owner ^ here) >> 1)
+        given * (panels // 2)
+        + exchange_of(apart >> 2, here ^ given) * 2
+        + ((apart >> 1) & 1)
     ) * struct_count + local_ref[...]
 
 
@@ -292,9 +301,13 @@
         cost_estimate=cost(10**6, 2**17),
         name="pair_sum",
     )(keep, got)
-    got = [
-        swap(sends[step - 1], panels, 4 * step + step % 2) for step in range(steps - 1, 0, -1)
-    ]
+    got = []
+    for step in range(steps - 1, 0, -1):
+        pairs = []
+        for i in range(panels):
+            far = exchange_of(step, i)
+            pairs.append((i, i ^ (4 * far + far % 2)))
+        got.append(lax.ppermute(sends[step - 1], "panel", pairs))
     one = jax.ShapeDtypeStruct((struct_rows, width), f32)
     columns = pl.pallas_call(
         functools.partial(column_kernel, machs),

time: 23.9 us -> 23.7 us (level)
  starting transfers between devices: 12.4 us -> 11.8 us
  waiting for transfers between devices: 7.41 us -> 7.89 us
    ppermute x6 -> x3, starting transfers between devices: 6.42 us -> 2.52 us  [swap(): return lax.ppermute(value, 'panel', [(i, i ^ apart) for i in range(panels)])]
    ppermute x0 -> x3, waiting for transfers between devices: none -> 3.71 us  [on_device(): got.append(lax.ppermute(sends[step - 1], 'panel', pairs))]
    ppermute x6 -> x3, waiting for transfers between devices: 6.28 us -> 2.76 us  [swap(): return lax.ppermute(value, 'panel', [(i, i ^ apart) for i in range(panels)])]
    ppermute x0 -> x3, starting transfers between devices: none -> 3.27 us  [on_device(): got.append(lax.ppermute(sends[step - 1], 'panel', pairs))]
    ppermute x3, waiting for transfers between devices: 1.13 us -> 1.42 us  [mach_swap(): return lax.ppermute(value, ('mach', 'panel'), pairs)]
  transfers between devices with their start and end apart: 10 -> 10, of which waited for: 8 -> 7; matrix products, arithmetic and copies ran while one was open for 3% -> 3% of each run, Pallas kernels for 3% -> 3%
where the time goes in v15:
time: 23.7 us; the launch traced here: 23.5 us
  starting transfers between devices  11.8 us (50%)
  waiting for transfers between devices  7.89 us (33%)
  Pallas kernels  2.34 us (10%)
  between operations  0.77 us (3%)
  other arithmetic  0.68 us (3%)
    ppermute x3, waiting for transfers between devices, on_device(): got.append(lax.ppermute(sends[step - 1], 'panel', pairs))  3.71 us
    ppermute x3, starting transfers between devices, on_device(): got.append(lax.ppermute(sends[step - 1], 'panel', pairs))  3.27 us
    ppermute x1, starting transfers between devices, on_device(): lax.ppermute(own, ('mach', 'panel'), [(mach * panels + i, (mach ^ (i in b...  3 us
    ppermute x3, starting transfers between devices, mach_swap(): return lax.ppermute(value, ('mach', 'panel'), pairs)  2.99 us
    ppermute x3, waiting for transfers between devices, swap(): return lax.ppermute(value, 'panel', [(i, i ^ apart) for i in range(panels)])  2.76 us
    ppermute x3, starting transfers between devices, swap(): return lax.ppermute(value, 'panel', [(i, i ^ apart) for i in range(panels)])  2.52 us
    ppermute x3, waiting for transfers between devices, mach_swap(): return lax.ppermute(value, ('mach', 'panel'), pairs)  1.42 us
    pallas_call x1, Pallas kernels, on_device(): pl.pallas_call(functools.partial(spline_kernel, rhs), out_shape=(jax.Shap...  0.84 us
  transfers between devices with their start and end apart: 10, of which 7 were waited for; matrix products, arithmetic and copies ran while one was open for 3% of the time, Pallas kernels for 3%

profile of v15, /device:TPU:0, one launch (start us, length us, event | category | flops | bytes accessed | tf_op | source)
XLA Modules:
  0.0 23.5 jit_solution(10880398587316003525)
XLA Ops:
  0.6 0.0 copy-start.3
  0.6 0.0 copy-start.4
  0.7 0.0 copy-start.5
  0.7 0.0 copy-start.6
  0.7 0.0 copy-start.7
  0.7 3.0 %collective-permute-start.2 = (bf16[32,128]{1,0:T(8,128)(2,1)}, bf16[32,128]{1,0:T(8,128)(2,1)S(1)}, u32[]{:S(2)}, u32[]{:S(2)}) collective-permute-start(bf16[32,128]{1,0:T(8,128)(2,1)} %bitcast.9), channel_id=1, source_target_pairs={{0,16},{1,2},{2,1},{3,4},{4,3},{5,6},{6,5},{7,8},{8,7},{9,10},{10,... | collective-permute-start | bytes 24584 | tf_op jit(solution)/shard_map/ppermute | solution.py:225
  3.7 1.9 %collective-permute-start.1 = (bf16[32,128]{1,0:T(8,128)(2,1)}, bf16[32,128]{1,0:T(8,128)(2,1)S(1)}, u32[]{:S(2)}, u32[]{:S(2)}) collective-permute-start(bf16[32,128]{1,0:T(8,128)(2,1)} %bitcast.10), channel_id=1, source_target_pairs={{0,8},{1,9},{2,10},{3,11},{4,12},{5,13},{6,14},{7,15},{8,0},{9,1},... | collective-permute-start | bytes 24584 | tf_op jit(solution)/shard_map/ppermute | solution.py:196
  5.6 0.5 %collective-permute-start = (bf16[32,128]{1,0:T(8,128)(2,1)}, bf16[32,128]{1,0:T(8,128)(2,1)S(1)}, u32[]{:S(2)}, u32[]{:S(2)}) collective-permute-start(bf16[32,128]{1,0:T(8,128)(2,1)} %bitcast.11), channel_id=1, source_target_pairs={{0,1},{1,0},{2,3},{3,2},{4,5},{5,4},{6,7},{7,6},{8,9},{9,8},{10,11... | collective-permute-start | bytes 24584 | tf_op jit(solution)/shard_map/ppermute | solution.py:196
  6.2 0.0 copy-start.1
  6.2 0.2 %pick_rows.1 = (bf16[192,128]{1,0:T(8,128)(2,1)S(1)}, f32[16,128]{1,0:T(8,128)S(1)}, bf16[32,128]{1,0:T(8,128)(2,1)S(1)}, s32[8,6]{1,0:T(8,128)S(1)}) custom-call(bf16[32,8]{1,0:T(8,128)(2,1)S(1)} %row_order.1.expand_ref, s32[8,8]{1,0:T(8,128)S(1)} %copy-done.4, s32[1,4]{1,0:T(1,128)S(1)} %copy-done.7, bf16[32,128]{1,0:T(8,128)(2,1)S(1)} %bitcast.12, ...), custom_call_target="tpu_custom_call" | custom-call | flops 1000000 | bytes 131072 | tf_op jit(solution)/shard_map/pick_rows/pallas_call | solution.py:246
  6.5 0.0 collective-permute-done.2.cross_ref
  6.5 0.7 %collective-permute-done.pair_ref._ = bf16[32,128]{1,0:T(8,128)(2,1)S(1)} collective-permute-done((bf16[32,128]{1,0:T(8,128)(2,1)}, bf16[32,128]{1,0:T(8,128)(2,1)S(1)}, u32[]{:S(2)}, u32[]{:S(2)}) %collective-permute-start) | collective-permute-done | bytes 8224 | tf_op jit(solution)/shard_map/ppermute | solution.py:196
  7.2 0.0 copy-done
  7.2 0.5 %near_field.1.part_ref = f32[32,128]{1,0:T(8,128)S(1)} custom-call(bf16[192,128]{1,0:T(8,128)(2,1)S(1)} %get-tuple-element.18.hot_ref, bf16[32,128]{1,0:T(8,128)(2,1)S(1)} %get-tuple-element.19.own_ref, bf16[32,128]{1,0:T(8,128)(2,1)S(1)} %collective-permute-done.pair_ref._, bf16[32,128]{1,0:T(8,128)(2,1)S(1)} %collective-permute-done.2.cross_ref, ...), custom_call_target="tpu_custom_call" | custom-call | flops 1000000 | bytes 131072 | tf_op jit(solution)/shard_map/near_field/pallas_call | solution.py:260
  7.6 0.8 %collective-permute-done.1.mirror_ref = bf16[32,128]{1,0:T(8,128)(2,1)S(1)} collective-permute-done((bf16[32,128]{1,0:T(8,128)(2,1)}, bf16[32,128]{1,0:T(8,128)(2,1)S(1)}, u32[]{:S(2)}, u32[]{:S(2)}) %collective-permute-start.1) | collective-permute-done | bytes 8224 | tf_op jit(solution)/shard_map/ppermute | solution.py:196
  8.5 0.8 %spline_loads.1 = (f32[32,128]{1,0:T(8,128)S(1)}, f32[8,32,128]{2,1,0:T(8,128)S(1)}, bf16[8,32,128]{2,1,0:T(8,128)(2,1)S(1)}) custom-call(bf16[32,128]{1,0:T(8,128)(2,1)S(1)} %collective-permute-done.pair_ref._, bf16[32,128]{1,0:T(8,128)(2,1)S(1)} %collective-permute-done.1.mirror_ref, s32[8,6]{1,0:T(8,128)S(1)} %get-tuple-element.17.code_vmem, ...), custom_call_target="tpu_custom_call" | custom-call | flops 1000000 | bytes 131072 | tf_op jit(solution)/shard_map/spline_loads/pallas_call | solution.py:270
  9.3 0.1 collective-permute-start.3
  9.4 1.2 %collective-permute-done.3.got_ref = bf16[8,32,128]{2,1,0:T(8,128)(2,1)S(1)} collective-permute-done((bf16[8,32,128]{2,1,0:T(8,128)(2,1)S(1)}, bf16[8,32,128]{2,1,0:T(8,128)(2,1)S(1)}, u32[]{:S(2)}, u32[]{:S(2)}) %collective-permute-start.3) | collective-permute-done | bytes 65568 | tf_op jit(solution)/shard_map/ppermute | solution.py:196
  10.6 2.0 %collective-permute-start.4 = (bf16[2,32,128]{2,1,0:T(8,128)(2,1)S(1)}, bf16[2,32,128]{2,1,0:T(8,128)(2,1)S(1)}, u32[]{:S(2)}, u32[]{:S(2)}) collective-permute-start(bf16[2,32,128]{2,1,0:T(8,128)(2,1)S(1)} %get-tuple-element.25), channel_id=1, source_target_pairs={{0,8},{1,12},{2,10},{3,14},{4,9},{5,13},{6,11},{7,15},{8,0},{9,4},... | collective-permute-start | bytes 49160 | tf_op jit(solution)/shard_map/ppermute | solution.py:310
  12.7 0.9 %collective-permute-start.5 = (bf16[2,32,128]{2,1,0:T(8,128)(2,1)S(1)}, bf16[2,32,128]{2,1,0:T(8,128)(2,1)S(1)}, u32[]{:S(2)}, u32[]{:S(2)}) collective-permute-start(bf16[2,32,128]{2,1,0:T(8,128)(2,1)S(1)} %get-tuple-element.26), channel_id=1, source_target_pairs={{0,13},{1,9},{2,15},{3,11},{4,12},{5,8},{6,14},{7,10},{8,5},{9,1},... | collective-permute-start | bytes 49160 | tf_op jit(solution)/shard_map/ppermute | solution.py:310
  13.5 0.4 %collective-permute-start.6 = (bf16[2,32,128]{2,1,0:T(8,128)(2,1)S(1)}, bf16[2,32,128]{2,1,0:T(8,128)(2,1)S(1)}, u32[]{:S(2)}, u32[]{:S(2)}) collective-permute-start(bf16[2,32,128]{2,1,0:T(8,128)(2,1)S(1)} %get-tuple-element.27), channel_id=1, source_target_pairs={{0,5},{1,4},{2,7},{3,6},{4,1},{5,0},{6,3},{7,2},{8,13},{9,12},{10,... | collective-permute-start | bytes 49160 | tf_op jit(solution)/shard_map/ppermute | solution.py:310
  13.9 1.4 %collective-permute-done.4.refs_0_ = bf16[2,32,128]{2,1,0:T(8,128)(2,1)S(1)} collective-permute-done((bf16[2,32,128]{2,1,0:T(8,128)(2,1)S(1)}, bf16[2,32,128]{2,1,0:T(8,128)(2,1)S(1)}, u32[]{:S(2)}, u32[]{:S(2)}) %collective-permute-start.4) | collective-permute-done | bytes 16416 | tf_op jit(solution)/shard_map/ppermute | solution.py:310
  15.3 2.3 %collective-permute-done.5.refs_1_ = bf16[2,32,128]{2,1,0:T(8,128)(2,1)S(1)} collective-permute-done((bf16[2,32,128]{2,1,0:T(8,128)(2,1)S(1)}, bf16[2,32,128]{2,1,0:T(8,128)(2,1)S(1)}, u32[]{:S(2)}, u32[]{:S(2)}) %collective-permute-start.5) | collective-permute-done | bytes 16416 | tf_op jit(solution)/shard_map/ppermute | solution.py:310
  17.6 0.0 collective-permute-done.6.refs_2_
  17.7 1.3 %collective-permute-start.7 = (f32[32,128]{1,0:T(8,128)S(1)}, f32[32,128]{1,0:T(8,128)S(1)}, u32[]{:S(2)}, u32[]{:S(2)}) collective-permute-start(f32[32,128]{1,0:T(8,128)S(1)} %get-tuple-element.28), channel_id=1, source_target_pairs={{0,19},{1,18},{2,17},{3,16},{4,23},{5,22},{6,21},{7,20},{8,27},{9,... | collective-permute-start | bytes 49160 | tf_op jit(solution)/shard_map/ppermute | solution.py:205
  19.0 0.6 %collective-permute-start.8 = (f32[32,128]{1,0:T(8,128)S(1)}, f32[32,128]{1,0:T(8,128)S(1)}, u32[]{:S(2)}, u32[]{:S(2)}) collective-permute-start(f32[32,128]{1,0:T(8,128)S(1)} %get-tuple-element.29), channel_id=1, source_target_pairs={{0,16},{1,17},{2,18},{3,19},{4,20},{5,21},{6,22},{7,23},{8,24},{9,... | collective-permute-start | bytes 49160 | tf_op jit(solution)/shard_map/ppermute | solution.py:205
  19.6 1.1 %collective-permute-start.9 = (f32[32,128]{1,0:T(8,128)S(1)}, f32[32,128]{1,0:T(8,128)S(1)}, u32[]{:S(2)}, u32[]{:S(2)}) collective-permute-start(f32[32,128]{1,0:T(8,128)S(1)} %get-tuple-element.30), channel_id=1, source_target_pairs={{0,3},{1,2},{2,1},{3,0},{4,7},{5,6},{6,5},{7,4},{8,11},{9,10},{10,... | collective-permute-start | bytes 49160 | tf_op jit(solution)/shard_map/ppermute | solution.py:205
  20.6 0.7 %broadcast_multiply_fusion = f32[1,8,4,128]{3,2,1,0:T(4,128)} fusion(f32[1,8,4,128]{3,2,1,0:T(4,128)S(1)} %bitcast.8, f32[4]{0:T(128)S(1)} %convert_bitcast_fusion), kind=kLoop, calls=%fused_computation | loop fusion | flops 4096 | bytes 32784 | tf_op jit(solution)/shard_map/mul | solution.py:289
  21.3 0.5 %collective-permute-done.7.refs_0_ = f32[32,128]{1,0:T(8,128)S(1)} collective-permute-done((f32[32,128]{1,0:T(8,128)S(1)}, f32[32,128]{1,0:T(8,128)S(1)}, u32[]{:S(2)}, u32[]{:S(2)}) %collective-permute-start.7) | collective-permute-done | bytes 16416 | tf_op jit(solution)/shard_map/ppermute | solution.py:205
  21.8 0.9 %collective-permute-done.8.refs_1_ = f32[32,128]{1,0:T(8,128)S(1)} collective-permute-done((f32[32,128]{1,0:T(8,128)S(1)}, f32[32,128]{1,0:T(8,128)S(1)}, u32[]{:S(2)}, u32[]{:S(2)}) %collective-permute-start.8) | collective-permute-done | bytes 16416 | tf_op jit(solution)/shard_map/ppermute | solution.py:205
  22.7 0.0 collective-permute-done.9.refs_2_
  22.8 0.8 %struct_solve.1 = f32[32,128]{1,0:T(8,128)} custom-call(f32[32,128]{1,0:T(8,128)S(1)} %collective-permute-done.7.refs_0_, f32[32,128]{1,0:T(8,128)S(1)} %collective-permute-done.8.refs_1_, f32[32,128]{1,0:T(8,128)S(1)} %collective-permute-done.9.refs_2_, f32[32,128]{1,0:T(8,128)S(1)} %get-tuple-element.31.refs_3_, bf16[8,128,128]{2,1,0:T(8,128)(2,1)S(1)} %copy-done.2), custom_call_target="tpu_custom_call" | custom-call | flops 1000000 | bytes 131072 | tf_op jit(solution)/shard_map/struct_solve/pallas_call | solution.py:326
  (13 shorter events, 0.1 us)
Async XLA Ops:
  0.6 5.5 %copy-start.3 = (bf16[1,8,4,128]{3,2,1,0:T(4,128)(2,1)S(1)}, bf16[1,8,4,128]{3,2,1,0:T(4,128)(2,1)}, u32[]{:S(2)}) copy-start(bf16[1,8,4,128]{3,2,1,0:T(4,128)(2,1)} %param.8) | copy-start | bytes 24580
  0.6 5.5 %copy-start.4 = (s32[8,8]{1,0:T(8,128)S(1)}, s32[8,8]{1,0:T(8,128)}, u32[]{:S(2)}) copy-start(s32[8,8]{1,0:T(8,128)} %pattern_ref.1) | copy-start | bytes 772
  0.7 5.5 %copy-start.5 = (s32[8,6]{1,0:T(8,128)S(1)}, s32[8,6]{1,0:T(8,128)}, u32[]{:S(2)}) copy-start(s32[8,6]{1,0:T(8,128)} %owner_ref.1) | copy-start | bytes 580
  0.7 5.5 %copy-start.6 = (s32[8,6]{1,0:T(8,128)S(1)}, s32[8,6]{1,0:T(8,128)}, u32[]{:S(2)}) copy-start(s32[8,6]{1,0:T(8,128)} %local_ref.1) | copy-start | bytes 580
  0.7 5.5 %copy-start.7 = (s32[1,4]{1,0:T(1,128)S(1)}, s32[1,4]{1,0:T(1,128)}, u32[]{:S(2)}) copy-start(s32[1,4]{1,0:T(1,128)} %trim_ref.1) | copy-start | bytes 52
  0.7 6.5 %copy-start = (bf16[1,8,8,128,128]{4,3,2,1,0:T(8,128)(2,1)S(1)}, bf16[1,8,8,128,128]{4,3,2,1,0:T(8,128)(2,1)}, u32[]{:S(2)}) copy-start(bf16[1,8,8,128,128]{4,3,2,1,0:T(8,128)(2,1)} %param.9) | copy-start | bytes 6291460
  0.7 5.8 %collective-permute-start.2 = (bf16[32,128]{1,0:T(8,128)(2,1)}, bf16[32,128]{1,0:T(8,128)(2,1)S(1)}, u32[]{:S(2)}, u32[]{:S(2)}) collective-permute-start(bf16[32,128]{1,0:T(8,128)(2,1)} %bitcast.9), channel_id=1, source_target_pairs={{0,16},{1,2},{2,1},{3,4},{4,3},{5,6},{6,5},{7,8},{8,7},{9,10},{10,... | collective-permute-start | bytes 24584 | tf_op jit(solution)/shard_map/ppermute | solution.py:225
  3.7 4.8 %collective-permute-start.1 = (bf16[32,128]{1,0:T(8,128)(2,1)}, bf16[32,128]{1,0:T(8,128)(2,1)S(1)}, u32[]{:S(2)}, u32[]{:S(2)}) collective-permute-start(bf16[32,128]{1,0:T(8,128)(2,1)} %bitcast.10), channel_id=1, source_target_pairs={{0,8},{1,9},{2,10},{3,11},{4,12},{5,13},{6,14},{7,15},{8,0},{9,1},... | collective-permute-start | bytes 24584 | tf_op jit(solution)/shard_map/ppermute | solution.py:196
  5.6 1.5 %collective-permute-start = (bf16[32,128]{1,0:T(8,128)(2,1)}, bf16[32,128]{1,0:T(8,128)(2,1)S(1)}, u32[]{:S(2)}, u32[]{:S(2)}) collective-permute-start(bf16[32,128]{1,0:T(8,128)(2,1)} %bitcast.11), channel_id=1, source_target_pairs={{0,1},{1,0},{2,3},{3,2},{4,5},{5,4},{6,7},{7,6},{8,9},{9,8},{10,11... | collective-permute-start | bytes 24584 | tf_op jit(solution)/shard_map/ppermute | solution.py:196
  6.2 2.3 %copy-start.1 = (bf16[8,6,128,128]{3,2,1,0:T(8,128)(2,1)S(1)}, bf16[8,6,128,128]{3,2,1,0:T(8,128)(2,1)}, u32[]{:S(2)}) copy-start(bf16[8,6,128,128]{3,2,1,0:T(8,128)(2,1)} %spline_ref.1) | copy-start | bytes 4718596
  7.6 15.1 %copy-start.2 = (bf16[8,128,128]{2,1,0:T(8,128)(2,1)S(1)}, bf16[8,128,128]{2,1,0:T(8,128)(2,1)}, u32[]{:S(2)}) copy-start(bf16[8,128,128]{2,1,0:T(8,128)(2,1)} %refs_4_.1) | copy-start | bytes 786436
  9.3 1.3 %collective-permute-start.3 = (bf16[8,32,128]{2,1,0:T(8,128)(2,1)S(1)}, bf16[8,32,128]{2,1,0:T(8,128)(2,1)S(1)}, u32[]{:S(2)}, u32[]{:S(2)}) collective-permute-start(bf16[8,32,128]{2,1,0:T(8,128)(2,1)S(1)} %get-tuple-element.23), channel_id=1, source_target_pairs={{0,1},{1,0},{2,3},{3,2},{4,5},{5,4},{6,7},{7,6},{8,9},{9,8},{10,11... | collective-permute-start | bytes 196616 | tf_op jit(solution)/shard_map/ppermute | solution.py:196
  10.6 4.7 %collective-permute-start.4 = (bf16[2,32,128]{2,1,0:T(8,128)(2,1)S(1)}, bf16[2,32,128]{2,1,0:T(8,128)(2,1)S(1)}, u32[]{:S(2)}, u32[]{:S(2)}) collective-permute-start(bf16[2,32,128]{2,1,0:T(8,128)(2,1)S(1)} %get-tuple-element.25), channel_id=1, source_target_pairs={{0,8},{1,12},{2,10},{3,14},{4,9},{5,13},{6,11},{7,15},{8,0},{9,4},... | collective-permute-start | bytes 49160 | tf_op jit(solution)/shard_map/ppermute | solution.py:310
  12.7 5.0 %collective-permute-start.5 = (bf16[2,32,128]{2,1,0:T(8,128)(2,1)S(1)}, bf16[2,32,128]{2,1,0:T(8,128)(2,1)S(1)}, u32[]{:S(2)}, u32[]{:S(2)}) collective-permute-start(bf16[2,32,128]{2,1,0:T(8,128)(2,1)S(1)} %get-tuple-element.26), channel_id=1, source_target_pairs={{0,13},{1,9},{2,15},{3,11},{4,12},{5,8},{6,14},{7,10},{8,5},{9,1},... | collective-permute-start | bytes 49160 | tf_op jit(solution)/shard_map/ppermute | solution.py:310
  13.5 4.1 %collective-permute-start.6 = (bf16[2,32,128]{2,1,0:T(8,128)(2,1)S(1)}, bf16[2,32,128]{2,1,0:T(8,128)(2,1)S(1)}, u32[]{:S(2)}, u32[]{:S(2)}) collective-permute-start(bf16[2,32,128]{2,1,0:T(8,128)(2,1)S(1)} %get-tuple-element.27), channel_id=1, source_target_pairs={{0,5},{1,4},{2,7},{3,6},{4,1},{5,0},{6,3},{7,2},{8,13},{9,12},{10,... | collective-permute-start | bytes 49160 | tf_op jit(solution)/shard_map/ppermute | solution.py:310
  17.7 4.2 %collective-permute-start.7 = (f32[32,128]{1,0:T(8,128)S(1)}, f32[32,128]{1,0:T(8,128)S(1)}, u32[]{:S(2)}, u32[]{:S(2)}) collective-permute-start(f32[32,128]{1,0:T(8,128)S(1)} %get-tuple-element.28), channel_id=1, source_target_pairs={{0,19},{1,18},{2,17},{3,16},{4,23},{5,22},{6,21},{7,20},{8,27},{9,... | collective-permute-start | bytes 49160 | tf_op jit(solution)/shard_map/ppermute | solution.py:205
  19.0 3.7 %collective-permute-start.8 = (f32[32,128]{1,0:T(8,128)S(1)}, f32[32,128]{1,0:T(8,128)S(1)}, u32[]{:S(2)}, u32[]{:S(2)}) collective-permute-start(f32[32,128]{1,0:T(8,128)S(1)} %get-tuple-element.29), channel_id=1, source_target_pairs={{0,16},{1,17},{2,18},{3,19},{4,20},{5,21},{6,22},{7,23},{8,24},{9,... | collective-permute-start | bytes 49160 | tf_op jit(solution)/shard_map/ppermute | solution.py:205
  19.6 3.2 %collective-permute-start.9 = (f32[32,128]{1,0:T(8,128)S(1)}, f32[32,128]{1,0:T(8,128)S(1)}, u32[]{:S(2)}, u32[]{:S(2)}) collective-permute-start(f32[32,128]{1,0:T(8,128)S(1)} %get-tuple-element.30), channel_id=1, source_target_pairs={{0,3},{1,2},{2,1},{3,0},{4,7},{5,6},{6,5},{7,4},{8,11},{9,10},{10,... | collective-permute-start | bytes 49160 | tf_op jit(solution)/shard_map/ppermute | solution.py:205

commit v16 on v15

--- a/solution.py
+++ b/solution.py
@@ -105,23 +105,28 @@
 
 def spline_kernel(
     rhs, _, mirror_ref, code_vmem, part_ref, gate_ref, near_ref, spline_ref,
-    sums_ref, keep_ref, send_ref, code_ref, loads_ref, acc, sem,
+    sums_ref, acc, send_ref, code_ref, sem,
 ):
     copy = pltpu.make_async_copy(code_vmem, code_ref, sem)
     copy.start()
     block_count, splines = code_ref.shape
     rows, width = part_ref.shape
+    tiles = acc.shape[0] // 2
+    loads = []
     for g in range(rows // PACK):
         group = slice(g * PACK, (g + 1) * PACK)
-        far = grouped_product(rhs, mirror_ref[group], lambda i: near_ref[i, 1], g)
-        sums_ref[group] = part_ref[group] + far
-        loads_ref[group] = gate_ref[...] * sums_ref[group]
+        sums = part_ref[group] + grouped_product(
+            rhs, mirror_ref[group], lambda i: near_ref[i, 1], g
+        )
+        sums_ref[group] = sums
+        gated = gate_ref[...] * sums
+        loads += [gated[row : row + TILE] for row in range(0, PACK, TILE)]
     acc[...] = jnp.zeros(acc.shape, jnp.float32)
     upper = lax.broadcasted_iota(jnp.int32, (TILE, width), 0) // rhs
     blank = jnp.zeros((TILE, width), jnp.float32)
 
     def pair_product(pair):
-        both = loads_ref[pair * rhs : (pair + 2) * rhs]
+        both = loads[pair // 2]
         turned = pltpu.roll(both, rhs, 0)
         mine = jnp.concatenate(
             [
@@ -155,17 +160,17 @@
                 sums.append(acc[place] + added)
             for place, value in zip(places, sums):
                 acc[place] = value
-    tiles = acc.shape[0] // 2
-    keep_ref[...] = acc[:tiles].reshape(keep_ref.shape)
     send_ref[...] = acc[tiles:].reshape(send_ref.shape).astype(send_ref.dtype)
 
 
-def split_kernel(held_ref, got_ref, *out_refs):
-    size = out_refs[0].shape[0]
+def split_kernel(acc, got_ref, *out_refs):
+    size, struct_rows, _ = out_refs[0].shape
+    height = struct_rows // TILE
     for step, out_ref in enumerate(out_refs):
         for place in range(size):
-            total = held_ref[step * size + place] + got_ref[step * size + place].astype(jnp.float32)
-            out_ref[place] = total.astype(out_ref.dtype)
+            index = step * size + place
+            held = acc[index * height : (index + 1) * height].reshape(out_ref.shape[1:])
+            out_ref[place] = (held + got_ref[index].astype(jnp.float32)).astype(out_ref.dtype)
 
 
 def column_kernel(machs, held_ref, *refs):
@@ -266,20 +271,17 @@
         cost_estimate=cost(10**6, 2**17),
         name="near_field",
     )(hot, held, pair, cross, near_blocks[0])
-    half = (panels // 2, struct_rows, width)
-    sums, keep, send = pl.pallas_call(
+    sums, acc, send = pl.pallas_call(
         functools.partial(spline_kernel, rhs),
         out_shape=(
             jax.ShapeDtypeStruct((rows, width), f32),
-            jax.ShapeDtypeStruct(half, f32),
-            jax.ShapeDtypeStruct(half, bf16),
+            jax.ShapeDtypeStruct((panels * struct_rows // TILE, TILE, width), f32),
+            jax.ShapeDtypeStruct((panels // 2, struct_rows, width), bf16),
         ),
         in_specs=[VMEM] * 7,
         out_specs=(VMEM,) * 3,
         scratch_shapes=[
             pltpu.SMEM(spline_owner.shape, jnp.int32),
-            pltpu.VMEM((rows, width), f32),
-            pltpu.VMEM((panels * struct_rows // TILE, TILE, width), f32),
             pltpu.SemaphoreType.DMA,
         ],
         compiler_params=params,
@@ -300,7 +302,7 @@
         compiler_params=params,
         cost_estimate=cost(10**6, 2**17),
         name="pair_sum",
-    )(keep, got)
+    )(acc, got)
     got = []
     for step in range(steps - 1, 0, -1):
         pairs = []

time: 23.7 us -> 23.6 us (level)
  no operation moved by 1% of the time
where the time goes in v16:
time: 23.6 us; the launch traced here: 23.5 us
  starting transfers between devices  11.8 us (50%)
  waiting for transfers between devices  7.9 us (33%)
  Pallas kernels  2.31 us (10%)
  between operations  0.77 us (3%)
  other arithmetic  0.68 us (3%)
    ppermute x3, waiting for transfers between devices, on_device(): got.append(lax.ppermute(sends[step - 1], 'panel', pairs))  3.72 us
    ppermute x3, starting transfers between devices, on_device(): got.append(lax.ppermute(sends[step - 1], 'panel', pairs))  3.27 us
    ppermute x1, starting transfers between devices, on_device(): lax.ppermute(own, ('mach', 'panel'), [(mach * panels + i, (mach ^ (i in b...  3 us
    ppermute x3, starting transfers between devices, mach_swap(): return lax.ppermute(value, ('mach', 'panel'), pairs)  2.99 us
    ppermute x3, waiting for transfers between devices, swap(): return lax.ppermute(value, 'panel', [(i, i ^ apart) for i in range(panels)])  2.76 us
    ppermute x3, starting transfers between devices, swap(): return lax.ppermute(value, 'panel', [(i, i ^ apart) for i in range(panels)])  2.52 us
    ppermute x3, waiting for transfers between devices, mach_swap(): return lax.ppermute(value, ('mach', 'panel'), pairs)  1.42 us
    pallas_call x1, Pallas kernels, on_device(): pl.pallas_call(functools.partial(spline_kernel, rhs), out_shape=(jax.Shap...  0.81 us
  transfers between devices with their start and end apart: 10, of which 7 were waited for; matrix products, arithmetic and copies ran while one was open for 3% of the time, Pallas kernels for 3%

profile of v16, /device:TPU:0, one launch (start us, length us, event | category | flops | bytes accessed | tf_op | source)
XLA Modules:
  0.0 23.5 jit_solution(13048322256731660037)
XLA Ops:
  0.6 0.0 copy-start.3
  0.6 0.0 copy-start.4
  0.7 0.0 copy-start.5
  0.7 0.0 copy-start.6
  0.7 0.0 copy-start.7
  0.7 0.0 copy-start
  0.7 3.0 %collective-permute-start.2 = (bf16[32,128]{1,0:T(8,128)(2,1)}, bf16[32,128]{1,0:T(8,128)(2,1)S(1)}, u32[]{:S(2)}, u32[]{:S(2)}) collective-permute-start(bf16[32,128]{1,0:T(8,128)(2,1)} %bitcast.9), channel_id=1, source_target_pairs={{0,16},{1,2},{2,1},{3,4},{4,3},{5,6},{6,5},{7,8},{8,7},{9,10},{10,... | collective-permute-start | bytes 24584 | tf_op jit(solution)/shard_map/ppermute | solution.py:230
  3.7 1.9 %collective-permute-start.1 = (bf16[32,128]{1,0:T(8,128)(2,1)}, bf16[32,128]{1,0:T(8,128)(2,1)S(1)}, u32[]{:S(2)}, u32[]{:S(2)}) collective-permute-start(bf16[32,128]{1,0:T(8,128)(2,1)} %bitcast.10), channel_id=1, source_target_pairs={{0,8},{1,9},{2,10},{3,11},{4,12},{5,13},{6,14},{7,15},{8,0},{9,1},... | collective-permute-start | bytes 24584 | tf_op jit(solution)/shard_map/ppermute | solution.py:201
  5.6 0.5 %collective-permute-start = (bf16[32,128]{1,0:T(8,128)(2,1)}, bf16[32,128]{1,0:T(8,128)(2,1)S(1)}, u32[]{:S(2)}, u32[]{:S(2)}) collective-permute-start(bf16[32,128]{1,0:T(8,128)(2,1)} %bitcast.11), channel_id=1, source_target_pairs={{0,1},{1,0},{2,3},{3,2},{4,5},{5,4},{6,7},{7,6},{8,9},{9,8},{10,11... | collective-permute-start | bytes 24584 | tf_op jit(solution)/shard_map/ppermute | solution.py:201
  6.2 0.0 copy-start.1
  6.2 0.2 %pick_rows.1 = (bf16[192,128]{1,0:T(8,128)(2,1)S(1)}, f32[16,128]{1,0:T(8,128)S(1)}, bf16[32,128]{1,0:T(8,128)(2,1)S(1)}, s32[8,6]{1,0:T(8,128)S(1)}) custom-call(bf16[32,8]{1,0:T(8,128)(2,1)S(1)} %row_order.1.expand_ref, s32[8,8]{1,0:T(8,128)S(1)} %copy-done.4, s32[1,4]{1,0:T(1,128)S(1)} %copy-done.7, bf16[32,128]{1,0:T(8,128)(2,1)S(1)} %bitcast.12, ...), custom_call_target="tpu_custom_call" | custom-call | flops 1000000 | bytes 131072 | tf_op jit(solution)/shard_map/pick_rows/pallas_call | solution.py:251
  6.5 0.0 collective-permute-done.2.cross_ref
  6.5 0.7 %collective-permute-done.pair_ref._ = bf16[32,128]{1,0:T(8,128)(2,1)S(1)} collective-permute-done((bf16[32,128]{1,0:T(8,128)(2,1)}, bf16[32,128]{1,0:T(8,128)(2,1)S(1)}, u32[]{:S(2)}, u32[]{:S(2)}) %collective-permute-start) | collective-permute-done | bytes 8224 | tf_op jit(solution)/shard_map/ppermute | solution.py:201
  7.2 0.5 %near_field.1.part_ref = f32[32,128]{1,0:T(8,128)S(1)} custom-call(bf16[192,128]{1,0:T(8,128)(2,1)S(1)} %get-tuple-element.18.hot_ref, bf16[32,128]{1,0:T(8,128)(2,1)S(1)} %get-tuple-element.19.own_ref, bf16[32,128]{1,0:T(8,128)(2,1)S(1)} %collective-permute-done.pair_ref._, bf16[32,128]{1,0:T(8,128)(2,1)S(1)} %collective-permute-done.2.cross_ref, ...), custom_call_target="tpu_custom_call" | custom-call | flops 1000000 | bytes 131072 | tf_op jit(solution)/shard_map/near_field/pallas_call | solution.py:265
  7.6 0.8 %collective-permute-done.1.mirror_ref = bf16[32,128]{1,0:T(8,128)(2,1)S(1)} collective-permute-done((bf16[32,128]{1,0:T(8,128)(2,1)}, bf16[32,128]{1,0:T(8,128)(2,1)S(1)}, u32[]{:S(2)}, u32[]{:S(2)}) %collective-permute-start.1) | collective-permute-done | bytes 8224 | tf_op jit(solution)/shard_map/ppermute | solution.py:201
  8.5 0.8 %spline_loads.1 = (f32[32,128]{1,0:T(8,128)S(1)}, f32[64,8,128]{2,1,0:T(8,128)S(1)}, bf16[8,32,128]{2,1,0:T(8,128)(2,1)S(1)}) custom-call(bf16[32,128]{1,0:T(8,128)(2,1)S(1)} %collective-permute-done.pair_ref._, bf16[32,128]{1,0:T(8,128)(2,1)S(1)} %collective-permute-done.1.mirror_ref, s32[8,6]{1,0:T(8,128)S(1)} %get-tuple-element.17.code_vmem, ...), custom_call_target="tpu_custom_call" | custom-call | flops 1000000 | bytes 131072 | tf_op jit(solution)/shard_map/spline_loads/pallas_call | solution.py:274
  9.3 0.1 collective-permute-start.3
  9.4 1.2 %collective-permute-done.3.got_ref = bf16[8,32,128]{2,1,0:T(8,128)(2,1)S(1)} collective-permute-done((bf16[8,32,128]{2,1,0:T(8,128)(2,1)S(1)}, bf16[8,32,128]{2,1,0:T(8,128)(2,1)S(1)}, u32[]{:S(2)}, u32[]{:S(2)}) %collective-permute-start.3) | collective-permute-done | bytes 65568 | tf_op jit(solution)/shard_map/ppermute | solution.py:201
  10.6 2.0 %collective-permute-start.4 = (bf16[2,32,128]{2,1,0:T(8,128)(2,1)S(1)}, bf16[2,32,128]{2,1,0:T(8,128)(2,1)S(1)}, u32[]{:S(2)}, u32[]{:S(2)}) collective-permute-start(bf16[2,32,128]{2,1,0:T(8,128)(2,1)S(1)} %get-tuple-element.25), channel_id=1, source_target_pairs={{0,8},{1,12},{2,10},{3,14},{4,9},{5,13},{6,11},{7,15},{8,0},{9,4},... | collective-permute-start | bytes 49160 | tf_op jit(solution)/shard_map/ppermute | solution.py:312
  12.6 0.8 %collective-permute-start.5 = (bf16[2,32,128]{2,1,0:T(8,128)(2,1)S(1)}, bf16[2,32,128]{2,1,0:T(8,128)(2,1)S(1)}, u32[]{:S(2)}, u32[]{:S(2)}) collective-permute-start(bf16[2,32,128]{2,1,0:T(8,128)(2,1)S(1)} %get-tuple-element.26), channel_id=1, source_target_pairs={{0,13},{1,9},{2,15},{3,11},{4,12},{5,8},{6,14},{7,10},{8,5},{9,1},... | collective-permute-start | bytes 49160 | tf_op jit(solution)/shard_map/ppermute | solution.py:312
  13.5 0.4 %collective-permute-start.6 = (bf16[2,32,128]{2,1,0:T(8,128)(2,1)S(1)}, bf16[2,32,128]{2,1,0:T(8,128)(2,1)S(1)}, u32[]{:S(2)}, u32[]{:S(2)}) collective-permute-start(bf16[2,32,128]{2,1,0:T(8,128)(2,1)S(1)} %get-tuple-element.27), channel_id=1, source_target_pairs={{0,5},{1,4},{2,7},{3,6},{4,1},{5,0},{6,3},{7,2},{8,13},{9,12},{10,... | collective-permute-start | bytes 49160 | tf_op jit(solution)/shard_map/ppermute | solution.py:312
  13.9 1.4 %collective-permute-done.4.refs_0_ = bf16[2,32,128]{2,1,0:T(8,128)(2,1)S(1)} collective-permute-done((bf16[2,32,128]{2,1,0:T(8,128)(2,1)S(1)}, bf16[2,32,128]{2,1,0:T(8,128)(2,1)S(1)}, u32[]{:S(2)}, u32[]{:S(2)}) %collective-permute-start.4) | collective-permute-done | bytes 16416 | tf_op jit(solution)/shard_map/ppermute | solution.py:312
  15.3 2.3 %collective-permute-done.5.refs_1_ = bf16[2,32,128]{2,1,0:T(8,128)(2,1)S(1)} collective-permute-done((bf16[2,32,128]{2,1,0:T(8,128)(2,1)S(1)}, bf16[2,32,128]{2,1,0:T(8,128)(2,1)S(1)}, u32[]{:S(2)}, u32[]{:S(2)}) %collective-permute-start.5) | collective-permute-done | bytes 16416 | tf_op jit(solution)/shard_map/ppermute | solution.py:312
  17.6 0.0 collective-permute-done.6.refs_2_
  17.6 1.3 %collective-permute-start.7 = (f32[32,128]{1,0:T(8,128)S(1)}, f32[32,128]{1,0:T(8,128)S(1)}, u32[]{:S(2)}, u32[]{:S(2)}) collective-permute-start(f32[32,128]{1,0:T(8,128)S(1)} %get-tuple-element.28), channel_id=1, source_target_pairs={{0,19},{1,18},{2,17},{3,16},{4,23},{5,22},{6,21},{7,20},{8,27},{9,... | collective-permute-start | bytes 49160 | tf_op jit(solution)/shard_map/ppermute | solution.py:210
  18.9 0.6 %collective-permute-start.8 = (f32[32,128]{1,0:T(8,128)S(1)}, f32[32,128]{1,0:T(8,128)S(1)}, u32[]{:S(2)}, u32[]{:S(2)}) collective-permute-start(f32[32,128]{1,0:T(8,128)S(1)} %get-tuple-element.29), channel_id=1, source_target_pairs={{0,16},{1,17},{2,18},{3,19},{4,20},{5,21},{6,22},{7,23},{8,24},{9,... | collective-permute-start | bytes 49160 | tf_op jit(solution)/shard_map/ppermute | solution.py:210
  19.6 1.1 %collective-permute-start.9 = (f32[32,128]{1,0:T(8,128)S(1)}, f32[32,128]{1,0:T(8,128)S(1)}, u32[]{:S(2)}, u32[]{:S(2)}) collective-permute-start(f32[32,128]{1,0:T(8,128)S(1)} %get-tuple-element.30), channel_id=1, source_target_pairs={{0,3},{1,2},{2,1},{3,0},{4,7},{5,6},{6,5},{7,4},{8,11},{9,10},{10,... | collective-permute-start | bytes 49160 | tf_op jit(solution)/shard_map/ppermute | solution.py:210
  20.6 0.7 %broadcast_multiply_fusion = f32[1,8,4,128]{3,2,1,0:T(4,128)} fusion(f32[1,8,4,128]{3,2,1,0:T(4,128)S(1)} %bitcast.8, f32[4]{0:T(128)S(1)} %convert_bitcast_fusion), kind=kLoop, calls=%fused_computation | loop fusion | flops 4096 | bytes 32784 | tf_op jit(solution)/shard_map/mul | solution.py:291
  21.3 0.5 %collective-permute-done.7.refs_0_ = f32[32,128]{1,0:T(8,128)S(1)} collective-permute-done((f32[32,128]{1,0:T(8,128)S(1)}, f32[32,128]{1,0:T(8,128)S(1)}, u32[]{:S(2)}, u32[]{:S(2)}) %collective-permute-start.7) | collective-permute-done | bytes 16416 | tf_op jit(solution)/shard_map/ppermute | solution.py:210
  21.8 0.9 %collective-permute-done.8.refs_1_ = f32[32,128]{1,0:T(8,128)S(1)} collective-permute-done((f32[32,128]{1,0:T(8,128)S(1)}, f32[32,128]{1,0:T(8,128)S(1)}, u32[]{:S(2)}, u32[]{:S(2)}) %collective-permute-start.8) | collective-permute-done | bytes 16416 | tf_op jit(solution)/shard_map/ppermute | solution.py:210
  22.7 0.0 collective-permute-done.9.refs_2_
  22.7 0.8 %struct_solve.1 = f32[32,128]{1,0:T(8,128)} custom-call(f32[32,128]{1,0:T(8,128)S(1)} %collective-permute-done.7.refs_0_, f32[32,128]{1,0:T(8,128)S(1)} %collective-permute-done.8.refs_1_, f32[32,128]{1,0:T(8,128)S(1)} %collective-permute-done.9.refs_2_, f32[32,128]{1,0:T(8,128)S(1)} %get-tuple-element.31.refs_3_, bf16[8,128,128]{2,1,0:T(8,128)(2,1)S(1)} %copy-done.2), custom_call_target="tpu_custom_call" | custom-call | flops 1000000 | bytes 131072 | tf_op jit(solution)/shard_map/struct_solve/pallas_call | solution.py:328
  (13 shorter events, 0.1 us)
Async XLA Ops:
  0.6 5.5 %copy-start.3 = (bf16[1,8,4,128]{3,2,1,0:T(4,128)(2,1)S(1)}, bf16[1,8,4,128]{3,2,1,0:T(4,128)(2,1)}, u32[]{:S(2)}) copy-start(bf16[1,8,4,128]{3,2,1,0:T(4,128)(2,1)} %param.8) | copy-start | bytes 24580
  0.6 5.5 %copy-start.4 = (s32[8,8]{1,0:T(8,128)S(1)}, s32[8,8]{1,0:T(8,128)}, u32[]{:S(2)}) copy-start(s32[8,8]{1,0:T(8,128)} %pattern_ref.1) | copy-start | bytes 772
  0.7 5.5 %copy-start.5 = (s32[8,6]{1,0:T(8,128)S(1)}, s32[8,6]{1,0:T(8,128)}, u32[]{:S(2)}) copy-start(s32[8,6]{1,0:T(8,128)} %owner_ref.1) | copy-start | bytes 580
  0.7 5.5 %copy-start.6 = (s32[8,6]{1,0:T(8,128)S(1)}, s32[8,6]{1,0:T(8,128)}, u32[]{:S(2)}) copy-start(s32[8,6]{1,0:T(8,128)} %local_ref.1) | copy-start | bytes 580
  0.7 5.5 %copy-start.7 = (s32[1,4]{1,0:T(1,128)S(1)}, s32[1,4]{1,0:T(1,128)}, u32[]{:S(2)}) copy-start(s32[1,4]{1,0:T(1,128)} %trim_ref.1) | copy-start | bytes 52
  0.7 6.5 %copy-start = (bf16[1,8,8,128,128]{4,3,2,1,0:T(8,128)(2,1)S(1)}, bf16[1,8,8,128,128]{4,3,2,1,0:T(8,128)(2,1)}, u32[]{:S(2)}) copy-start(bf16[1,8,8,128,128]{4,3,2,1,0:T(8,128)(2,1)} %param.9) | copy-start | bytes 6291460
  0.7 5.8 %collective-permute-start.2 = (bf16[32,128]{1,0:T(8,128)(2,1)}, bf16[32,128]{1,0:T(8,128)(2,1)S(1)}, u32[]{:S(2)}, u32[]{:S(2)}) collective-permute-start(bf16[32,128]{1,0:T(8,128)(2,1)} %bitcast.9), channel_id=1, source_target_pairs={{0,16},{1,2},{2,1},{3,4},{4,3},{5,6},{6,5},{7,8},{8,7},{9,10},{10,... | collective-permute-start | bytes 24584 | tf_op jit(solution)/shard_map/ppermute | solution.py:230
  3.7 4.8 %collective-permute-start.1 = (bf16[32,128]{1,0:T(8,128)(2,1)}, bf16[32,128]{1,0:T(8,128)(2,1)S(1)}, u32[]{:S(2)}, u32[]{:S(2)}) collective-permute-start(bf16[32,128]{1,0:T(8,128)(2,1)} %bitcast.10), channel_id=1, source_target_pairs={{0,8},{1,9},{2,10},{3,11},{4,12},{5,13},{6,14},{7,15},{8,0},{9,1},... | collective-permute-start | bytes 24584 | tf_op jit(solution)/shard_map/ppermute | solution.py:201
  5.6 1.5 %collective-permute-start = (bf16[32,128]{1,0:T(8,128)(2,1)}, bf16[32,128]{1,0:T(8,128)(2,1)S(1)}, u32[]{:S(2)}, u32[]{:S(2)}) collective-permute-start(bf16[32,128]{1,0:T(8,128)(2,1)} %bitcast.11), channel_id=1, source_target_pairs={{0,1},{1,0},{2,3},{3,2},{4,5},{5,4},{6,7},{7,6},{8,9},{9,8},{10,11... | collective-permute-start | bytes 24584 | tf_op jit(solution)/shard_map/ppermute | solution.py:201
  6.2 2.3 %copy-start.1 = (bf16[8,6,128,128]{3,2,1,0:T(8,128)(2,1)S(1)}, bf16[8,6,128,128]{3,2,1,0:T(8,128)(2,1)}, u32[]{:S(2)}) copy-start(bf16[8,6,128,128]{3,2,1,0:T(8,128)(2,1)} %spline_ref.1) | copy-start | bytes 4718596
  7.6 15.1 %copy-start.2 = (bf16[8,128,128]{2,1,0:T(8,128)(2,1)S(1)}, bf16[8,128,128]{2,1,0:T(8,128)(2,1)}, u32[]{:S(2)}) copy-start(bf16[8,128,128]{2,1,0:T(8,128)(2,1)} %refs_4_.1) | copy-start | bytes 786436
  9.3 1.3 %collective-permute-start.3 = (bf16[8,32,128]{2,1,0:T(8,128)(2,1)S(1)}, bf16[8,32,128]{2,1,0:T(8,128)(2,1)S(1)}, u32[]{:S(2)}, u32[]{:S(2)}) collective-permute-start(bf16[8,32,128]{2,1,0:T(8,128)(2,1)S(1)} %get-tuple-element.23), channel_id=1, source_target_pairs={{0,1},{1,0},{2,3},{3,2},{4,5},{5,4},{6,7},{7,6},{8,9},{9,8},{10,11... | collective-permute-start | bytes 196616 | tf_op jit(solution)/shard_map/ppermute | solution.py:201
  10.6 4.7 %collective-permute-start.4 = (bf16[2,32,128]{2,1,0:T(8,128)(2,1)S(1)}, bf16[2,32,128]{2,1,0:T(8,128)(2,1)S(1)}, u32[]{:S(2)}, u32[]{:S(2)}) collective-permute-start(bf16[2,32,128]{2,1,0:T(8,128)(2,1)S(1)} %get-tuple-element.25), channel_id=1, source_target_pairs={{0,8},{1,12},{2,10},{3,14},{4,9},{5,13},{6,11},{7,15},{8,0},{9,4},... | collective-permute-start | bytes 49160 | tf_op jit(solution)/shard_map/ppermute | solution.py:312
  12.6 5.0 %collective-permute-start.5 = (bf16[2,32,128]{2,1,0:T(8,128)(2,1)S(1)}, bf16[2,32,128]{2,1,0:T(8,128)(2,1)S(1)}, u32[]{:S(2)}, u32[]{:S(2)}) collective-permute-start(bf16[2,32,128]{2,1,0:T(8,128)(2,1)S(1)} %get-tuple-element.26), channel_id=1, source_target_pairs={{0,13},{1,9},{2,15},{3,11},{4,12},{5,8},{6,14},{7,10},{8,5},{9,1},... | collective-permute-start | bytes 49160 | tf_op jit(solution)/shard_map/ppermute | solution.py:312
  13.5 4.1 %collective-permute-start.6 = (bf16[2,32,128]{2,1,0:T(8,128)(2,1)S(1)}, bf16[2,32,128]{2,1,0:T(8,128)(2,1)S(1)}, u32[]{:S(2)}, u32[]{:S(2)}) collective-permute-start(bf16[2,32,128]{2,1,0:T(8,128)(2,1)S(1)} %get-tuple-element.27), channel_id=1, source_target_pairs={{0,5},{1,4},{2,7},{3,6},{4,1},{5,0},{6,3},{7,2},{8,13},{9,12},{10,... | collective-permute-start | bytes 49160 | tf_op jit(solution)/shard_map/ppermute | solution.py:312
  17.6 4.2 %collective-permute-start.7 = (f32[32,128]{1,0:T(8,128)S(1)}, f32[32,128]{1,0:T(8,128)S(1)}, u32[]{:S(2)}, u32[]{:S(2)}) collective-permute-start(f32[32,128]{1,0:T(8,128)S(1)} %get-tuple-element.28), channel_id=1, source_target_pairs={{0,19},{1,18},{2,17},{3,16},{4,23},{5,22},{6,21},{7,20},{8,27},{9,... | collective-permute-start | bytes 49160 | tf_op jit(solution)/shard_map/ppermute | solution.py:210
  18.9 3.7 %collective-permute-start.8 = (f32[32,128]{1,0:T(8,128)S(1)}, f32[32,128]{1,0:T(8,128)S(1)}, u32[]{:S(2)}, u32[]{:S(2)}) collective-permute-start(f32[32,128]{1,0:T(8,128)S(1)} %get-tuple-element.29), channel_id=1, source_target_pairs={{0,16},{1,17},{2,18},{3,19},{4,20},{5,21},{6,22},{7,23},{8,24},{9,... | collective-permute-start | bytes 49160 | tf_op jit(solution)/shard_map/ppermute | solution.py:210
  19.6 3.2 %collective-permute-start.9 = (f32[32,128]{1,0:T(8,128)S(1)}, f32[32,128]{1,0:T(8,128)S(1)}, u32[]{:S(2)}, u32[]{:S(2)}) collective-permute-start(f32[32,128]{1,0:T(8,128)S(1)} %get-tuple-element.30), channel_id=1, source_target_pairs={{0,3},{1,2},{2,1},{3,0},{4,7},{5,6},{6,5},{7,4},{8,11},{9,10},{10,... | collective-permute-start | bytes 49160 | tf_op jit(solution)/shard_map/ppermute | solution.py:210

commit v17 on v16

--- a/solution.py
+++ b/solution.py
@@ -14,12 +14,7 @@
 
 
 def device_class(index):
-    return (index ^ (index >> 1) ^ (index >> 2)) & 1
-
-
-def exchange_of(far, here):
-    half = 1 - ((here ^ (here >> 2)) & 1)
-    return far ^ (half & ((far >> 1) | (far >> 2) | (far >> 3)) & 1)
+    return (index ^ (index >> 1) ^ (index >> 3)) & 1
 
 
 def spread_kernel(rhs, expand_ref):
@@ -61,12 +56,8 @@
     gate_ref[...] = jnp.broadcast_to(gate, gate_ref.shape)
     held_ref[...] = own_ref[...]
     owner = owner_ref[...]
-    apart = owner ^ here
-    given = device_class(owner) ^ device_class(here)
     code_ref[...] = (
-        given * (panels // 2)
-        + exchange_of(apart >> 2, here ^ given) * 2
-        + ((apart >> 1) & 1)
+        (device_class(owner) ^ device_class(here)) * (panels // 2) + ((owner ^ here) >> 1)
     ) * struct_count + local_ref[...]
 
 
@@ -105,13 +96,12 @@
 
 def spline_kernel(
     rhs, _, mirror_ref, code_vmem, part_ref, gate_ref, near_ref, spline_ref,
-    sums_ref, acc, send_ref, code_ref, sem,
+    sums_ref, acc, pair_ref, far_ref, code_ref, sem,
 ):
     copy = pltpu.make_async_copy(code_vmem, code_ref, sem)
     copy.start()
     block_count, splines = code_ref.shape
     rows, width = part_ref.shape
-    tiles = acc.shape[0] // 2
     loads = []
     for g in range(rows // PACK):
         group = slice(g * PACK, (g + 1) * PACK)
@@ -160,7 +150,12 @@
                 sums.append(acc[place] + added)
             for place, value in zip(places, sums):
                 acc[place] = value
-    send_ref[...] = acc[tiles:].reshape(send_ref.shape).astype(send_ref.dtype)
+    tiles, far_tiles = acc.shape[0] // 2, far_ref.shape[1] * far_ref.shape[2] // TILE
+    kept = slice(tiles, 2 * tiles - far_tiles)
+    pair_ref[...] = acc[kept].reshape(pair_ref.shape).astype(pair_ref.dtype)
+    for which in range(2):
+        group = slice((which + 1) * tiles - far_tiles, (which + 1) * tiles)
+        far_ref[which] = acc[group].reshape(far_ref.shape[1:]).astype(far_ref.dtype)
 
 
 def split_kernel(acc, got_ref, *out_refs):
@@ -173,12 +168,22 @@
             out_ref[place] = (held + got_ref[index].astype(jnp.float32)).astype(out_ref.dtype)
 
 
-def column_kernel(machs, held_ref, *refs):
-    got_refs, out_refs = refs[: -2 * machs], refs[-2 * machs :]
+def hand_kernel(held_ref, far_ref, keep_ref, given_ref):
+    keep_ref[...] = held_ref[...] + far_ref[0].astype(jnp.float32)
+    given_ref[...] = far_ref[1]
+
+
+def gather_kernel(held_ref, *refs):
+    got_refs, out_ref = refs[:-1], refs[-1]
+    total = held_ref[...]
+    for got_ref in got_refs:
+        total = total + got_ref[...].astype(jnp.float32)
+    out_ref[...] = total
+
+
+def column_kernel(machs, held_ref, got_ref, *out_refs):
     for place in range(2):
-        total = held_ref[place]
-        for got_ref in got_refs:
-            total = total + got_ref[place].astype(jnp.float32)
+        total = held_ref[place] + got_ref[place].astype(jnp.float32)
         for out_ref in out_refs[place * machs : (place + 1) * machs]:
             out_ref[...] = total.astype(out_ref.dtype)
 
@@ -195,6 +200,10 @@
         out_ref[g * PACK : (g + 1) * PACK] = grouped_product(
             rhs, rounded[g * PACK : (g + 1) * PACK], lambda t: inverse_ref[t], g
         )
+
+
+def mask_of(step):
+    return 4 * step + (step >> 1) % 2
 
 
 def swap(value, panels, apart):
@@ -271,15 +280,18 @@
         cost_estimate=cost(10**6, 2**17),
         name="near_field",
     )(hot, held, pair, cross, near_blocks[0])
-    sums, acc, send = pl.pallas_call(
+    steps = panels // 4
+    two = (2, struct_rows, width)
+    sums, acc, send, far = pl.pallas_call(
         functools.partial(spline_kernel, rhs),
         out_shape=(
             jax.ShapeDtypeStruct((rows, width), f32),
             jax.ShapeDtypeStruct((panels * struct_rows // TILE, TILE, width), f32),
-            jax.ShapeDtypeStruct((panels // 2, struct_rows, width), bf16),
+            jax.ShapeDtypeStruct((2 * (steps - 1), struct_rows, width), bf16),
+            jax.ShapeDtypeStruct((2, *two), bf16),
         ),
         in_specs=[VMEM] * 7,
-        out_specs=(VMEM,) * 3,
+        out_specs=(VMEM,) * 4,
         scratch_shapes=[
             pltpu.SMEM(spline_owner.shape, jnp.int32),
             pltpu.SemaphoreType.DMA,
@@ -290,36 +302,48 @@
     )(pair, mirror, code, part, gate, near_blocks[0], spline_blocks)
     loads = sums.reshape(adjoint.shape) * trim_mask[0].astype(f32)[None, None, :, None]
     got = swap(send, panels, 1)
-    steps = panels // 4
-    two = (2, struct_rows, width)
+    far = swap(far, panels, mask_of(steps - 1))
     keep, *sends = pl.pallas_call(
         split_kernel,
         out_shape=tuple(
-            jax.ShapeDtypeStruct(two, f32 if step == 0 else bf16) for step in range(steps)
+            jax.ShapeDtypeStruct(two, f32 if step == 0 else bf16) for step in range(steps - 1)
         ),
         in_specs=[VMEM, VMEM],
-        out_specs=(VMEM,) * steps,
+        out_specs=(VMEM,) * (steps - 1),
         compiler_params=params,
         cost_estimate=cost(10**6, 2**17),
         name="pair_sum",
     )(acc, got)
-    got = []
-    for step in range(steps - 1, 0, -1):
-        pairs = []
-        for i in range(panels):
-            far = exchange_of(step, i)
-            pairs.append((i, i ^ (4 * far + far % 2)))
-        got.append(lax.ppermute(sends[step - 1], "panel", pairs))
+    got = [swap(sends[step - 1], panels, mask_of(step)) for step in range(steps - 2, 0, -1)]
+    keep, given = pl.pallas_call(
+        hand_kernel,
+        out_shape=(jax.ShapeDtypeStruct(two, f32), jax.ShapeDtypeStruct(two, bf16)),
+        in_specs=[VMEM, VMEM],
+        out_specs=(VMEM, VMEM),
+        compiler_params=params,
+        cost_estimate=cost(10**6, 2**17),
+        name="hand_over",
+    )(keep, far)
+    given = swap(given, panels, 1)
+    keep = pl.pallas_call(
+        gather_kernel,
+        out_shape=jax.ShapeDtypeStruct(two, f32),
+        in_specs=[VMEM] * (steps - 1),
+        out_specs=VMEM,
+        compiler_params=params,
+        cost_estimate=cost(4 * 10**9, 16 * 2**20),
+        name="far_sum",
+    )(keep, *got)
     one = jax.ShapeDtypeStruct((struct_rows, width), f32)
     columns = pl.pallas_call(
         functools.partial(column_kernel, machs),
         out_shape=(one,) * (2 * machs),
-        in_specs=[VMEM] * steps,
+        in_specs=[VMEM] * 2,
         out_specs=(VMEM,) * (2 * machs),
         compiler_params=params,
         cost_estimate=cost(10**6, 2**17),
         name="column_sum",
-    )(keep, *got)
+    )(keep, given)
     sames = [
         mach_swap(columns[turn], machs, panels, turn, 0) if turn else columns[0]
         for turn in range(machs)

time: 23.6 us -> 22.9 us (0.970)
  waiting for transfers between devices: 7.9 us -> 5.26 us
  starting transfers between devices: 11.8 us -> 13.6 us
    ppermute x3 -> x7, starting transfers between devices: 2.52 us -> 7.52 us  [swap(): return lax.ppermute(value, 'panel', [(i, i ^ apart) for i in range(panels)])]
    ppermute x3 -> x0, waiting for transfers between devices: 3.72 us -> none  [on_device(): got.append(lax.ppermute(sends[step - 1], 'panel', pairs))]
    ppermute x3 -> x0, starting transfers between devices: 3.27 us -> none  [on_device(): got.append(lax.ppermute(sends[step - 1], 'panel', pairs))]
    ppermute x3 -> x7, waiting for transfers between devices: 2.76 us -> 3.7 us  [swap(): return lax.ppermute(value, 'panel', [(i, i ^ apart) for i in range(panels)])]
  transfers between devices with their start and end apart: 10 -> 11, of which waited for: 7 -> 7; matrix products, arithmetic and copies ran while one was open for 3% -> 3% of each run, Pallas kernels for 3% -> 3%
where the time goes in v17:
time: 22.9 us; the launch traced here: 22.8 us
  starting transfers between devices  13.6 us (59%)
  waiting for transfers between devices  5.26 us (23%)
  Pallas kernels  2.46 us (11%)
  between operations  0.79 us (3%)
  other arithmetic  0.68 us (3%)
    ppermute x7, starting transfers between devices, swap(): return lax.ppermute(value, 'panel', [(i, i ^ apart) for i in range(panels)])  7.52 us
    ppermute x7, waiting for transfers between devices, swap(): return lax.ppermute(value, 'panel', [(i, i ^ apart) for i in range(panels)])  3.7 us
    ppermute x3, starting transfers between devices, mach_swap(): return lax.ppermute(value, ('mach', 'panel'), pairs)  3.03 us
    ppermute x1, starting transfers between devices, on_device(): lax.ppermute(own, ('mach', 'panel'), [(mach * panels + i, (mach ^ (i in b...  3 us
    ppermute x3, waiting for transfers between devices, mach_swap(): return lax.ppermute(value, ('mach', 'panel'), pairs)  1.56 us
    pallas_call x1, Pallas kernels, on_device(): pl.pallas_call(functools.partial(spline_kernel, rhs), out_shape=(jax.Shap...  0.95 us
    pallas_call x1, Pallas kernels, on_device(): pl.pallas_call(functools.partial(inverse_kernel, rhs, machs), out_shape=j...  0.76 us
    mul x1, other arithmetic, on_device(): sums.reshape(adjoint.shape) * trim_mask[0].astype(f32)[None, None, :, None]  0.68 us
  transfers between devices with their start and end apart: 11, of which 7 were waited for; matrix products, arithmetic and copies ran while one was open for 3% of the time, Pallas kernels for 3%

profile of v17, /device:TPU:0, one launch (start us, length us, event | category | flops | bytes accessed | tf_op | source)
XLA Modules:
  0.0 22.8 jit_solution(4851822246228352236)
XLA Ops:
  0.6 0.0 copy-start.3
  0.6 0.0 copy-start.4
  0.7 0.0 copy-start.5
  0.7 0.0 copy-start.6
  0.7 3.0 %collective-permute-start.2 = (bf16[32,128]{1,0:T(8,128)(2,1)}, bf16[32,128]{1,0:T(8,128)(2,1)S(1)}, u32[]{:S(2)}, u32[]{:S(2)}) collective-permute-start(bf16[32,128]{1,0:T(8,128)(2,1)} %bitcast.9), channel_id=1, source_target_pairs={{0,16},{1,2},{2,1},{3,4},{4,3},{5,6},{6,5},{7,8},{8,7},{9,10},{10,... | collective-permute-start | bytes 24584 | tf_op jit(solution)/shard_map/ppermute | solution.py:239
  3.7 1.9 %collective-permute-start.1 = (bf16[32,128]{1,0:T(8,128)(2,1)}, bf16[32,128]{1,0:T(8,128)(2,1)S(1)}, u32[]{:S(2)}, u32[]{:S(2)}) collective-permute-start(bf16[32,128]{1,0:T(8,128)(2,1)} %bitcast.10), channel_id=1, source_target_pairs={{0,8},{1,9},{2,10},{3,11},{4,12},{5,13},{6,14},{7,15},{8,0},{9,1},... | collective-permute-start | bytes 24584 | tf_op jit(solution)/shard_map/ppermute | solution.py:210
  5.6 0.5 %collective-permute-start = (bf16[32,128]{1,0:T(8,128)(2,1)}, bf16[32,128]{1,0:T(8,128)(2,1)S(1)}, u32[]{:S(2)}, u32[]{:S(2)}) collective-permute-start(bf16[32,128]{1,0:T(8,128)(2,1)} %bitcast.11), channel_id=1, source_target_pairs={{0,1},{1,0},{2,3},{3,2},{4,5},{5,4},{6,7},{7,6},{8,9},{9,8},{10,11... | collective-permute-start | bytes 24584 | tf_op jit(solution)/shard_map/ppermute | solution.py:210
  6.2 0.0 copy-start.1
  6.2 0.2 %pick_rows.1 = (bf16[192,128]{1,0:T(8,128)(2,1)S(1)}, f32[16,128]{1,0:T(8,128)S(1)}, bf16[32,128]{1,0:T(8,128)(2,1)S(1)}, s32[8,6]{1,0:T(8,128)S(1)}) custom-call(bf16[32,8]{1,0:T(8,128)(2,1)S(1)} %row_order.1.expand_ref, s32[8,8]{1,0:T(8,128)S(1)} %copy-done.4, s32[1,4]{1,0:T(1,128)S(1)} %copy-done.7, bf16[32,128]{1,0:T(8,128)(2,1)S(1)} %bitcast.12, ...), custom_call_target="tpu_custom_call" | custom-call | flops 1000000 | bytes 131072 | tf_op jit(solution)/shard_map/pick_rows/pallas_call | solution.py:260
  6.5 0.0 collective-permute-done.2.cross_ref
  6.5 0.7 %collective-permute-done.pair_ref._ = bf16[32,128]{1,0:T(8,128)(2,1)S(1)} collective-permute-done((bf16[32,128]{1,0:T(8,128)(2,1)}, bf16[32,128]{1,0:T(8,128)(2,1)S(1)}, u32[]{:S(2)}, u32[]{:S(2)}) %collective-permute-start) | collective-permute-done | bytes 8224 | tf_op jit(solution)/shard_map/ppermute | solution.py:210
  7.2 0.5 %near_field.1.part_ref = f32[32,128]{1,0:T(8,128)S(1)} custom-call(bf16[192,128]{1,0:T(8,128)(2,1)S(1)} %get-tuple-element.20.hot_ref, bf16[32,128]{1,0:T(8,128)(2,1)S(1)} %get-tuple-element.21.own_ref, bf16[32,128]{1,0:T(8,128)(2,1)S(1)} %collective-permute-done.pair_ref._, bf16[32,128]{1,0:T(8,128)(2,1)S(1)} %collective-permute-done.2.cross_ref, ...), custom_call_target="tpu_custom_call" | custom-call | flops 1000000 | bytes 131072 | tf_op jit(solution)/shard_map/near_field/pallas_call | solution.py:274
  7.6 0.8 %collective-permute-done.1.mirror_ref = bf16[32,128]{1,0:T(8,128)(2,1)S(1)} collective-permute-done((bf16[32,128]{1,0:T(8,128)(2,1)}, bf16[32,128]{1,0:T(8,128)(2,1)S(1)}, u32[]{:S(2)}, u32[]{:S(2)}) %collective-permute-start.1) | collective-permute-done | bytes 8224 | tf_op jit(solution)/shard_map/ppermute | solution.py:210
  8.5 0.9 %spline_loads.1 = (f32[32,128]{1,0:T(8,128)S(1)}, f32[64,8,128]{2,1,0:T(8,128)S(1)}, bf16[6,32,128]{2,1,0:T(8,128)(2,1)S(1)}, bf16[2,2,32,128]{3,2,1,0:T(8,128)(2,1)S(1)}) custom-call(bf16[32,128]{1,0:T(8,128)(2,1)S(1)} %collective-permute-done.pair_ref._, bf16[32,128]{1,0:T(8,128)(2,1)S(1)} %collective-permute-done.1.mirror_ref, ...), custom_call_target="tpu_custom_call" | custom-call | flops 1000000 | bytes 131072 | tf_op jit(solution)/shard_map/spline_loads/pallas_call | solution.py:285
  9.4 0.1 collective-permute-start.3
  9.5 3.1 %collective-permute-start.4 = (bf16[2,2,32,128]{3,2,1,0:T(8,128)(2,1)S(1)}, bf16[2,2,32,128]{3,2,1,0:T(8,128)(2,1)S(1)}, u32[]{:S(2)}, u32[]{:S(2)}) collective-permute-start(bf16[2,2,32,128]{3,2,1,0:T(8,128)(2,1)S(1)} %get-tuple-element.27), channel_id=1, source_target_pairs={{0,13},{1,12},{2,15},{3,14},{4,9},{5,8},{6,11},{7,10},{8,5},{9,4},... | collective-permute-start | bytes 98312 | tf_op jit(solution)/shard_map/ppermute | solution.py:210
  12.6 0.0 collective-permute-done.3.got_ref
  12.6 0.1 collective-permute-start.5
  12.7 1.4 %collective-permute-start.6 = (bf16[2,32,128]{2,1,0:T(8,128)(2,1)S(1)}, bf16[2,32,128]{2,1,0:T(8,128)(2,1)S(1)}, u32[]{:S(2)}, u32[]{:S(2)}) collective-permute-start(bf16[2,32,128]{2,1,0:T(8,128)(2,1)S(1)} %get-tuple-element.30), channel_id=1, source_target_pairs={{0,4},{1,5},{2,6},{3,7},{4,0},{5,1},{6,2},{7,3},{8,12},{9,13},{10,... | collective-permute-start | bytes 49160 | tf_op jit(solution)/shard_map/ppermute | solution.py:210
  14.1 0.6 %collective-permute-done.4.far_ref = bf16[2,2,32,128]{3,2,1,0:T(8,128)(2,1)S(1)} collective-permute-done((bf16[2,2,32,128]{3,2,1,0:T(8,128)(2,1)S(1)}, bf16[2,2,32,128]{3,2,1,0:T(8,128)(2,1)S(1)}, u32[]{:S(2)}, u32[]{:S(2)}) %collective-permute-start.4) | collective-permute-done | bytes 32800 | tf_op jit(solution)/shard_map/ppermute | solution.py:210
  14.7 0.4 %collective-permute-start.7 = (bf16[2,32,128]{2,1,0:T(8,128)(2,1)S(1)}, bf16[2,32,128]{2,1,0:T(8,128)(2,1)S(1)}, u32[]{:S(2)}, u32[]{:S(2)}) collective-permute-start(bf16[2,32,128]{2,1,0:T(8,128)(2,1)S(1)} %get-tuple-element.31), channel_id=1, source_target_pairs={{0,1},{1,0},{2,3},{3,2},{4,5},{5,4},{6,7},{7,6},{8,9},{9,8},{10,11... | collective-permute-start | bytes 49160 | tf_op jit(solution)/shard_map/ppermute | solution.py:210
  15.2 1.6 %collective-permute-done.5.refs_0_ = bf16[2,32,128]{2,1,0:T(8,128)(2,1)S(1)} collective-permute-done((bf16[2,32,128]{2,1,0:T(8,128)(2,1)S(1)}, bf16[2,32,128]{2,1,0:T(8,128)(2,1)S(1)}, u32[]{:S(2)}, u32[]{:S(2)}) %collective-permute-start.5) | collective-permute-done | bytes 16416 | tf_op jit(solution)/shard_map/ppermute | solution.py:210
  16.7 0.0 collective-permute-done.6.refs_1_
  16.7 0.0 collective-permute-done.7.got_ref
  16.8 1.5 %collective-permute-start.8 = (f32[32,128]{1,0:T(8,128)S(1)}, f32[32,128]{1,0:T(8,128)S(1)}, u32[]{:S(2)}, u32[]{:S(2)}) collective-permute-start(f32[32,128]{1,0:T(8,128)S(1)} %get-tuple-element.32), channel_id=1, source_target_pairs={{0,19},{1,18},{2,17},{3,16},{4,23},{5,22},{6,21},{7,20},{8,27},{9,... | collective-permute-start | bytes 49160 | tf_op jit(solution)/shard_map/ppermute | solution.py:219
  18.2 0.6 %collective-permute-start.9 = (f32[32,128]{1,0:T(8,128)S(1)}, f32[32,128]{1,0:T(8,128)S(1)}, u32[]{:S(2)}, u32[]{:S(2)}) collective-permute-start(f32[32,128]{1,0:T(8,128)S(1)} %get-tuple-element.33), channel_id=1, source_target_pairs={{0,16},{1,17},{2,18},{3,19},{4,20},{5,21},{6,22},{7,23},{8,24},{9,... | collective-permute-start | bytes 49160 | tf_op jit(solution)/shard_map/ppermute | solution.py:219
  18.9 0.9 %collective-permute-start.10 = (f32[32,128]{1,0:T(8,128)S(1)}, f32[32,128]{1,0:T(8,128)S(1)}, u32[]{:S(2)}, u32[]{:S(2)}) collective-permute-start(f32[32,128]{1,0:T(8,128)S(1)} %get-tuple-element.34), channel_id=1, source_target_pairs={{0,3},{1,2},{2,1},{3,0},{4,7},{5,6},{6,5},{7,4},{8,11},{9,10},{10,... | collective-permute-start | bytes 49160 | tf_op jit(solution)/shard_map/ppermute | solution.py:219
  19.8 0.7 %broadcast_multiply_fusion = f32[1,8,4,128]{3,2,1,0:T(4,128)} fusion(f32[1,8,4,128]{3,2,1,0:T(4,128)S(1)} %bitcast.8, f32[4]{0:T(128)S(1)} %convert_bitcast_fusion), kind=kLoop, calls=%fused_computation | loop fusion | flops 4096 | bytes 32784 | tf_op jit(solution)/shard_map/mul | solution.py:303
  20.5 0.4 %collective-permute-done.8.refs_0_ = f32[32,128]{1,0:T(8,128)S(1)} collective-permute-done((f32[32,128]{1,0:T(8,128)S(1)}, f32[32,128]{1,0:T(8,128)S(1)}, u32[]{:S(2)}, u32[]{:S(2)}) %collective-permute-start.8) | collective-permute-done | bytes 16416 | tf_op jit(solution)/shard_map/ppermute | solution.py:219
  20.9 1.1 %collective-permute-done.9.refs_1_ = f32[32,128]{1,0:T(8,128)S(1)} collective-permute-done((f32[32,128]{1,0:T(8,128)S(1)}, f32[32,128]{1,0:T(8,128)S(1)}, u32[]{:S(2)}, u32[]{:S(2)}) %collective-permute-start.9) | collective-permute-done | bytes 16416 | tf_op jit(solution)/shard_map/ppermute | solution.py:219
  22.0 0.1 collective-permute-done.10.refs_2_
  22.0 0.8 %struct_solve.1 = f32[32,128]{1,0:T(8,128)} custom-call(f32[32,128]{1,0:T(8,128)S(1)} %collective-permute-done.8.refs_0_, f32[32,128]{1,0:T(8,128)S(1)} %collective-permute-done.9.refs_1_, f32[32,128]{1,0:T(8,128)S(1)} %collective-permute-done.10.refs_2_, f32[32,128]{1,0:T(8,128)S(1)} %get-tuple-element.35.refs_3_, bf16[8,128,128]{2,1,0:T(8,128)(2,1)S(1)} %copy-done.2), custom_call_target="tpu_custom_call" | custom-call | flops 1000000 | bytes 131072 | tf_op jit(solution)/shard_map/struct_solve/pallas_call | solution.py:352
  (17 shorter events, 0.1 us)
Async XLA Ops:
  0.6 5.5 %copy-start.3 = (bf16[1,8,4,128]{3,2,1,0:T(4,128)(2,1)S(1)}, bf16[1,8,4,128]{3,2,1,0:T(4,128)(2,1)}, u32[]{:S(2)}) copy-start(bf16[1,8,4,128]{3,2,1,0:T(4,128)(2,1)} %param.8) | copy-start | bytes 24580
  0.6 5.5 %copy-start.4 = (s32[8,8]{1,0:T(8,128)S(1)}, s32[8,8]{1,0:T(8,128)}, u32[]{:S(2)}) copy-start(s32[8,8]{1,0:T(8,128)} %pattern_ref.1) | copy-start | bytes 772
  0.7 5.5 %copy-start.5 = (s32[8,6]{1,0:T(8,128)S(1)}, s32[8,6]{1,0:T(8,128)}, u32[]{:S(2)}) copy-start(s32[8,6]{1,0:T(8,128)} %owner_ref.1) | copy-start | bytes 580
  0.7 5.5 %copy-start.6 = (s32[8,6]{1,0:T(8,128)S(1)}, s32[8,6]{1,0:T(8,128)}, u32[]{:S(2)}) copy-start(s32[8,6]{1,0:T(8,128)} %local_ref.1) | copy-start | bytes 580
  0.7 5.5 %copy-start.7 = (s32[1,4]{1,0:T(1,128)S(1)}, s32[1,4]{1,0:T(1,128)}, u32[]{:S(2)}) copy-start(s32[1,4]{1,0:T(1,128)} %trim_ref.1) | copy-start | bytes 52
  0.7 6.5 %copy-start = (bf16[1,8,8,128,128]{4,3,2,1,0:T(8,128)(2,1)S(1)}, bf16[1,8,8,128,128]{4,3,2,1,0:T(8,128)(2,1)}, u32[]{:S(2)}) copy-start(bf16[1,8,8,128,128]{4,3,2,1,0:T(8,128)(2,1)} %param.9) | copy-start | bytes 6291460
  0.7 5.8 %collective-permute-start.2 = (bf16[32,128]{1,0:T(8,128)(2,1)}, bf16[32,128]{1,0:T(8,128)(2,1)S(1)}, u32[]{:S(2)}, u32[]{:S(2)}) collective-permute-start(bf16[32,128]{1,0:T(8,128)(2,1)} %bitcast.9), channel_id=1, source_target_pairs={{0,16},{1,2},{2,1},{3,4},{4,3},{5,6},{6,5},{7,8},{8,7},{9,10},{10,... | collective-permute-start | bytes 24584 | tf_op jit(solution)/shard_map/ppermute | solution.py:239
  3.7 4.8 %collective-permute-start.1 = (bf16[32,128]{1,0:T(8,128)(2,1)}, bf16[32,128]{1,0:T(8,128)(2,1)S(1)}, u32[]{:S(2)}, u32[]{:S(2)}) collective-permute-start(bf16[32,128]{1,0:T(8,128)(2,1)} %bitcast.10), channel_id=1, source_target_pairs={{0,8},{1,9},{2,10},{3,11},{4,12},{5,13},{6,14},{7,15},{8,0},{9,1},... | collective-permute-start | bytes 24584 | tf_op jit(solution)/shard_map/ppermute | solution.py:210
  5.6 1.5 %collective-permute-start = (bf16[32,128]{1,0:T(8,128)(2,1)}, bf16[32,128]{1,0:T(8,128)(2,1)S(1)}, u32[]{:S(2)}, u32[]{:S(2)}) collective-permute-start(bf16[32,128]{1,0:T(8,128)(2,1)} %bitcast.11), channel_id=1, source_target_pairs={{0,1},{1,0},{2,3},{3,2},{4,5},{5,4},{6,7},{7,6},{8,9},{9,8},{10,11... | collective-permute-start | bytes 24584 | tf_op jit(solution)/shard_map/ppermute | solution.py:210
  6.2 2.3 %copy-start.1 = (bf16[8,6,128,128]{3,2,1,0:T(8,128)(2,1)S(1)}, bf16[8,6,128,128]{3,2,1,0:T(8,128)(2,1)}, u32[]{:S(2)}) copy-start(bf16[8,6,128,128]{3,2,1,0:T(8,128)(2,1)} %spline_ref.1) | copy-start | bytes 4718596
  9.4 3.2 %collective-permute-start.3 = (bf16[6,32,128]{2,1,0:T(8,128)(2,1)S(1)}, bf16[6,32,128]{2,1,0:T(8,128)(2,1)S(1)}, u32[]{:S(2)}, u32[]{:S(2)}) collective-permute-start(bf16[6,32,128]{2,1,0:T(8,128)(2,1)S(1)} %get-tuple-element.25), channel_id=1, source_target_pairs={{0,1},{1,0},{2,3},{3,2},{4,5},{5,4},{6,7},{7,6},{8,9},{9,8},{10,11... | collective-permute-start | bytes 147464 | tf_op jit(solution)/shard_map/ppermute | solution.py:210
  9.5 5.2 %collective-permute-start.4 = (bf16[2,2,32,128]{3,2,1,0:T(8,128)(2,1)S(1)}, bf16[2,2,32,128]{3,2,1,0:T(8,128)(2,1)S(1)}, u32[]{:S(2)}, u32[]{:S(2)}) collective-permute-start(bf16[2,2,32,128]{3,2,1,0:T(8,128)(2,1)S(1)} %get-tuple-element.27), channel_id=1, source_target_pairs={{0,13},{1,12},{2,15},{3,14},{4,9},{5,8},{6,11},{7,10},{8,5},{9,4},... | collective-permute-start | bytes 98312 | tf_op jit(solution)/shard_map/ppermute | solution.py:210
  12.6 4.1 %collective-permute-start.5 = (bf16[2,32,128]{2,1,0:T(8,128)(2,1)S(1)}, bf16[2,32,128]{2,1,0:T(8,128)(2,1)S(1)}, u32[]{:S(2)}, u32[]{:S(2)}) collective-permute-start(bf16[2,32,128]{2,1,0:T(8,128)(2,1)S(1)} %get-tuple-element.29), channel_id=1, source_target_pairs={{0,9},{1,8},{2,11},{3,10},{4,13},{5,12},{6,15},{7,14},{8,1},{9,0},... | collective-permute-start | bytes 49160 | tf_op jit(solution)/shard_map/ppermute | solution.py:210
  12.7 4.1 %collective-permute-start.6 = (bf16[2,32,128]{2,1,0:T(8,128)(2,1)S(1)}, bf16[2,32,128]{2,1,0:T(8,128)(2,1)S(1)}, u32[]{:S(2)}, u32[]{:S(2)}) collective-permute-start(bf16[2,32,128]{2,1,0:T(8,128)(2,1)S(1)} %get-tuple-element.30), channel_id=1, source_target_pairs={{0,4},{1,5},{2,6},{3,7},{4,0},{5,1},{6,2},{7,3},{8,12},{9,13},{10,... | collective-permute-start | bytes 49160 | tf_op jit(solution)/shard_map/ppermute | solution.py:210
  14.7 2.0 %collective-permute-start.7 = (bf16[2,32,128]{2,1,0:T(8,128)(2,1)S(1)}, bf16[2,32,128]{2,1,0:T(8,128)(2,1)S(1)}, u32[]{:S(2)}, u32[]{:S(2)}) collective-permute-start(bf16[2,32,128]{2,1,0:T(8,128)(2,1)S(1)} %get-tuple-element.31), channel_id=1, source_target_pairs={{0,1},{1,0},{2,3},{3,2},{4,5},{5,4},{6,7},{7,6},{8,9},{9,8},{10,11... | collective-permute-start | bytes 49160 | tf_op jit(solution)/shard_map/ppermute | solution.py:210
  16.7 5.3 %copy-start.2 = (bf16[8,128,128]{2,1,0:T(8,128)(2,1)S(1)}, bf16[8,128,128]{2,1,0:T(8,128)(2,1)}, u32[]{:S(2)}) copy-start(bf16[8,128,128]{2,1,0:T(8,128)(2,1)} %refs_4_.1) | copy-start | bytes 786436
  16.8 4.1 %collective-permute-start.8 = (f32[32,128]{1,0:T(8,128)S(1)}, f32[32,128]{1,0:T(8,128)S(1)}, u32[]{:S(2)}, u32[]{:S(2)}) collective-permute-start(f32[32,128]{1,0:T(8,128)S(1)} %get-tuple-element.32), channel_id=1, source_target_pairs={{0,19},{1,18},{2,17},{3,16},{4,23},{5,22},{6,21},{7,20},{8,27},{9,... | collective-permute-start | bytes 49160 | tf_op jit(solution)/shard_map/ppermute | solution.py:219
  18.2 3.7 %collective-permute-start.9 = (f32[32,128]{1,0:T(8,128)S(1)}, f32[32,128]{1,0:T(8,128)S(1)}, u32[]{:S(2)}, u32[]{:S(2)}) collective-permute-start(f32[32,128]{1,0:T(8,128)S(1)} %get-tuple-element.33), channel_id=1, source_target_pairs={{0,16},{1,17},{2,18},{3,19},{4,20},{5,21},{6,22},{7,23},{8,24},{9,... | collective-permute-start | bytes 49160 | tf_op jit(solution)/shard_map/ppermute | solution.py:219
  18.9 3.2 %collective-permute-start.10 = (f32[32,128]{1,0:T(8,128)S(1)}, f32[32,128]{1,0:T(8,128)S(1)}, u32[]{:S(2)}, u32[]{:S(2)}) collective-permute-start(f32[32,128]{1,0:T(8,128)S(1)} %get-tuple-element.34), channel_id=1, source_target_pairs={{0,3},{1,2},{2,1},{3,0},{4,7},{5,6},{6,5},{7,4},{8,11},{9,10},{10,... | collective-permute-start | bytes 49160 | tf_op jit(solution)/shard_map/ppermute | solution.py:219

commit v18 on v17

--- a/solution.py
+++ b/solution.py
@@ -96,7 +96,7 @@
 
 def spline_kernel(
     rhs, _, mirror_ref, code_vmem, part_ref, gate_ref, near_ref, spline_ref,
-    sums_ref, acc, pair_ref, far_ref, code_ref, sem,
+    sums_ref, acc, pair_ref, code_ref, sem,
 ):
     copy = pltpu.make_async_copy(code_vmem, code_ref, sem)
     copy.start()
@@ -150,11 +150,15 @@
                 sums.append(acc[place] + added)
             for place, value in zip(places, sums):
                 acc[place] = value
-    tiles, far_tiles = acc.shape[0] // 2, far_ref.shape[1] * far_ref.shape[2] // TILE
-    kept = slice(tiles, 2 * tiles - far_tiles)
-    pair_ref[...] = acc[kept].reshape(pair_ref.shape).astype(pair_ref.dtype)
+    tiles = acc.shape[0] // 2
+    size = pair_ref.shape[0] * pair_ref.shape[1] // TILE
+    pair_ref[...] = acc[tiles : tiles + size].reshape(pair_ref.shape).astype(pair_ref.dtype)
+
+
+def far_kernel(acc, far_ref):
+    tiles, size = acc.shape[0] // 2, far_ref.shape[1] * far_ref.shape[2] // TILE
     for which in range(2):
-        group = slice((which + 1) * tiles - far_tiles, (which + 1) * tiles)
+        group = slice((which + 1) * tiles - size, (which + 1) * tiles)
         far_ref[which] = acc[group].reshape(far_ref.shape[1:]).astype(far_ref.dtype)
 
 
@@ -282,16 +286,15 @@
     )(hot, held, pair, cross, near_blocks[0])
     steps = panels // 4
     two = (2, struct_rows, width)
-    sums, acc, send, far = pl.pallas_call(
+    sums, acc, send = pl.pallas_call(
         functools.partial(spline_kernel, rhs),
         out_shape=(
             jax.ShapeDtypeStruct((rows, width), f32),
             jax.ShapeDtypeStruct((panels * struct_rows // TILE, TILE, width), f32),
             jax.ShapeDtypeStruct((2 * (steps - 1), struct_rows, width), bf16),
-            jax.ShapeDtypeStruct((2, *two), bf16),
         ),
         in_specs=[VMEM] * 7,
-        out_specs=(VMEM,) * 4,
+        out_specs=(VMEM,) * 3,
         scratch_shapes=[
             pltpu.SMEM(spline_owner.shape, jnp.int32),
             pltpu.SemaphoreType.DMA,
@@ -300,6 +303,15 @@
         cost_estimate=cost(10**6, 2**17),
         name="spline_loads",
     )(pair, mirror, code, part, gate, near_blocks[0], spline_blocks)
+    far = pl.pallas_call(
+        far_kernel,
+        out_shape=jax.ShapeDtypeStruct((2, *two), bf16),
+        in_specs=[VMEM],
+        out_specs=VMEM,
+        compiler_params=params,
+        cost_estimate=cost(10**6, 2**17),
+        name="far_loads",
+    )(acc)
     loads = sums.reshape(adjoint.shape) * trim_mask[0].astype(f32)[None, None, :, None]
     got = swap(send, panels, 1)
     far = swap(far, panels, mask_of(steps - 1))

time: 22.9 us -> 24 us (1.048)
  waiting for transfers between devices: 5.26 us -> 6.53 us
    ppermute x1, waiting for transfers between devices: 0.01 us -> 2.04 us  [on_device(): lax.ppermute(own, ('mach', 'panel'), [(mach * panels + i, (mach ^ (i in b...]
    ppermute x1, starting transfers between devices: 3 us -> 1.49 us  [on_device(): lax.ppermute(own, ('mach', 'panel'), [(mach * panels + i, (mach ^ (i in b...]
    ppermute x7, waiting for transfers between devices: 3.7 us -> 2.26 us  [swap(): return lax.ppermute(value, 'panel', [(i, i ^ apart) for i in range(panels)])]
    ppermute x7, starting transfers between devices: 7.52 us -> 8.94 us  [swap(): return lax.ppermute(value, 'panel', [(i, i ^ apart) for i in range(panels)])]
    ppermute x3, waiting for transfers between devices: 1.56 us -> 2.23 us  [mach_swap(): return lax.ppermute(value, ('mach', 'panel'), pairs)]
  transfers between devices with their start and end apart: 11 -> 11, of which waited for: 7 -> 6; matrix products, arithmetic and copies ran while one was open for 3% -> 3% of each run, Pallas kernels for 3% -> 3%
where the time goes in v18:
time: 24 us; the launch traced here: 23.8 us
  starting transfers between devices  13.4 us (56%)
  waiting for transfers between devices  6.53 us (27%)
  Pallas kernels  2.33 us (10%)
  between operations  0.8 us (3%)
  other arithmetic  0.68 us (3%)
    ppermute x7, starting transfers between devices, swap(): return lax.ppermute(value, 'panel', [(i, i ^ apart) for i in range(panels)])  8.94 us
    ppermute x3, starting transfers between devices, mach_swap(): return lax.ppermute(value, ('mach', 'panel'), pairs)  3.01 us
    ppermute x7, waiting for transfers between devices, swap(): return lax.ppermute(value, 'panel', [(i, i ^ apart) for i in range(panels)])  2.26 us
    ppermute x3, waiting for transfers between devices, mach_swap(): return lax.ppermute(value, ('mach', 'panel'), pairs)  2.23 us
    ppermute x1, waiting for transfers between devices, on_device(): lax.ppermute(own, ('mach', 'panel'), [(mach * panels + i, (mach ^ (i in b...  2.04 us
    ppermute x1, starting transfers between devices, on_device(): lax.ppermute(own, ('mach', 'panel'), [(mach * panels + i, (mach ^ (i in b...  1.49 us
    pallas_call x1, Pallas kernels, on_device(): pl.pallas_call(functools.partial(spline_kernel, rhs), out_shape=(jax.Shap...  0.81 us
    pallas_call x1, Pallas kernels, on_device(): pl.pallas_call(functools.partial(inverse_kernel, rhs, machs), out_shape=j...  0.76 us
  transfers between devices with their start and end apart: 11, of which 6 were waited for; matrix products, arithmetic and copies ran while one was open for 3% of the time, Pallas kernels for 3%

profile of v18, /device:TPU:0, one launch (start us, length us, event | category | flops | bytes accessed | tf_op | source)
XLA Modules:
  0.0 23.8 jit_solution(2696626227656593839)
XLA Ops:
  0.6 0.0 copy-start.3
  0.6 0.0 copy-start.4
  0.7 0.0 copy-start.5
  0.7 0.0 copy-start.6
  0.7 0.5 %collective-permute-start = (bf16[32,128]{1,0:T(8,128)(2,1)}, bf16[32,128]{1,0:T(8,128)(2,1)S(1)}, u32[]{:S(2)}, u32[]{:S(2)}) collective-permute-start(bf16[32,128]{1,0:T(8,128)(2,1)} %bitcast.9), channel_id=1, source_target_pairs={{0,1},{1,0},{2,3},{3,2},{4,5},{5,4},{6,7},{7,6},{8,9},{9,8},{10,11... | collective-permute-start | bytes 24584 | tf_op jit(solution)/shard_map/ppermute | solution.py:214
  1.2 3.7 %collective-permute-start.1 = (bf16[32,128]{1,0:T(8,128)(2,1)}, bf16[32,128]{1,0:T(8,128)(2,1)S(1)}, u32[]{:S(2)}, u32[]{:S(2)}) collective-permute-start(bf16[32,128]{1,0:T(8,128)(2,1)} %bitcast.10), channel_id=1, source_target_pairs={{0,8},{1,9},{2,10},{3,11},{4,12},{5,13},{6,14},{7,15},{8,0},{9,1},... | collective-permute-start | bytes 24584 | tf_op jit(solution)/shard_map/ppermute | solution.py:214
  4.9 1.5 %collective-permute-start.2 = (bf16[32,128]{1,0:T(8,128)(2,1)}, bf16[32,128]{1,0:T(8,128)(2,1)S(1)}, u32[]{:S(2)}, u32[]{:S(2)}) collective-permute-start(bf16[32,128]{1,0:T(8,128)(2,1)} %bitcast.11), channel_id=1, source_target_pairs={{0,16},{1,2},{2,1},{3,4},{4,3},{5,6},{6,5},{7,8},{8,7},{9,10},{10,... | collective-permute-start | bytes 24584 | tf_op jit(solution)/shard_map/ppermute | solution.py:243
  6.4 0.0 copy-start.1
  6.4 0.2 %pick_rows.1 = (bf16[192,128]{1,0:T(8,128)(2,1)S(1)}, f32[16,128]{1,0:T(8,128)S(1)}, bf16[32,128]{1,0:T(8,128)(2,1)S(1)}, s32[8,6]{1,0:T(8,128)S(1)}) custom-call(bf16[32,8]{1,0:T(8,128)(2,1)S(1)} %row_order.1.expand_ref, s32[8,8]{1,0:T(8,128)S(1)} %copy-done.4, s32[1,4]{1,0:T(1,128)S(1)} %copy-done.7, bf16[32,128]{1,0:T(8,128)(2,1)S(1)} %bitcast.12, ...), custom_call_target="tpu_custom_call" | custom-call | flops 1000000 | bytes 131072 | tf_op jit(solution)/shard_map/pick_rows/pallas_call | solution.py:264
  6.7 0.0 collective-permute-done.pair_ref._
  6.7 2.0 %collective-permute-done.2.cross_ref = bf16[32,128]{1,0:T(8,128)(2,1)S(1)} collective-permute-done((bf16[32,128]{1,0:T(8,128)(2,1)}, bf16[32,128]{1,0:T(8,128)(2,1)S(1)}, u32[]{:S(2)}, u32[]{:S(2)}) %collective-permute-start.2) | collective-permute-done | bytes 8224 | tf_op jit(solution)/shard_map/ppermute | solution.py:243
  8.7 0.5 %near_field.1.part_ref = f32[32,128]{1,0:T(8,128)S(1)} custom-call(bf16[192,128]{1,0:T(8,128)(2,1)S(1)} %get-tuple-element.19.hot_ref, bf16[32,128]{1,0:T(8,128)(2,1)S(1)} %get-tuple-element.20.own_ref, bf16[32,128]{1,0:T(8,128)(2,1)S(1)} %collective-permute-done.pair_ref._, bf16[32,128]{1,0:T(8,128)(2,1)S(1)} %collective-permute-done.2.cross_ref, ...), custom_call_target="tpu_custom_call" | custom-call | flops 1000000 | bytes 131072 | tf_op jit(solution)/shard_map/near_field/pallas_call | solution.py:278
  9.2 0.0 collective-permute-done.1.mirror_ref
  9.2 0.8 %spline_loads.1 = (f32[32,128]{1,0:T(8,128)S(1)}, f32[64,8,128]{2,1,0:T(8,128)S(1)}, bf16[6,32,128]{2,1,0:T(8,128)(2,1)S(1)}) custom-call(bf16[32,128]{1,0:T(8,128)(2,1)S(1)} %collective-permute-done.pair_ref._, bf16[32,128]{1,0:T(8,128)(2,1)S(1)} %collective-permute-done.1.mirror_ref, s32[8,6]{1,0:T(8,128)S(1)} %get-tuple-element.18.code_vmem, ...), custom_call_target="tpu_custom_call" | custom-call | flops 1000000 | bytes 131072 | tf_op jit(solution)/shard_map/spline_loads/pallas_call | solution.py:289
  10.0 0.1 collective-permute-start.3
  10.1 1.8 %collective-permute-start.4 = (bf16[2,2,32,128]{3,2,1,0:T(8,128)(2,1)S(1)}, bf16[2,2,32,128]{3,2,1,0:T(8,128)(2,1)S(1)}, u32[]{:S(2)}, u32[]{:S(2)}) collective-permute-start(bf16[2,2,32,128]{3,2,1,0:T(8,128)(2,1)S(1)} %far_loads.1), channel_id=1, source_target_pairs={{0,13},{1,12},{2,15},{3,14},{4,9},{5,8},{6,11},{7,10},{8,5},{9,4},... | collective-permute-start | bytes 98312 | tf_op jit(solution)/shard_map/ppermute | solution.py:214
  11.9 0.0 collective-permute-done.3.got_ref
  11.9 1.4 %collective-permute-start.5 = (bf16[2,32,128]{2,1,0:T(8,128)(2,1)S(1)}, bf16[2,32,128]{2,1,0:T(8,128)(2,1)S(1)}, u32[]{:S(2)}, u32[]{:S(2)}) collective-permute-start(bf16[2,32,128]{2,1,0:T(8,128)(2,1)S(1)} %get-tuple-element.27), channel_id=1, source_target_pairs={{0,9},{1,8},{2,11},{3,10},{4,13},{5,12},{6,15},{7,14},{8,1},{9,0},... | collective-permute-start | bytes 49160 | tf_op jit(solution)/shard_map/ppermute | solution.py:214
  13.3 1.0 %collective-permute-start.6 = (bf16[2,32,128]{2,1,0:T(8,128)(2,1)S(1)}, bf16[2,32,128]{2,1,0:T(8,128)(2,1)S(1)}, u32[]{:S(2)}, u32[]{:S(2)}) collective-permute-start(bf16[2,32,128]{2,1,0:T(8,128)(2,1)S(1)} %get-tuple-element.28), channel_id=1, source_target_pairs={{0,4},{1,5},{2,6},{3,7},{4,0},{5,1},{6,2},{7,3},{8,12},{9,13},{10,... | collective-permute-start | bytes 49160 | tf_op jit(solution)/shard_map/ppermute | solution.py:214
  14.4 1.0 %collective-permute-done.4.far_ref = bf16[2,2,32,128]{3,2,1,0:T(8,128)(2,1)S(1)} collective-permute-done((bf16[2,2,32,128]{3,2,1,0:T(8,128)(2,1)S(1)}, bf16[2,2,32,128]{3,2,1,0:T(8,128)(2,1)S(1)}, u32[]{:S(2)}, u32[]{:S(2)}) %collective-permute-start.4) | collective-permute-done | bytes 32800 | tf_op jit(solution)/shard_map/ppermute | solution.py:214
  15.3 0.5 %collective-permute-start.7 = (bf16[2,32,128]{2,1,0:T(8,128)(2,1)S(1)}, bf16[2,32,128]{2,1,0:T(8,128)(2,1)S(1)}, u32[]{:S(2)}, u32[]{:S(2)}) collective-permute-start(bf16[2,32,128]{2,1,0:T(8,128)(2,1)S(1)} %get-tuple-element.29), channel_id=1, source_target_pairs={{0,1},{1,0},{2,3},{3,2},{4,5},{5,4},{6,7},{7,6},{8,9},{9,8},{10,11... | collective-permute-start | bytes 49160 | tf_op jit(solution)/shard_map/ppermute | solution.py:214
  15.8 0.5 %collective-permute-done.5.refs_0_ = bf16[2,32,128]{2,1,0:T(8,128)(2,1)S(1)} collective-permute-done((bf16[2,32,128]{2,1,0:T(8,128)(2,1)S(1)}, bf16[2,32,128]{2,1,0:T(8,128)(2,1)S(1)}, u32[]{:S(2)}, u32[]{:S(2)}) %collective-permute-start.5) | collective-permute-done | bytes 16416 | tf_op jit(solution)/shard_map/ppermute | solution.py:214
  16.3 0.8 %collective-permute-done.6.refs_1_ = bf16[2,32,128]{2,1,0:T(8,128)(2,1)S(1)} collective-permute-done((bf16[2,32,128]{2,1,0:T(8,128)(2,1)S(1)}, bf16[2,32,128]{2,1,0:T(8,128)(2,1)S(1)}, u32[]{:S(2)}, u32[]{:S(2)}) %collective-permute-start.6) | collective-permute-done | bytes 16416 | tf_op jit(solution)/shard_map/ppermute | solution.py:214
  17.1 0.0 collective-permute-done.7.got_ref
  17.1 2.2 %collective-permute-start.8 = (f32[32,128]{1,0:T(8,128)S(1)}, f32[32,128]{1,0:T(8,128)S(1)}, u32[]{:S(2)}, u32[]{:S(2)}) collective-permute-start(f32[32,128]{1,0:T(8,128)S(1)} %get-tuple-element.30), channel_id=1, source_target_pairs={{0,19},{1,18},{2,17},{3,16},{4,23},{5,22},{6,21},{7,20},{8,27},{9,... | collective-permute-start | bytes 49160 | tf_op jit(solution)/shard_map/ppermute | solution.py:223
  19.3 0.5 %collective-permute-start.9 = (f32[32,128]{1,0:T(8,128)S(1)}, f32[32,128]{1,0:T(8,128)S(1)}, u32[]{:S(2)}, u32[]{:S(2)}) collective-permute-start(f32[32,128]{1,0:T(8,128)S(1)} %get-tuple-element.31), channel_id=1, source_target_pairs={{0,16},{1,17},{2,18},{3,19},{4,20},{5,21},{6,22},{7,23},{8,24},{9,... | collective-permute-start | bytes 49160 | tf_op jit(solution)/shard_map/ppermute | solution.py:223
  19.8 0.3 %collective-permute-start.10 = (f32[32,128]{1,0:T(8,128)S(1)}, f32[32,128]{1,0:T(8,128)S(1)}, u32[]{:S(2)}, u32[]{:S(2)}) collective-permute-start(f32[32,128]{1,0:T(8,128)S(1)} %get-tuple-element.32), channel_id=1, source_target_pairs={{0,3},{1,2},{2,1},{3,0},{4,7},{5,6},{6,5},{7,4},{8,11},{9,10},{10,... | collective-permute-start | bytes 49160 | tf_op jit(solution)/shard_map/ppermute | solution.py:223
  20.1 0.7 %broadcast_multiply_fusion = f32[1,8,4,128]{3,2,1,0:T(4,128)} fusion(f32[1,8,4,128]{3,2,1,0:T(4,128)S(1)} %bitcast.8, f32[4]{0:T(128)S(1)} %convert_bitcast_fusion), kind=kLoop, calls=%fused_computation | loop fusion | flops 4096 | bytes 32784 | tf_op jit(solution)/shard_map/mul | solution.py:315
  20.8 0.4 %collective-permute-done.8.refs_0_ = f32[32,128]{1,0:T(8,128)S(1)} collective-permute-done((f32[32,128]{1,0:T(8,128)S(1)}, f32[32,128]{1,0:T(8,128)S(1)}, u32[]{:S(2)}, u32[]{:S(2)}) %collective-permute-start.8) | collective-permute-done | bytes 16416 | tf_op jit(solution)/shard_map/ppermute | solution.py:223
  21.3 1.8 %collective-permute-done.9.refs_1_ = f32[32,128]{1,0:T(8,128)S(1)} collective-permute-done((f32[32,128]{1,0:T(8,128)S(1)}, f32[32,128]{1,0:T(8,128)S(1)}, u32[]{:S(2)}, u32[]{:S(2)}) %collective-permute-start.9) | collective-permute-done | bytes 16416 | tf_op jit(solution)/shard_map/ppermute | solution.py:223
  23.0 0.0 collective-permute-done.10.refs_2_
  23.0 0.8 %struct_solve.1 = f32[32,128]{1,0:T(8,128)} custom-call(f32[32,128]{1,0:T(8,128)S(1)} %collective-permute-done.8.refs_0_, f32[32,128]{1,0:T(8,128)S(1)} %collective-permute-done.9.refs_1_, f32[32,128]{1,0:T(8,128)S(1)} %collective-permute-done.10.refs_2_, f32[32,128]{1,0:T(8,128)S(1)} %get-tuple-element.33.refs_3_, bf16[8,128,128]{2,1,0:T(8,128)(2,1)S(1)} %copy-done.2), custom_call_target="tpu_custom_call" | custom-call | flops 1000000 | bytes 131072 | tf_op jit(solution)/shard_map/struct_solve/pallas_call | solution.py:364
  (18 shorter events, 0.1 us)
Async XLA Ops:
  0.6 5.7 %copy-start.3 = (bf16[1,8,4,128]{3,2,1,0:T(4,128)(2,1)S(1)}, bf16[1,8,4,128]{3,2,1,0:T(4,128)(2,1)}, u32[]{:S(2)}) copy-start(bf16[1,8,4,128]{3,2,1,0:T(4,128)(2,1)} %param.8) | copy-start | bytes 24580
  0.6 5.7 %copy-start.4 = (s32[8,8]{1,0:T(8,128)S(1)}, s32[8,8]{1,0:T(8,128)}, u32[]{:S(2)}) copy-start(s32[8,8]{1,0:T(8,128)} %pattern_ref.1) | copy-start | bytes 772
  0.7 5.7 %copy-start.5 = (s32[8,6]{1,0:T(8,128)S(1)}, s32[8,6]{1,0:T(8,128)}, u32[]{:S(2)}) copy-start(s32[8,6]{1,0:T(8,128)} %owner_ref.1) | copy-start | bytes 580
  0.7 5.7 %copy-start.6 = (s32[8,6]{1,0:T(8,128)S(1)}, s32[8,6]{1,0:T(8,128)}, u32[]{:S(2)}) copy-start(s32[8,6]{1,0:T(8,128)} %local_ref.1) | copy-start | bytes 580
  0.7 5.7 %copy-start.7 = (s32[1,4]{1,0:T(1,128)S(1)}, s32[1,4]{1,0:T(1,128)}, u32[]{:S(2)}) copy-start(s32[1,4]{1,0:T(1,128)} %trim_ref.1) | copy-start | bytes 52
  0.7 8.1 %copy-start = (bf16[1,8,8,128,128]{4,3,2,1,0:T(8,128)(2,1)S(1)}, bf16[1,8,8,128,128]{4,3,2,1,0:T(8,128)(2,1)}, u32[]{:S(2)}) copy-start(bf16[1,8,8,128,128]{4,3,2,1,0:T(8,128)(2,1)} %param.9) | copy-start | bytes 6291460
  0.7 6.0 %collective-permute-start = (bf16[32,128]{1,0:T(8,128)(2,1)}, bf16[32,128]{1,0:T(8,128)(2,1)S(1)}, u32[]{:S(2)}, u32[]{:S(2)}) collective-permute-start(bf16[32,128]{1,0:T(8,128)(2,1)} %bitcast.9), channel_id=1, source_target_pairs={{0,1},{1,0},{2,3},{3,2},{4,5},{5,4},{6,7},{7,6},{8,9},{9,8},{10,11... | collective-permute-start | bytes 24584 | tf_op jit(solution)/shard_map/ppermute | solution.py:214
  1.2 8.0 %collective-permute-start.1 = (bf16[32,128]{1,0:T(8,128)(2,1)}, bf16[32,128]{1,0:T(8,128)(2,1)S(1)}, u32[]{:S(2)}, u32[]{:S(2)}) collective-permute-start(bf16[32,128]{1,0:T(8,128)(2,1)} %bitcast.10), channel_id=1, source_target_pairs={{0,8},{1,9},{2,10},{3,11},{4,12},{5,13},{6,14},{7,15},{8,0},{9,1},... | collective-permute-start | bytes 24584 | tf_op jit(solution)/shard_map/ppermute | solution.py:214
  4.9 3.9 %collective-permute-start.2 = (bf16[32,128]{1,0:T(8,128)(2,1)}, bf16[32,128]{1,0:T(8,128)(2,1)S(1)}, u32[]{:S(2)}, u32[]{:S(2)}) collective-permute-start(bf16[32,128]{1,0:T(8,128)(2,1)} %bitcast.11), channel_id=1, source_target_pairs={{0,16},{1,2},{2,1},{3,4},{4,3},{5,6},{6,5},{7,8},{8,7},{9,10},{10,... | collective-permute-start | bytes 24584 | tf_op jit(solution)/shard_map/ppermute | solution.py:243
  6.4 2.8 %copy-start.1 = (bf16[8,6,128,128]{3,2,1,0:T(8,128)(2,1)S(1)}, bf16[8,6,128,128]{3,2,1,0:T(8,128)(2,1)}, u32[]{:S(2)}) copy-start(bf16[8,6,128,128]{3,2,1,0:T(8,128)(2,1)} %spline_ref.1) | copy-start | bytes 4718596
  10.0 1.9 %collective-permute-start.3 = (bf16[6,32,128]{2,1,0:T(8,128)(2,1)S(1)}, bf16[6,32,128]{2,1,0:T(8,128)(2,1)S(1)}, u32[]{:S(2)}, u32[]{:S(2)}) collective-permute-start(bf16[6,32,128]{2,1,0:T(8,128)(2,1)S(1)} %get-tuple-element.24), channel_id=1, source_target_pairs={{0,1},{1,0},{2,3},{3,2},{4,5},{5,4},{6,7},{7,6},{8,9},{9,8},{10,11... | collective-permute-start | bytes 147464 | tf_op jit(solution)/shard_map/ppermute | solution.py:214
  10.1 5.2 %collective-permute-start.4 = (bf16[2,2,32,128]{3,2,1,0:T(8,128)(2,1)S(1)}, bf16[2,2,32,128]{3,2,1,0:T(8,128)(2,1)S(1)}, u32[]{:S(2)}, u32[]{:S(2)}) collective-permute-start(bf16[2,2,32,128]{3,2,1,0:T(8,128)(2,1)S(1)} %far_loads.1), channel_id=1, source_target_pairs={{0,13},{1,12},{2,15},{3,14},{4,9},{5,8},{6,11},{7,10},{8,5},{9,4},... | collective-permute-start | bytes 98312 | tf_op jit(solution)/shard_map/ppermute | solution.py:214
  11.9 4.4 %collective-permute-start.5 = (bf16[2,32,128]{2,1,0:T(8,128)(2,1)S(1)}, bf16[2,32,128]{2,1,0:T(8,128)(2,1)S(1)}, u32[]{:S(2)}, u32[]{:S(2)}) collective-permute-start(bf16[2,32,128]{2,1,0:T(8,128)(2,1)S(1)} %get-tuple-element.27), channel_id=1, source_target_pairs={{0,9},{1,8},{2,11},{3,10},{4,13},{5,12},{6,15},{7,14},{8,1},{9,0},... | collective-permute-start | bytes 49160 | tf_op jit(solution)/shard_map/ppermute | solution.py:214
  13.3 3.7 %collective-permute-start.6 = (bf16[2,32,128]{2,1,0:T(8,128)(2,1)S(1)}, bf16[2,32,128]{2,1,0:T(8,128)(2,1)S(1)}, u32[]{:S(2)}, u32[]{:S(2)}) collective-permute-start(bf16[2,32,128]{2,1,0:T(8,128)(2,1)S(1)} %get-tuple-element.28), channel_id=1, source_target_pairs={{0,4},{1,5},{2,6},{3,7},{4,0},{5,1},{6,2},{7,3},{8,12},{9,13},{10,... | collective-permute-start | bytes 49160 | tf_op jit(solution)/shard_map/ppermute | solution.py:214
  15.3 1.8 %collective-permute-start.7 = (bf16[2,32,128]{2,1,0:T(8,128)(2,1)S(1)}, bf16[2,32,128]{2,1,0:T(8,128)(2,1)S(1)}, u32[]{:S(2)}, u32[]{:S(2)}) collective-permute-start(bf16[2,32,128]{2,1,0:T(8,128)(2,1)S(1)} %get-tuple-element.29), channel_id=1, source_target_pairs={{0,1},{1,0},{2,3},{3,2},{4,5},{5,4},{6,7},{7,6},{8,9},{9,8},{10,11... | collective-permute-start | bytes 49160 | tf_op jit(solution)/shard_map/ppermute | solution.py:214
  17.1 6.0 %copy-start.2 = (bf16[8,128,128]{2,1,0:T(8,128)(2,1)S(1)}, bf16[8,128,128]{2,1,0:T(8,128)(2,1)}, u32[]{:S(2)}) copy-start(bf16[8,128,128]{2,1,0:T(8,128)(2,1)} %refs_4_.1) | copy-start | bytes 786436
  17.1 4.1 %collective-permute-start.8 = (f32[32,128]{1,0:T(8,128)S(1)}, f32[32,128]{1,0:T(8,128)S(1)}, u32[]{:S(2)}, u32[]{:S(2)}) collective-permute-start(f32[32,128]{1,0:T(8,128)S(1)} %get-tuple-element.30), channel_id=1, source_target_pairs={{0,19},{1,18},{2,17},{3,16},{4,23},{5,22},{6,21},{7,20},{8,27},{9,... | collective-permute-start | bytes 49160 | tf_op jit(solution)/shard_map/ppermute | solution.py:223
  19.3 3.7 %collective-permute-start.9 = (f32[32,128]{1,0:T(8,128)S(1)}, f32[32,128]{1,0:T(8,128)S(1)}, u32[]{:S(2)}, u32[]{:S(2)}) collective-permute-start(f32[32,128]{1,0:T(8,128)S(1)} %get-tuple-element.31), channel_id=1, source_target_pairs={{0,16},{1,17},{2,18},{3,19},{4,20},{5,21},{6,22},{7,23},{8,24},{9,... | collective-permute-start | bytes 49160 | tf_op jit(solution)/shard_map/ppermute | solution.py:223
  19.8 3.2 %collective-permute-start.10 = (f32[32,128]{1,0:T(8,128)S(1)}, f32[32,128]{1,0:T(8,128)S(1)}, u32[]{:S(2)}, u32[]{:S(2)}) collective-permute-start(f32[32,128]{1,0:T(8,128)S(1)} %get-tuple-element.32), channel_id=1, source_target_pairs={{0,3},{1,2},{2,1},{3,0},{4,7},{5,6},{6,5},{7,4},{8,11},{9,10},{10,... | collective-permute-start | bytes 49160 | tf_op jit(solution)/shard_map/ppermute | solution.py:223

commit v19 on v18

--- a/solution.py
+++ b/solution.py
@@ -302,7 +302,7 @@
         compiler_params=params,
         cost_estimate=cost(10**6, 2**17),
         name="spline_loads",
-    )(pair, mirror, code, part, gate, near_blocks[0], spline_blocks)
+    )(cross, mirror, code, part, gate, near_blocks[0], spline_blocks)
     far = pl.pallas_call(
         far_kernel,
         out_shape=jax.ShapeDtypeStruct((2, *two), bf16),

time: 24 us -> 22.8 us (0.950)
  waiting for transfers between devices: 6.53 us -> 5.28 us
    ppermute x1, waiting for transfers between devices: 2.04 us -> 0.01 us  [on_device(): lax.ppermute(own, ('mach', 'panel'), [(mach * panels + i, (mach ^ (i in b...]
    ppermute x1, starting transfers between devices: 1.49 us -> 3 us  [on_device(): lax.ppermute(own, ('mach', 'panel'), [(mach * panels + i, (mach ^ (i in b...]
    ppermute x7, waiting for transfers between devices: 2.26 us -> 3.72 us  [swap(): return lax.ppermute(value, 'panel', [(i, i ^ apart) for i in range(panels)])]
    ppermute x7, starting transfers between devices: 8.94 us -> 7.5 us  [swap(): return lax.ppermute(value, 'panel', [(i, i ^ apart) for i in range(panels)])]
    ppermute x3, waiting for transfers between devices: 2.23 us -> 1.56 us  [mach_swap(): return lax.ppermute(value, ('mach', 'panel'), pairs)]
  transfers between devices with their start and end apart: 11 -> 11, of which waited for: 6 -> 7; matrix products, arithmetic and copies ran while one was open for 3% -> 3% of each run, Pallas kernels for 3% -> 3%
where the time goes in v19:
time: 22.8 us; the launch traced here: 22.7 us
  starting transfers between devices  13.5 us (59%)
  waiting for transfers between devices  5.28 us (23%)
  Pallas kernels  2.32 us (10%)
  between operations  0.8 us (4%)
  other arithmetic  0.68 us (3%)
    ppermute x7, starting transfers between devices, swap(): return lax.ppermute(value, 'panel', [(i, i ^ apart) for i in range(panels)])  7.5 us
    ppermute x7, waiting for transfers between devices, swap(): return lax.ppermute(value, 'panel', [(i, i ^ apart) for i in range(panels)])  3.72 us
    ppermute x3, starting transfers between devices, mach_swap(): return lax.ppermute(value, ('mach', 'panel'), pairs)  3.03 us
    ppermute x1, starting transfers between devices, on_device(): lax.ppermute(own, ('mach', 'panel'), [(mach * panels + i, (mach ^ (i in b...  3 us
    ppermute x3, waiting for transfers between devices, mach_swap(): return lax.ppermute(value, ('mach', 'panel'), pairs)  1.56 us
    pallas_call x1, Pallas kernels, on_device(): pl.pallas_call(functools.partial(spline_kernel, rhs), out_shape=(jax.Shap...  0.81 us
    pallas_call x1, Pallas kernels, on_device(): pl.pallas_call(functools.partial(inverse_kernel, rhs, machs), out_shape=j...  0.76 us
    mul x1, other arithmetic, on_device(): sums.reshape(adjoint.shape) * trim_mask[0].astype(f32)[None, None, :, None]  0.68 us
  transfers between devices with their start and end apart: 11, of which 7 were waited for; matrix products, arithmetic and copies ran while one was open for 3% of the time, Pallas kernels for 3%

profile of v19, /device:TPU:0, one launch (start us, length us, event | category | flops | bytes accessed | tf_op | source)
XLA Modules:
  0.0 22.7 jit_solution(6638446507093947771)
XLA Ops:
  0.7 3.0 %collective-permute-start = (bf16[32,128]{1,0:T(8,128)(2,1)}, bf16[32,128]{1,0:T(8,128)(2,1)S(1)}, u32[]{:S(2)}, u32[]{:S(2)}) collective-permute-start(bf16[32,128]{1,0:T(8,128)(2,1)} %bitcast.9), channel_id=1, source_target_pairs={{0,16},{1,2},{2,1},{3,4},{4,3},{5,6},{6,5},{7,8},{8,7},{9,10},{10,... | collective-permute-start | bytes 24584 | tf_op jit(solution)/shard_map/ppermute | solution.py:243
  3.7 1.9 %collective-permute-start.1 = (bf16[32,128]{1,0:T(8,128)(2,1)}, bf16[32,128]{1,0:T(8,128)(2,1)S(1)}, u32[]{:S(2)}, u32[]{:S(2)}) collective-permute-start(bf16[32,128]{1,0:T(8,128)(2,1)} %bitcast.10), channel_id=1, source_target_pairs={{0,8},{1,9},{2,10},{3,11},{4,12},{5,13},{6,14},{7,15},{8,0},{9,1},... | collective-permute-start | bytes 24584 | tf_op jit(solution)/shard_map/ppermute | solution.py:214
  5.6 0.5 %collective-permute-start.2 = (bf16[32,128]{1,0:T(8,128)(2,1)}, bf16[32,128]{1,0:T(8,128)(2,1)S(1)}, u32[]{:S(2)}, u32[]{:S(2)}) collective-permute-start(bf16[32,128]{1,0:T(8,128)(2,1)} %bitcast.11), channel_id=1, source_target_pairs={{0,1},{1,0},{2,3},{3,2},{4,5},{5,4},{6,7},{7,6},{8,9},{9,8},{10,11... | collective-permute-start | bytes 24584 | tf_op jit(solution)/shard_map/ppermute | solution.py:214
  6.2 0.0 copy-done.4
  6.2 0.0 copy-done.5
  6.2 0.0 copy-done.6
  6.2 0.0 copy-done.7
  6.2 0.0 copy-start.1
  6.2 0.2 %pick_rows.1 = (bf16[192,128]{1,0:T(8,128)(2,1)S(1)}, f32[16,128]{1,0:T(8,128)S(1)}, bf16[32,128]{1,0:T(8,128)(2,1)S(1)}, s32[8,6]{1,0:T(8,128)S(1)}) custom-call(bf16[32,8]{1,0:T(8,128)(2,1)S(1)} %row_order.1.expand_ref, s32[8,8]{1,0:T(8,128)S(1)} %copy-done.4, s32[1,4]{1,0:T(1,128)S(1)} %copy-done.7, bf16[32,128]{1,0:T(8,128)(2,1)S(1)} %bitcast.12, ...), custom_call_target="tpu_custom_call" | custom-call | flops 1000000 | bytes 131072 | tf_op jit(solution)/shard_map/pick_rows/pallas_call | solution.py:264
  6.5 0.0 collective-permute-done.cross_ref._
  6.5 0.7 %collective-permute-done.2.pair_ref = bf16[32,128]{1,0:T(8,128)(2,1)S(1)} collective-permute-done((bf16[32,128]{1,0:T(8,128)(2,1)}, bf16[32,128]{1,0:T(8,128)(2,1)S(1)}, u32[]{:S(2)}, u32[]{:S(2)}) %collective-permute-start.2) | collective-permute-done | bytes 8224 | tf_op jit(solution)/shard_map/ppermute | solution.py:214
  7.2 0.5 %near_field.1.part_ref = f32[32,128]{1,0:T(8,128)S(1)} custom-call(bf16[192,128]{1,0:T(8,128)(2,1)S(1)} %get-tuple-element.19.hot_ref, bf16[32,128]{1,0:T(8,128)(2,1)S(1)} %get-tuple-element.20.own_ref, bf16[32,128]{1,0:T(8,128)(2,1)S(1)} %collective-permute-done.2.pair_ref, bf16[32,128]{1,0:T(8,128)(2,1)S(1)} %collective-permute-done.cross_ref._, ...), custom_call_target="tpu_custom_call" | custom-call | flops 1000000 | bytes 131072 | tf_op jit(solution)/shard_map/near_field/pallas_call | solution.py:278
  7.6 0.8 %collective-permute-done.1.mirror_ref = bf16[32,128]{1,0:T(8,128)(2,1)S(1)} collective-permute-done((bf16[32,128]{1,0:T(8,128)(2,1)}, bf16[32,128]{1,0:T(8,128)(2,1)S(1)}, u32[]{:S(2)}, u32[]{:S(2)}) %collective-permute-start.1) | collective-permute-done | bytes 8224 | tf_op jit(solution)/shard_map/ppermute | solution.py:214
  8.5 0.8 %spline_loads.1 = (f32[32,128]{1,0:T(8,128)S(1)}, f32[64,8,128]{2,1,0:T(8,128)S(1)}, bf16[6,32,128]{2,1,0:T(8,128)(2,1)S(1)}) custom-call(bf16[32,128]{1,0:T(8,128)(2,1)S(1)} %collective-permute-done.cross_ref._, bf16[32,128]{1,0:T(8,128)(2,1)S(1)} %collective-permute-done.1.mirror_ref, s32[8,6]{1,0:T(8,128)S(1)} %get-tuple-element.18.code_vmem, ...), custom_call_target="tpu_custom_call" | custom-call | flops 1000000 | bytes 131072 | tf_op jit(solution)/shard_map/spline_loads/pallas_call | solution.py:289
  9.3 0.1 collective-permute-start.3
  9.4 3.1 %collective-permute-start.4 = (bf16[2,2,32,128]{3,2,1,0:T(8,128)(2,1)S(1)}, bf16[2,2,32,128]{3,2,1,0:T(8,128)(2,1)S(1)}, u32[]{:S(2)}, u32[]{:S(2)}) collective-permute-start(bf16[2,2,32,128]{3,2,1,0:T(8,128)(2,1)S(1)} %far_loads.1), channel_id=1, source_target_pairs={{0,13},{1,12},{2,15},{3,14},{4,9},{5,8},{6,11},{7,10},{8,5},{9,4},... | collective-permute-start | bytes 98312 | tf_op jit(solution)/shard_map/ppermute | solution.py:214
  12.4 0.0 collective-permute-done.3.got_ref
  12.5 0.1 collective-permute-start.5
  12.5 1.4 %collective-permute-start.6 = (bf16[2,32,128]{2,1,0:T(8,128)(2,1)S(1)}, bf16[2,32,128]{2,1,0:T(8,128)(2,1)S(1)}, u32[]{:S(2)}, u32[]{:S(2)}) collective-permute-start(bf16[2,32,128]{2,1,0:T(8,128)(2,1)S(1)} %get-tuple-element.28), channel_id=1, source_target_pairs={{0,4},{1,5},{2,6},{3,7},{4,0},{5,1},{6,2},{7,3},{8,12},{9,13},{10,... | collective-permute-start | bytes 49160 | tf_op jit(solution)/shard_map/ppermute | solution.py:214
  13.9 0.6 %collective-permute-done.4.far_ref = bf16[2,2,32,128]{3,2,1,0:T(8,128)(2,1)S(1)} collective-permute-done((bf16[2,2,32,128]{3,2,1,0:T(8,128)(2,1)S(1)}, bf16[2,2,32,128]{3,2,1,0:T(8,128)(2,1)S(1)}, u32[]{:S(2)}, u32[]{:S(2)}) %collective-permute-start.4) | collective-permute-done | bytes 32800 | tf_op jit(solution)/shard_map/ppermute | solution.py:214
  14.6 0.4 %collective-permute-start.7 = (bf16[2,32,128]{2,1,0:T(8,128)(2,1)S(1)}, bf16[2,32,128]{2,1,0:T(8,128)(2,1)S(1)}, u32[]{:S(2)}, u32[]{:S(2)}) collective-permute-start(bf16[2,32,128]{2,1,0:T(8,128)(2,1)S(1)} %get-tuple-element.29), channel_id=1, source_target_pairs={{0,1},{1,0},{2,3},{3,2},{4,5},{5,4},{6,7},{7,6},{8,9},{9,8},{10,11... | collective-permute-start | bytes 49160 | tf_op jit(solution)/shard_map/ppermute | solution.py:214
  15.0 1.6 %collective-permute-done.5.refs_0_ = bf16[2,32,128]{2,1,0:T(8,128)(2,1)S(1)} collective-permute-done((bf16[2,32,128]{2,1,0:T(8,128)(2,1)S(1)}, bf16[2,32,128]{2,1,0:T(8,128)(2,1)S(1)}, u32[]{:S(2)}, u32[]{:S(2)}) %collective-permute-start.5) | collective-permute-done | bytes 16416 | tf_op jit(solution)/shard_map/ppermute | solution.py:214
  16.6 0.0 collective-permute-done.6.refs_1_
  16.6 0.0 collective-permute-done.7.got_ref
  16.6 1.5 %collective-permute-start.8 = (f32[32,128]{1,0:T(8,128)S(1)}, f32[32,128]{1,0:T(8,128)S(1)}, u32[]{:S(2)}, u32[]{:S(2)}) collective-permute-start(f32[32,128]{1,0:T(8,128)S(1)} %get-tuple-element.30), channel_id=1, source_target_pairs={{0,19},{1,18},{2,17},{3,16},{4,23},{5,22},{6,21},{7,20},{8,27},{9,... | collective-permute-start | bytes 49160 | tf_op jit(solution)/shard_map/ppermute | solution.py:223
  18.1 0.6 %collective-permute-start.9 = (f32[32,128]{1,0:T(8,128)S(1)}, f32[32,128]{1,0:T(8,128)S(1)}, u32[]{:S(2)}, u32[]{:S(2)}) collective-permute-start(f32[32,128]{1,0:T(8,128)S(1)} %get-tuple-element.31), channel_id=1, source_target_pairs={{0,16},{1,17},{2,18},{3,19},{4,20},{5,21},{6,22},{7,23},{8,24},{9,... | collective-permute-start | bytes 49160 | tf_op jit(solution)/shard_map/ppermute | solution.py:223
  18.7 0.9 %collective-permute-start.10 = (f32[32,128]{1,0:T(8,128)S(1)}, f32[32,128]{1,0:T(8,128)S(1)}, u32[]{:S(2)}, u32[]{:S(2)}) collective-permute-start(f32[32,128]{1,0:T(8,128)S(1)} %get-tuple-element.32), channel_id=1, source_target_pairs={{0,3},{1,2},{2,1},{3,0},{4,7},{5,6},{6,5},{7,4},{8,11},{9,10},{10,... | collective-permute-start | bytes 49160 | tf_op jit(solution)/shard_map/ppermute | solution.py:223
  19.7 0.7 %broadcast_multiply_fusion = f32[1,8,4,128]{3,2,1,0:T(4,128)} fusion(f32[1,8,4,128]{3,2,1,0:T(4,128)S(1)} %bitcast.8, f32[4]{0:T(128)S(1)} %convert_bitcast_fusion), kind=kLoop, calls=%fused_computation | loop fusion | flops 4096 | bytes 32784 | tf_op jit(solution)/shard_map/mul | solution.py:315
  20.3 0.4 %collective-permute-done.8.refs_0_ = f32[32,128]{1,0:T(8,128)S(1)} collective-permute-done((f32[32,128]{1,0:T(8,128)S(1)}, f32[32,128]{1,0:T(8,128)S(1)}, u32[]{:S(2)}, u32[]{:S(2)}) %collective-permute-start.8) | collective-permute-done | bytes 16416 | tf_op jit(solution)/shard_map/ppermute | solution.py:223
  20.8 1.1 %collective-permute-done.9.refs_1_ = f32[32,128]{1,0:T(8,128)S(1)} collective-permute-done((f32[32,128]{1,0:T(8,128)S(1)}, f32[32,128]{1,0:T(8,128)S(1)}, u32[]{:S(2)}, u32[]{:S(2)}) %collective-permute-start.9) | collective-permute-done | bytes 16416 | tf_op jit(solution)/shard_map/ppermute | solution.py:223
  21.8 0.1 collective-permute-done.10.refs_2_
  21.9 0.8 %struct_solve.1 = f32[32,128]{1,0:T(8,128)} custom-call(f32[32,128]{1,0:T(8,128)S(1)} %collective-permute-done.8.refs_0_, f32[32,128]{1,0:T(8,128)S(1)} %collective-permute-done.9.refs_1_, f32[32,128]{1,0:T(8,128)S(1)} %collective-permute-done.10.refs_2_, f32[32,128]{1,0:T(8,128)S(1)} %get-tuple-element.33.refs_3_, bf16[8,128,128]{2,1,0:T(8,128)(2,1)S(1)} %copy-done.2), custom_call_target="tpu_custom_call" | custom-call | flops 1000000 | bytes 131072 | tf_op jit(solution)/shard_map/struct_solve/pallas_call | solution.py:364
  (18 shorter events, 0.1 us)
Async XLA Ops:
  0.6 5.5 %copy-start.3 = (bf16[1,8,4,128]{3,2,1,0:T(4,128)(2,1)S(1)}, bf16[1,8,4,128]{3,2,1,0:T(4,128)(2,1)}, u32[]{:S(2)}) copy-start(bf16[1,8,4,128]{3,2,1,0:T(4,128)(2,1)} %param.8) | copy-start | bytes 24580
  0.6 5.5 %copy-start.4 = (s32[8,8]{1,0:T(8,128)S(1)}, s32[8,8]{1,0:T(8,128)}, u32[]{:S(2)}) copy-start(s32[8,8]{1,0:T(8,128)} %pattern_ref.1) | copy-start | bytes 772
  0.7 5.5 %copy-start.5 = (s32[8,6]{1,0:T(8,128)S(1)}, s32[8,6]{1,0:T(8,128)}, u32[]{:S(2)}) copy-start(s32[8,6]{1,0:T(8,128)} %owner_ref.1) | copy-start | bytes 580
  0.7 5.5 %copy-start.6 = (s32[8,6]{1,0:T(8,128)S(1)}, s32[8,6]{1,0:T(8,128)}, u32[]{:S(2)}) copy-start(s32[8,6]{1,0:T(8,128)} %local_ref.1) | copy-start | bytes 580
  0.7 5.5 %copy-start.7 = (s32[1,4]{1,0:T(1,128)S(1)}, s32[1,4]{1,0:T(1,128)}, u32[]{:S(2)}) copy-start(s32[1,4]{1,0:T(1,128)} %trim_ref.1) | copy-start | bytes 52
  0.7 6.5 %copy-start = (bf16[1,8,8,128,128]{4,3,2,1,0:T(8,128)(2,1)S(1)}, bf16[1,8,8,128,128]{4,3,2,1,0:T(8,128)(2,1)}, u32[]{:S(2)}) copy-start(bf16[1,8,8,128,128]{4,3,2,1,0:T(8,128)(2,1)} %param.9) | copy-start | bytes 6291460
  0.7 5.8 %collective-permute-start = (bf16[32,128]{1,0:T(8,128)(2,1)}, bf16[32,128]{1,0:T(8,128)(2,1)S(1)}, u32[]{:S(2)}, u32[]{:S(2)}) collective-permute-start(bf16[32,128]{1,0:T(8,128)(2,1)} %bitcast.9), channel_id=1, source_target_pairs={{0,16},{1,2},{2,1},{3,4},{4,3},{5,6},{6,5},{7,8},{8,7},{9,10},{10,... | collective-permute-start | bytes 24584 | tf_op jit(solution)/shard_map/ppermute | solution.py:243
  3.7 4.8 %collective-permute-start.1 = (bf16[32,128]{1,0:T(8,128)(2,1)}, bf16[32,128]{1,0:T(8,128)(2,1)S(1)}, u32[]{:S(2)}, u32[]{:S(2)}) collective-permute-start(bf16[32,128]{1,0:T(8,128)(2,1)} %bitcast.10), channel_id=1, source_target_pairs={{0,8},{1,9},{2,10},{3,11},{4,12},{5,13},{6,14},{7,15},{8,0},{9,1},... | collective-permute-start | bytes 24584 | tf_op jit(solution)/shard_map/ppermute | solution.py:214
  5.6 1.5 %collective-permute-start.2 = (bf16[32,128]{1,0:T(8,128)(2,1)}, bf16[32,128]{1,0:T(8,128)(2,1)S(1)}, u32[]{:S(2)}, u32[]{:S(2)}) collective-permute-start(bf16[32,128]{1,0:T(8,128)(2,1)} %bitcast.11), channel_id=1, source_target_pairs={{0,1},{1,0},{2,3},{3,2},{4,5},{5,4},{6,7},{7,6},{8,9},{9,8},{10,11... | collective-permute-start | bytes 24584 | tf_op jit(solution)/shard_map/ppermute | solution.py:214
  6.2 2.3 %copy-start.1 = (bf16[8,6,128,128]{3,2,1,0:T(8,128)(2,1)S(1)}, bf16[8,6,128,128]{3,2,1,0:T(8,128)(2,1)}, u32[]{:S(2)}) copy-start(bf16[8,6,128,128]{3,2,1,0:T(8,128)(2,1)} %spline_ref.1) | copy-start | bytes 4718596
  9.3 3.2 %collective-permute-start.3 = (bf16[6,32,128]{2,1,0:T(8,128)(2,1)S(1)}, bf16[6,32,128]{2,1,0:T(8,128)(2,1)S(1)}, u32[]{:S(2)}, u32[]{:S(2)}) collective-permute-start(bf16[6,32,128]{2,1,0:T(8,128)(2,1)S(1)} %get-tuple-element.24), channel_id=1, source_target_pairs={{0,1},{1,0},{2,3},{3,2},{4,5},{5,4},{6,7},{7,6},{8,9},{9,8},{10,11... | collective-permute-start | bytes 147464 | tf_op jit(solution)/shard_map/ppermute | solution.py:214
  9.4 5.2 %collective-permute-start.4 = (bf16[2,2,32,128]{3,2,1,0:T(8,128)(2,1)S(1)}, bf16[2,2,32,128]{3,2,1,0:T(8,128)(2,1)S(1)}, u32[]{:S(2)}, u32[]{:S(2)}) collective-permute-start(bf16[2,2,32,128]{3,2,1,0:T(8,128)(2,1)S(1)} %far_loads.1), channel_id=1, source_target_pairs={{0,13},{1,12},{2,15},{3,14},{4,9},{5,8},{6,11},{7,10},{8,5},{9,4},... | collective-permute-start | bytes 98312 | tf_op jit(solution)/shard_map/ppermute | solution.py:214
  12.5 4.1 %collective-permute-start.5 = (bf16[2,32,128]{2,1,0:T(8,128)(2,1)S(1)}, bf16[2,32,128]{2,1,0:T(8,128)(2,1)S(1)}, u32[]{:S(2)}, u32[]{:S(2)}) collective-permute-start(bf16[2,32,128]{2,1,0:T(8,128)(2,1)S(1)} %get-tuple-element.27), channel_id=1, source_target_pairs={{0,9},{1,8},{2,11},{3,10},{4,13},{5,12},{6,15},{7,14},{8,1},{9,0},... | collective-permute-start | bytes 49160 | tf_op jit(solution)/shard_map/ppermute | solution.py:214
  12.5 4.1 %collective-permute-start.6 = (bf16[2,32,128]{2,1,0:T(8,128)(2,1)S(1)}, bf16[2,32,128]{2,1,0:T(8,128)(2,1)S(1)}, u32[]{:S(2)}, u32[]{:S(2)}) collective-permute-start(bf16[2,32,128]{2,1,0:T(8,128)(2,1)S(1)} %get-tuple-element.28), channel_id=1, source_target_pairs={{0,4},{1,5},{2,6},{3,7},{4,0},{5,1},{6,2},{7,3},{8,12},{9,13},{10,... | collective-permute-start | bytes 49160 | tf_op jit(solution)/shard_map/ppermute | solution.py:214
  14.6 2.0 %collective-permute-start.7 = (bf16[2,32,128]{2,1,0:T(8,128)(2,1)S(1)}, bf16[2,32,128]{2,1,0:T(8,128)(2,1)S(1)}, u32[]{:S(2)}, u32[]{:S(2)}) collective-permute-start(bf16[2,32,128]{2,1,0:T(8,128)(2,1)S(1)} %get-tuple-element.29), channel_id=1, source_target_pairs={{0,1},{1,0},{2,3},{3,2},{4,5},{5,4},{6,7},{7,6},{8,9},{9,8},{10,11... | collective-permute-start | bytes 49160 | tf_op jit(solution)/shard_map/ppermute | solution.py:214
  16.6 5.3 %copy-start.2 = (bf16[8,128,128]{2,1,0:T(8,128)(2,1)S(1)}, bf16[8,128,128]{2,1,0:T(8,128)(2,1)}, u32[]{:S(2)}) copy-start(bf16[8,128,128]{2,1,0:T(8,128)(2,1)} %refs_4_.1) | copy-start | bytes 786436
  16.6 4.1 %collective-permute-start.8 = (f32[32,128]{1,0:T(8,128)S(1)}, f32[32,128]{1,0:T(8,128)S(1)}, u32[]{:S(2)}, u32[]{:S(2)}) collective-permute-start(f32[32,128]{1,0:T(8,128)S(1)} %get-tuple-element.30), channel_id=1, source_target_pairs={{0,19},{1,18},{2,17},{3,16},{4,23},{5,22},{6,21},{7,20},{8,27},{9,... | collective-permute-start | bytes 49160 | tf_op jit(solution)/shard_map/ppermute | solution.py:223
  18.1 3.7 %collective-permute-start.9 = (f32[32,128]{1,0:T(8,128)S(1)}, f32[32,128]{1,0:T(8,128)S(1)}, u32[]{:S(2)}, u32[]{:S(2)}) collective-permute-start(f32[32,128]{1,0:T(8,128)S(1)} %get-tuple-element.31), channel_id=1, source_target_pairs={{0,16},{1,17},{2,18},{3,19},{4,20},{5,21},{6,22},{7,23},{8,24},{9,... | collective-permute-start | bytes 49160 | tf_op jit(solution)/shard_map/ppermute | solution.py:223
  18.7 3.2 %collective-permute-start.10 = (f32[32,128]{1,0:T(8,128)S(1)}, f32[32,128]{1,0:T(8,128)S(1)}, u32[]{:S(2)}, u32[]{:S(2)}) collective-permute-start(f32[32,128]{1,0:T(8,128)S(1)} %get-tuple-element.32), channel_id=1, source_target_pairs={{0,3},{1,2},{2,1},{3,0},{4,7},{5,6},{6,5},{7,4},{8,11},{9,10},{10,... | collective-permute-start | bytes 49160 | tf_op jit(solution)/shard_map/ppermute | solution.py:223

commit v20 on v19

--- a/solution.py
+++ b/solution.py
@@ -135,10 +135,11 @@
         return jnp.dot(mine, blocks, preferred_element_type=jnp.float32)
 
     pairs = range(0, block_count, 2)
-    products = {pair: pair_product(pair) for pair in pairs[:-1]}
+    ready = len(pairs) // 2
+    products = {pair: pair_product(pair) for pair in pairs[:ready]}
     copy.wait()
-    products[pairs[-1]] = pair_product(pairs[-1])
-    for pair, product in products.items():
+    for pair in pairs:
+        product = products[pair] if pair in products else pair_product(pair)
         for i in (pair, pair + 1):
             total = product[(i - pair) * TILE : (i - pair + 1) * TILE]
             places, sums = [], []

time: 22.8 us -> 23 us (level)
  no operation moved by 1% of the time
where the time goes in v20:
time: 23 us; the launch traced here: 22.8 us
  starting transfers between devices  13.5 us (59%)
  waiting for transfers between devices  5.28 us (23%)
  Pallas kernels  2.51 us (11%)
  between operations  0.8 us (3%)
  other arithmetic  0.68 us (3%)
    ppermute x7, starting transfers between devices, swap(): return lax.ppermute(value, 'panel', [(i, i ^ apart) for i in range(panels)])  7.51 us
    ppermute x7, waiting for transfers between devices, swap(): return lax.ppermute(value, 'panel', [(i, i ^ apart) for i in range(panels)])  3.72 us
    ppermute x3, starting transfers between devices, mach_swap(): return lax.ppermute(value, ('mach', 'panel'), pairs)  3.03 us
    ppermute x1, starting transfers between devices, on_device(): lax.ppermute(own, ('mach', 'panel'), [(mach * panels + i, (mach ^ (i in b...  3 us
    ppermute x3, waiting for transfers between devices, mach_swap(): return lax.ppermute(value, ('mach', 'panel'), pairs)  1.56 us
    pallas_call x1, Pallas kernels, on_device(): pl.pallas_call(functools.partial(spline_kernel, rhs), out_shape=(jax.Shap...  0.99 us
    pallas_call x1, Pallas kernels, on_device(): pl.pallas_call(functools.partial(inverse_kernel, rhs, machs), out_shape=j...  0.76 us
    mul x1, other arithmetic, on_device(): sums.reshape(adjoint.shape) * trim_mask[0].astype(f32)[None, None, :, None]  0.68 us
  transfers between devices with their start and end apart: 11, of which 7 were waited for; matrix products, arithmetic and copies ran while one was open for 3% of the time, Pallas kernels for 3%

profile of v20, /device:TPU:0, one launch (start us, length us, event | category | flops | bytes accessed | tf_op | source)
XLA Modules:
  0.0 22.8 jit_solution(14094208737719140100)
XLA Ops:
  0.6 0.0 copy-start.3
  0.6 0.0 copy-start.4
  0.7 3.0 %collective-permute-start = (bf16[32,128]{1,0:T(8,128)(2,1)}, bf16[32,128]{1,0:T(8,128)(2,1)S(1)}, u32[]{:S(2)}, u32[]{:S(2)}) collective-permute-start(bf16[32,128]{1,0:T(8,128)(2,1)} %bitcast.9), channel_id=1, source_target_pairs={{0,16},{1,2},{2,1},{3,4},{4,3},{5,6},{6,5},{7,8},{8,7},{9,10},{10,... | collective-permute-start | bytes 24584 | tf_op jit(solution)/shard_map/ppermute | solution.py:244
  3.7 1.9 %collective-permute-start.1 = (bf16[32,128]{1,0:T(8,128)(2,1)}, bf16[32,128]{1,0:T(8,128)(2,1)S(1)}, u32[]{:S(2)}, u32[]{:S(2)}) collective-permute-start(bf16[32,128]{1,0:T(8,128)(2,1)} %bitcast.10), channel_id=1, source_target_pairs={{0,8},{1,9},{2,10},{3,11},{4,12},{5,13},{6,14},{7,15},{8,0},{9,1},... | collective-permute-start | bytes 24584 | tf_op jit(solution)/shard_map/ppermute | solution.py:215
  5.6 0.5 %collective-permute-start.2 = (bf16[32,128]{1,0:T(8,128)(2,1)}, bf16[32,128]{1,0:T(8,128)(2,1)S(1)}, u32[]{:S(2)}, u32[]{:S(2)}) collective-permute-start(bf16[32,128]{1,0:T(8,128)(2,1)} %bitcast.11), channel_id=1, source_target_pairs={{0,1},{1,0},{2,3},{3,2},{4,5},{5,4},{6,7},{7,6},{8,9},{9,8},{10,11... | collective-permute-start | bytes 24584 | tf_op jit(solution)/shard_map/ppermute | solution.py:215
  6.2 0.0 copy-done.3
  6.2 0.0 copy-start.1
  6.2 0.2 %pick_rows.1 = (bf16[192,128]{1,0:T(8,128)(2,1)S(1)}, f32[16,128]{1,0:T(8,128)S(1)}, bf16[32,128]{1,0:T(8,128)(2,1)S(1)}, s32[8,6]{1,0:T(8,128)S(1)}) custom-call(bf16[32,8]{1,0:T(8,128)(2,1)S(1)} %row_order.1.expand_ref, s32[8,8]{1,0:T(8,128)S(1)} %copy-done.4, s32[1,4]{1,0:T(1,128)S(1)} %copy-done.7, bf16[32,128]{1,0:T(8,128)(2,1)S(1)} %bitcast.12, ...), custom_call_target="tpu_custom_call" | custom-call | flops 1000000 | bytes 131072 | tf_op jit(solution)/shard_map/pick_rows/pallas_call | solution.py:265
  6.5 0.0 collective-permute-done.cross_ref._
  6.5 0.7 %collective-permute-done.2.pair_ref = bf16[32,128]{1,0:T(8,128)(2,1)S(1)} collective-permute-done((bf16[32,128]{1,0:T(8,128)(2,1)}, bf16[32,128]{1,0:T(8,128)(2,1)S(1)}, u32[]{:S(2)}, u32[]{:S(2)}) %collective-permute-start.2) | collective-permute-done | bytes 8224 | tf_op jit(solution)/shard_map/ppermute | solution.py:215
  7.2 0.5 %near_field.1.part_ref = f32[32,128]{1,0:T(8,128)S(1)} custom-call(bf16[192,128]{1,0:T(8,128)(2,1)S(1)} %get-tuple-element.19.hot_ref, bf16[32,128]{1,0:T(8,128)(2,1)S(1)} %get-tuple-element.20.own_ref, bf16[32,128]{1,0:T(8,128)(2,1)S(1)} %collective-permute-done.2.pair_ref, bf16[32,128]{1,0:T(8,128)(2,1)S(1)} %collective-permute-done.cross_ref._, ...), custom_call_target="tpu_custom_call" | custom-call | flops 1000000 | bytes 131072 | tf_op jit(solution)/shard_map/near_field/pallas_call | solution.py:279
  7.6 0.8 %collective-permute-done.1.mirror_ref = bf16[32,128]{1,0:T(8,128)(2,1)S(1)} collective-permute-done((bf16[32,128]{1,0:T(8,128)(2,1)}, bf16[32,128]{1,0:T(8,128)(2,1)S(1)}, u32[]{:S(2)}, u32[]{:S(2)}) %collective-permute-start.1) | collective-permute-done | bytes 8224 | tf_op jit(solution)/shard_map/ppermute | solution.py:215
  8.5 0.0 copy-done.1
  8.5 1.0 %spline_loads.1 = (f32[32,128]{1,0:T(8,128)S(1)}, f32[64,8,128]{2,1,0:T(8,128)S(1)}, bf16[6,32,128]{2,1,0:T(8,128)(2,1)S(1)}) custom-call(bf16[32,128]{1,0:T(8,128)(2,1)S(1)} %collective-permute-done.cross_ref._, bf16[32,128]{1,0:T(8,128)(2,1)S(1)} %collective-permute-done.1.mirror_ref, s32[8,6]{1,0:T(8,128)S(1)} %get-tuple-element.18.code_vmem, ...), custom_call_target="tpu_custom_call" | custom-call | flops 1000000 | bytes 131072 | tf_op jit(solution)/shard_map/spline_loads/pallas_call | solution.py:290
  9.5 0.1 collective-permute-start.3
  9.6 3.1 %collective-permute-start.4 = (bf16[2,2,32,128]{3,2,1,0:T(8,128)(2,1)S(1)}, bf16[2,2,32,128]{3,2,1,0:T(8,128)(2,1)S(1)}, u32[]{:S(2)}, u32[]{:S(2)}) collective-permute-start(bf16[2,2,32,128]{3,2,1,0:T(8,128)(2,1)S(1)} %far_loads.1), channel_id=1, source_target_pairs={{0,13},{1,12},{2,15},{3,14},{4,9},{5,8},{6,11},{7,10},{8,5},{9,4},... | collective-permute-start | bytes 98312 | tf_op jit(solution)/shard_map/ppermute | solution.py:215
  12.6 0.0 collective-permute-done.3.got_ref
  12.6 0.1 collective-permute-start.5
  12.7 1.4 %collective-permute-start.6 = (bf16[2,32,128]{2,1,0:T(8,128)(2,1)S(1)}, bf16[2,32,128]{2,1,0:T(8,128)(2,1)S(1)}, u32[]{:S(2)}, u32[]{:S(2)}) collective-permute-start(bf16[2,32,128]{2,1,0:T(8,128)(2,1)S(1)} %get-tuple-element.28), channel_id=1, source_target_pairs={{0,4},{1,5},{2,6},{3,7},{4,0},{5,1},{6,2},{7,3},{8,12},{9,13},{10,... | collective-permute-start | bytes 49160 | tf_op jit(solution)/shard_map/ppermute | solution.py:215
  14.1 0.6 %collective-permute-done.4.far_ref = bf16[2,2,32,128]{3,2,1,0:T(8,128)(2,1)S(1)} collective-permute-done((bf16[2,2,32,128]{3,2,1,0:T(8,128)(2,1)S(1)}, bf16[2,2,32,128]{3,2,1,0:T(8,128)(2,1)S(1)}, u32[]{:S(2)}, u32[]{:S(2)}) %collective-permute-start.4) | collective-permute-done | bytes 32800 | tf_op jit(solution)/shard_map/ppermute | solution.py:215
  14.8 0.4 %collective-permute-start.7 = (bf16[2,32,128]{2,1,0:T(8,128)(2,1)S(1)}, bf16[2,32,128]{2,1,0:T(8,128)(2,1)S(1)}, u32[]{:S(2)}, u32[]{:S(2)}) collective-permute-start(bf16[2,32,128]{2,1,0:T(8,128)(2,1)S(1)} %get-tuple-element.29), channel_id=1, source_target_pairs={{0,1},{1,0},{2,3},{3,2},{4,5},{5,4},{6,7},{7,6},{8,9},{9,8},{10,11... | collective-permute-start | bytes 49160 | tf_op jit(solution)/shard_map/ppermute | solution.py:215
  15.2 1.6 %collective-permute-done.5.refs_0_ = bf16[2,32,128]{2,1,0:T(8,128)(2,1)S(1)} collective-permute-done((bf16[2,32,128]{2,1,0:T(8,128)(2,1)S(1)}, bf16[2,32,128]{2,1,0:T(8,128)(2,1)S(1)}, u32[]{:S(2)}, u32[]{:S(2)}) %collective-permute-start.5) | collective-permute-done | bytes 16416 | tf_op jit(solution)/shard_map/ppermute | solution.py:215
  16.8 0.0 collective-permute-done.6.refs_1_
  16.8 0.0 collective-permute-done.7.got_ref
  16.8 1.5 %collective-permute-start.8 = (f32[32,128]{1,0:T(8,128)S(1)}, f32[32,128]{1,0:T(8,128)S(1)}, u32[]{:S(2)}, u32[]{:S(2)}) collective-permute-start(f32[32,128]{1,0:T(8,128)S(1)} %get-tuple-element.30), channel_id=1, source_target_pairs={{0,19},{1,18},{2,17},{3,16},{4,23},{5,22},{6,21},{7,20},{8,27},{9,... | collective-permute-start | bytes 49160 | tf_op jit(solution)/shard_map/ppermute | solution.py:224
  18.3 0.6 %collective-permute-start.9 = (f32[32,128]{1,0:T(8,128)S(1)}, f32[32,128]{1,0:T(8,128)S(1)}, u32[]{:S(2)}, u32[]{:S(2)}) collective-permute-start(f32[32,128]{1,0:T(8,128)S(1)} %get-tuple-element.31), channel_id=1, source_target_pairs={{0,16},{1,17},{2,18},{3,19},{4,20},{5,21},{6,22},{7,23},{8,24},{9,... | collective-permute-start | bytes 49160 | tf_op jit(solution)/shard_map/ppermute | solution.py:224
  18.9 0.9 %collective-permute-start.10 = (f32[32,128]{1,0:T(8,128)S(1)}, f32[32,128]{1,0:T(8,128)S(1)}, u32[]{:S(2)}, u32[]{:S(2)}) collective-permute-start(f32[32,128]{1,0:T(8,128)S(1)} %get-tuple-element.32), channel_id=1, source_target_pairs={{0,3},{1,2},{2,1},{3,0},{4,7},{5,6},{6,5},{7,4},{8,11},{9,10},{10,... | collective-permute-start | bytes 49160 | tf_op jit(solution)/shard_map/ppermute | solution.py:224
  19.8 0.7 %broadcast_multiply_fusion = f32[1,8,4,128]{3,2,1,0:T(4,128)} fusion(f32[1,8,4,128]{3,2,1,0:T(4,128)S(1)} %bitcast.8, f32[4]{0:T(128)S(1)} %convert_bitcast_fusion), kind=kLoop, calls=%fused_computation | loop fusion | flops 4096 | bytes 32784 | tf_op jit(solution)/shard_map/mul | solution.py:316
  20.5 0.4 %collective-permute-done.8.refs_0_ = f32[32,128]{1,0:T(8,128)S(1)} collective-permute-done((f32[32,128]{1,0:T(8,128)S(1)}, f32[32,128]{1,0:T(8,128)S(1)}, u32[]{:S(2)}, u32[]{:S(2)}) %collective-permute-start.8) | collective-permute-done | bytes 16416 | tf_op jit(solution)/shard_map/ppermute | solution.py:224
  20.9 1.1 %collective-permute-done.9.refs_1_ = f32[32,128]{1,0:T(8,128)S(1)} collective-permute-done((f32[32,128]{1,0:T(8,128)S(1)}, f32[32,128]{1,0:T(8,128)S(1)}, u32[]{:S(2)}, u32[]{:S(2)}) %collective-permute-start.9) | collective-permute-done | bytes 16416 | tf_op jit(solution)/shard_map/ppermute | solution.py:224
  22.0 0.1 collective-permute-done.10.refs_2_
  22.1 0.8 %struct_solve.1 = f32[32,128]{1,0:T(8,128)} custom-call(f32[32,128]{1,0:T(8,128)S(1)} %collective-permute-done.8.refs_0_, f32[32,128]{1,0:T(8,128)S(1)} %collective-permute-done.9.refs_1_, f32[32,128]{1,0:T(8,128)S(1)} %collective-permute-done.10.refs_2_, f32[32,128]{1,0:T(8,128)S(1)} %get-tuple-element.33.refs_3_, bf16[8,128,128]{2,1,0:T(8,128)(2,1)S(1)} %copy-done.2), custom_call_target="tpu_custom_call" | custom-call | flops 1000000 | bytes 131072 | tf_op jit(solution)/shard_map/struct_solve/pallas_call | solution.py:365
  (18 shorter events, 0.1 us)
Async XLA Ops:
  0.6 5.5 %copy-start.3 = (bf16[1,8,4,128]{3,2,1,0:T(4,128)(2,1)S(1)}, bf16[1,8,4,128]{3,2,1,0:T(4,128)(2,1)}, u32[]{:S(2)}) copy-start(bf16[1,8,4,128]{3,2,1,0:T(4,128)(2,1)} %param.8) | copy-start | bytes 24580
  0.6 5.5 %copy-start.4 = (s32[8,8]{1,0:T(8,128)S(1)}, s32[8,8]{1,0:T(8,128)}, u32[]{:S(2)}) copy-start(s32[8,8]{1,0:T(8,128)} %pattern_ref.1) | copy-start | bytes 772
  0.7 5.5 %copy-start.5 = (s32[8,6]{1,0:T(8,128)S(1)}, s32[8,6]{1,0:T(8,128)}, u32[]{:S(2)}) copy-start(s32[8,6]{1,0:T(8,128)} %owner_ref.1) | copy-start | bytes 580
  0.7 5.5 %copy-start.6 = (s32[8,6]{1,0:T(8,128)S(1)}, s32[8,6]{1,0:T(8,128)}, u32[]{:S(2)}) copy-start(s32[8,6]{1,0:T(8,128)} %local_ref.1) | copy-start | bytes 580
  0.7 5.5 %copy-start.7 = (s32[1,4]{1,0:T(1,128)S(1)}, s32[1,4]{1,0:T(1,128)}, u32[]{:S(2)}) copy-start(s32[1,4]{1,0:T(1,128)} %trim_ref.1) | copy-start | bytes 52
  0.7 6.5 %copy-start = (bf16[1,8,8,128,128]{4,3,2,1,0:T(8,128)(2,1)S(1)}, bf16[1,8,8,128,128]{4,3,2,1,0:T(8,128)(2,1)}, u32[]{:S(2)}) copy-start(bf16[1,8,8,128,128]{4,3,2,1,0:T(8,128)(2,1)} %param.9) | copy-start | bytes 6291460
  0.7 5.8 %collective-permute-start = (bf16[32,128]{1,0:T(8,128)(2,1)}, bf16[32,128]{1,0:T(8,128)(2,1)S(1)}, u32[]{:S(2)}, u32[]{:S(2)}) collective-permute-start(bf16[32,128]{1,0:T(8,128)(2,1)} %bitcast.9), channel_id=1, source_target_pairs={{0,16},{1,2},{2,1},{3,4},{4,3},{5,6},{6,5},{7,8},{8,7},{9,10},{10,... | collective-permute-start | bytes 24584 | tf_op jit(solution)/shard_map/ppermute | solution.py:244
  3.7 4.8 %collective-permute-start.1 = (bf16[32,128]{1,0:T(8,128)(2,1)}, bf16[32,128]{1,0:T(8,128)(2,1)S(1)}, u32[]{:S(2)}, u32[]{:S(2)}) collective-permute-start(bf16[32,128]{1,0:T(8,128)(2,1)} %bitcast.10), channel_id=1, source_target_pairs={{0,8},{1,9},{2,10},{3,11},{4,12},{5,13},{6,14},{7,15},{8,0},{9,1},... | collective-permute-start | bytes 24584 | tf_op jit(solution)/shard_map/ppermute | solution.py:215
  5.6 1.5 %collective-permute-start.2 = (bf16[32,128]{1,0:T(8,128)(2,1)}, bf16[32,128]{1,0:T(8,128)(2,1)S(1)}, u32[]{:S(2)}, u32[]{:S(2)}) collective-permute-start(bf16[32,128]{1,0:T(8,128)(2,1)} %bitcast.11), channel_id=1, source_target_pairs={{0,1},{1,0},{2,3},{3,2},{4,5},{5,4},{6,7},{7,6},{8,9},{9,8},{10,11... | collective-permute-start | bytes 24584 | tf_op jit(solution)/shard_map/ppermute | solution.py:215
  6.2 2.3 %copy-start.1 = (bf16[8,6,128,128]{3,2,1,0:T(8,128)(2,1)S(1)}, bf16[8,6,128,128]{3,2,1,0:T(8,128)(2,1)}, u32[]{:S(2)}) copy-start(bf16[8,6,128,128]{3,2,1,0:T(8,128)(2,1)} %spline_ref.1) | copy-start | bytes 4718596
  9.5 3.2 %collective-permute-start.3 = (bf16[6,32,128]{2,1,0:T(8,128)(2,1)S(1)}, bf16[6,32,128]{2,1,0:T(8,128)(2,1)S(1)}, u32[]{:S(2)}, u32[]{:S(2)}) collective-permute-start(bf16[6,32,128]{2,1,0:T(8,128)(2,1)S(1)} %get-tuple-element.24), channel_id=1, source_target_pairs={{0,1},{1,0},{2,3},{3,2},{4,5},{5,4},{6,7},{7,6},{8,9},{9,8},{10,11... | collective-permute-start | bytes 147464 | tf_op jit(solution)/shard_map/ppermute | solution.py:215
  9.6 5.2 %collective-permute-start.4 = (bf16[2,2,32,128]{3,2,1,0:T(8,128)(2,1)S(1)}, bf16[2,2,32,128]{3,2,1,0:T(8,128)(2,1)S(1)}, u32[]{:S(2)}, u32[]{:S(2)}) collective-permute-start(bf16[2,2,32,128]{3,2,1,0:T(8,128)(2,1)S(1)} %far_loads.1), channel_id=1, source_target_pairs={{0,13},{1,12},{2,15},{3,14},{4,9},{5,8},{6,11},{7,10},{8,5},{9,4},... | collective-permute-start | bytes 98312 | tf_op jit(solution)/shard_map/ppermute | solution.py:215
  12.6 4.1 %collective-permute-start.5 = (bf16[2,32,128]{2,1,0:T(8,128)(2,1)S(1)}, bf16[2,32,128]{2,1,0:T(8,128)(2,1)S(1)}, u32[]{:S(2)}, u32[]{:S(2)}) collective-permute-start(bf16[2,32,128]{2,1,0:T(8,128)(2,1)S(1)} %get-tuple-element.27), channel_id=1, source_target_pairs={{0,9},{1,8},{2,11},{3,10},{4,13},{5,12},{6,15},{7,14},{8,1},{9,0},... | collective-permute-start | bytes 49160 | tf_op jit(solution)/shard_map/ppermute | solution.py:215
  12.7 4.1 %collective-permute-start.6 = (bf16[2,32,128]{2,1,0:T(8,128)(2,1)S(1)}, bf16[2,32,128]{2,1,0:T(8,128)(2,1)S(1)}, u32[]{:S(2)}, u32[]{:S(2)}) collective-permute-start(bf16[2,32,128]{2,1,0:T(8,128)(2,1)S(1)} %get-tuple-element.28), channel_id=1, source_target_pairs={{0,4},{1,5},{2,6},{3,7},{4,0},{5,1},{6,2},{7,3},{8,12},{9,13},{10,... | collective-permute-start | bytes 49160 | tf_op jit(solution)/shard_map/ppermute | solution.py:215
  14.8 2.0 %collective-permute-start.7 = (bf16[2,32,128]{2,1,0:T(8,128)(2,1)S(1)}, bf16[2,32,128]{2,1,0:T(8,128)(2,1)S(1)}, u32[]{:S(2)}, u32[]{:S(2)}) collective-permute-start(bf16[2,32,128]{2,1,0:T(8,128)(2,1)S(1)} %get-tuple-element.29), channel_id=1, source_target_pairs={{0,1},{1,0},{2,3},{3,2},{4,5},{5,4},{6,7},{7,6},{8,9},{9,8},{10,11... | collective-permute-start | bytes 49160 | tf_op jit(solution)/shard_map/ppermute | solution.py:215
  16.8 5.3 %copy-start.2 = (bf16[8,128,128]{2,1,0:T(8,128)(2,1)S(1)}, bf16[8,128,128]{2,1,0:T(8,128)(2,1)}, u32[]{:S(2)}) copy-start(bf16[8,128,128]{2,1,0:T(8,128)(2,1)} %refs_4_.1) | copy-start | bytes 786436
  16.8 4.1 %collective-permute-start.8 = (f32[32,128]{1,0:T(8,128)S(1)}, f32[32,128]{1,0:T(8,128)S(1)}, u32[]{:S(2)}, u32[]{:S(2)}) collective-permute-start(f32[32,128]{1,0:T(8,128)S(1)} %get-tuple-element.30), channel_id=1, source_target_pairs={{0,19},{1,18},{2,17},{3,16},{4,23},{5,22},{6,21},{7,20},{8,27},{9,... | collective-permute-start | bytes 49160 | tf_op jit(solution)/shard_map/ppermute | solution.py:224
  18.3 3.7 %collective-permute-start.9 = (f32[32,128]{1,0:T(8,128)S(1)}, f32[32,128]{1,0:T(8,128)S(1)}, u32[]{:S(2)}, u32[]{:S(2)}) collective-permute-start(f32[32,128]{1,0:T(8,128)S(1)} %get-tuple-element.31), channel_id=1, source_target_pairs={{0,16},{1,17},{2,18},{3,19},{4,20},{5,21},{6,22},{7,23},{8,24},{9,... | collective-permute-start | bytes 49160 | tf_op jit(solution)/shard_map/ppermute | solution.py:224
  18.9 3.2 %collective-permute-start.10 = (f32[32,128]{1,0:T(8,128)S(1)}, f32[32,128]{1,0:T(8,128)S(1)}, u32[]{:S(2)}, u32[]{:S(2)}) collective-permute-start(f32[32,128]{1,0:T(8,128)S(1)} %get-tuple-element.32), channel_id=1, source_target_pairs={{0,3},{1,2},{2,1},{3,0},{4,7},{5,6},{6,5},{7,4},{8,11},{9,10},{10,... | collective-permute-start | bytes 49160 | tf_op jit(solution)/shard_map/ppermute | solution.py:224

commit v21 on v19

--- a/solution.py
+++ b/solution.py
@@ -135,9 +135,8 @@
         return jnp.dot(mine, blocks, preferred_element_type=jnp.float32)
 
     pairs = range(0, block_count, 2)
-    products = {pair: pair_product(pair) for pair in pairs[:-1]}
+    products = {pair: pair_product(pair) for pair in pairs}
     copy.wait()
-    products[pairs[-1]] = pair_product(pairs[-1])
     for pair, product in products.items():
         for i in (pair, pair + 1):
             total = product[(i - pair) * TILE : (i - pair + 1) * TILE]

time: 22.8 us -> 22.7 us (level)
  no operation moved by 1% of the time
where the time goes in v21:
time: 22.7 us; the launch traced here: 22.5 us
  starting transfers between devices  13.5 us (59%)
  waiting for transfers between devices  5.28 us (23%)
  Pallas kernels  2.21 us (10%)
  between operations  0.8 us (4%)
  other arithmetic  0.68 us (3%)
    ppermute x7, starting transfers between devices, swap(): return lax.ppermute(value, 'panel', [(i, i ^ apart) for i in range(panels)])  7.5 us
    ppermute x7, waiting for transfers between devices, swap(): return lax.ppermute(value, 'panel', [(i, i ^ apart) for i in range(panels)])  3.72 us
    ppermute x3, starting transfers between devices, mach_swap(): return lax.ppermute(value, ('mach', 'panel'), pairs)  3.03 us
    ppermute x1, starting transfers between devices, on_device(): lax.ppermute(own, ('mach', 'panel'), [(mach * panels + i, (mach ^ (i in b...  3 us
    ppermute x3, waiting for transfers between devices, mach_swap(): return lax.ppermute(value, ('mach', 'panel'), pairs)  1.56 us
    pallas_call x1, Pallas kernels, on_device(): pl.pallas_call(functools.partial(inverse_kernel, rhs, machs), out_shape=j...  0.76 us
    pallas_call x1, Pallas kernels, on_device(): pl.pallas_call(functools.partial(spline_kernel, rhs), out_shape=(jax.Shap...  0.69 us
    mul x1, other arithmetic, on_device(): sums.reshape(adjoint.shape) * trim_mask[0].astype(f32)[None, None, :, None]  0.68 us
  transfers between devices with their start and end apart: 11, of which 7 were waited for; matrix products, arithmetic and copies ran while one was open for 3% of the time, Pallas kernels for 3%

profile of v21, /device:TPU:0, one launch (start us, length us, event | category | flops | bytes accessed | tf_op | source)
XLA Modules:
  0.0 22.5 jit_solution(3104161848269116284)
XLA Ops:
  0.6 0.0 copy-start.3
  0.6 0.0 copy-start.4
  0.7 0.0 copy-start.5
  0.7 0.0 copy-start.6
  0.7 3.0 %collective-permute-start = (bf16[32,128]{1,0:T(8,128)(2,1)}, bf16[32,128]{1,0:T(8,128)(2,1)S(1)}, u32[]{:S(2)}, u32[]{:S(2)}) collective-permute-start(bf16[32,128]{1,0:T(8,128)(2,1)} %bitcast.9), channel_id=1, source_target_pairs={{0,16},{1,2},{2,1},{3,4},{4,3},{5,6},{6,5},{7,8},{8,7},{9,10},{10,... | collective-permute-start | bytes 24584 | tf_op jit(solution)/shard_map/ppermute | solution.py:242
  3.7 1.9 %collective-permute-start.1 = (bf16[32,128]{1,0:T(8,128)(2,1)}, bf16[32,128]{1,0:T(8,128)(2,1)S(1)}, u32[]{:S(2)}, u32[]{:S(2)}) collective-permute-start(bf16[32,128]{1,0:T(8,128)(2,1)} %bitcast.10), channel_id=1, source_target_pairs={{0,8},{1,9},{2,10},{3,11},{4,12},{5,13},{6,14},{7,15},{8,0},{9,1},... | collective-permute-start | bytes 24584 | tf_op jit(solution)/shard_map/ppermute | solution.py:213
  5.6 0.5 %collective-permute-start.2 = (bf16[32,128]{1,0:T(8,128)(2,1)}, bf16[32,128]{1,0:T(8,128)(2,1)S(1)}, u32[]{:S(2)}, u32[]{:S(2)}) collective-permute-start(bf16[32,128]{1,0:T(8,128)(2,1)} %bitcast.11), channel_id=1, source_target_pairs={{0,1},{1,0},{2,3},{3,2},{4,5},{5,4},{6,7},{7,6},{8,9},{9,8},{10,11... | collective-permute-start | bytes 24584 | tf_op jit(solution)/shard_map/ppermute | solution.py:213
  6.2 0.0 copy-start.1
  6.2 0.2 %pick_rows.1 = (bf16[192,128]{1,0:T(8,128)(2,1)S(1)}, f32[16,128]{1,0:T(8,128)S(1)}, bf16[32,128]{1,0:T(8,128)(2,1)S(1)}, s32[8,6]{1,0:T(8,128)S(1)}) custom-call(bf16[32,8]{1,0:T(8,128)(2,1)S(1)} %row_order.1.expand_ref, s32[8,8]{1,0:T(8,128)S(1)} %copy-done.4, s32[1,4]{1,0:T(1,128)S(1)} %copy-done.7, bf16[32,128]{1,0:T(8,128)(2,1)S(1)} %bitcast.12, ...), custom_call_target="tpu_custom_call" | custom-call | flops 1000000 | bytes 131072 | tf_op jit(solution)/shard_map/pick_rows/pallas_call | solution.py:263
  6.5 0.0 collective-permute-done.cross_ref._
  6.5 0.7 %collective-permute-done.2.pair_ref = bf16[32,128]{1,0:T(8,128)(2,1)S(1)} collective-permute-done((bf16[32,128]{1,0:T(8,128)(2,1)}, bf16[32,128]{1,0:T(8,128)(2,1)S(1)}, u32[]{:S(2)}, u32[]{:S(2)}) %collective-permute-start.2) | collective-permute-done | bytes 8224 | tf_op jit(solution)/shard_map/ppermute | solution.py:213
  7.2 0.5 %near_field.1.part_ref = f32[32,128]{1,0:T(8,128)S(1)} custom-call(bf16[192,128]{1,0:T(8,128)(2,1)S(1)} %get-tuple-element.19.hot_ref, bf16[32,128]{1,0:T(8,128)(2,1)S(1)} %get-tuple-element.20.own_ref, bf16[32,128]{1,0:T(8,128)(2,1)S(1)} %collective-permute-done.2.pair_ref, bf16[32,128]{1,0:T(8,128)(2,1)S(1)} %collective-permute-done.cross_ref._, ...), custom_call_target="tpu_custom_call" | custom-call | flops 1000000 | bytes 131072 | tf_op jit(solution)/shard_map/near_field/pallas_call | solution.py:277
  7.6 0.8 %collective-permute-done.1.mirror_ref = bf16[32,128]{1,0:T(8,128)(2,1)S(1)} collective-permute-done((bf16[32,128]{1,0:T(8,128)(2,1)}, bf16[32,128]{1,0:T(8,128)(2,1)S(1)}, u32[]{:S(2)}, u32[]{:S(2)}) %collective-permute-start.1) | collective-permute-done | bytes 8224 | tf_op jit(solution)/shard_map/ppermute | solution.py:213
  8.5 0.7 %spline_loads.1 = (f32[32,128]{1,0:T(8,128)S(1)}, f32[64,8,128]{2,1,0:T(8,128)S(1)}, bf16[6,32,128]{2,1,0:T(8,128)(2,1)S(1)}) custom-call(bf16[32,128]{1,0:T(8,128)(2,1)S(1)} %collective-permute-done.cross_ref._, bf16[32,128]{1,0:T(8,128)(2,1)S(1)} %collective-permute-done.1.mirror_ref, s32[8,6]{1,0:T(8,128)S(1)} %get-tuple-element.18.code_vmem, ...), custom_call_target="tpu_custom_call" | custom-call | flops 1000000 | bytes 131072 | tf_op jit(solution)/shard_map/spline_loads/pallas_call | solution.py:288
  9.2 0.1 collective-permute-start.3
  9.3 3.1 %collective-permute-start.4 = (bf16[2,2,32,128]{3,2,1,0:T(8,128)(2,1)S(1)}, bf16[2,2,32,128]{3,2,1,0:T(8,128)(2,1)S(1)}, u32[]{:S(2)}, u32[]{:S(2)}) collective-permute-start(bf16[2,2,32,128]{3,2,1,0:T(8,128)(2,1)S(1)} %far_loads.1), channel_id=1, source_target_pairs={{0,13},{1,12},{2,15},{3,14},{4,9},{5,8},{6,11},{7,10},{8,5},{9,4},... | collective-permute-start | bytes 98312 | tf_op jit(solution)/shard_map/ppermute | solution.py:213
  12.3 0.0 collective-permute-done.3.got_ref
  12.3 0.1 collective-permute-start.5
  12.4 1.4 %collective-permute-start.6 = (bf16[2,32,128]{2,1,0:T(8,128)(2,1)S(1)}, bf16[2,32,128]{2,1,0:T(8,128)(2,1)S(1)}, u32[]{:S(2)}, u32[]{:S(2)}) collective-permute-start(bf16[2,32,128]{2,1,0:T(8,128)(2,1)S(1)} %get-tuple-element.28), channel_id=1, source_target_pairs={{0,4},{1,5},{2,6},{3,7},{4,0},{5,1},{6,2},{7,3},{8,12},{9,13},{10,... | collective-permute-start | bytes 49160 | tf_op jit(solution)/shard_map/ppermute | solution.py:213
  13.8 0.6 %collective-permute-done.4.far_ref = bf16[2,2,32,128]{3,2,1,0:T(8,128)(2,1)S(1)} collective-permute-done((bf16[2,2,32,128]{3,2,1,0:T(8,128)(2,1)S(1)}, bf16[2,2,32,128]{3,2,1,0:T(8,128)(2,1)S(1)}, u32[]{:S(2)}, u32[]{:S(2)}) %collective-permute-start.4) | collective-permute-done | bytes 32800 | tf_op jit(solution)/shard_map/ppermute | solution.py:213
  14.5 0.4 %collective-permute-start.7 = (bf16[2,32,128]{2,1,0:T(8,128)(2,1)S(1)}, bf16[2,32,128]{2,1,0:T(8,128)(2,1)S(1)}, u32[]{:S(2)}, u32[]{:S(2)}) collective-permute-start(bf16[2,32,128]{2,1,0:T(8,128)(2,1)S(1)} %get-tuple-element.29), channel_id=1, source_target_pairs={{0,1},{1,0},{2,3},{3,2},{4,5},{5,4},{6,7},{7,6},{8,9},{9,8},{10,11... | collective-permute-start | bytes 49160 | tf_op jit(solution)/shard_map/ppermute | solution.py:213
  14.9 1.6 %collective-permute-done.5.refs_0_ = bf16[2,32,128]{2,1,0:T(8,128)(2,1)S(1)} collective-permute-done((bf16[2,32,128]{2,1,0:T(8,128)(2,1)S(1)}, bf16[2,32,128]{2,1,0:T(8,128)(2,1)S(1)}, u32[]{:S(2)}, u32[]{:S(2)}) %collective-permute-start.5) | collective-permute-done | bytes 16416 | tf_op jit(solution)/shard_map/ppermute | solution.py:213
  16.5 0.0 collective-permute-done.6.refs_1_
  16.5 0.0 collective-permute-done.7.got_ref
  16.5 1.5 %collective-permute-start.8 = (f32[32,128]{1,0:T(8,128)S(1)}, f32[32,128]{1,0:T(8,128)S(1)}, u32[]{:S(2)}, u32[]{:S(2)}) collective-permute-start(f32[32,128]{1,0:T(8,128)S(1)} %get-tuple-element.30), channel_id=1, source_target_pairs={{0,19},{1,18},{2,17},{3,16},{4,23},{5,22},{6,21},{7,20},{8,27},{9,... | collective-permute-start | bytes 49160 | tf_op jit(solution)/shard_map/ppermute | solution.py:222
  18.0 0.6 %collective-permute-start.9 = (f32[32,128]{1,0:T(8,128)S(1)}, f32[32,128]{1,0:T(8,128)S(1)}, u32[]{:S(2)}, u32[]{:S(2)}) collective-permute-start(f32[32,128]{1,0:T(8,128)S(1)} %get-tuple-element.31), channel_id=1, source_target_pairs={{0,16},{1,17},{2,18},{3,19},{4,20},{5,21},{6,22},{7,23},{8,24},{9,... | collective-permute-start | bytes 49160 | tf_op jit(solution)/shard_map/ppermute | solution.py:222
  18.6 0.9 %collective-permute-start.10 = (f32[32,128]{1,0:T(8,128)S(1)}, f32[32,128]{1,0:T(8,128)S(1)}, u32[]{:S(2)}, u32[]{:S(2)}) collective-permute-start(f32[32,128]{1,0:T(8,128)S(1)} %get-tuple-element.32), channel_id=1, source_target_pairs={{0,3},{1,2},{2,1},{3,0},{4,7},{5,6},{6,5},{7,4},{8,11},{9,10},{10,... | collective-permute-start | bytes 49160 | tf_op jit(solution)/shard_map/ppermute | solution.py:222
  19.5 0.7 %broadcast_multiply_fusion = f32[1,8,4,128]{3,2,1,0:T(4,128)} fusion(f32[1,8,4,128]{3,2,1,0:T(4,128)S(1)} %bitcast.8, f32[4]{0:T(128)S(1)} %convert_bitcast_fusion), kind=kLoop, calls=%fused_computation | loop fusion | flops 4096 | bytes 32784 | tf_op jit(solution)/shard_map/mul | solution.py:314
  20.2 0.4 %collective-permute-done.8.refs_0_ = f32[32,128]{1,0:T(8,128)S(1)} collective-permute-done((f32[32,128]{1,0:T(8,128)S(1)}, f32[32,128]{1,0:T(8,128)S(1)}, u32[]{:S(2)}, u32[]{:S(2)}) %collective-permute-start.8) | collective-permute-done | bytes 16416 | tf_op jit(solution)/shard_map/ppermute | solution.py:222
  20.6 1.1 %collective-permute-done.9.refs_1_ = f32[32,128]{1,0:T(8,128)S(1)} collective-permute-done((f32[32,128]{1,0:T(8,128)S(1)}, f32[32,128]{1,0:T(8,128)S(1)}, u32[]{:S(2)}, u32[]{:S(2)}) %collective-permute-start.9) | collective-permute-done | bytes 16416 | tf_op jit(solution)/shard_map/ppermute | solution.py:222
  21.7 0.1 collective-permute-done.10.refs_2_
  21.8 0.8 %struct_solve.1 = f32[32,128]{1,0:T(8,128)} custom-call(f32[32,128]{1,0:T(8,128)S(1)} %collective-permute-done.8.refs_0_, f32[32,128]{1,0:T(8,128)S(1)} %collective-permute-done.9.refs_1_, f32[32,128]{1,0:T(8,128)S(1)} %collective-permute-done.10.refs_2_, f32[32,128]{1,0:T(8,128)S(1)} %get-tuple-element.33.refs_3_, bf16[8,128,128]{2,1,0:T(8,128)(2,1)S(1)} %copy-done.2), custom_call_target="tpu_custom_call" | custom-call | flops 1000000 | bytes 131072 | tf_op jit(solution)/shard_map/struct_solve/pallas_call | solution.py:363
  (18 shorter events, 0.1 us)
Async XLA Ops:
  0.6 5.5 %copy-start.3 = (bf16[1,8,4,128]{3,2,1,0:T(4,128)(2,1)S(1)}, bf16[1,8,4,128]{3,2,1,0:T(4,128)(2,1)}, u32[]{:S(2)}) copy-start(bf16[1,8,4,128]{3,2,1,0:T(4,128)(2,1)} %param.8) | copy-start | bytes 24580
  0.6 5.5 %copy-start.4 = (s32[8,8]{1,0:T(8,128)S(1)}, s32[8,8]{1,0:T(8,128)}, u32[]{:S(2)}) copy-start(s32[8,8]{1,0:T(8,128)} %pattern_ref.1) | copy-start | bytes 772
  0.7 5.5 %copy-start.5 = (s32[8,6]{1,0:T(8,128)S(1)}, s32[8,6]{1,0:T(8,128)}, u32[]{:S(2)}) copy-start(s32[8,6]{1,0:T(8,128)} %owner_ref.1) | copy-start | bytes 580
  0.7 5.5 %copy-start.6 = (s32[8,6]{1,0:T(8,128)S(1)}, s32[8,6]{1,0:T(8,128)}, u32[]{:S(2)}) copy-start(s32[8,6]{1,0:T(8,128)} %local_ref.1) | copy-start | bytes 580
  0.7 5.5 %copy-start.7 = (s32[1,4]{1,0:T(1,128)S(1)}, s32[1,4]{1,0:T(1,128)}, u32[]{:S(2)}) copy-start(s32[1,4]{1,0:T(1,128)} %trim_ref.1) | copy-start | bytes 52
  0.7 6.5 %copy-start = (bf16[1,8,8,128,128]{4,3,2,1,0:T(8,128)(2,1)S(1)}, bf16[1,8,8,128,128]{4,3,2,1,0:T(8,128)(2,1)}, u32[]{:S(2)}) copy-start(bf16[1,8,8,128,128]{4,3,2,1,0:T(8,128)(2,1)} %param.9) | copy-start | bytes 6291460
  0.7 5.8 %collective-permute-start = (bf16[32,128]{1,0:T(8,128)(2,1)}, bf16[32,128]{1,0:T(8,128)(2,1)S(1)}, u32[]{:S(2)}, u32[]{:S(2)}) collective-permute-start(bf16[32,128]{1,0:T(8,128)(2,1)} %bitcast.9), channel_id=1, source_target_pairs={{0,16},{1,2},{2,1},{3,4},{4,3},{5,6},{6,5},{7,8},{8,7},{9,10},{10,... | collective-permute-start | bytes 24584 | tf_op jit(solution)/shard_map/ppermute | solution.py:242
  3.7 4.8 %collective-permute-start.1 = (bf16[32,128]{1,0:T(8,128)(2,1)}, bf16[32,128]{1,0:T(8,128)(2,1)S(1)}, u32[]{:S(2)}, u32[]{:S(2)}) collective-permute-start(bf16[32,128]{1,0:T(8,128)(2,1)} %bitcast.10), channel_id=1, source_target_pairs={{0,8},{1,9},{2,10},{3,11},{4,12},{5,13},{6,14},{7,15},{8,0},{9,1},... | collective-permute-start | bytes 24584 | tf_op jit(solution)/shard_map/ppermute | solution.py:213
  5.6 1.5 %collective-permute-start.2 = (bf16[32,128]{1,0:T(8,128)(2,1)}, bf16[32,128]{1,0:T(8,128)(2,1)S(1)}, u32[]{:S(2)}, u32[]{:S(2)}) collective-permute-start(bf16[32,128]{1,0:T(8,128)(2,1)} %bitcast.11), channel_id=1, source_target_pairs={{0,1},{1,0},{2,3},{3,2},{4,5},{5,4},{6,7},{7,6},{8,9},{9,8},{10,11... | collective-permute-start | bytes 24584 | tf_op jit(solution)/shard_map/ppermute | solution.py:213
  6.2 2.3 %copy-start.1 = (bf16[8,6,128,128]{3,2,1,0:T(8,128)(2,1)S(1)}, bf16[8,6,128,128]{3,2,1,0:T(8,128)(2,1)}, u32[]{:S(2)}) copy-start(bf16[8,6,128,128]{3,2,1,0:T(8,128)(2,1)} %spline_ref.1) | copy-start | bytes 4718596
  9.2 3.2 %collective-permute-start.3 = (bf16[6,32,128]{2,1,0:T(8,128)(2,1)S(1)}, bf16[6,32,128]{2,1,0:T(8,128)(2,1)S(1)}, u32[]{:S(2)}, u32[]{:S(2)}) collective-permute-start(bf16[6,32,128]{2,1,0:T(8,128)(2,1)S(1)} %get-tuple-element.24), channel_id=1, source_target_pairs={{0,1},{1,0},{2,3},{3,2},{4,5},{5,4},{6,7},{7,6},{8,9},{9,8},{10,11... | collective-permute-start | bytes 147464 | tf_op jit(solution)/shard_map/ppermute | solution.py:213
  9.3 5.2 %collective-permute-start.4 = (bf16[2,2,32,128]{3,2,1,0:T(8,128)(2,1)S(1)}, bf16[2,2,32,128]{3,2,1,0:T(8,128)(2,1)S(1)}, u32[]{:S(2)}, u32[]{:S(2)}) collective-permute-start(bf16[2,2,32,128]{3,2,1,0:T(8,128)(2,1)S(1)} %far_loads.1), channel_id=1, source_target_pairs={{0,13},{1,12},{2,15},{3,14},{4,9},{5,8},{6,11},{7,10},{8,5},{9,4},... | collective-permute-start | bytes 98312 | tf_op jit(solution)/shard_map/ppermute | solution.py:213
  12.3 4.1 %collective-permute-start.5 = (bf16[2,32,128]{2,1,0:T(8,128)(2,1)S(1)}, bf16[2,32,128]{2,1,0:T(8,128)(2,1)S(1)}, u32[]{:S(2)}, u32[]{:S(2)}) collective-permute-start(bf16[2,32,128]{2,1,0:T(8,128)(2,1)S(1)} %get-tuple-element.27), channel_id=1, source_target_pairs={{0,9},{1,8},{2,11},{3,10},{4,13},{5,12},{6,15},{7,14},{8,1},{9,0},... | collective-permute-start | bytes 49160 | tf_op jit(solution)/shard_map/ppermute | solution.py:213
  12.4 4.1 %collective-permute-start.6 = (bf16[2,32,128]{2,1,0:T(8,128)(2,1)S(1)}, bf16[2,32,128]{2,1,0:T(8,128)(2,1)S(1)}, u32[]{:S(2)}, u32[]{:S(2)}) collective-permute-start(bf16[2,32,128]{2,1,0:T(8,128)(2,1)S(1)} %get-tuple-element.28), channel_id=1, source_target_pairs={{0,4},{1,5},{2,6},{3,7},{4,0},{5,1},{6,2},{7,3},{8,12},{9,13},{10,... | collective-permute-start | bytes 49160 | tf_op jit(solution)/shard_map/ppermute | solution.py:213
  14.5 2.0 %collective-permute-start.7 = (bf16[2,32,128]{2,1,0:T(8,128)(2,1)S(1)}, bf16[2,32,128]{2,1,0:T(8,128)(2,1)S(1)}, u32[]{:S(2)}, u32[]{:S(2)}) collective-permute-start(bf16[2,32,128]{2,1,0:T(8,128)(2,1)S(1)} %get-tuple-element.29), channel_id=1, source_target_pairs={{0,1},{1,0},{2,3},{3,2},{4,5},{5,4},{6,7},{7,6},{8,9},{9,8},{10,11... | collective-permute-start | bytes 49160 | tf_op jit(solution)/shard_map/ppermute | solution.py:213
  16.5 5.3 %copy-start.2 = (bf16[8,128,128]{2,1,0:T(8,128)(2,1)S(1)}, bf16[8,128,128]{2,1,0:T(8,128)(2,1)}, u32[]{:S(2)}) copy-start(bf16[8,128,128]{2,1,0:T(8,128)(2,1)} %refs_4_.1) | copy-start | bytes 786436
  16.5 4.1 %collective-permute-start.8 = (f32[32,128]{1,0:T(8,128)S(1)}, f32[32,128]{1,0:T(8,128)S(1)}, u32[]{:S(2)}, u32[]{:S(2)}) collective-permute-start(f32[32,128]{1,0:T(8,128)S(1)} %get-tuple-element.30), channel_id=1, source_target_pairs={{0,19},{1,18},{2,17},{3,16},{4,23},{5,22},{6,21},{7,20},{8,27},{9,... | collective-permute-start | bytes 49160 | tf_op jit(solution)/shard_map/ppermute | solution.py:222
  18.0 3.7 %collective-permute-start.9 = (f32[32,128]{1,0:T(8,128)S(1)}, f32[32,128]{1,0:T(8,128)S(1)}, u32[]{:S(2)}, u32[]{:S(2)}) collective-permute-start(f32[32,128]{1,0:T(8,128)S(1)} %get-tuple-element.31), channel_id=1, source_target_pairs={{0,16},{1,17},{2,18},{3,19},{4,20},{5,21},{6,22},{7,23},{8,24},{9,... | collective-permute-start | bytes 49160 | tf_op jit(solution)/shard_map/ppermute | solution.py:222
  18.6 3.2 %collective-permute-start.10 = (f32[32,128]{1,0:T(8,128)S(1)}, f32[32,128]{1,0:T(8,128)S(1)}, u32[]{:S(2)}, u32[]{:S(2)}) collective-permute-start(f32[32,128]{1,0:T(8,128)S(1)} %get-tuple-element.32), channel_id=1, source_target_pairs={{0,3},{1,2},{2,1},{3,0},{4,7},{5,6},{6,5},{7,4},{8,11},{9,10},{10,... | collective-permute-start | bytes 49160 | tf_op jit(solution)/shard_map/ppermute | solution.py:222

commit v22 on v21

--- a/solution.py
+++ b/solution.py
@@ -138,27 +138,28 @@
     products = {pair: pair_product(pair) for pair in pairs}
     copy.wait()
     for pair, product in products.items():
-        for i in (pair, pair + 1):
-            total = product[(i - pair) * TILE : (i - pair + 1) * TILE]
-            places, sums = [], []
+        places, sums = [], []
+        for which in range(2):
+            total = product[which * TILE : (which + 1) * TILE]
             for s in range(splines):
-                code = code_ref[i, s]
-                place = code >> 1
+                code = code_ref[pair + which, s]
+                place = (which, code >> 1)
                 added = jnp.where(upper == (code & 1), total[:, s * width : (s + 1) * width], 0.0)
                 places.append(place)
                 sums.append(acc[place] + added)
-            for place, value in zip(places, sums):
-                acc[place] = value
-    tiles = acc.shape[0] // 2
+        for place, value in zip(places, sums):
+            acc[place] = value
+    tiles = acc.shape[1] // 2
     size = pair_ref.shape[0] * pair_ref.shape[1] // TILE
-    pair_ref[...] = acc[tiles : tiles + size].reshape(pair_ref.shape).astype(pair_ref.dtype)
+    kept = acc[0, tiles : tiles + size] + acc[1, tiles : tiles + size]
+    pair_ref[...] = kept.reshape(pair_ref.shape).astype(pair_ref.dtype)
 
 
 def far_kernel(acc, far_ref):
-    tiles, size = acc.shape[0] // 2, far_ref.shape[1] * far_ref.shape[2] // TILE
+    tiles, size = acc.shape[1] // 2, far_ref.shape[1] * far_ref.shape[2] // TILE
     for which in range(2):
         group = slice((which + 1) * tiles - size, (which + 1) * tiles)
-        far_ref[which] = acc[group].reshape(far_ref.shape[1:]).astype(far_ref.dtype)
+        far_ref[which] = (acc[0, group] + acc[1, group]).reshape(far_ref.shape[1:]).astype(far_ref.dtype)
 
 
 def split_kernel(acc, got_ref, *out_refs):
@@ -167,7 +168,8 @@
     for step, out_ref in enumerate(out_refs):
         for place in range(size):
             index = step * size + place
-            held = acc[index * height : (index + 1) * height].reshape(out_ref.shape[1:])
+            rows = slice(index * height, (index + 1) * height)
+            held = (acc[0, rows] + acc[1, rows]).reshape(out_ref.shape[1:])
             out_ref[place] = (held + got_ref[index].astype(jnp.float32)).astype(out_ref.dtype)
 
 
@@ -289,7 +291,7 @@
         functools.partial(spline_kernel, rhs),
         out_shape=(
             jax.ShapeDtypeStruct((rows, width), f32),
-            jax.ShapeDtypeStruct((panels * struct_rows // TILE, TILE, width), f32),
+            jax.ShapeDtypeStruct((2, panels * struct_rows // TILE, TILE, width), f32),
             jax.ShapeDtypeStruct((2 * (steps - 1), struct_rows, width), bf16),
         ),
         in_specs=[VMEM] * 7,

time: 22.7 us -> 22.8 us (level)
  no operation moved by 1% of the time
where the time goes in v22:
time: 22.8 us; the launch traced here: 22.6 us
  starting transfers between devices  13.6 us (60%)
  waiting for transfers between devices  5.3 us (23%)
  Pallas kernels  2.22 us (10%)
  between operations  0.81 us (4%)
  other arithmetic  0.68 us (3%)
    ppermute x7, starting transfers between devices, swap(): return lax.ppermute(value, 'panel', [(i, i ^ apart) for i in range(panels)])  7.55 us
    ppermute x7, waiting for transfers between devices, swap(): return lax.ppermute(value, 'panel', [(i, i ^ apart) for i in range(panels)])  3.72 us
    ppermute x3, starting transfers between devices, mach_swap(): return lax.ppermute(value, ('mach', 'panel'), pairs)  3.03 us
    ppermute x1, starting transfers between devices, on_device(): lax.ppermute(own, ('mach', 'panel'), [(mach * panels + i, (mach ^ (i in b...  3 us
    ppermute x3, waiting for transfers between devices, mach_swap(): return lax.ppermute(value, ('mach', 'panel'), pairs)  1.58 us
    pallas_call x1, Pallas kernels, on_device(): pl.pallas_call(functools.partial(inverse_kernel, rhs, machs), out_shape=j...  0.76 us
    pallas_call x1, Pallas kernels, on_device(): pl.pallas_call(functools.partial(spline_kernel, rhs), out_shape=(jax.Shap...  0.7 us
    mul x1, other arithmetic, on_device(): sums.reshape(adjoint.shape) * trim_mask[0].astype(f32)[None, None, :, None]  0.68 us
  transfers between devices with their start and end apart: 11, of which 7 were waited for; matrix products, arithmetic and copies ran while one was open for 3% of the time, Pallas kernels for 3%

profile of v22, /device:TPU:0, one launch (start us, length us, event | category | flops | bytes accessed | tf_op | source)
XLA Modules:
  0.0 22.6 jit_solution(13900470014287787873)
XLA Ops:
  0.6 0.0 copy-start.3
  0.6 0.0 copy-start.4
  0.7 0.0 copy-start.5
  0.7 0.0 copy-start.6
  0.7 3.0 %collective-permute-start = (bf16[32,128]{1,0:T(8,128)(2,1)}, bf16[32,128]{1,0:T(8,128)(2,1)S(1)}, u32[]{:S(2)}, u32[]{:S(2)}) collective-permute-start(bf16[32,128]{1,0:T(8,128)(2,1)} %bitcast.9), channel_id=1, source_target_pairs={{0,16},{1,2},{2,1},{3,4},{4,3},{5,6},{6,5},{7,8},{8,7},{9,10},{10,... | collective-permute-start | bytes 24584 | tf_op jit(solution)/shard_map/ppermute | solution.py:244
  3.7 1.9 %collective-permute-start.1 = (bf16[32,128]{1,0:T(8,128)(2,1)}, bf16[32,128]{1,0:T(8,128)(2,1)S(1)}, u32[]{:S(2)}, u32[]{:S(2)}) collective-permute-start(bf16[32,128]{1,0:T(8,128)(2,1)} %bitcast.10), channel_id=1, source_target_pairs={{0,8},{1,9},{2,10},{3,11},{4,12},{5,13},{6,14},{7,15},{8,0},{9,1},... | collective-permute-start | bytes 24584 | tf_op jit(solution)/shard_map/ppermute | solution.py:215
  5.6 0.5 %collective-permute-start.2 = (bf16[32,128]{1,0:T(8,128)(2,1)}, bf16[32,128]{1,0:T(8,128)(2,1)S(1)}, u32[]{:S(2)}, u32[]{:S(2)}) collective-permute-start(bf16[32,128]{1,0:T(8,128)(2,1)} %bitcast.11), channel_id=1, source_target_pairs={{0,1},{1,0},{2,3},{3,2},{4,5},{5,4},{6,7},{7,6},{8,9},{9,8},{10,11... | collective-permute-start | bytes 24584 | tf_op jit(solution)/shard_map/ppermute | solution.py:215
  6.2 0.0 copy-start.1
  6.2 0.2 %pick_rows.1 = (bf16[192,128]{1,0:T(8,128)(2,1)S(1)}, f32[16,128]{1,0:T(8,128)S(1)}, bf16[32,128]{1,0:T(8,128)(2,1)S(1)}, s32[8,6]{1,0:T(8,128)S(1)}) custom-call(bf16[32,8]{1,0:T(8,128)(2,1)S(1)} %row_order.1.expand_ref, s32[8,8]{1,0:T(8,128)S(1)} %copy-done.4, s32[1,4]{1,0:T(1,128)S(1)} %copy-done.7, bf16[32,128]{1,0:T(8,128)(2,1)S(1)} %bitcast.12, ...), custom_call_target="tpu_custom_call" | custom-call | flops 1000000 | bytes 131072 | tf_op jit(solution)/shard_map/pick_rows/pallas_call | solution.py:265
  6.5 0.0 collective-permute-done.cross_ref._
  6.5 0.7 %collective-permute-done.2.pair_ref = bf16[32,128]{1,0:T(8,128)(2,1)S(1)} collective-permute-done((bf16[32,128]{1,0:T(8,128)(2,1)}, bf16[32,128]{1,0:T(8,128)(2,1)S(1)}, u32[]{:S(2)}, u32[]{:S(2)}) %collective-permute-start.2) | collective-permute-done | bytes 8224 | tf_op jit(solution)/shard_map/ppermute | solution.py:215
  7.2 0.5 %near_field.1.part_ref = f32[32,128]{1,0:T(8,128)S(1)} custom-call(bf16[192,128]{1,0:T(8,128)(2,1)S(1)} %get-tuple-element.19.hot_ref, bf16[32,128]{1,0:T(8,128)(2,1)S(1)} %get-tuple-element.20.own_ref, bf16[32,128]{1,0:T(8,128)(2,1)S(1)} %collective-permute-done.2.pair_ref, bf16[32,128]{1,0:T(8,128)(2,1)S(1)} %collective-permute-done.cross_ref._, ...), custom_call_target="tpu_custom_call" | custom-call | flops 1000000 | bytes 131072 | tf_op jit(solution)/shard_map/near_field/pallas_call | solution.py:279
  7.6 0.8 %collective-permute-done.1.mirror_ref = bf16[32,128]{1,0:T(8,128)(2,1)S(1)} collective-permute-done((bf16[32,128]{1,0:T(8,128)(2,1)}, bf16[32,128]{1,0:T(8,128)(2,1)S(1)}, u32[]{:S(2)}, u32[]{:S(2)}) %collective-permute-start.1) | collective-permute-done | bytes 8224 | tf_op jit(solution)/shard_map/ppermute | solution.py:215
  8.5 0.7 %spline_loads.1 = (f32[32,128]{1,0:T(8,128)S(1)}, f32[2,64,8,128]{3,2,1,0:T(8,128)S(1)}, bf16[6,32,128]{2,1,0:T(8,128)(2,1)S(1)}) custom-call(bf16[32,128]{1,0:T(8,128)(2,1)S(1)} %collective-permute-done.cross_ref._, bf16[32,128]{1,0:T(8,128)(2,1)S(1)} %collective-permute-done.1.mirror_ref, s32[8,6]{1,0:T(8,128)S(1)} %get-tuple-element.18.code_vmem, ...), custom_call_target="tpu_custom_call" | custom-call | flops 1000000 | bytes 131072 | tf_op jit(solution)/shard_map/spline_loads/pallas_call | solution.py:290
  9.2 0.1 collective-permute-start.3
  9.3 3.1 %collective-permute-start.4 = (bf16[2,2,32,128]{3,2,1,0:T(8,128)(2,1)S(1)}, bf16[2,2,32,128]{3,2,1,0:T(8,128)(2,1)S(1)}, u32[]{:S(2)}, u32[]{:S(2)}) collective-permute-start(bf16[2,2,32,128]{3,2,1,0:T(8,128)(2,1)S(1)} %far_loads.1), channel_id=1, source_target_pairs={{0,13},{1,12},{2,15},{3,14},{4,9},{5,8},{6,11},{7,10},{8,5},{9,4},... | collective-permute-start | bytes 98312 | tf_op jit(solution)/shard_map/ppermute | solution.py:215
  12.4 0.0 collective-permute-done.3.got_ref
  12.4 0.1 collective-permute-start.5
  12.5 1.4 %collective-permute-start.6 = (bf16[2,32,128]{2,1,0:T(8,128)(2,1)S(1)}, bf16[2,32,128]{2,1,0:T(8,128)(2,1)S(1)}, u32[]{:S(2)}, u32[]{:S(2)}) collective-permute-start(bf16[2,32,128]{2,1,0:T(8,128)(2,1)S(1)} %get-tuple-element.28), channel_id=1, source_target_pairs={{0,4},{1,5},{2,6},{3,7},{4,0},{5,1},{6,2},{7,3},{8,12},{9,13},{10,... | collective-permute-start | bytes 49160 | tf_op jit(solution)/shard_map/ppermute | solution.py:215
  13.8 0.6 %collective-permute-done.4.far_ref = bf16[2,2,32,128]{3,2,1,0:T(8,128)(2,1)S(1)} collective-permute-done((bf16[2,2,32,128]{3,2,1,0:T(8,128)(2,1)S(1)}, bf16[2,2,32,128]{3,2,1,0:T(8,128)(2,1)S(1)}, u32[]{:S(2)}, u32[]{:S(2)}) %collective-permute-start.4) | collective-permute-done | bytes 32800 | tf_op jit(solution)/shard_map/ppermute | solution.py:215
  14.5 0.5 %collective-permute-start.7 = (bf16[2,32,128]{2,1,0:T(8,128)(2,1)S(1)}, bf16[2,32,128]{2,1,0:T(8,128)(2,1)S(1)}, u32[]{:S(2)}, u32[]{:S(2)}) collective-permute-start(bf16[2,32,128]{2,1,0:T(8,128)(2,1)S(1)} %get-tuple-element.29), channel_id=1, source_target_pairs={{0,1},{1,0},{2,3},{3,2},{4,5},{5,4},{6,7},{7,6},{8,9},{9,8},{10,11... | collective-permute-start | bytes 49160 | tf_op jit(solution)/shard_map/ppermute | solution.py:215
  15.0 1.6 %collective-permute-done.5.refs_0_ = bf16[2,32,128]{2,1,0:T(8,128)(2,1)S(1)} collective-permute-done((bf16[2,32,128]{2,1,0:T(8,128)(2,1)S(1)}, bf16[2,32,128]{2,1,0:T(8,128)(2,1)S(1)}, u32[]{:S(2)}, u32[]{:S(2)}) %collective-permute-start.5) | collective-permute-done | bytes 16416 | tf_op jit(solution)/shard_map/ppermute | solution.py:215
  16.5 0.0 collective-permute-done.6.refs_1_
  16.5 0.0 collective-permute-done.7.got_ref
  16.6 1.5 %collective-permute-start.8 = (f32[32,128]{1,0:T(8,128)S(1)}, f32[32,128]{1,0:T(8,128)S(1)}, u32[]{:S(2)}, u32[]{:S(2)}) collective-permute-start(f32[32,128]{1,0:T(8,128)S(1)} %get-tuple-element.30), channel_id=1, source_target_pairs={{0,19},{1,18},{2,17},{3,16},{4,23},{5,22},{6,21},{7,20},{8,27},{9,... | collective-permute-start | bytes 49160 | tf_op jit(solution)/shard_map/ppermute | solution.py:224
  18.0 0.7 %collective-permute-start.9 = (f32[32,128]{1,0:T(8,128)S(1)}, f32[32,128]{1,0:T(8,128)S(1)}, u32[]{:S(2)}, u32[]{:S(2)}) collective-permute-start(f32[32,128]{1,0:T(8,128)S(1)} %get-tuple-element.31), channel_id=1, source_target_pairs={{0,16},{1,17},{2,18},{3,19},{4,20},{5,21},{6,22},{7,23},{8,24},{9,... | collective-permute-start | bytes 49160 | tf_op jit(solution)/shard_map/ppermute | solution.py:224
  18.7 0.9 %collective-permute-start.10 = (f32[32,128]{1,0:T(8,128)S(1)}, f32[32,128]{1,0:T(8,128)S(1)}, u32[]{:S(2)}, u32[]{:S(2)}) collective-permute-start(f32[32,128]{1,0:T(8,128)S(1)} %get-tuple-element.32), channel_id=1, source_target_pairs={{0,3},{1,2},{2,1},{3,0},{4,7},{5,6},{6,5},{7,4},{8,11},{9,10},{10,... | collective-permute-start | bytes 49160 | tf_op jit(solution)/shard_map/ppermute | solution.py:224
  19.6 0.7 %broadcast_multiply_fusion = f32[1,8,4,128]{3,2,1,0:T(4,128)} fusion(f32[1,8,4,128]{3,2,1,0:T(4,128)S(1)} %bitcast.8, f32[4]{0:T(128)S(1)} %convert_bitcast_fusion), kind=kLoop, calls=%fused_computation | loop fusion | flops 4096 | bytes 32784 | tf_op jit(solution)/shard_map/mul | solution.py:316
  20.3 0.4 %collective-permute-done.8.refs_0_ = f32[32,128]{1,0:T(8,128)S(1)} collective-permute-done((f32[32,128]{1,0:T(8,128)S(1)}, f32[32,128]{1,0:T(8,128)S(1)}, u32[]{:S(2)}, u32[]{:S(2)}) %collective-permute-start.8) | collective-permute-done | bytes 16416 | tf_op jit(solution)/shard_map/ppermute | solution.py:224
  20.7 1.1 %collective-permute-done.9.refs_1_ = f32[32,128]{1,0:T(8,128)S(1)} collective-permute-done((f32[32,128]{1,0:T(8,128)S(1)}, f32[32,128]{1,0:T(8,128)S(1)}, u32[]{:S(2)}, u32[]{:S(2)}) %collective-permute-start.9) | collective-permute-done | bytes 16416 | tf_op jit(solution)/shard_map/ppermute | solution.py:224
  21.8 0.1 collective-permute-done.10.refs_2_
  21.9 0.8 %struct_solve.1 = f32[32,128]{1,0:T(8,128)} custom-call(f32[32,128]{1,0:T(8,128)S(1)} %collective-permute-done.8.refs_0_, f32[32,128]{1,0:T(8,128)S(1)} %collective-permute-done.9.refs_1_, f32[32,128]{1,0:T(8,128)S(1)} %collective-permute-done.10.refs_2_, f32[32,128]{1,0:T(8,128)S(1)} %get-tuple-element.33.refs_3_, bf16[8,128,128]{2,1,0:T(8,128)(2,1)S(1)} %copy-done.2), custom_call_target="tpu_custom_call" | custom-call | flops 1000000 | bytes 131072 | tf_op jit(solution)/shard_map/struct_solve/pallas_call | solution.py:365
  (18 shorter events, 0.1 us)
Async XLA Ops:
  0.6 5.5 %copy-start.3 = (bf16[1,8,4,128]{3,2,1,0:T(4,128)(2,1)S(1)}, bf16[1,8,4,128]{3,2,1,0:T(4,128)(2,1)}, u32[]{:S(2)}) copy-start(bf16[1,8,4,128]{3,2,1,0:T(4,128)(2,1)} %param.8) | copy-start | bytes 24580
  0.6 5.5 %copy-start.4 = (s32[8,8]{1,0:T(8,128)S(1)}, s32[8,8]{1,0:T(8,128)}, u32[]{:S(2)}) copy-start(s32[8,8]{1,0:T(8,128)} %pattern_ref.1) | copy-start | bytes 772
  0.7 5.5 %copy-start.5 = (s32[8,6]{1,0:T(8,128)S(1)}, s32[8,6]{1,0:T(8,128)}, u32[]{:S(2)}) copy-start(s32[8,6]{1,0:T(8,128)} %owner_ref.1) | copy-start | bytes 580
  0.7 5.5 %copy-start.6 = (s32[8,6]{1,0:T(8,128)S(1)}, s32[8,6]{1,0:T(8,128)}, u32[]{:S(2)}) copy-start(s32[8,6]{1,0:T(8,128)} %local_ref.1) | copy-start | bytes 580
  0.7 5.5 %copy-start.7 = (s32[1,4]{1,0:T(1,128)S(1)}, s32[1,4]{1,0:T(1,128)}, u32[]{:S(2)}) copy-start(s32[1,4]{1,0:T(1,128)} %trim_ref.1) | copy-start | bytes 52
  0.7 6.5 %copy-start = (bf16[1,8,8,128,128]{4,3,2,1,0:T(8,128)(2,1)S(1)}, bf16[1,8,8,128,128]{4,3,2,1,0:T(8,128)(2,1)}, u32[]{:S(2)}) copy-start(bf16[1,8,8,128,128]{4,3,2,1,0:T(8,128)(2,1)} %param.9) | copy-start | bytes 6291460
  0.7 5.8 %collective-permute-start = (bf16[32,128]{1,0:T(8,128)(2,1)}, bf16[32,128]{1,0:T(8,128)(2,1)S(1)}, u32[]{:S(2)}, u32[]{:S(2)}) collective-permute-start(bf16[32,128]{1,0:T(8,128)(2,1)} %bitcast.9), channel_id=1, source_target_pairs={{0,16},{1,2},{2,1},{3,4},{4,3},{5,6},{6,5},{7,8},{8,7},{9,10},{10,... | collective-permute-start | bytes 24584 | tf_op jit(solution)/shard_map/ppermute | solution.py:244
  3.7 4.8 %collective-permute-start.1 = (bf16[32,128]{1,0:T(8,128)(2,1)}, bf16[32,128]{1,0:T(8,128)(2,1)S(1)}, u32[]{:S(2)}, u32[]{:S(2)}) collective-permute-start(bf16[32,128]{1,0:T(8,128)(2,1)} %bitcast.10), channel_id=1, source_target_pairs={{0,8},{1,9},{2,10},{3,11},{4,12},{5,13},{6,14},{7,15},{8,0},{9,1},... | collective-permute-start | bytes 24584 | tf_op jit(solution)/shard_map/ppermute | solution.py:215
  5.6 1.5 %collective-permute-start.2 = (bf16[32,128]{1,0:T(8,128)(2,1)}, bf16[32,128]{1,0:T(8,128)(2,1)S(1)}, u32[]{:S(2)}, u32[]{:S(2)}) collective-permute-start(bf16[32,128]{1,0:T(8,128)(2,1)} %bitcast.11), channel_id=1, source_target_pairs={{0,1},{1,0},{2,3},{3,2},{4,5},{5,4},{6,7},{7,6},{8,9},{9,8},{10,11... | collective-permute-start | bytes 24584 | tf_op jit(solution)/shard_map/ppermute | solution.py:215
  6.2 2.3 %copy-start.1 = (bf16[8,6,128,128]{3,2,1,0:T(8,128)(2,1)S(1)}, bf16[8,6,128,128]{3,2,1,0:T(8,128)(2,1)}, u32[]{:S(2)}) copy-start(bf16[8,6,128,128]{3,2,1,0:T(8,128)(2,1)} %spline_ref.1) | copy-start | bytes 4718596
  9.2 3.2 %collective-permute-start.3 = (bf16[6,32,128]{2,1,0:T(8,128)(2,1)S(1)}, bf16[6,32,128]{2,1,0:T(8,128)(2,1)S(1)}, u32[]{:S(2)}, u32[]{:S(2)}) collective-permute-start(bf16[6,32,128]{2,1,0:T(8,128)(2,1)S(1)} %get-tuple-element.24), channel_id=1, source_target_pairs={{0,1},{1,0},{2,3},{3,2},{4,5},{5,4},{6,7},{7,6},{8,9},{9,8},{10,11... | collective-permute-start | bytes 147464 | tf_op jit(solution)/shard_map/ppermute | solution.py:215
  9.3 5.2 %collective-permute-start.4 = (bf16[2,2,32,128]{3,2,1,0:T(8,128)(2,1)S(1)}, bf16[2,2,32,128]{3,2,1,0:T(8,128)(2,1)S(1)}, u32[]{:S(2)}, u32[]{:S(2)}) collective-permute-start(bf16[2,2,32,128]{3,2,1,0:T(8,128)(2,1)S(1)} %far_loads.1), channel_id=1, source_target_pairs={{0,13},{1,12},{2,15},{3,14},{4,9},{5,8},{6,11},{7,10},{8,5},{9,4},... | collective-permute-start | bytes 98312 | tf_op jit(solution)/shard_map/ppermute | solution.py:215
  12.4 4.1 %collective-permute-start.5 = (bf16[2,32,128]{2,1,0:T(8,128)(2,1)S(1)}, bf16[2,32,128]{2,1,0:T(8,128)(2,1)S(1)}, u32[]{:S(2)}, u32[]{:S(2)}) collective-permute-start(bf16[2,32,128]{2,1,0:T(8,128)(2,1)S(1)} %get-tuple-element.27), channel_id=1, source_target_pairs={{0,9},{1,8},{2,11},{3,10},{4,13},{5,12},{6,15},{7,14},{8,1},{9,0},... | collective-permute-start | bytes 49160 | tf_op jit(solution)/shard_map/ppermute | solution.py:215
  12.5 4.1 %collective-permute-start.6 = (bf16[2,32,128]{2,1,0:T(8,128)(2,1)S(1)}, bf16[2,32,128]{2,1,0:T(8,128)(2,1)S(1)}, u32[]{:S(2)}, u32[]{:S(2)}) collective-permute-start(bf16[2,32,128]{2,1,0:T(8,128)(2,1)S(1)} %get-tuple-element.28), channel_id=1, source_target_pairs={{0,4},{1,5},{2,6},{3,7},{4,0},{5,1},{6,2},{7,3},{8,12},{9,13},{10,... | collective-permute-start | bytes 49160 | tf_op jit(solution)/shard_map/ppermute | solution.py:215
  14.5 2.1 %collective-permute-start.7 = (bf16[2,32,128]{2,1,0:T(8,128)(2,1)S(1)}, bf16[2,32,128]{2,1,0:T(8,128)(2,1)S(1)}, u32[]{:S(2)}, u32[]{:S(2)}) collective-permute-start(bf16[2,32,128]{2,1,0:T(8,128)(2,1)S(1)} %get-tuple-element.29), channel_id=1, source_target_pairs={{0,1},{1,0},{2,3},{3,2},{4,5},{5,4},{6,7},{7,6},{8,9},{9,8},{10,11... | collective-permute-start | bytes 49160 | tf_op jit(solution)/shard_map/ppermute | solution.py:215
  16.5 5.3 %copy-start.2 = (bf16[8,128,128]{2,1,0:T(8,128)(2,1)S(1)}, bf16[8,128,128]{2,1,0:T(8,128)(2,1)}, u32[]{:S(2)}) copy-start(bf16[8,128,128]{2,1,0:T(8,128)(2,1)} %refs_4_.1) | copy-start | bytes 786436
  16.6 4.1 %collective-permute-start.8 = (f32[32,128]{1,0:T(8,128)S(1)}, f32[32,128]{1,0:T(8,128)S(1)}, u32[]{:S(2)}, u32[]{:S(2)}) collective-permute-start(f32[32,128]{1,0:T(8,128)S(1)} %get-tuple-element.30), channel_id=1, source_target_pairs={{0,19},{1,18},{2,17},{3,16},{4,23},{5,22},{6,21},{7,20},{8,27},{9,... | collective-permute-start | bytes 49160 | tf_op jit(solution)/shard_map/ppermute | solution.py:224
  18.0 3.7 %collective-permute-start.9 = (f32[32,128]{1,0:T(8,128)S(1)}, f32[32,128]{1,0:T(8,128)S(1)}, u32[]{:S(2)}, u32[]{:S(2)}) collective-permute-start(f32[32,128]{1,0:T(8,128)S(1)} %get-tuple-element.31), channel_id=1, source_target_pairs={{0,16},{1,17},{2,18},{3,19},{4,20},{5,21},{6,22},{7,23},{8,24},{9,... | collective-permute-start | bytes 49160 | tf_op jit(solution)/shard_map/ppermute | solution.py:224
  18.7 3.2 %collective-permute-start.10 = (f32[32,128]{1,0:T(8,128)S(1)}, f32[32,128]{1,0:T(8,128)S(1)}, u32[]{:S(2)}, u32[]{:S(2)}) collective-permute-start(f32[32,128]{1,0:T(8,128)S(1)} %get-tuple-element.32), channel_id=1, source_target_pairs={{0,3},{1,2},{2,1},{3,0},{4,7},{5,6},{6,5},{7,4},{8,11},{9,10},{10,... | collective-permute-start | bytes 49160 | tf_op jit(solution)/shard_map/ppermute | solution.py:224
